TPU v7x, 32 devices: a whole 2x2x4 slice. The times are simulated.
32 devices in a mesh: seq: 8 (over z, y), hx: 4 (over x, core).
Axes of the slice: x: 2, y: 2, z: 4, core: 2. Of those that a mesh axis runs over, the one named last changes fastest.
Arguments:
- queries: bfloat16 [1024, 4096], P('seq', 'hx'), may hold values from -6 to 6
- keys: bfloat16 [1024, 4096], P('seq', 'hx'), may hold values from -6 to 6
- values: bfloat16 [1024, 4096], P('seq', 'hx'), may hold values from -6 to 6
- log_decay: float32 [1024, 32], P('seq', 'hx'), may hold values from -1 to 0
- doc_ids: int32 [1024], P('seq'), may hold values from 0 to 3, as said below
- residual: bfloat16 [1024, 6144], P('seq'), may hold values from -6 to 6
- out_weight: bfloat16 [4096, 6144], P('hx'), may hold values from -0.09375 to 0.09375
- norm_gain: float32 [6144], replicated, may hold values from 0.1 to 1.9
- expert_ids: int32 [1024, 2], P('seq'), may hold values from 0 to 3, all different within a row; in each aligned block of 128 rows (0 to 127, 128 to 255, ...) at most 80 rows name the same one
- route_weight: float32 [1024, 2], P('seq'), may hold values from 0.2 to 1
- w_gate: bfloat16 [4, 6144, 4608], P('hx', None, 'seq'), may hold values from -0.078125 to 0.078125
- w_up: bfloat16 [4, 6144, 4608], P('hx', None, 'seq'), may hold values from -0.078125 to 0.078125
- w_down: bfloat16 [4, 4608, 6144], P('hx', 'seq'), may hold values from -0.09375 to 0.09375
Outputs:
- layer_out: bfloat16 [1024, 6144], P('seq', 'hx')
Inputs may be any that keep to these rules, and one draw needn't show every extreme that they name: `expert_ids`: the two experts of a token differ; among the tokens of one sequence shard no expert is named more than 80 times, and some expert reaches 80. `doc_ids`: document numbers start at 0, never fall along the sequence, and rise by one at each of three positions.
All inputs are finite; a program needn't handle non-finite values.
Results may differ from a plain program's by a relative error of at most 0.022.
Values may be sent and summed in bfloat16 or wider, within the bound.
No kernel may reach another device: no remote copies, remote signals or barrier semaphores. Data moves between devices by JAX's collectives and lax.ppermute only.
A program may use at most 128 MiB of HBM per device.

v0:
```python
import jax
import jax.numpy as jnp
from jax import lax
from jax.sharding import PartitionSpec as P

HS = 128


def prefix(shard, axis, join, neutral):
    place = lax.axis_index(axis)
    gathered = jax.tree.map(
        lambda a, kind: lax.all_gather(a.astype(kind), axis),
        shard,
        (jnp.bfloat16, jnp.bfloat16, jnp.bfloat16, jnp.bfloat16),
    )
    state = jax.tree.map(lambda a, e: jnp.zeros_like(a) + jnp.asarray(e, a.dtype), shard, neutral)

    def one(turn, state):
        return join(
            state,
            jax.tree.map(
                lambda a, own: lax.dynamic_index_in_dim(a, turn, 0, False).astype(own.dtype),
                gathered,
                shard,
            ),
        )

    return lax.fori_loop(0, place, one, state)


def link_states(earlier, later):
    through_one, state_one, first_one, last_one = earlier
    through_two, state_two, first_two, last_two = later
    passes = ((last_one < 0) | (first_two < 0) | (last_one == first_two)).astype(jnp.float32)
    through = through_one * through_two * passes
    head_state = passes * through_two[:, None, None] * state_one + state_two
    first_doc = jnp.where(first_one >= 0, first_one, first_two)
    last_doc = jnp.where(last_two >= 0, last_two, last_one)
    return (through, head_state, first_doc, last_doc)


def expert_act(row_block, w_gate, w_up):
    gate_part = jnp.dot(row_block, w_gate[0], preferred_element_type=jnp.float32)
    up_part = jnp.dot(row_block, w_up[0], preferred_element_type=jnp.float32)
    return (jax.nn.silu(gate_part) * up_part).astype(jnp.bfloat16)


def shards(
    queries,
    keys,
    values,
    log_decay,
    doc_ids,
    residual,
    out_weight,
    norm_gain,
    expert_ids,
    route_weight,
    w_gate,
    w_up,
    w_down,
):
    tok_count = queries.shape[0]
    heads_local = log_decay.shape[1]
    query_heads = queries.reshape(tok_count, heads_local, HS)
    key_heads = keys.reshape(tok_count, heads_local, HS)
    value_float = values.reshape(tok_count, heads_local, HS).astype(jnp.float32)
    log_cum = jnp.cumsum(log_decay, axis=0)
    positions = jnp.arange(tok_count)
    allowed = (positions[:, None] >= positions[None, :]) & (doc_ids[:, None] == doc_ids[None, :])
    exponent = jnp.where(allowed[None], log_cum.T[:, :, None] - log_cum.T[:, None, :], -jnp.inf)
    scores = jnp.einsum("thd,shd->hts", query_heads, key_heads, preferred_element_type=jnp.float32)
    intra = jnp.einsum(
        "hts,shd->thd", scores * jnp.exp(exponent), value_float, precision=lax.Precision.HIGHEST
    )
    first_doc = doc_ids[0]
    last_doc = doc_ids[tok_count - 1]
    end_weight = (
        jnp.exp(log_cum[tok_count - 1][None, :] - log_cum)
        * (doc_ids == last_doc).astype(jnp.float32)[:, None]
    )
    key_weighted = key_heads.astype(jnp.float32) * end_weight[:, :, None]
    head_state = jnp.einsum(
        "shi,shj->hij", key_weighted, value_float, precision=lax.Precision.HIGHEST
    )
    through = jnp.exp(log_cum[tok_count - 1]) * (first_doc == last_doc).astype(jnp.float32)
    first_float = jnp.full((1,), first_doc).astype(jnp.float32)
    last_float = jnp.full((1,), last_doc).astype(jnp.float32)
    identity = (
        jnp.ones((heads_local,), jnp.float32),
        jnp.zeros_like(head_state),
        jnp.full((1,), -1.0, jnp.float32),
        jnp.full((1,), -1.0, jnp.float32),
    )
    carried = prefix((through, head_state, first_float, last_float), "seq", link_states, identity)
    incoming = carried[1]
    before_doc = carried[3]
    entry_gate = (before_doc[0] == first_float[0]).astype(jnp.float32)
    carry_weight = (
        jnp.exp(log_cum) * (doc_ids == first_doc).astype(jnp.float32)[:, None] * entry_gate
    )
    query_weighted = query_heads.astype(jnp.float32) * carry_weight[:, :, None]
    carried_out = jnp.einsum(
        "thi,hij->thj", query_weighted, incoming, precision=lax.Precision.HIGHEST
    )
    head_out = intra + carried_out
    normed_heads = head_out * lax.rsqrt(
        jnp.mean(head_out * head_out, axis=-1, keepdims=True) + 1e-05
    )
    attn_in = normed_heads.reshape(tok_count, heads_local * HS).astype(jnp.bfloat16)
    expert_count = lax.axis_size("hx")
    capacity = tok_count * 5 // (2 * expert_count)
    flat_ids = expert_ids.reshape(-1)
    choice_count = flat_ids.shape[0]
    one_hot = (flat_ids[:, None] == jnp.arange(expert_count)[None, :]).astype(jnp.int32)
    rank_before = jnp.cumsum(one_hot, axis=0) - one_hot
    slot_index = flat_ids * capacity + jnp.sum(rank_before * one_hot, axis=1)
    token_of = jnp.arange(choice_count) // 2
    slot_match = slot_index[None, :] == jnp.arange(expert_count * capacity)[:, None]
    slot_valid = jnp.any(slot_match, axis=1)
    slot_token = jnp.sum(jnp.where(slot_match, token_of[None, :], 0), axis=1)
    expert_index = lax.axis_index("hx")
    first_slot = slot_index[0::2]
    second_slot = slot_index[1::2]
    row_block = jnp.where(slot_valid[:, None], attn_in[slot_token], jnp.zeros((), jnp.bfloat16))
    attn_slots = lax.psum_scatter(
        jnp.dot(row_block, out_weight, preferred_element_type=jnp.float32).astype(jnp.bfloat16),
        "hx",
        scatter_dimension=0,
        tiled=True,
    ).astype(jnp.float32)
    my_tokens = lax.dynamic_slice_in_dim(slot_token, expert_index * capacity, capacity)
    hidden_slots = residual[my_tokens].astype(jnp.float32) + attn_slots
    normed = (
        hidden_slots
        * lax.rsqrt(jnp.mean(hidden_slots * hidden_slots, axis=-1, keepdims=True) + 1e-06)
        * norm_gain
    ).astype(jnp.bfloat16)
    gathered = lax.all_gather(normed, "seq", axis=0, tiled=True)
    row_block = gathered
    act = expert_act(row_block, w_gate, w_up)
    expert_out = lax.psum_scatter(
        jnp.dot(act, w_down[0], preferred_element_type=jnp.float32).astype(jnp.bfloat16),
        "seq",
        scatter_dimension=0,
        tiled=True,
    ).astype(jnp.float32)
    back_hidden, back_expert = (
        lax.all_to_all(
            hidden_slots.astype(jnp.bfloat16), "hx", split_axis=1, concat_axis=0, tiled=True
        ).astype(hidden_slots.dtype),
        lax.all_to_all(
            expert_out.astype(jnp.bfloat16), "hx", split_axis=1, concat_axis=0, tiled=True
        ).astype(expert_out.dtype),
    )
    layer_out = (
        back_hidden[first_slot]
        + route_weight[:, 0:1] * back_expert[first_slot]
        + route_weight[:, 1:2] * back_expert[second_slot]
    )
    return layer_out.astype(jnp.bfloat16)


def solution(mesh):
    return jax.shard_map(
        shards,
        mesh=mesh,
        in_specs=(
            P("seq", "hx"),
            P("seq", "hx"),
            P("seq", "hx"),
            P("seq", "hx"),
            P("seq"),
            P("seq", None),
            P("hx", None),
            P(),
            P("seq", None),
            P("seq", None),
            P("hx", None, "seq"),
            P("hx", None, "seq"),
            P("hx", "seq", None),
        ),
        out_specs=P("seq", "hx"),
        check_vma=False,
    )
```

profile of v0, /device:TPU:0, one launch (start us, length us, event | category | flops | bytes accessed | tf_op | source)
XLA Modules:
  0.0 477.6 jit_solution(16292115162404517593)
XLA Ops:
  6.6 1.4 fusion.40
  9.3 1.9 compare_convert_fusion.1
  13.5 2.1 convolution_convert_fusion.2
  19.4 23.4 %all-reduce.2 = (bf16[8]{0:T(256)(128)(2,1)S(1)}, bf16[8]{0:T(256)(128)(2,1)S(1)}) all-reduce(bf16[8]{0:T(256)(128)(2,1)S(1)} %dynamic-update-slice, bf16[8]{0:T(256)(128)(2,1)S(1)} %dynamic-update-slice.1), channel_id=2, replica_groups=mesh['seq'=8,'hx'=4] {'seq'}, use_global_device_ids=true, to_apply=%add | all-reduce | flops 16 | bytes 64
  46.0 16.4 %all-gather.3 = bf16[8,1,8]{2,1,0:T(2,128)(2,1)S(1)} all-gather(bf16[1,1,8]{2,1,0:T(2,128)(2,1)S(1)} %get-tuple-element.100), channel_id=1, replica_groups=mesh['seq'=8,'hx'=4] {'seq'}, dimensions={0}, use_global_device_ids=true | all-gather | bytes 144 | tf_op jit(solution)/shard_map/all_gather | solution.py:12
  64.0 4.0 all-gather.9.cloned.1.call-done
  69.6 2.1 gather_fusion.1
  71.7 10.4 %convolution_convert_fusion.1 = bf16[320,6144]{1,0:T(8,128)(2,1)} fusion(bf16[1024,6144]{1,0:T(8,128)(2,1)} %param.21, bf16[320,1024]{1,0:T(8,128)(2,1)S(1)} %gather_fusion.1, pred[320]{0:T(512)(128)(4,1)S(1)} %fusion.23), kind=kOutput, calls=%fused_computation.13 | convolution fusion | flops 4028825600 | bytes 17170752 | tf_op jit(solution)/shard_map/dot_general | solution.py:127
  83.5 69.3 %reduce-scatter.3.cloned.1.call-done = bf16[80,6144]{1,0:T(8,128)(2,1)} async-done(((bf16[320,6144]{1,0:T(8,128)(2,1)}), bf16[80,6144]{1,0:T(8,128)(2,1)}) %reduce-scatter.3.cloned.1.call-update) | async-done | bytes 983056 | tf_op jit(solution)/shard_map/reduce_scatter | solution.py:126
  152.8 1.7 fusion.8
  154.6 1.4 multiply_convert_fusion
  156.2 118.3 %all-gather.7.cloned.1.call-done = bf16[640,6144]{1,0:T(8,128)(2,1)} async-done(((bf16[80,6144]{1,0:T(8,128)(2,1)}), bf16[640,6144]{1,0:T(8,128)(2,1)}) %all-gather.7.cloned.1.call-update) | async-done | bytes 7864336 | tf_op jit(solution)/shard_map/all_gather | solution.py:139
  274.6 10.9 %fusion.6 = f32[640,576]{0,1:T(8,128)S(1)} fusion(bf16[640,6144]{1,0:T(8,128)(2,1)} %all-gather.7.cloned.1.call-done, bf16[1,6144,576]{1,2,0:T(8,128)(2,1)} %param.25), kind=kOutput, calls=%fused_computation.17 | convolution fusion | flops 4529848320 | bytes 16416768 | tf_op jit(solution)/shard_map/dot_general | solution.py:43
  285.5 8.5 %fusion.12 = bf16[640,576]{0,1:T(8,128)(2,1)S(1)} fusion(bf16[640,6144]{1,0:T(8,128)(2,1)S(1)} %copy-done.8, bf16[1,6144,576]{1,2,0:T(8,128)(2,1)} %param.26, f32[640,576]{0,1:T(8,128)S(1)} %fusion.6), kind=kOutput, calls=%fused_computation.24 | convolution fusion | flops 4532060160 | bytes 17154048 | tf_op jit(solution)/shard_map/dot_general | solution.py:44
  294.0 10.5 %convolution_convert_fusion = bf16[640,6144]{1,0:T(8,128)(2,1)} fusion(bf16[640,576]{0,1:T(8,128)(2,1)S(1)} %fusion.12, bf16[1,576,6144]{2,1,0:T(8,128)(2,1)} %param.27), kind=kOutput, calls=%fused_computation.12 | convolution fusion | flops 4533780480 | bytes 15679488 | tf_op jit(solution)/shard_map/dot_general | solution.py:143
  305.7 3.5 all-to-all-start
  309.5 133.8 %reduce-scatter.5.cloned.1.call-done = bf16[80,6144]{1,0:T(8,128)(2,1)} async-done(((bf16[640,6144]{1,0:T(8,128)(2,1)}), bf16[80,6144]{1,0:T(8,128)(2,1)}) %reduce-scatter.5.cloned.1.call-update) | async-done | bytes 983056 | tf_op jit(solution)/shard_map/reduce_scatter | solution.py:142
  443.3 2.2 copy.114
  445.5 4.2 all-to-all-start.1
  450.3 1.7 gather_fusion.2
  452.1 11.6 %all-to-all-done.1 = bf16[80,4,1536]{2,0,1:T(8,128)(2,1)} async-done(((bf16[80,4,1536]{2,0,1:T(8,128)(2,1)}), bf16[80,4,1536]{2,0,1:T(8,128)(2,1)}, u32[]{:S(2)}, u32[]{:S(2)}) %all-to-all-start.1) | async-done | bytes 983072 | tf_op jit(solution)/shard_map/all_to_all | solution.py:152
  465.0 1.8 gather_fusion.3
  466.8 1.7 gather_fusion.4
  468.5 2.6 add_convert_fusion
  (82 shorter events, 16.7 us)
Async XLA Ops:
  6.5 75.8 %copy-start = (bf16[128,6144]{1,0:T(8,128)(2,1)S(1)}, bf16[128,6144]{1,0:T(8,128)(2,1)}, u32[]{:S(2)}) copy-start(bf16[128,6144]{1,0:T(8,128)(2,1)} %param.20) | copy-start | bytes 4718596
  6.5 56.4 %copy-start.6 = (s32[128]{0:T(128)S(1)}, s32[128]{0:T(128)}, u32[]{:S(2)}) copy-start(s32[128]{0:T(128)} %param.19) | copy-start | bytes 1540
  6.5 56.7 %copy-start.3 = (bf16[128,1024]{1,0:T(8,128)(2,1)S(1)}, bf16[128,1024]{1,0:T(8,128)(2,1)}, u32[]{:S(2)}) copy-start(bf16[128,1024]{1,0:T(8,128)(2,1)} %param.17) | copy-start | bytes 786436
  6.5 56.5 %copy-start.4 = (bf16[128,1024]{1,0:T(8,128)(2,1)S(1)}, bf16[128,1024]{1,0:T(8,128)(2,1)}, u32[]{:S(2)}) copy-start(bf16[128,1024]{1,0:T(8,128)(2,1)} %param.15) | copy-start | bytes 786436
  6.5 61.4 %all-gather.9.cloned.1.call-start = ((), (), s32[]{:S(2)}) async-start(), calls=%async_computation.7 | async-start | bytes 2359296 | tf_op jit(solution)/shard_map/all_gather | solution.py:12
  15.5 137.2 %reduce-scatter.3.cloned.1.call-start = ((), (), s32[]{:S(2)}) async-start(), calls=%async_computation.4 | async-start | bytes 4915200 | tf_op jit(solution)/shard_map/reduce_scatter | solution.py:126
  82.2 192.4 %all-gather.7.cloned.1.call-start = ((), (), s32[]{:S(2)}) async-start(), calls=%async_computation.5 | async-start | bytes 8847360 | tf_op jit(solution)/shard_map/all_gather | solution.py:139
  83.5 71.1 %copy-start.5 = (f32[6144]{0:T(1024)S(1)}, f32[6144]{0:T(1024)}, u32[]{:S(2)}) copy-start(f32[6144]{0:T(1024)} %param.22) | copy-start | bytes 73732
  152.8 1.8 copy-start.2
  156.0 287.3 %reduce-scatter.5.cloned.1.call-start = ((), (), s32[]{:S(2)}) async-start(), calls=%async_computation.6 | async-start | bytes 8847360 | tf_op jit(solution)/shard_map/reduce_scatter | solution.py:142
  274.6 10.9 %copy-start.8 = (bf16[640,6144]{1,0:T(8,128)(2,1)S(1)}, bf16[640,6144]{1,0:T(8,128)(2,1)}, u32[]{:S(2)}) copy-start(bf16[640,6144]{1,0:T(8,128)(2,1)} %all-gather.7.cloned.1.call-done) | copy-start | bytes 23592964
  305.7 139.8 %all-to-all-start = ((bf16[80,4,1536]{2,0,1:T(8,128)(2,1)}), bf16[80,4,1536]{2,0,1:T(8,128)(2,1)S(1)}, u32[]{:S(2)}, u32[]{:S(2)}) async-start(bf16[80,4,1536]{2,0,1:T(8,128)(2,1)} %bitcast.116), calls=%async_computation.1 | async-start | bytes 1966080 | tf_op jit(solution)/shard_map/all_to_all | solution.py:149
  309.2 140.8 %copy-start.7 = (f32[128,2]{0,1:T(2,128)S(1)}, f32[128,2]{0,1:T(2,128)}, u32[]{:S(2)}) copy-start(f32[128,2]{0,1:T(2,128)} %param.24) | copy-start | bytes 3076
  445.5 18.1 %all-to-all-start.1 = ((bf16[80,4,1536]{2,0,1:T(8,128)(2,1)}), bf16[80,4,1536]{2,0,1:T(8,128)(2,1)}, u32[]{:S(2)}, u32[]{:S(2)}) async-start(bf16[80,4,1536]{2,0,1:T(8,128)(2,1)} %bitcast.115), calls=%async_computation.3 | async-start | bytes 1966080 | tf_op jit(solution)/shard_map/all_to_all | solution.py:152
  466.8 4.3 copy-start.1
Sparse Core Ops, SparseCore 0:
  15.7 52.1 all-gather.8
  82.3 70.4 reduce-scatter.2
  156.1 118.3 all-gather.6
  304.7 138.5 reduce-scatter.4
where the time goes:
time: 479 us; the launch traced here: 478 us
  waiting for transfers between devices  337 us (70%)
  matrix products  44.7 us (9%)
  blocking collectives  39.8 us (8%)
  local copies, waits for them, and re-layouts  19.7 us (4%)
  between operations  15.4 us (3%)
  other arithmetic  13 us (3%)
  starting transfers between devices  8.08 us (2%)
    reduce_scatter x1, waiting for transfers between devices, shards(): lax.psum_scatter(jnp.dot(act, w_down[0], preferred_element_type=jnp.float...  134 us
    all_gather x1, waiting for transfers between devices, shards(): gathered = lax.all_gather(normed, 'seq', axis=0, tiled=True)  118 us
    reduce_scatter x1, waiting for transfers between devices, shards(): lax.psum_scatter(jnp.dot(row_block, out_weight, preferred_element_type=jn...  69.3 us
    unnamed x1, blocking collectives  23.4 us
    all_gather x1, blocking collectives, prefix(): lax.all_gather(a.astype(kind), axis)  16.4 us
    all_to_all x1, waiting for transfers between devices, shards(): lax.all_to_all(expert_out.astype(jnp.bfloat16), 'hx', split_axis=1, conca...  11.6 us
    dot_general x1, matrix products, expert_act(): jnp.dot(row_block, w_gate[0], preferred_element_type=jnp.float32)  10.9 us
    dot_general x1, matrix products, shards(): jnp.dot(act, w_down[0], preferred_element_type=jnp.float32)  10.5 us
  transfers between devices with their start and end apart: 6, of which 5 were waited for; matrix products, arithmetic and copies ran while one was open for 3% of the time, Pallas kernels for 0%

commit v1 on v0

v1 whole, which is shorter than its diff:
```python
import functools

import jax
import jax.numpy as jnp
from jax import lax
from jax.experimental import pallas as pl
from jax.experimental.pallas import tpu as pltpu
from jax.sharding import PartitionSpec as P

HS = 128
AXES = ("seq", "hx")
HALVES = 2
EXTRA = 16
VMEM_LIMIT = 48 * 1024 * 1024
F32, BF16 = jnp.float32, jnp.bfloat16


def bits(low, high):
    out = []
    bit = high // 2
    while bit >= low:
        out.append(bit)
        bit //= 2
    return out


def exchange(x, mask, count):
    even, odd = mask
    pairs = [(d, d ^ (odd if d & 1 else even)) for d in range(count)]
    return lax.ppermute(x, AXES, pairs)


def total(parts):
    return functools.reduce(lambda a, b: a + b, [p.astype(F32) for p in parts])


def add(a, b):
    return total([a, b]).astype(BF16)


def gather_rows(x, masks, count):
    for mask in masks:
        x = jnp.concatenate([x, exchange(x, mask, count)], axis=0)
    return x


def reduce_rows(x, masks, count):
    for mask in reversed(masks):
        half = x.shape[0] // 2
        x = add(x[:half], exchange(x[half:], mask, count))
    return x


def offsets(masks):
    out = [0]
    for mask in masks:
        out = out + [o ^ mask for o in out]
    return out


def split3(x):
    high = x.astype(BF16)
    rest = x - high.astype(F32)
    mid = rest.astype(BF16)
    low = (rest - mid.astype(F32)).astype(BF16)
    return [high, mid, low]


def whole():
    return pl.BlockSpec(memory_space=pltpu.VMEM)


def column_cumsum(decay):
    tok = decay.shape[0]
    row = lax.broadcasted_iota(jnp.int32, (tok, tok), 0)
    col = lax.broadcasted_iota(jnp.int32, (tok, tok), 1)
    lower = (row >= col).astype(F32)
    return jnp.dot(lower, decay, precision=lax.Precision.HIGHEST, preferred_element_type=F32)


def state_kernel(k_ref, v_ref, decay_ref, doc_col_ref, doc_row_ref, weight_ref, out_ref):
    tok, heads = decay_ref.shape
    chunks = out_ref.shape[0]
    chunk = out_ref.shape[1] - EXTRA
    decay = decay_ref[...]
    log_cum = column_cumsum(decay)
    total = log_cum[tok - 1 : tok, :]
    last = doc_col_ref[tok - 1 : tok, :]
    end_weight = jnp.exp(total - log_cum) * (doc_col_ref[...] == last).astype(F32)
    through = jnp.exp(total)
    doc_row = doc_row_ref[...]
    row = lax.broadcasted_iota(jnp.int32, (EXTRA, HS), 0)
    routing = split3(weight_ref[...])
    fixed = [
        jnp.broadcast_to(doc_row[:, :1].astype(F32), (EXTRA, HS)),
        jnp.broadcast_to(doc_row[:, tok - 1 :].astype(F32), (EXTRA, HS)),
    ] + [jnp.broadcast_to(w.astype(F32), (EXTRA, HS)) for w in routing]
    per_head = chunks // heads
    for h in range(heads):
        lanes = slice(h * HS, (h + 1) * HS)
        weighted = (k_ref[:, lanes].astype(F32) * end_weight[:, h : h + 1]).astype(BF16)
        state = lax.dot_general(
            weighted, v_ref[:, lanes], (((0,), (0,)), ((), ())), preferred_element_type=F32
        ).astype(BF16)
        parts = [
            jnp.broadcast_to(p.astype(F32), (EXTRA, HS)) for p in split3(through[:, h : h + 1])
        ] + fixed
        extra = jnp.zeros((EXTRA, HS), F32)
        for i, part in enumerate(parts):
            extra = jnp.where(row == i, part, extra)
        for j in range(per_head):
            at = h * per_head + j
            out_ref[at, :chunk, :] = state[j * chunk : (j + 1) * chunk, :]
            out_ref[at, chunk:, :] = extra.astype(BF16)


def prefix_kernel(in_ref, out_ref):
    shards_n = in_ref.shape[0]
    chunk = out_ref.shape[1]
    carry = jnp.zeros((chunk, HS), F32)
    before = None
    for s in range(shards_n):
        extra = in_ref[s, chunk:, :].astype(F32)
        decay = extra[0:1] + extra[1:2] + extra[2:3]
        first, last = extra[3:4], extra[4:5]
        if s:
            out_ref[s] = (carry * (before == first).astype(F32)).astype(BF16)
            decay = decay * (before == last).astype(F32)
        else:
            out_ref[s] = carry.astype(BF16)
        carry = decay * carry + in_ref[s, :chunk, :].astype(F32)
        before = last


def intra_kernel(q_ref, k_ref, v_ref, decay_ref, decay_t_ref, doc_col_ref, doc_row_ref, out_ref, qw_ref):
    tok, heads = decay_ref.shape
    log_cum = column_cumsum(decay_ref[...])
    row = lax.broadcasted_iota(jnp.int32, (tok, tok), 0)
    col = lax.broadcasted_iota(jnp.int32, (tok, tok), 1)
    upper = (row <= col).astype(F32)
    log_cum_t = jnp.dot(
        decay_t_ref[...], upper, precision=lax.Precision.HIGHEST, preferred_element_type=F32
    )
    doc_col, doc_row = doc_col_ref[...], doc_row_ref[...]
    allowed = (row >= col) & (doc_col == doc_row)
    carry = jnp.exp(log_cum) * (doc_col == doc_row[:, :1]).astype(F32)
    for h in range(heads):
        lanes = slice(h * HS, (h + 1) * HS)
        scores = lax.dot_general(
            q_ref[:, lanes], k_ref[:, lanes], (((1,), (1,)), ((), ())), preferred_element_type=F32
        )
        exponent = jnp.where(allowed, log_cum[:, h : h + 1] - log_cum_t[h : h + 1, :], -jnp.inf)
        weighted = (scores * jnp.exp(exponent)).astype(BF16)
        out_ref[:, lanes] = jnp.dot(weighted, v_ref[:, lanes], preferred_element_type=F32)
        qw_ref[:, lanes] = (q_ref[:, lanes].astype(F32) * carry[:, h : h + 1]).astype(BF16)


def attend_kernel(intra_ref, qw_ref, state_ref, out_ref):
    heads = state_ref.shape[0]
    for h in range(heads):
        lanes = slice(h * HS, (h + 1) * HS)
        head_out = intra_ref[:, lanes] + jnp.dot(
            qw_ref[:, lanes], state_ref[h], preferred_element_type=F32
        )
        scale = lax.rsqrt(jnp.mean(head_out * head_out, axis=-1, keepdims=True) + 1e-05)
        out_ref[:, lanes] = (head_out * scale).astype(BF16)


def expert_kernel(
    steps, xa_ref, xb_ref, gate_ref, up_ref, down_ref, scale_ref, after_ref, oa_ref, ob_ref, done_ref, gate, up, act
):
    step = pl.program_id(0)
    rows = xa_ref.shape[0]
    over_width = (((1,), (1,)), ((), ()))

    @pl.when(step < steps)
    def _():
        x = jnp.concatenate([xa_ref[...], xb_ref[...]], axis=0)
        gate_part = lax.dot_general(gate_ref[...], x, over_width, preferred_element_type=F32)
        up_part = lax.dot_general(up_ref[...], x, over_width, preferred_element_type=F32)

        @pl.when(step == 0)
        def _():
            gate[...] = gate_part
            up[...] = up_part
            done_ref[...] = after_ref[...]

        @pl.when(step > 0)
        def _():
            gate[...] += gate_part
            up[...] += up_part

        @pl.when(step == steps - 1)
        def _():
            g = gate[...]
            acted = g / (1.0 + jnp.exp(-g)) * up[...] * scale_ref[...]
            act[...] = acted.T.astype(BF16)

    @pl.when(step >= steps)
    def _():
        out = jnp.dot(act[...], down_ref[...], preferred_element_type=F32).astype(BF16)
        oa_ref[...] = out[:rows]
        ob_ref[...] = out[rows:]


def expert(xa, xb, w_gate, w_up, w_down, scale, after):
    rows, width = xa.shape
    hidden = w_gate.shape[1]
    block = min(1024, width)
    steps = width // block
    into = lambda i: jnp.minimum(i, steps - 1)
    out_of = lambda i: jnp.maximum(i - steps, 0)
    return pl.pallas_call(
        functools.partial(expert_kernel, steps),
        grid=(2 * steps,),
        in_specs=[
            pl.BlockSpec((rows, block), lambda i: (0, into(i))),
            pl.BlockSpec((rows, block), lambda i: (0, into(i))),
            pl.BlockSpec((None, hidden, block), lambda i: (0, 0, into(i))),
            pl.BlockSpec((None, hidden, block), lambda i: (0, 0, into(i))),
            pl.BlockSpec((None, hidden, block), lambda i: (0, 0, out_of(i))),
            pl.BlockSpec((1, 2 * rows), lambda i: (0, 0)),
            pl.BlockSpec((8, 128), lambda i: (0, 0)),
        ],
        out_specs=[pl.BlockSpec((rows, block), lambda i: (0, out_of(i)))] * 2
        + [pl.BlockSpec((8, 128), lambda i: (0, 0))],
        out_shape=[jax.ShapeDtypeStruct((rows, width), BF16)] * 2 + [jax.ShapeDtypeStruct((8, 128), F32)],
        scratch_shapes=[
            pltpu.VMEM((hidden, 2 * rows), F32),
            pltpu.VMEM((hidden, 2 * rows), F32),
            pltpu.VMEM((2 * rows, hidden), BF16),
        ],
        compiler_params=pltpu.CompilerParams(vmem_limit_bytes=VMEM_LIMIT),
        cost_estimate=pl.CostEstimate(
            flops=12 * rows * width * hidden,
            bytes_accessed=6 * width * hidden + 8 * rows * width,
            transcendentals=2 * rows * hidden,
        ),
    )(xa, xb, w_gate, w_up, w_down, scale, after)


def call(kernel, out_shapes, *operands):
    return pl.pallas_call(
        kernel,
        in_specs=[whole()] * len(operands),
        out_specs=[whole()] * len(out_shapes),
        out_shape=out_shapes,
        compiler_params=pltpu.CompilerParams(vmem_limit_bytes=VMEM_LIMIT),
    )(*operands)


def shards(
    queries,
    keys,
    values,
    log_decay,
    doc_ids,
    residual,
    out_weight,
    norm_gain,
    expert_ids,
    route_weight,
    w_gate,
    w_up,
    w_down,
):
    n_seq, n_hx = lax.axis_size("seq"), lax.axis_size("hx")
    count = n_seq * n_hx
    inner = max(1, n_seq // 4)
    z_masks = bits(n_hx * inner, count)
    y_masks = bits(n_hx, n_hx * inner)
    x_masks = bits(2, n_hx)
    order_even = z_masks + y_masks + x_masks
    order_odd = z_masks + (x_masks + y_masks if len(x_masks) == len(y_masks) else y_masks + x_masks)
    masks = list(zip(order_even, order_odd))
    core = (1, 1)
    hx_masks = [(m, m) for m in x_masks] + [core]
    hx_index = lax.axis_index("hx")
    device = lax.axis_index("seq") * n_hx + hx_index

    tok_count = queries.shape[0]
    own_count = tok_count // n_hx
    half_count = own_count // HALVES
    heads = log_decay.shape[1]
    chunk = heads * HS // n_seq

    doc_col, doc_row = doc_ids.reshape(tok_count, 1), doc_ids.reshape(1, tok_count)
    own_weight = jnp.sum(jnp.where(expert_ids == hx_index, route_weight, 0.0), axis=1).reshape(1, tok_count)
    shape = jax.ShapeDtypeStruct
    (payload,) = call(
        state_kernel,
        [shape((n_seq, chunk + EXTRA, HS), BF16)],
        keys, values, log_decay, doc_col, doc_row, own_weight,
    )
    arrived = lax.all_to_all(payload, "seq", split_axis=0, concat_axis=0, tiled=True)
    intra, query_weighted = call(
        intra_kernel,
        [shape((tok_count, heads * HS), F32), shape((tok_count, heads * HS), BF16)],
        queries, keys, values, log_decay, log_decay.T, doc_col, doc_row,
    )
    (incoming,) = call(prefix_kernel, [shape((n_seq, chunk, HS), BF16)], arrived)
    incoming = lax.all_to_all(incoming, "seq", split_axis=0, concat_axis=0, tiled=True)

    order = offsets([even for even, _ in hx_masks])

    def by_neighbour(x):
        blocks = [
            lax.dynamic_slice_in_dim(x, (hx_index ^ o) * own_count + i * half_count, half_count)
            for i in range(HALVES)
            for o in order
        ]
        return jnp.concatenate(blocks, axis=0)

    (attn_in,) = call(
        attend_kernel,
        [shape((tok_count, heads * HS), BF16)],
        by_neighbour(intra), by_neighbour(query_weighted), incoming.reshape(heads, HS, HS),
    )
    projected = jnp.dot(attn_in, out_weight, preferred_element_type=F32).astype(BF16)
    own_residual = lax.dynamic_slice_in_dim(residual, hx_index * own_count, own_count)

    extra = arrived[:, chunk + 5 : chunk + 8, :].astype(F32)
    weights = jnp.sum(extra, axis=1).reshape(count, own_count)
    even_off, odd_off = offsets(order_even), offsets(order_odd)
    even_off, odd_off = (
        even_off + [o ^ 1 for o in odd_off],
        odd_off + [o ^ 1 for o in even_off],
    )
    sources = device ^ jnp.where(device & 1 == 1, jnp.array(odd_off), jnp.array(even_off))
    weights = weights[sources].reshape(2, 2, count // 4, HALVES, half_count)

    halves = []
    for i in range(HALVES):
        rows = projected[i * n_hx * half_count : (i + 1) * n_hx * half_count]
        rows = reduce_rows(rows, hx_masks, count)
        hidden = own_residual[i * half_count : (i + 1) * half_count].astype(F32) + rows.astype(F32)
        normed = (
            hidden
            * lax.rsqrt(jnp.mean(hidden * hidden, axis=-1, keepdims=True) + 1e-06)
            * norm_gain
        ).astype(BF16)
        halves.append((hidden, normed))

    gate_t, up_t = jnp.swapaxes(w_gate, 1, 2), jnp.swapaxes(w_up, 1, 2)
    done = jnp.zeros((8, 128), F32)
    outs = []
    for i, (hidden, normed) in enumerate(halves):
        near = gather_rows(normed, masks[:-1], count)
        far = exchange(near, masks[-1], count)
        near_other = exchange(near, core, count)
        scale = [weights[:, step, :, i].reshape(1, -1) for step in range(2)]
        near_out, near_back, done = expert(near, near_other, gate_t, up_t, w_down, scale[0], done)
        far, done = lax.optimization_barrier((far, done))
        far_other = exchange(far, core, count)
        far_out, far_back, done = expert(far, far_other, gate_t, up_t, w_down, scale[1], done)
        far_sum = add(far_out, exchange(far_back, core, count))
        parts = [near_out, exchange(near_back, core, count), exchange(far_sum, masks[-1], count)]
        for mask in reversed(masks[:-1]):
            half = parts[0].shape[0] // 2
            sent = total([p[half:] for p in parts]).astype(BF16)
            parts = [total([p[:half] for p in parts]), exchange(sent, mask, count)]
        outs.append(total([hidden] + parts).astype(BF16))
    return lax.all_to_all(jnp.concatenate(outs, axis=0), "hx", split_axis=1, concat_axis=0, tiled=True)


def solution(mesh):
    return jax.shard_map(
        shards,
        mesh=mesh,
        in_specs=(
            P("seq", "hx"),
            P("seq", "hx"),
            P("seq", "hx"),
            P("seq", "hx"),
            P("seq"),
            P("seq", None),
            P("hx", None),
            P(),
            P("seq", None),
            P("seq", None),
            P("hx", None, "seq"),
            P("hx", None, "seq"),
            P("hx", "seq", None),
        ),
        out_specs=P("seq", "hx"),
        check_vma=False,
    )
```

time: 479 us -> 282 us (0.59)
  waiting for transfers between devices: 337 us -> 145 us
  Pallas kernels: 0 us -> 69.8 us
  matrix products: 44.7 us -> 6.39 us
  blocking collectives: 39.8 us -> 9.84 us
  starting transfers between devices: 8.08 us -> 29.2 us
  between operations: 15.4 us -> 0.69 us
  local copies, waits for them, and re-layouts: 19.7 us -> 10 us
    reduce_scatter x2 -> x0, waiting for transfers between devices: 203 us -> none  [the longest x1 134 us: shards(): lax.psum_scatter(jnp.dot(act, w_down[0], preferred_element_type=jnp.float...]
    ppermute x0 -> x28, waiting for transfers between devices: none -> 129 us  [exchange(): return lax.ppermute(x, AXES, pairs)]
    all_gather x2 -> x0, waiting for transfers between devices: 122 us -> none  [the longest x1 118 us: shards(): gathered = lax.all_gather(normed, 'seq', axis=0, tiled=True)]
    pallas_call x0 -> x8, Pallas kernels: none -> 69.8 us  [the longest x4 65.7 us: expert(): pl.pallas_call(functools.partial(expert_kernel, steps), grid=(2 * steps,)...]
    dot_general x8 -> x1, matrix products: 44.7 us -> 6.39 us  [shards(): jnp.dot(attn_in, out_weight, preferred_element_type=F32).astype(BF16)]
    unnamed x1 -> x0, blocking collectives: 23.4 us -> none
    ppermute x0 -> x28, starting transfers between devices: none -> 18.3 us  [exchange(): return lax.ppermute(x, AXES, pairs)]
    all_gather x1 -> x0, blocking collectives: 16.4 us -> none  [prefix(): lax.all_gather(a.astype(kind), axis)]
  transfers between devices with their start and end apart: 6 -> 30, of which waited for: 5 -> 17; matrix products, arithmetic and copies ran while one was open for 3% -> 4% of each run, Pallas kernels for 0% -> 24%
where the time goes in v1:
time: 282 us; the launch traced here: 281 us
  waiting for transfers between devices  145 us (51%)
  Pallas kernels  69.8 us (25%)
  starting transfers between devices  29.2 us (10%)
  other arithmetic  10.3 us (4%)
  local copies, waits for them, and re-layouts  10 us (4%)
  blocking collectives  9.84 us (3%)
  matrix products  6.39 us (2%)
    ppermute x28, waiting for transfers between devices, exchange(): return lax.ppermute(x, AXES, pairs)  129 us
    pallas_call x4, Pallas kernels, expert(): pl.pallas_call(functools.partial(expert_kernel, steps), grid=(2 * steps,)...  65.7 us
    ppermute x28, starting transfers between devices, exchange(): return lax.ppermute(x, AXES, pairs)  18.3 us
    all_to_all x1, blocking collectives, shards(): lax.all_to_all(jnp.concatenate(outs, axis=0), 'hx', split_axis=1, concat_...  9.84 us
    all_to_all x1, waiting for transfers between devices, shards(): lax.all_to_all(incoming, 'seq', split_axis=0, concat_axis=0, tiled=True)  8.43 us
    all_to_all x1, waiting for transfers between devices, shards(): lax.all_to_all(payload, 'seq', split_axis=0, concat_axis=0, tiled=True)  7.76 us
    all_to_all x1, starting transfers between devices, shards(): lax.all_to_all(payload, 'seq', split_axis=0, concat_axis=0, tiled=True)  7.28 us
    unnamed x82, local copies, waits for them, and re-layouts  6.77 us
  transfers between devices with their start and end apart: 30, of which 17 were waited for; matrix products, arithmetic and copies ran while one was open for 4% of the time, Pallas kernels for 24%

profile of v1, /device:TPU:0, one launch (start us, length us, event | category | flops | bytes accessed | tf_op | source)
XLA Modules:
  0.0 281.0 jit_solution(11144013289928604809)
XLA Ops:
  6.3 7.3 %all-to-all-start = ((bf16[8,144,128]{2,1,0:T(8,128)(2,1)}), bf16[8,144,128]{2,1,0:T(8,128)(2,1)S(1)}, u32[]{:S(2)}, u32[]{:S(2)}) async-start(bf16[8,144,128]{2,1,0:T(8,128)(2,1)} %shard_map.146), calls=%async_computation | async-start | bytes 589824 | tf_op jit(solution)/shard_map/all_to_all | solution.py:295
  15.4 7.8 %all-to-all-done.in_ref = bf16[8,144,128]{2,1,0:T(8,128)(2,1)S(1)} async-done(((bf16[8,144,128]{2,1,0:T(8,128)(2,1)}), bf16[8,144,128]{2,1,0:T(8,128)(2,1)S(1)}, u32[]{:S(2)}, u32[]{:S(2)}) %all-to-all-start) | async-done | bytes 294944 | tf_op jit(solution)/shard_map/all_to_all | solution.py:295
  24.0 3.6 %all-to-all-start.1 = ((bf16[8,128,128]{2,1,0:T(8,128)(2,1)}), bf16[8,128,128]{2,1,0:T(8,128)(2,1)S(1)}, u32[]{:S(2)}, u32[]{:S(2)}) async-start(bf16[8,128,128]{2,1,0:T(8,128)(2,1)} %shard_map.147), calls=%async_computation.1 | async-start | bytes 524288 | tf_op jit(solution)/shard_map/all_to_all | solution.py:302
  27.7 8.4 %all-to-all-done.1.state_ref = bf16[8,128,128]{2,1,0:T(8,128)(2,1)S(1)} async-done(((bf16[8,128,128]{2,1,0:T(8,128)(2,1)}), bf16[8,128,128]{2,1,0:T(8,128)(2,1)S(1)}, u32[]{:S(2)}, u32[]{:S(2)}) %all-to-all-start.1) | async-done | bytes 262176 | tf_op jit(solution)/shard_map/all_to_all | solution.py:302
  36.5 6.4 %convolution_convert_fusion = bf16[128,6144]{1,0:T(8,128)(2,1)S(1)} fusion(bf16[128,1024]{1,0:T(8,128)(2,1)S(1)} %shard_map.148, bf16[1024,6144]{1,0:T(8,128)(2,1)} %param.21), kind=kOutput, calls=%fused_computation.1 | convolution fusion | flops 1611399168 | bytes 14417920 | tf_op jit(solution)/shard_map/dot_general | solution.py:319
  47.7 5.6 %collective-permute-done.1 = bf16[16,6144]{1,0:T(8,128)(2,1)S(1)} collective-permute-done((bf16[16,6144]{1,0:T(8,128)(2,1)S(1)}, bf16[16,6144]{1,0:T(8,128)(2,1)S(1)}, u32[]{:S(2)}, u32[]{:S(2)}) %collective-permute-start.1) | collective-permute-done | bytes 196640 | tf_op jit(solution)/shard_map/ppermute | solution.py:30
  53.4 3.4 %collective-permute-done.15 = bf16[16,6144]{1,0:T(8,128)(2,1)S(1)} collective-permute-done((bf16[16,6144]{1,0:T(8,128)(2,1)S(1)}, bf16[16,6144]{1,0:T(8,128)(2,1)S(1)}, u32[]{:S(2)}, u32[]{:S(2)}) %collective-permute-start.15) | collective-permute-done | bytes 196640 | tf_op jit(solution)/shard_map/ppermute | solution.py:30
  58.4 10.2 %collective-permute-done.2 = bf16[16,6144]{1,0:T(8,128)(2,1)S(1)} collective-permute-done((bf16[16,6144]{1,0:T(8,128)(2,1)S(1)}, bf16[16,6144]{1,0:T(8,128)(2,1)S(1)}, u32[]{:S(2)}, u32[]{:S(2)}) %collective-permute-start.2) | collective-permute-done | bytes 196640 | tf_op jit(solution)/shard_map/ppermute | solution.py:30
  68.7 10.4 %collective-permute-done.3 = bf16[32,6144]{1,0:T(8,128)(2,1)S(1)} collective-permute-done((bf16[32,6144]{1,0:T(8,128)(2,1)S(1)}, bf16[32,6144]{1,0:T(8,128)(2,1)S(1)}, u32[]{:S(2)}, u32[]{:S(2)}) %collective-permute-start.3) | collective-permute-done | bytes 393248 | tf_op jit(solution)/shard_map/ppermute | solution.py:30
  81.4 9.9 %collective-permute-done.4 = bf16[64,6144]{1,0:T(8,128)(2,1)S(1)} collective-permute-done((bf16[64,6144]{1,0:T(8,128)(2,1)S(1)}, bf16[64,6144]{1,0:T(8,128)(2,1)S(1)}, u32[]{:S(2)}, u32[]{:S(2)}) %collective-permute-start.4) | collective-permute-done | bytes 786464 | tf_op jit(solution)/shard_map/ppermute | solution.py:30
  94.2 9.9 %collective-permute-done.17 = bf16[32,6144]{1,0:T(8,128)(2,1)S(1)} collective-permute-done((bf16[32,6144]{1,0:T(8,128)(2,1)}, bf16[32,6144]{1,0:T(8,128)(2,1)S(1)}, u32[]{:S(2)}, u32[]{:S(2)}) %collective-permute-start.17) | collective-permute-done | bytes 393248 | tf_op jit(solution)/shard_map/ppermute | solution.py:30
  108.1 16.0 %shard_map.149 = (bf16[128,6144]{1,0:T(8,128)(2,1)S(1)}, bf16[128,6144]{1,0:T(8,128)(2,1)S(1)}, f32[8,128]{1,0:T(8,128)S(1)}) custom-call(bf16[128,6144]{1,0:T(8,128)(2,1)S(1)} %pad_maximum_fusion.xa_ref, bf16[128,6144]{1,0:T(8,128)(2,1)} %collective-permute-done.5.xb_ref, bf16[1,576,6144]{2,1,0:T(8,128)(2,1)} %bitcast.40, bf16[1,576,6144]{2,1,0:T(8,128)(2,1)} %bitcast.44, ...), custom_call_target="tpu_custom_call" | custom-call | flops 5435817984 | bytes 27525120 | tf_op jit(solution)/shard_map/pallas_call | solution.py:213
  128.4 16.8 %shard_map.150 = (bf16[128,6144]{1,0:T(8,128)(2,1)S(1)}, bf16[128,6144]{1,0:T(8,128)(2,1)}, f32[8,128]{1,0:T(8,128)S(1)}) custom-call(bf16[128,6144]{1,0:T(8,128)(2,1)} %collective-permute-done.7.xa_ref, bf16[128,6144]{1,0:T(8,128)(2,1)} %collective-permute-done.8.xb_ref, bf16[1,576,6144]{2,1,0:T(8,128)(2,1)} %bitcast.41, bf16[1,576,6144]{2,1,0:T(8,128)(2,1)} %bitcast.45, ...), custom_call_target="tpu_custom_call" | custom-call | flops 5435817984 | bytes 27525120 | tf_op jit(solution)/shard_map/pallas_call | solution.py:213
  145.2 16.4 %shard_map.151 = (bf16[128,6144]{1,0:T(8,128)(2,1)S(1)}, bf16[128,6144]{1,0:T(8,128)(2,1)S(1)}, f32[8,128]{1,0:T(8,128)S(1)}) custom-call(bf16[128,6144]{1,0:T(8,128)(2,1)S(1)} %pad_maximum_fusion.1.xa_ref, bf16[128,6144]{1,0:T(8,128)(2,1)} %collective-permute-done.19.xb_ref, bf16[1,576,6144]{2,1,0:T(8,128)(2,1)} %bitcast.42, ...), custom_call_target="tpu_custom_call" | custom-call | flops 5435817984 | bytes 27525120 | tf_op jit(solution)/shard_map/pallas_call | solution.py:213
  164.5 3.2 %collective-permute-done.22.xb_ref = bf16[128,6144]{1,0:T(8,128)(2,1)} collective-permute-done((bf16[128,6144]{1,0:T(8,128)(2,1)}, bf16[128,6144]{1,0:T(8,128)(2,1)}, u32[]{:S(2)}, u32[]{:S(2)}) %collective-permute-start.22) | collective-permute-done | bytes 1572896 | tf_op jit(solution)/shard_map/ppermute | solution.py:30
  167.7 16.5 %shard_map.152 = (bf16[128,6144]{1,0:T(8,128)(2,1)S(1)}, bf16[128,6144]{1,0:T(8,128)(2,1)S(1)}, f32[8,128]{1,0:T(8,128)}) custom-call(bf16[128,6144]{1,0:T(8,128)(2,1)} %collective-permute-done.21.xa_ref, bf16[128,6144]{1,0:T(8,128)(2,1)} %collective-permute-done.22.xb_ref, bf16[1,576,6144]{2,1,0:T(8,128)(2,1)} %bitcast.43, bf16[1,576,6144]{2,1,0:T(8,128)(2,1)} %bitcast.47, ...), custom_call_target="tpu_custom_call" | custom-call | flops 5435817984 | bytes 27525120 | tf_op jit(solution)/shard_map/pallas_call | solution.py:213
  184.8 1.9 add_convert_fusion.1
  189.9 17.2 %collective-permute-done.10 = bf16[128,6144]{1,0:T(8,128)(2,1)S(1)} collective-permute-done((bf16[128,6144]{1,0:T(8,128)(2,1)S(1)}, bf16[128,6144]{1,0:T(8,128)(2,1)S(1)}, u32[]{:S(2)}, u32[]{:S(2)}) %collective-permute-start.10) | collective-permute-done | bytes 1572896 | tf_op jit(solution)/shard_map/ppermute | solution.py:30
  208.3 24.1 %collective-permute-done.24 = bf16[128,6144]{1,0:T(8,128)(2,1)S(1)} collective-permute-done((bf16[128,6144]{1,0:T(8,128)(2,1)S(1)}, bf16[128,6144]{1,0:T(8,128)(2,1)S(1)}, u32[]{:S(2)}, u32[]{:S(2)}) %collective-permute-start.24) | collective-permute-done | bytes 1572896 | tf_op jit(solution)/shard_map/ppermute | solution.py:30
  234.1 11.0 %collective-permute-done.25 = bf16[64,6144]{1,0:T(8,128)(2,1)S(1)} collective-permute-done((bf16[64,6144]{1,0:T(8,128)(2,1)S(1)}, bf16[64,6144]{1,0:T(8,128)(2,1)S(1)}, u32[]{:S(2)}, u32[]{:S(2)}) %collective-permute-start.25) | collective-permute-done | bytes 786464 | tf_op jit(solution)/shard_map/ppermute | solution.py:30
  245.7 2.1 collective-permute-start.13
  247.7 11.3 %collective-permute-done.26 = bf16[32,6144]{1,0:T(8,128)(2,1)S(1)} collective-permute-done((bf16[32,6144]{1,0:T(8,128)(2,1)S(1)}, bf16[32,6144]{1,0:T(8,128)(2,1)S(1)}, u32[]{:S(2)}, u32[]{:S(2)}) %collective-permute-start.26) | collective-permute-done | bytes 393248 | tf_op jit(solution)/shard_map/ppermute | solution.py:30
  259.1 9.9 %collective-permute-done.27 = bf16[16,6144]{1,0:T(8,128)(2,1)S(1)} collective-permute-done((bf16[16,6144]{1,0:T(8,128)(2,1)S(1)}, bf16[16,6144]{1,0:T(8,128)(2,1)S(1)}, u32[]{:S(2)}, u32[]{:S(2)}) %collective-permute-start.27) | collective-permute-done | bytes 196640 | tf_op jit(solution)/shard_map/ppermute | solution.py:30
  270.4 9.8 %all_to_all.29 = bf16[32,4,1536]{2,0,1:T(8,128)(2,1)S(1)} all-to-all(bf16[32,4,1536]{2,0,1:T(8,128)(2,1)S(1)} %bitcast.49), channel_id=1, replica_groups=mesh['seq'=8,'hx'=4] {'hx'}, dimensions={1} | all-to-all | bytes 786432 | tf_op jit(solution)/shard_map/all_to_all | solution.py:363
  (168 shorter events, 41.3 us)
Async XLA Ops:
  6.3 16.9 %all-to-all-start = ((bf16[8,144,128]{2,1,0:T(8,128)(2,1)}), bf16[8,144,128]{2,1,0:T(8,128)(2,1)S(1)}, u32[]{:S(2)}, u32[]{:S(2)}) async-start(bf16[8,144,128]{2,1,0:T(8,128)(2,1)} %shard_map.146), calls=%async_computation | async-start | bytes 589824 | tf_op jit(solution)/shard_map/all_to_all | solution.py:295
  24.0 12.1 %all-to-all-start.1 = ((bf16[8,128,128]{2,1,0:T(8,128)(2,1)}), bf16[8,128,128]{2,1,0:T(8,128)(2,1)S(1)}, u32[]{:S(2)}, u32[]{:S(2)}) async-start(bf16[8,128,128]{2,1,0:T(8,128)(2,1)} %shard_map.147), calls=%async_computation.1 | async-start | bytes 524288 | tf_op jit(solution)/shard_map/all_to_all | solution.py:302
  45.5 7.8 %collective-permute-start.1 = (bf16[16,6144]{1,0:T(8,128)(2,1)S(1)}, bf16[16,6144]{1,0:T(8,128)(2,1)S(1)}, u32[]{:S(2)}, u32[]{:S(2)}) collective-permute-start(bf16[16,6144]{1,0:T(8,128)(2,1)S(1)} %slice.183), channel_id=1, source_target_pairs={{0,2},{1,3},{2,0},{3,1},{4,6},{5,7},{6,4},{7,5},{8,10},{9,11},{10,... | collective-permute-start | bytes 589832 | tf_op jit(solution)/shard_map/ppermute | solution.py:30
  47.1 9.6 %collective-permute-start.15 = (bf16[16,6144]{1,0:T(8,128)(2,1)S(1)}, bf16[16,6144]{1,0:T(8,128)(2,1)S(1)}, u32[]{:S(2)}, u32[]{:S(2)}) collective-permute-start(bf16[16,6144]{1,0:T(8,128)(2,1)S(1)} %slice.202), channel_id=1, source_target_pairs={{0,2},{1,3},{2,0},{3,1},{4,6},{5,7},{6,4},{7,5},{8,10},{9,11},{10,... | collective-permute-start | bytes 589832 | tf_op jit(solution)/shard_map/ppermute | solution.py:30
  57.3 11.3 %collective-permute-start.2 = (bf16[16,6144]{1,0:T(8,128)(2,1)S(1)}, bf16[16,6144]{1,0:T(8,128)(2,1)S(1)}, u32[]{:S(2)}, u32[]{:S(2)}) collective-permute-start(bf16[16,6144]{1,0:T(8,128)(2,1)S(1)} %get-tuple-element.49), channel_id=1, source_target_pairs={{0,16},{1,17},{2,18},{3,19},{4,20},{5,21},{6,22},{7,23},{8,24},{9,... | collective-permute-start | bytes 589832 | tf_op jit(solution)/shard_map/ppermute | solution.py:30
  68.7 10.5 %collective-permute-start.3 = (bf16[32,6144]{1,0:T(8,128)(2,1)S(1)}, bf16[32,6144]{1,0:T(8,128)(2,1)S(1)}, u32[]{:S(2)}, u32[]{:S(2)}) collective-permute-start(bf16[32,6144]{1,0:T(8,128)(2,1)S(1)} %pad_maximum_fusion.4), channel_id=1, source_target_pairs={{0,8},{1,9},{2,10},{3,11},{4,12},{5,13},{6,14},{7,15},{8,0},{9,1},... | collective-permute-start | bytes 1179656 | tf_op jit(solution)/shard_map/ppermute | solution.py:30
  79.2 12.1 %collective-permute-start.4 = (bf16[64,6144]{1,0:T(8,128)(2,1)S(1)}, bf16[64,6144]{1,0:T(8,128)(2,1)S(1)}, u32[]{:S(2)}, u32[]{:S(2)}) collective-permute-start(bf16[64,6144]{1,0:T(8,128)(2,1)S(1)} %pad_maximum_fusion.2), channel_id=1, source_target_pairs={{0,4},{1,3},{2,6},{3,1},{4,0},{5,7},{6,2},{7,5},{8,12},{9,11},{10,... | collective-permute-start | bytes 2359304 | tf_op jit(solution)/shard_map/ppermute | solution.py:30
  80.8 10.7 %collective-permute-start.16 = (bf16[16,6144]{1,0:T(8,128)(2,1)S(1)}, bf16[16,6144]{1,0:T(8,128)(2,1)S(1)}, u32[]{:S(2)}, u32[]{:S(2)}) collective-permute-start(bf16[16,6144]{1,0:T(8,128)(2,1)S(1)} %get-tuple-element.50), channel_id=1, source_target_pairs={{0,16},{1,17},{2,18},{3,19},{4,20},{5,21},{6,22},{7,23},{8,24},{9,... | collective-permute-start | bytes 589832 | tf_op jit(solution)/shard_map/ppermute | solution.py:30
  91.4 16.6 %collective-permute-start.5 = (bf16[128,6144]{1,0:T(8,128)(2,1)S(1)}, bf16[128,6144]{1,0:T(8,128)(2,1)}, u32[]{:S(2)}, u32[]{:S(2)}) collective-permute-start(bf16[128,6144]{1,0:T(8,128)(2,1)S(1)} %pad_maximum_fusion.xa_ref), channel_id=1, source_target_pairs={{0,1},{1,0},{2,3},{3,2},{4,5},{5,4},{6,7},{7,6},{8,9},{9,8},{10,11... | collective-permute-start | bytes 4718600 | tf_op jit(solution)/shard_map/ppermute | solution.py:30
  92.3 11.7 %collective-permute-start.17 = (bf16[32,6144]{1,0:T(8,128)(2,1)}, bf16[32,6144]{1,0:T(8,128)(2,1)S(1)}, u32[]{:S(2)}, u32[]{:S(2)}) collective-permute-start(bf16[32,6144]{1,0:T(8,128)(2,1)} %pad_maximum_fusion.5), channel_id=1, source_target_pairs={{0,8},{1,9},{2,10},{3,11},{4,12},{5,13},{6,14},{7,15},{8,0},{9,1},... | collective-permute-start | bytes 1179656 | tf_op jit(solution)/shard_map/ppermute | solution.py:30
  92.6 31.5 %collective-permute-start.7 = (bf16[128,6144]{1,0:T(8,128)(2,1)S(1)}, bf16[128,6144]{1,0:T(8,128)(2,1)}, u32[]{:S(2)}, u32[]{:S(2)}) collective-permute-start(bf16[128,6144]{1,0:T(8,128)(2,1)S(1)} %pad_maximum_fusion.xa_ref), channel_id=1, source_target_pairs={{0,2},{1,5},{2,0},{3,7},{4,6},{5,1},{6,4},{7,3},{8,10},{9,13},{10,... | collective-permute-start | bytes 4718600 | tf_op jit(solution)/shard_map/ppermute | solution.py:30
  105.0 19.1 %collective-permute-start.18 = (bf16[64,6144]{1,0:T(8,128)(2,1)}, bf16[64,6144]{1,0:T(8,128)(2,1)}, u32[]{:S(2)}, u32[]{:S(2)}) collective-permute-start(bf16[64,6144]{1,0:T(8,128)(2,1)} %pad_maximum_fusion.3), channel_id=1, source_target_pairs={{0,4},{1,3},{2,6},{3,1},{4,0},{5,7},{6,2},{7,5},{8,12},{9,11},{10,... | collective-permute-start | bytes 2359304 | tf_op jit(solution)/shard_map/ppermute | solution.py:30
  125.9 19.3 %collective-permute-start.19 = (bf16[128,6144]{1,0:T(8,128)(2,1)S(1)}, bf16[128,6144]{1,0:T(8,128)(2,1)}, u32[]{:S(2)}, u32[]{:S(2)}) collective-permute-start(bf16[128,6144]{1,0:T(8,128)(2,1)S(1)} %pad_maximum_fusion.1.xa_ref), channel_id=1, source_target_pairs={{0,1},{1,0},{2,3},{3,2},{4,5},{5,4},{6,7},{7,6},{8,9},{9,8},{10,11... | collective-permute-start | bytes 4718600 | tf_op jit(solution)/shard_map/ppermute | solution.py:30
  126.0 38.0 %collective-permute-start.21 = (bf16[128,6144]{1,0:T(8,128)(2,1)S(1)}, bf16[128,6144]{1,0:T(8,128)(2,1)}, u32[]{:S(2)}, u32[]{:S(2)}) collective-permute-start(bf16[128,6144]{1,0:T(8,128)(2,1)S(1)} %pad_maximum_fusion.1.xa_ref), channel_id=1, source_target_pairs={{0,2},{1,5},{2,0},{3,7},{4,6},{5,1},{6,4},{7,3},{8,10},{9,13},{10,... | collective-permute-start | bytes 4718600 | tf_op jit(solution)/shard_map/ppermute | solution.py:30
  164.0 20.8 %collective-permute-start.9 = (bf16[128,6144]{1,0:T(8,128)(2,1)}, bf16[128,6144]{1,0:T(8,128)(2,1)}, u32[]{:S(2)}, u32[]{:S(2)}) collective-permute-start(bf16[128,6144]{1,0:T(8,128)(2,1)} %get-tuple-element.30), channel_id=1, source_target_pairs={{0,1},{1,0},{2,3},{3,2},{4,5},{5,4},{6,7},{7,6},{8,9},{9,8},{10,11... | collective-permute-start | bytes 4718600 | tf_op jit(solution)/shard_map/ppermute | solution.py:30
  186.7 20.5 %collective-permute-start.10 = (bf16[128,6144]{1,0:T(8,128)(2,1)S(1)}, bf16[128,6144]{1,0:T(8,128)(2,1)S(1)}, u32[]{:S(2)}, u32[]{:S(2)}) collective-permute-start(bf16[128,6144]{1,0:T(8,128)(2,1)S(1)} %add_convert_fusion.1), channel_id=1, source_target_pairs={{0,2},{1,5},{2,0},{3,7},{4,6},{5,1},{6,4},{7,3},{8,10},{9,13},{10,... | collective-permute-start | bytes 4718600 | tf_op jit(solution)/shard_map/ppermute | solution.py:30
  187.7 20.6 %collective-permute-start.20 = (bf16[128,6144]{1,0:T(8,128)(2,1)S(1)}, bf16[128,6144]{1,0:T(8,128)(2,1)S(1)}, u32[]{:S(2)}, u32[]{:S(2)}) collective-permute-start(bf16[128,6144]{1,0:T(8,128)(2,1)S(1)} %copy-done.15), channel_id=1, source_target_pairs={{0,1},{1,0},{2,3},{3,2},{4,5},{5,4},{6,7},{7,6},{8,9},{9,8},{10,11... | collective-permute-start | bytes 4718600 | tf_op jit(solution)/shard_map/ppermute | solution.py:30
  188.1 44.3 %collective-permute-start.24 = (bf16[128,6144]{1,0:T(8,128)(2,1)S(1)}, bf16[128,6144]{1,0:T(8,128)(2,1)S(1)}, u32[]{:S(2)}, u32[]{:S(2)}) collective-permute-start(bf16[128,6144]{1,0:T(8,128)(2,1)S(1)} %add_convert_fusion), channel_id=1, source_target_pairs={{0,2},{1,5},{2,0},{3,7},{4,6},{5,1},{6,4},{7,3},{8,10},{9,13},{10,... | collective-permute-start | bytes 4718600 | tf_op jit(solution)/shard_map/ppermute | solution.py:30
  207.8 25.8 %collective-permute-start.11 = (bf16[64,6144]{1,0:T(8,128)(2,1)S(1)}, bf16[64,6144]{1,0:T(8,128)(2,1)S(1)}, u32[]{:S(2)}, u32[]{:S(2)}) collective-permute-start(bf16[64,6144]{1,0:T(8,128)(2,1)S(1)} %get-tuple-element.41), channel_id=1, source_target_pairs={{0,4},{1,3},{2,6},{3,1},{4,0},{5,7},{6,2},{7,5},{8,12},{9,11},{10,... | collective-permute-start | bytes 2359304 | tf_op jit(solution)/shard_map/ppermute | solution.py:30
  233.0 12.1 %collective-permute-start.25 = (bf16[64,6144]{1,0:T(8,128)(2,1)S(1)}, bf16[64,6144]{1,0:T(8,128)(2,1)S(1)}, u32[]{:S(2)}, u32[]{:S(2)}) collective-permute-start(bf16[64,6144]{1,0:T(8,128)(2,1)S(1)} %get-tuple-element.43), channel_id=1, source_target_pairs={{0,4},{1,3},{2,6},{3,1},{4,0},{5,7},{6,2},{7,5},{8,12},{9,11},{10,... | collective-permute-start | bytes 2359304 | tf_op jit(solution)/shard_map/ppermute | solution.py:30
  233.7 11.9 %collective-permute-start.12 = (bf16[32,6144]{1,0:T(8,128)(2,1)S(1)}, bf16[32,6144]{1,0:T(8,128)(2,1)S(1)}, u32[]{:S(2)}, u32[]{:S(2)}) collective-permute-start(bf16[32,6144]{1,0:T(8,128)(2,1)S(1)} %get-tuple-element.45), channel_id=1, source_target_pairs={{0,8},{1,9},{2,10},{3,11},{4,12},{5,13},{6,14},{7,15},{8,0},{9,1},... | collective-permute-start | bytes 1179656 | tf_op jit(solution)/shard_map/ppermute | solution.py:30
  245.3 13.7 %collective-permute-start.26 = (bf16[32,6144]{1,0:T(8,128)(2,1)S(1)}, bf16[32,6144]{1,0:T(8,128)(2,1)S(1)}, u32[]{:S(2)}, u32[]{:S(2)}) collective-permute-start(bf16[32,6144]{1,0:T(8,128)(2,1)S(1)} %get-tuple-element.47), channel_id=1, source_target_pairs={{0,8},{1,9},{2,10},{3,11},{4,12},{5,13},{6,14},{7,15},{8,0},{9,1},... | collective-permute-start | bytes 1179656 | tf_op jit(solution)/shard_map/ppermute | solution.py:30
  245.7 13.4 %collective-permute-start.13 = (bf16[16,6144]{1,0:T(8,128)(2,1)S(1)}, bf16[16,6144]{1,0:T(8,128)(2,1)S(1)}, u32[]{:S(2)}, u32[]{:S(2)}) collective-permute-start(bf16[16,6144]{1,0:T(8,128)(2,1)S(1)} %fusion.6), channel_id=1, source_target_pairs={{0,16},{1,17},{2,18},{3,19},{4,20},{5,21},{6,22},{7,23},{8,24},{9,... | collective-permute-start | bytes 589832 | tf_op jit(solution)/shard_map/ppermute | solution.py:30
  259.0 10.0 %collective-permute-start.27 = (bf16[16,6144]{1,0:T(8,128)(2,1)S(1)}, bf16[16,6144]{1,0:T(8,128)(2,1)S(1)}, u32[]{:S(2)}, u32[]{:S(2)}) collective-permute-start(bf16[16,6144]{1,0:T(8,128)(2,1)S(1)} %fusion.2), channel_id=1, source_target_pairs={{0,16},{1,17},{2,18},{3,19},{4,20},{5,21},{6,22},{7,23},{8,24},{9,... | collective-permute-start | bytes 589832 | tf_op jit(solution)/shard_map/ppermute | solution.py:30
  (39 other events, 459.9 us)

commit v2 on v1

v2 whole, which is shorter than its diff:
```python
import functools

import jax
import jax.numpy as jnp
from jax import lax
from jax.experimental import pallas as pl
from jax.experimental.pallas import tpu as pltpu
from jax.sharding import PartitionSpec as P

HS = 128
AXES = ("seq", "hx")
HALVES = 2
EXTRA = 16
VMEM_LIMIT = 16 * 1024 * 1024
F32, BF16 = jnp.float32, jnp.bfloat16


def bits(low, high):
    out = []
    bit = high // 2
    while bit >= low:
        out.append(bit)
        bit //= 2
    return out


def exchange(x, mask, count):
    even, odd = mask
    pairs = [(d, d ^ (odd if d & 1 else even)) for d in range(count)]
    return lax.ppermute(x, AXES, pairs)


def total(parts):
    return functools.reduce(lambda a, b: a + b, [p.astype(F32) for p in parts])


def add(a, b):
    return total([a, b]).astype(BF16)


def gather_rows(x, masks, count):
    for mask in masks:
        x = jnp.concatenate([x, exchange(x, mask, count)], axis=0)
    return x


def reduce_rows(x, masks, count):
    for mask in reversed(masks):
        half = x.shape[0] // 2
        x = add(x[:half], exchange(x[half:], mask, count))
    return x


def offsets(masks):
    out = [0]
    for mask in masks:
        out = out + [o ^ mask for o in out]
    return out


def split3(x):
    high = x.astype(BF16)
    rest = x - high.astype(F32)
    mid = rest.astype(BF16)
    low = (rest - mid.astype(F32)).astype(BF16)
    return [high, mid, low]


def whole():
    return pl.BlockSpec(memory_space=pltpu.VMEM)


def over_last(a, b):
    return lax.dot_general(
        a, b, (((1,), (1,)), ((), ())), precision=lax.Precision.HIGHEST, preferred_element_type=F32
    )


def by_column(decay_t, doc_row):
    tok = doc_row.shape[1]
    row = lax.broadcasted_iota(jnp.int32, (tok, tok), 0)
    col = lax.broadcasted_iota(jnp.int32, (tok, tok), 1)
    doc_rows = jnp.broadcast_to(doc_row.astype(F32), (8, tok))
    log_cum = over_last((row >= col).astype(F32), decay_t)
    return log_cum, over_last((row == col).astype(F32), doc_rows)[:, :1]


def state_kernel(me_ref, k_hbm, v_hbm, decay_ref, doc_ref, ids_ref, route_ref, out_ref, k_ref, v_ref, sems):
    copies = [
        pltpu.make_async_copy(k_hbm, k_ref, sems.at[0]),
        pltpu.make_async_copy(v_hbm, v_ref, sems.at[1]),
    ]
    for copy in copies:
        copy.start()
    heads, tok = decay_ref.shape
    chunks = out_ref.shape[0]
    chunk = out_ref.shape[1] - EXTRA
    doc_row = doc_ref[...].astype(F32)
    log_cum, doc_col = by_column(decay_ref[...], doc_row)
    total = log_cum[tok - 1 : tok, :]
    first, last = doc_row[:, :1], doc_row[:, tok - 1 :]
    end_weight = jnp.exp(total - log_cum) * (doc_col == last).astype(F32)
    through = jnp.exp(total)
    weight = jnp.sum(jnp.where(ids_ref[...] == me_ref[0], route_ref[...], 0.0), axis=0, keepdims=True)
    row = lax.broadcasted_iota(jnp.int32, (EXTRA, HS), 0)
    fixed = [jnp.broadcast_to(w.astype(F32), (EXTRA, HS)) for w in [first, last] + split3(weight)]
    per_head = chunks // heads
    for copy in copies:
        copy.wait()
    for h in range(heads):
        lanes = slice(h * HS, (h + 1) * HS)
        weighted = (k_ref[:, lanes].astype(F32) * end_weight[:, h : h + 1]).astype(BF16)
        state = lax.dot_general(
            weighted, v_ref[:, lanes], (((0,), (0,)), ((), ())), preferred_element_type=F32
        ).astype(BF16)
        parts = [
            jnp.broadcast_to(p.astype(F32), (EXTRA, HS)) for p in split3(through[:, h : h + 1])
        ] + fixed
        extra = jnp.zeros((EXTRA, HS), F32)
        for i, part in enumerate(parts):
            extra = jnp.where(row == i, part, extra)
        for j in range(per_head):
            at = h * per_head + j
            out_ref[at, :chunk, :] = state[j * chunk : (j + 1) * chunk, :]
            out_ref[at, chunk:, :] = extra.astype(BF16)


def prefix_kernel(in_ref, out_ref):
    shards_n = in_ref.shape[0]
    chunk = out_ref.shape[1]
    carry = jnp.zeros((chunk, HS), F32)
    before = None
    for s in range(shards_n):
        extra = in_ref[s, chunk:, :].astype(F32)
        decay = extra[0:1] + extra[1:2] + extra[2:3]
        first, last = extra[3:4], extra[4:5]
        if s:
            out_ref[s] = (carry * (before == first).astype(F32)).astype(BF16)
            decay = decay * (before == last).astype(F32)
        else:
            out_ref[s] = carry.astype(BF16)
        carry = decay * carry + in_ref[s, :chunk, :].astype(F32)
        before = last


def intra_kernel(q_hbm, k_hbm, v_hbm, decay_ref, doc_ref, out_ref, qw_ref, q_ref, k_ref, v_ref, sems):
    copies = [
        pltpu.make_async_copy(q_hbm, q_ref, sems.at[0]),
        pltpu.make_async_copy(k_hbm, k_ref, sems.at[1]),
        pltpu.make_async_copy(v_hbm, v_ref, sems.at[2]),
    ]
    for copy in copies:
        copy.start()
    heads, tok = decay_ref.shape
    doc_row = doc_ref[...].astype(F32)
    log_cum, doc_col = by_column(decay_ref[...], doc_row)
    row = lax.broadcasted_iota(jnp.int32, (tok, tok), 0)
    col = lax.broadcasted_iota(jnp.int32, (tok, tok), 1)
    log_cum_t = jnp.dot(
        decay_ref[...], (row <= col).astype(F32), precision=lax.Precision.HIGHEST, preferred_element_type=F32
    )
    allowed = (row >= col) & (doc_col == doc_row)
    carry = jnp.exp(log_cum) * (doc_col == doc_row[:, :1]).astype(F32)
    for copy in copies:
        copy.wait()
    for h in range(heads):
        lanes = slice(h * HS, (h + 1) * HS)
        scores = lax.dot_general(
            q_ref[:, lanes], k_ref[:, lanes], (((1,), (1,)), ((), ())), preferred_element_type=F32
        )
        exponent = jnp.where(allowed, log_cum[:, h : h + 1] - log_cum_t[h : h + 1, :], -jnp.inf)
        weighted = (scores * jnp.exp(exponent)).astype(BF16)
        out_ref[:, lanes] = jnp.dot(weighted, v_ref[:, lanes], preferred_element_type=F32)
        qw_ref[:, lanes] = (q_ref[:, lanes].astype(F32) * carry[:, h : h + 1]).astype(BF16)


def attend_kernel(intra_ref, qw_ref, state_ref, out_ref):
    heads = state_ref.shape[0]
    for h in range(heads):
        lanes = slice(h * HS, (h + 1) * HS)
        head_out = intra_ref[:, lanes] + jnp.dot(
            qw_ref[:, lanes], state_ref[h], preferred_element_type=F32
        )
        scale = lax.rsqrt(jnp.mean(head_out * head_out, axis=-1, keepdims=True) + 1e-05)
        out_ref[:, lanes] = (head_out * scale).astype(BF16)


def load_kernel(*refs):
    count = (len(refs) - 2) // 2
    sems = refs[-1]
    copies = [
        pltpu.make_async_copy(refs[i].at[0], refs[count + i], sems.at[i]) for i in range(count)
    ]
    for copy in copies:
        copy.start()
    for copy in copies:
        copy.wait()
    refs[2 * count][...] = jnp.zeros_like(refs[2 * count])


def load(*weights):
    shapes = [w.shape[1:] for w in weights]
    weights = [pltpu.with_memory_space_constraint(w, pltpu.HBM) for w in weights]
    *loaded, done = pl.pallas_call(
        load_kernel,
        in_specs=[pl.BlockSpec(memory_space=pltpu.HBM)] * len(weights),
        out_specs=[whole()] * (len(weights) + 1),
        out_shape=[pltpu.VMEM(s, BF16) for s in shapes] + [jax.ShapeDtypeStruct((8, 128), F32)],
        scratch_shapes=[pltpu.SemaphoreType.DMA((len(weights),))],
        compiler_params=pltpu.CompilerParams(vmem_limit_bytes=VMEM_LIMIT),
    )(*weights)
    return loaded, done


def expert_kernel(blocks, *refs):
    x_refs, (gate_ref, up_ref, down_ref, scale_ref) = refs[:blocks], refs[blocks : blocks + 4]
    out_refs, (x, act) = refs[blocks + 5 : 2 * blocks + 5], refs[2 * blocks + 5 :]
    rows, width = x_refs[0].shape
    for i, ref in enumerate(x_refs):
        x[i * rows : (i + 1) * rows, :] = ref[...]
    over_width = (((1,), (1,)), ((), ()))
    g = lax.dot_general(gate_ref[...], x[...], over_width, preferred_element_type=F32)
    u = lax.dot_general(up_ref[...], x[...], over_width, preferred_element_type=F32)
    act[...] = (g / (1.0 + jnp.exp(-g)) * u * scale_ref[...]).T.astype(BF16)
    block = min(1024, width)
    for start in range(0, width, block):
        lanes = slice(start, start + block)
        out = jnp.dot(act[...], down_ref[:, lanes], preferred_element_type=F32).astype(BF16)
        for i, ref in enumerate(out_refs):
            ref[:, lanes] = out[i * rows : (i + 1) * rows]


def expert(xs, w_gate, w_up, w_down, loaded, scale):
    rows, width = xs[0].shape
    hidden = w_gate.shape[0]
    blocks = len(xs)
    return pl.pallas_call(
        functools.partial(expert_kernel, blocks),
        in_specs=[whole()] * (blocks + 5),
        out_specs=[whole()] * blocks,
        out_shape=[jax.ShapeDtypeStruct((rows, width), BF16)] * blocks,
        scratch_shapes=[pltpu.VMEM((blocks * rows, width), BF16), pltpu.VMEM((blocks * rows, hidden), BF16)],
        compiler_params=pltpu.CompilerParams(vmem_limit_bytes=VMEM_LIMIT),
        cost_estimate=pl.CostEstimate(
            flops=6 * blocks * rows * width * hidden,
            bytes_accessed=6 * width * hidden + 4 * blocks * rows * width,
            transcendentals=blocks * rows * hidden,
        ),
    )(*xs, w_gate, w_up, w_down, scale, loaded)


def call(kernel, out_shapes, *operands, scalars=0, far=0):
    fetched = operands[scalars : scalars + far]
    specs = [pl.BlockSpec(memory_space=pltpu.SMEM)] * scalars + [pl.BlockSpec(memory_space=pltpu.HBM)] * far
    operands = (
        operands[:scalars]
        + tuple(pltpu.with_memory_space_constraint(f, pltpu.HBM) for f in fetched)
        + operands[scalars + far :]
    )
    scratch = [pltpu.VMEM(f.shape, f.dtype) for f in fetched]
    return pl.pallas_call(
        kernel,
        in_specs=specs + [whole()] * (len(operands) - len(specs)),
        out_specs=[whole()] * len(out_shapes),
        out_shape=out_shapes,
        scratch_shapes=scratch + [pltpu.SemaphoreType.DMA((far,))] * (far > 0),
        compiler_params=pltpu.CompilerParams(vmem_limit_bytes=VMEM_LIMIT),
    )(*operands)


def shards(
    queries,
    keys,
    values,
    log_decay,
    doc_ids,
    residual,
    out_weight,
    norm_gain,
    expert_ids,
    route_weight,
    w_gate,
    w_up,
    w_down,
):
    n_seq, n_hx = lax.axis_size("seq"), lax.axis_size("hx")
    count = n_seq * n_hx
    inner = max(1, n_seq // 4)
    z_masks = bits(n_hx * inner, count)
    y_masks = bits(n_hx, n_hx * inner)
    x_masks = bits(2, n_hx)
    order_even = y_masks + x_masks
    order_odd = x_masks + y_masks if len(x_masks) == len(y_masks) else order_even
    net = list(zip(order_even, order_odd))
    core = (1, 1)
    hx_masks = [(m, m) for m in x_masks] + [core]
    hx_index = lax.axis_index("hx")
    device = lax.axis_index("seq") * n_hx + hx_index

    tok_count = queries.shape[0]
    own_count = tok_count // n_hx
    half_count = own_count // HALVES
    heads = log_decay.shape[1]
    chunk = heads * HS // n_seq

    decay_t, doc_row = log_decay.T, doc_ids.reshape(1, tok_count)
    shape = jax.ShapeDtypeStruct
    (payload,) = call(
        state_kernel,
        [shape((n_seq, chunk + EXTRA, HS), BF16)],
        hx_index.reshape(1), keys, values, decay_t, doc_row, expert_ids.T, route_weight.T,
        scalars=1, far=2,
    )
    arrived = lax.all_to_all(payload, "seq", split_axis=0, concat_axis=0, tiled=True)
    intra, query_weighted = call(
        intra_kernel,
        [shape((tok_count, heads * HS), F32), shape((tok_count, heads * HS), BF16)],
        queries, keys, values, decay_t, doc_row,
        far=3,
    )
    (incoming,) = call(prefix_kernel, [shape((n_seq, chunk, HS), BF16)], arrived)
    incoming = lax.all_to_all(incoming, "seq", split_axis=0, concat_axis=0, tiled=True)

    order = offsets([even for even, _ in hx_masks])

    def by_neighbour(x):
        blocks = [
            lax.dynamic_slice_in_dim(x, (hx_index ^ o) * own_count + i * half_count, half_count)
            for i in range(HALVES)
            for o in order
        ]
        return jnp.concatenate(blocks, axis=0)

    extra = arrived[:, chunk + 5 : chunk + 8, :].astype(F32)
    weights = jnp.sum(extra, axis=1).reshape(count, HALVES, half_count)
    units = {}
    for name, group in (("near", [0]), ("far", [z_masks[1]])):
        even = [o ^ g for g in group for o in offsets([z_masks[0]] + [m for m, _ in net])]
        odd = [o ^ g for g in group for o in offsets([z_masks[0]] + [m for _, m in net])]
        even, odd = even + [o ^ 1 for o in odd], odd + [o ^ 1 for o in even]
        units[name] = device ^ jnp.where(device & 1 == 1, jnp.array(odd), jnp.array(even))
    scale = {
        name + str(i): weights[rows, i].reshape(1, -1) for name, rows in units.items() for i in range(HALVES)
    }
    own_residual = lax.dynamic_slice_in_dim(residual, hx_index * own_count, own_count)
    wait = lax.optimization_barrier
    intra, query_weighted, scale, own_residual = wait(
        (by_neighbour(intra), by_neighbour(query_weighted), scale, own_residual)
    )

    (attn_in,) = call(
        attend_kernel,
        [shape((tok_count, heads * HS), BF16)],
        intra, query_weighted, incoming.reshape(heads, HS, HS),
    )
    projected = jnp.dot(attn_in, out_weight, preferred_element_type=F32).astype(BF16)

    def hx_send(i):
        rows = projected[i * n_hx * half_count : (i + 1) * n_hx * half_count]
        half = rows.shape[0] // 2
        return rows[:half], exchange(rows[half:], core, count)

    def hx_rest(rows, got):
        return reduce_rows(add(rows, got), hx_masks[:-1], count)

    def norm(i, rows, own_residual):
        hidden = own_residual[i * half_count : (i + 1) * half_count].astype(F32) + rows.astype(F32)
        normed = (
            hidden
            * lax.rsqrt(jnp.mean(hidden * hidden, axis=-1, keepdims=True) + 1e-06)
            * norm_gain
        ).astype(BF16)
        return hidden, normed

    def z_step(rows, mask):
        return exchange(rows, (mask, mask), count)

    def spread(unit):
        return gather_rows(unit, net[:-1], count)

    def to_core(rows):
        return exchange(rows, core, count)

    def back(outs):
        mine, mine_last, other, other_last = outs
        return add(mine_last, to_core(other_last)), [mine, to_core(other)]

    def fold(terms, got):
        terms = terms + [got]
        for mask in reversed(net[:-1]):
            half = terms[0].shape[0] // 2
            sent = total([t[half:] for t in terms]).astype(BF16)
            terms = [total([t[:half] for t in terms]), exchange(sent, mask, count)]
        return total(terms)

    last = net[-1]
    rows_a, got_a = hx_send(0)
    rows_b, got_b = hx_send(1)
    a = hx_rest(rows_a, got_a)
    a, rows_b, got_b, weights_in, scale, own_residual = wait(
        (a, rows_b, got_b, (w_gate, w_up, w_down), scale, own_residual)
    )
    hidden_a, a = norm(0, a, own_residual)
    w_gate, w_up, w_down = weights_in
    weights_in, loaded = load(jnp.swapaxes(w_gate, 1, 2), jnp.swapaxes(w_up, 1, 2), w_down)
    a1 = jnp.concatenate([a, z_step(a, z_masks[0])], axis=0)
    a1, rows_b, got_b, loaded = wait((a1, rows_b, got_b, loaded))
    a2 = z_step(a1, z_masks[1])
    a1 = spread(a1)
    b = hx_rest(rows_b, got_b)
    a1, a2, b, own_residual = wait((a1, a2, b, own_residual))
    a1_last, a1_other = exchange(a1, last, count), to_core(a1)
    a2 = spread(a2)
    hidden_b, b = norm(1, b, own_residual)
    b1 = jnp.concatenate([b, z_step(b, z_masks[0])], axis=0)
    a1, a1_last, a1_other, a2, b1 = wait((a1, a1_last, a1_other, a2, b1))
    a2_last, a2_other = exchange(a2, last, count), to_core(a2)
    a1_out = expert([a1, a1_last, a1_other, to_core(a1_last)], *weights_in, loaded, scale["near0"])
    b2 = z_step(b1, z_masks[1])
    b1 = spread(b1)
    a2, a2_last, a2_other, b1, b2, a1_out = wait((a2, a2_last, a2_other, b1, b2, a1_out))
    b1_last, b1_other = exchange(b1, last, count), to_core(b1)
    a2_out = expert([a2, a2_last, a2_other, to_core(a2_last)], *weights_in, loaded, scale["far0"])
    b2 = spread(b2)
    a1_send, a1_rest = back(a1_out)
    a2_send, a2_rest = back(a2_out)
    b1, b1_last, b1_other, b2, a1_send, a1_rest, a2_send, a2_rest = wait(
        (b1, b1_last, b1_other, b2, a1_send, a1_rest, a2_send, a2_rest)
    )
    b2_last, b2_other = exchange(b2, last, count), to_core(b2)
    a2_got = exchange(a2_send, last, count)
    b1_out = expert([b1, b1_last, b1_other, to_core(b1_last)], *weights_in, loaded, scale["near1"])
    b1_send, b1_rest = back(b1_out)
    b2, b2_last, b2_other, a2_got, b1_send, b1_rest, a1_send = wait(
        (b2, b2_last, b2_other, a2_got, b1_send, b1_rest, a1_send)
    )
    a1_got = exchange(a1_send, last, count)
    a2_sum = fold(a2_rest, a2_got)
    b2_out = expert([b2, b2_last, b2_other, to_core(b2_last)], *weights_in, loaded, scale["far1"])
    b2_send, b2_rest = back(b2_out)
    a2_sum, a1_got, b2_send, b2_rest, b1_send, b1_rest = wait(
        (a2_sum, a1_got, b2_send, b2_rest, b1_send, b1_rest)
    )
    a_z = z_step(a2_sum.astype(BF16), z_masks[1])
    a1_sum = fold(a1_rest, a1_got)
    b2_got = exchange(b2_send, last, count)
    a_sum = a1_sum + a_z.astype(F32)
    a_sum, b2_got, b1_send = wait((a_sum, b2_got, b1_send))
    a_z = z_step(a_sum[half_count:].astype(BF16), z_masks[0])
    b2_sum = fold(b2_rest, b2_got)
    b1_got = exchange(b1_send, last, count)
    a_out = total([hidden_a, a_sum[:half_count], a_z]).astype(BF16)
    a_out, b2_sum, b1_got = wait((a_out, b2_sum, b1_got))
    b_z = z_step(b2_sum.astype(BF16), z_masks[1])
    b1_sum = fold(b1_rest, b1_got)
    a_out = lax.all_to_all(a_out, "hx", split_axis=1, concat_axis=0, tiled=True)
    b_sum = b1_sum + b_z.astype(F32)
    b_sum, a_out = wait((b_sum, a_out))
    b_z = z_step(b_sum[half_count:].astype(BF16), z_masks[0])
    b_out = total([hidden_b, b_sum[:half_count], b_z]).astype(BF16)
    b_out = lax.all_to_all(b_out, "hx", split_axis=1, concat_axis=0, tiled=True)
    outs = [o.reshape(n_hx, half_count, -1) for o in (a_out, b_out)]
    return jnp.concatenate(outs, axis=1).reshape(tok_count, -1)


def solution(mesh):
    return jax.shard_map(
        shards,
        mesh=mesh,
        in_specs=(
            P("seq", "hx"),
            P("seq", "hx"),
            P("seq", "hx"),
            P("seq", "hx"),
            P("seq"),
            P("seq", None),
            P("hx", None),
            P(),
            P("seq", None),
            P("seq", None),
            P("hx", None, "seq"),
            P("hx", None, "seq"),
            P("hx", "seq", None),
        ),
        out_specs=P("seq", "hx"),
        check_vma=False,
    )
```

time: 282 us -> 244 us (0.87)
  Pallas kernels: 69.8 us -> 39.3 us
  starting transfers between devices: 29.2 us -> 49.7 us
  waiting for transfers between devices: 145 us -> 125 us
  other arithmetic: 10.3 us -> 5.59 us
    pallas_call x8 -> x9, Pallas kernels: 69.8 us -> 39.3 us  [the longest x4 26.1 us: expert(): pl.pallas_call(functools.partial(expert_kernel, blocks), in_specs=[whole(...]
    ppermute x28 -> x44, starting transfers between devices: 18.3 us -> 35.4 us  [exchange(): return lax.ppermute(x, AXES, pairs)]
    ppermute x28 -> x44, waiting for transfers between devices: 129 us -> 114 us  [exchange(): return lax.ppermute(x, AXES, pairs)]
    concatenate x6 -> x4, other arithmetic: 3.68 us -> 0.21 us  [gather_rows(): x = jnp.concatenate([x, exchange(x, mask, count)], axis=0)]
    all_to_all x0 -> x1, starting transfers between devices: none -> 3.37 us  [shards(): a_out = lax.all_to_all(a_out, 'hx', split_axis=1, concat_axis=0, tiled=True)]
    all_to_all x1, waiting for transfers between devices: 7.76 us -> 4.73 us  [shards(): lax.all_to_all(payload, 'seq', split_axis=0, concat_axis=0, tiled=True)]
    all_to_all x1, waiting for transfers between devices: 8.43 us -> 5.52 us  [shards(): lax.all_to_all(incoming, 'seq', split_axis=0, concat_axis=0, tiled=True)]
    unnamed x82 -> x46, local copies, waits for them, and re-layouts: 6.77 us -> 4.39 us
  transfers between devices with their start and end apart: 30 -> 47, of which waited for: 17 -> 28; matrix products, arithmetic and copies ran while one was open for 4% -> 3% of each run, Pallas kernels for 24% -> 12%
where the time goes in v2:
time: 244 us
  waiting for transfers between devices  125 us (51%)
  starting transfers between devices  49.7 us (20%)
  Pallas kernels  39.3 us (16%)
  local copies, waits for them, and re-layouts  8.92 us (4%)
  blocking collectives  8.36 us (3%)
  matrix products  6.4 us (3%)
  other arithmetic  5.59 us (2%)
    ppermute x44, waiting for transfers between devices, exchange(): return lax.ppermute(x, AXES, pairs)  114 us
    ppermute x44, starting transfers between devices, exchange(): return lax.ppermute(x, AXES, pairs)  35.4 us
    pallas_call x4, Pallas kernels, expert(): pl.pallas_call(functools.partial(expert_kernel, blocks), in_specs=[whole(...  26.1 us
    all_to_all x1, blocking collectives, shards(): b_out = lax.all_to_all(b_out, 'hx', split_axis=1, concat_axis=0, tiled=True)  8.36 us
    all_to_all x1, starting transfers between devices, shards(): lax.all_to_all(payload, 'seq', split_axis=0, concat_axis=0, tiled=True)  7.29 us
    pallas_call x1, Pallas kernels, load(): pl.pallas_call(load_kernel, in_specs=[pl.BlockSpec(memory_space=pltpu.HBM...  7.06 us
    dot_general x1, matrix products, shards(): jnp.dot(attn_in, out_weight, preferred_element_type=F32).astype(BF16)  6.4 us
    pallas_call x4, Pallas kernels, call(): pl.pallas_call(kernel, in_specs=specs + [whole()] * (len(operands) - len(...  6.14 us
  transfers between devices with their start and end apart: 47, of which 28 were waited for; matrix products, arithmetic and copies ran while one was open for 3% of the time, Pallas kernels for 12%

profile of v2, /device:TPU:0, one launch (start us, length us, event | category | flops | bytes accessed | tf_op | source)
XLA Modules:
  0.0 243.7 jit_solution(7191882160749953532)
XLA Ops:
  5.4 7.3 %all-to-all-start = ((bf16[8,144,128]{2,1,0:T(8,128)(2,1)}), bf16[8,144,128]{2,1,0:T(8,128)(2,1)S(1)}, u32[]{:S(2)}, u32[]{:S(2)}) async-start(bf16[8,144,128]{2,1,0:T(8,128)(2,1)} %shard_map.164), calls=%async_computation | async-start | bytes 589824 | tf_op jit(solution)/shard_map/all_to_all | solution.py:314
  17.6 4.7 %all-to-all-done.in_ref = bf16[8,144,128]{2,1,0:T(8,128)(2,1)S(1)} async-done(((bf16[8,144,128]{2,1,0:T(8,128)(2,1)}), bf16[8,144,128]{2,1,0:T(8,128)(2,1)S(1)}, u32[]{:S(2)}, u32[]{:S(2)}) %all-to-all-start) | async-done | bytes 294944 | tf_op jit(solution)/shard_map/all_to_all | solution.py:314
  23.1 3.6 %all-to-all-start.1 = ((bf16[8,128,128]{2,1,0:T(8,128)(2,1)}), bf16[8,128,128]{2,1,0:T(8,128)(2,1)S(1)}, u32[]{:S(2)}, u32[]{:S(2)}) async-start(bf16[8,128,128]{2,1,0:T(8,128)(2,1)} %shard_map.165), calls=%async_computation.1 | async-start | bytes 524288 | tf_op jit(solution)/shard_map/all_to_all | solution.py:322
  29.7 5.5 %all-to-all-done.1.state_ref = bf16[8,128,128]{2,1,0:T(8,128)(2,1)S(1)} async-done(((bf16[8,128,128]{2,1,0:T(8,128)(2,1)}), bf16[8,128,128]{2,1,0:T(8,128)(2,1)S(1)}, u32[]{:S(2)}, u32[]{:S(2)}) %all-to-all-start.1) | async-done | bytes 262176 | tf_op jit(solution)/shard_map/all_to_all | solution.py:322
  35.6 6.4 %convolution_convert_fusion = bf16[128,6144]{1,0:T(8,128)(2,1)S(1)} fusion(bf16[128,1024]{1,0:T(8,128)(2,1)S(1)} %shard_map.166, bf16[1024,6144]{1,0:T(8,128)(2,1)} %param.23), kind=kOutput, calls=%fused_computation.4 | convolution fusion | flops 1611399168 | bytes 14417920 | tf_op jit(solution)/shard_map/dot_general | solution.py:356
  45.6 5.4 %collective-permute-done.1 = bf16[16,6144]{1,0:T(8,128)(2,1)S(1)} collective-permute-done((bf16[16,6144]{1,0:T(8,128)(2,1)S(1)}, bf16[16,6144]{1,0:T(8,128)(2,1)S(1)}, u32[]{:S(2)}, u32[]{:S(2)}) %collective-permute-start.1) | collective-permute-done | bytes 196640 | tf_op jit(solution)/shard_map/ppermute | solution.py:30
  52.6 7.1 %shard_map.167 = (bf16[576,6144]{1,0:T(8,128)(2,1)S(1)}, bf16[576,6144]{1,0:T(8,128)(2,1)S(1)}, bf16[576,6144]{1,0:T(8,128)(2,1)S(1)}, f32[8,128]{1,0:T(8,128)S(1)}) custom-call(bf16[1,576,6144]{2,1,0:T(8,128)(2,1)} %bitcast.29, bf16[1,576,6144]{2,1,0:T(8,128)(2,1)} %bitcast.30, bf16[1,576,6144]{2,1,0:T(8,128)(2,1)} %refs_2_), custom_call_target="tpu_custom_call" | custom-call | tf_op jit(solution)/shard_map/pallas_call | solution.py:204
  65.4 5.4 %collective-permute-done.6 = bf16[16,6144]{1,0:T(8,128)(2,1)S(1)} collective-permute-done((bf16[16,6144]{1,0:T(8,128)(2,1)S(1)}, bf16[16,6144]{1,0:T(8,128)(2,1)S(1)}, u32[]{:S(2)}, u32[]{:S(2)}) %collective-permute-start.6) | collective-permute-done | bytes 196640 | tf_op jit(solution)/shard_map/ppermute | solution.py:30
  77.6 7.5 %collective-permute-done.10 = bf16[16,6144]{1,0:T(8,128)(2,1)S(1)} collective-permute-done((bf16[16,6144]{1,0:T(8,128)(2,1)S(1)}, bf16[16,6144]{1,0:T(8,128)(2,1)S(1)}, u32[]{:S(2)}, u32[]{:S(2)}) %collective-permute-start.10) | collective-permute-done | bytes 196640 | tf_op jit(solution)/shard_map/ppermute | solution.py:30
  87.7 3.6 %collective-permute-done.7.refs_1_ = bf16[64,6144]{1,0:T(8,128)(2,1)S(1)} collective-permute-done((bf16[64,6144]{1,0:T(8,128)(2,1)S(1)}, bf16[64,6144]{1,0:T(8,128)(2,1)S(1)}, u32[]{:S(2)}, u32[]{:S(2)}) %collective-permute-start.7) | collective-permute-done | bytes 786464 | tf_op jit(solution)/shard_map/ppermute | solution.py:30
  95.3 5.3 %collective-permute-done.13 = bf16[32,6144]{1,0:T(8,128)(2,1)S(1)} collective-permute-done((bf16[32,6144]{1,0:T(8,128)(2,1)S(1)}, bf16[32,6144]{1,0:T(8,128)(2,1)S(1)}, u32[]{:S(2)}, u32[]{:S(2)}) %collective-permute-start.13) | collective-permute-done | bytes 393248 | tf_op jit(solution)/shard_map/ppermute | solution.py:30
  100.7 6.4 %shard_map.168 = (bf16[64,6144]{1,0:T(8,128)(2,1)S(1)}, bf16[64,6144]{1,0:T(8,128)(2,1)S(1)}, bf16[64,6144]{1,0:T(8,128)(2,1)S(1)}, bf16[64,6144]{1,0:T(8,128)(2,1)S(1)}) custom-call(bf16[64,6144]{1,0:T(8,128)(2,1)S(1)} %pad_maximum_fusion.refs_0_, bf16[64,6144]{1,0:T(8,128)(2,1)S(1)} %collective-permute-done.7.refs_1_, ...), custom_call_target="tpu_custom_call" | custom-call | flops 5435817984 | bytes 27525120 | tf_op jit(solution)/shard_map/pallas_call | solution.py:237
  110.2 9.0 %collective-permute-done.18 = bf16[32,6144]{1,0:T(8,128)(2,1)S(1)} collective-permute-done((bf16[32,6144]{1,0:T(8,128)(2,1)S(1)}, bf16[32,6144]{1,0:T(8,128)(2,1)S(1)}, u32[]{:S(2)}, u32[]{:S(2)}) %collective-permute-start.18) | collective-permute-done | bytes 393248 | tf_op jit(solution)/shard_map/ppermute | solution.py:30
  119.3 6.6 %shard_map.169 = (bf16[64,6144]{1,0:T(8,128)(2,1)S(1)}, bf16[64,6144]{1,0:T(8,128)(2,1)S(1)}, bf16[64,6144]{1,0:T(8,128)(2,1)S(1)}, bf16[64,6144]{1,0:T(8,128)(2,1)S(1)}) custom-call(bf16[64,6144]{1,0:T(8,128)(2,1)S(1)} %pad_maximum_fusion.1.refs_0_, bf16[64,6144]{1,0:T(8,128)(2,1)S(1)} %collective-permute-done.11.refs_1_, ...), custom_call_target="tpu_custom_call" | custom-call | flops 5435817984 | bytes 27525120 | tf_op jit(solution)/shard_map/pallas_call | solution.py:237
  131.8 6.4 %shard_map.170 = (bf16[64,6144]{1,0:T(8,128)(2,1)S(1)}, bf16[64,6144]{1,0:T(8,128)(2,1)S(1)}, bf16[64,6144]{1,0:T(8,128)(2,1)S(1)}, bf16[64,6144]{1,0:T(8,128)(2,1)S(1)}) custom-call(bf16[64,6144]{1,0:T(8,128)(2,1)S(1)} %pad_maximum_fusion.2.refs_0_, bf16[64,6144]{1,0:T(8,128)(2,1)S(1)} %collective-permute-done.16.refs_1_, ...), custom_call_target="tpu_custom_call" | custom-call | flops 5435817984 | bytes 27525120 | tf_op jit(solution)/shard_map/pallas_call | solution.py:237
  141.6 17.6 %collective-permute-done.26 = bf16[64,6144]{1,0:T(8,128)(2,1)S(1)} collective-permute-done((bf16[64,6144]{1,0:T(8,128)(2,1)S(1)}, bf16[64,6144]{1,0:T(8,128)(2,1)S(1)}, u32[]{:S(2)}, u32[]{:S(2)}) %collective-permute-start.26) | collective-permute-done | bytes 786464 | tf_op jit(solution)/shard_map/ppermute | solution.py:30
  162.0 6.7 %shard_map.171 = (bf16[64,6144]{1,0:T(8,128)(2,1)S(1)}, bf16[64,6144]{1,0:T(8,128)(2,1)S(1)}, bf16[64,6144]{1,0:T(8,128)(2,1)S(1)}, bf16[64,6144]{1,0:T(8,128)(2,1)S(1)}) custom-call(bf16[64,6144]{1,0:T(8,128)(2,1)S(1)} %pad_maximum_fusion.3.refs_0_, bf16[64,6144]{1,0:T(8,128)(2,1)S(1)} %collective-permute-done.24.refs_1_, ...), custom_call_target="tpu_custom_call" | custom-call | flops 5435817984 | bytes 27525120 | tf_op jit(solution)/shard_map/pallas_call | solution.py:237
  181.4 4.1 %collective-permute-done.35 = bf16[32,6144]{1,0:T(8,128)(2,1)S(1)} collective-permute-done((bf16[32,6144]{1,0:T(8,128)(2,1)S(1)}, bf16[32,6144]{1,0:T(8,128)(2,1)S(1)}, u32[]{:S(2)}, u32[]{:S(2)}) %collective-permute-start.35) | collective-permute-done | bytes 393248 | tf_op jit(solution)/shard_map/ppermute | solution.py:30
  188.9 4.2 %collective-permute-done.37 = bf16[64,6144]{1,0:T(8,128)(2,1)S(1)} collective-permute-done((bf16[64,6144]{1,0:T(8,128)(2,1)S(1)}, bf16[64,6144]{1,0:T(8,128)(2,1)S(1)}, u32[]{:S(2)}, u32[]{:S(2)}) %collective-permute-start.37) | collective-permute-done | bytes 786464 | tf_op jit(solution)/shard_map/ppermute | solution.py:30
  197.7 7.0 %collective-permute-done.38 = bf16[16,6144]{1,0:T(8,128)(2,1)S(1)} collective-permute-done((bf16[16,6144]{1,0:T(8,128)(2,1)S(1)}, bf16[16,6144]{1,0:T(8,128)(2,1)S(1)}, u32[]{:S(2)}, u32[]{:S(2)}) %collective-permute-start.38) | collective-permute-done | bytes 196640 | tf_op jit(solution)/shard_map/ppermute | solution.py:30
  213.4 3.4 %all-to-all-start.2 = ((bf16[16,4,1536]{2,0,1:T(8,128)(2,1)}), bf16[16,4,1536]{2,0,1:T(8,128)(2,1)S(1)}, u32[]{:S(2)}, u32[]{:S(2)}) async-start(bf16[16,4,1536]{2,0,1:T(8,128)(2,1)} %bitcast.22), calls=%async_computation.2 | async-start | bytes 393216 | tf_op jit(solution)/shard_map/all_to_all | solution.py:456
  218.6 4.2 %collective-permute-done.42 = bf16[32,6144]{1,0:T(8,128)(2,1)} collective-permute-done((bf16[32,6144]{1,0:T(8,128)(2,1)S(1)}, bf16[32,6144]{1,0:T(8,128)(2,1)}, u32[]{:S(2)}, u32[]{:S(2)}) %collective-permute-start.42) | collective-permute-done | bytes 393248 | tf_op jit(solution)/shard_map/ppermute | solution.py:30
  225.3 9.1 %collective-permute-done.43 = bf16[16,6144]{1,0:T(8,128)(2,1)S(1)} collective-permute-done((bf16[16,6144]{1,0:T(8,128)(2,1)S(1)}, bf16[16,6144]{1,0:T(8,128)(2,1)S(1)}, u32[]{:S(2)}, u32[]{:S(2)}) %collective-permute-start.43) | collective-permute-done | bytes 196640 | tf_op jit(solution)/shard_map/ppermute | solution.py:30
  234.6 8.4 %all_to_all.45 = bf16[16,4,1536]{2,0,1:T(8,128)(2,1)S(1)} all-to-all(bf16[16,4,1536]{2,0,1:T(8,128)(2,1)S(1)} %bitcast.33), channel_id=1, replica_groups=mesh['seq'=8,'hx'=4] {'hx'}, dimensions={1} | all-to-all | bytes 393216 | tf_op jit(solution)/shard_map/all_to_all | solution.py:461
  (179 shorter events, 87.9 us)
Async XLA Ops:
  5.4 16.9 %all-to-all-start = ((bf16[8,144,128]{2,1,0:T(8,128)(2,1)}), bf16[8,144,128]{2,1,0:T(8,128)(2,1)S(1)}, u32[]{:S(2)}, u32[]{:S(2)}) async-start(bf16[8,144,128]{2,1,0:T(8,128)(2,1)} %shard_map.164), calls=%async_computation | async-start | bytes 589824 | tf_op jit(solution)/shard_map/all_to_all | solution.py:314
  23.1 12.1 %all-to-all-start.1 = ((bf16[8,128,128]{2,1,0:T(8,128)(2,1)}), bf16[8,128,128]{2,1,0:T(8,128)(2,1)S(1)}, u32[]{:S(2)}, u32[]{:S(2)}) async-start(bf16[8,128,128]{2,1,0:T(8,128)(2,1)} %shard_map.165), calls=%async_computation.1 | async-start | bytes 524288 | tf_op jit(solution)/shard_map/all_to_all | solution.py:322
  51.5 11.3 %collective-permute-start.3 = (bf16[16,6144]{1,0:T(8,128)(2,1)S(1)}, bf16[16,6144]{1,0:T(8,128)(2,1)S(1)}, u32[]{:S(2)}, u32[]{:S(2)}) collective-permute-start(bf16[16,6144]{1,0:T(8,128)(2,1)S(1)} %multiply_convert_fusion.1), channel_id=1, source_target_pairs={{0,16},{1,17},{2,18},{3,19},{4,20},{5,21},{6,22},{7,23},{8,24},{9,... | collective-permute-start | bytes 589832 | tf_op jit(solution)/shard_map/ppermute | solution.py:30
  75.0 12.7 %collective-permute-start.8 = (bf16[64,6144]{1,0:T(8,128)(2,1)S(1)}, bf16[64,6144]{1,0:T(8,128)(2,1)S(1)}, u32[]{:S(2)}, u32[]{:S(2)}) collective-permute-start(bf16[64,6144]{1,0:T(8,128)(2,1)S(1)} %pad_maximum_fusion.refs_0_), channel_id=1, source_target_pairs={{0,1},{1,0},{2,3},{3,2},{4,5},{5,4},{6,7},{7,6},{8,9},{9,8},{10,11... | collective-permute-start | bytes 2359304 | tf_op jit(solution)/shard_map/ppermute | solution.py:30
  75.1 16.3 %collective-permute-start.7 = (bf16[64,6144]{1,0:T(8,128)(2,1)S(1)}, bf16[64,6144]{1,0:T(8,128)(2,1)S(1)}, u32[]{:S(2)}, u32[]{:S(2)}) collective-permute-start(bf16[64,6144]{1,0:T(8,128)(2,1)S(1)} %pad_maximum_fusion.refs_0_), channel_id=1, source_target_pairs={{0,2},{1,5},{2,0},{3,7},{4,6},{5,1},{6,4},{7,3},{8,10},{9,13},{10,... | collective-permute-start | bytes 2359304 | tf_op jit(solution)/shard_map/ppermute | solution.py:30
  75.7 12.0 %collective-permute-start.9 = (bf16[32,6144]{1,0:T(8,128)(2,1)S(1)}, bf16[32,6144]{1,0:T(8,128)(2,1)S(1)}, u32[]{:S(2)}, u32[]{:S(2)}) collective-permute-start(bf16[32,6144]{1,0:T(8,128)(2,1)S(1)} %collective-permute-done.5), channel_id=1, source_target_pairs={{0,4},{1,3},{2,6},{3,1},{4,0},{5,7},{6,2},{7,5},{8,12},{9,11},{10,... | collective-permute-start | bytes 1179656 | tf_op jit(solution)/shard_map/ppermute | solution.py:30
  92.8 14.3 %collective-permute-start.14 = (bf16[32,6144]{1,0:T(8,128)(2,1)S(1)}, bf16[32,6144]{1,0:T(8,128)(2,1)S(1)}, u32[]{:S(2)}, u32[]{:S(2)}) collective-permute-start(bf16[32,6144]{1,0:T(8,128)(2,1)S(1)} %pad_maximum_fusion.5), channel_id=1, source_target_pairs={{0,8},{1,9},{2,10},{3,11},{4,12},{5,13},{6,14},{7,15},{8,0},{9,1},... | collective-permute-start | bytes 1179656 | tf_op jit(solution)/shard_map/ppermute | solution.py:30
  94.6 12.6 %collective-permute-start.12 = (bf16[64,6144]{1,0:T(8,128)(2,1)S(1)}, bf16[64,6144]{1,0:T(8,128)(2,1)S(1)}, u32[]{:S(2)}, u32[]{:S(2)}) collective-permute-start(bf16[64,6144]{1,0:T(8,128)(2,1)S(1)} %pad_maximum_fusion.1.refs_0_), channel_id=1, source_target_pairs={{0,1},{1,0},{2,3},{3,2},{4,5},{5,4},{6,7},{7,6},{8,9},{9,8},{10,11... | collective-permute-start | bytes 2359304 | tf_op jit(solution)/shard_map/ppermute | solution.py:30
  94.8 12.3 %collective-permute-start.11 = (bf16[64,6144]{1,0:T(8,128)(2,1)S(1)}, bf16[64,6144]{1,0:T(8,128)(2,1)S(1)}, u32[]{:S(2)}, u32[]{:S(2)}) collective-permute-start(bf16[64,6144]{1,0:T(8,128)(2,1)S(1)} %pad_maximum_fusion.1.refs_0_), channel_id=1, source_target_pairs={{0,2},{1,5},{2,0},{3,7},{4,6},{5,1},{6,4},{7,3},{8,10},{9,13},{10,... | collective-permute-start | bytes 2359304 | tf_op jit(solution)/shard_map/ppermute | solution.py:30
  107.2 12.1 %collective-permute-start.18 = (bf16[32,6144]{1,0:T(8,128)(2,1)S(1)}, bf16[32,6144]{1,0:T(8,128)(2,1)S(1)}, u32[]{:S(2)}, u32[]{:S(2)}) collective-permute-start(bf16[32,6144]{1,0:T(8,128)(2,1)S(1)} %collective-permute-done.14), channel_id=1, source_target_pairs={{0,4},{1,3},{2,6},{3,1},{4,0},{5,7},{6,2},{7,5},{8,12},{9,11},{10,... | collective-permute-start | bytes 1179656 | tf_op jit(solution)/shard_map/ppermute | solution.py:30
  109.7 18.9 %collective-permute-start.17 = (bf16[64,6144]{1,0:T(8,128)(2,1)S(1)}, bf16[64,6144]{1,0:T(8,128)(2,1)S(1)}, u32[]{:S(2)}, u32[]{:S(2)}) collective-permute-start(bf16[64,6144]{1,0:T(8,128)(2,1)S(1)} %pad_maximum_fusion.2.refs_0_), channel_id=1, source_target_pairs={{0,1},{1,0},{2,3},{3,2},{4,5},{5,4},{6,7},{7,6},{8,9},{9,8},{10,11... | collective-permute-start | bytes 2359304 | tf_op jit(solution)/shard_map/ppermute | solution.py:30
  110.2 18.4 %collective-permute-start.16 = (bf16[64,6144]{1,0:T(8,128)(2,1)S(1)}, bf16[64,6144]{1,0:T(8,128)(2,1)S(1)}, u32[]{:S(2)}, u32[]{:S(2)}) collective-permute-start(bf16[64,6144]{1,0:T(8,128)(2,1)S(1)} %pad_maximum_fusion.2.refs_0_), channel_id=1, source_target_pairs={{0,2},{1,5},{2,0},{3,7},{4,6},{5,1},{6,4},{7,3},{8,10},{9,13},{10,... | collective-permute-start | bytes 2359304 | tf_op jit(solution)/shard_map/ppermute | solution.py:30
  110.2 16.3 %collective-permute-start.19 = (bf16[64,6144]{1,0:T(8,128)(2,1)S(1)}, bf16[64,6144]{1,0:T(8,128)(2,1)S(1)}, u32[]{:S(2)}, u32[]{:S(2)}) collective-permute-start(bf16[64,6144]{1,0:T(8,128)(2,1)S(1)} %get-tuple-element.142), channel_id=1, source_target_pairs={{0,1},{1,0},{2,3},{3,2},{4,5},{5,4},{6,7},{7,6},{8,9},{9,8},{10,11... | collective-permute-start | bytes 2359304 | tf_op jit(solution)/shard_map/ppermute | solution.py:30
  138.7 20.6 %collective-permute-start.25 = (bf16[64,6144]{1,0:T(8,128)(2,1)S(1)}, bf16[64,6144]{1,0:T(8,128)(2,1)S(1)}, u32[]{:S(2)}, u32[]{:S(2)}) collective-permute-start(bf16[64,6144]{1,0:T(8,128)(2,1)S(1)} %pad_maximum_fusion.3.refs_0_), channel_id=1, source_target_pairs={{0,1},{1,0},{2,3},{3,2},{4,5},{5,4},{6,7},{7,6},{8,9},{9,8},{10,11... | collective-permute-start | bytes 2359304 | tf_op jit(solution)/shard_map/ppermute | solution.py:30
  138.8 20.4 %collective-permute-start.24 = (bf16[64,6144]{1,0:T(8,128)(2,1)S(1)}, bf16[64,6144]{1,0:T(8,128)(2,1)S(1)}, u32[]{:S(2)}, u32[]{:S(2)}) collective-permute-start(bf16[64,6144]{1,0:T(8,128)(2,1)S(1)} %pad_maximum_fusion.3.refs_0_), channel_id=1, source_target_pairs={{0,2},{1,5},{2,0},{3,7},{4,6},{5,1},{6,4},{7,3},{8,10},{9,13},{10,... | collective-permute-start | bytes 2359304 | tf_op jit(solution)/shard_map/ppermute | solution.py:30
  138.8 20.4 %collective-permute-start.26 = (bf16[64,6144]{1,0:T(8,128)(2,1)S(1)}, bf16[64,6144]{1,0:T(8,128)(2,1)S(1)}, u32[]{:S(2)}, u32[]{:S(2)}) collective-permute-start(bf16[64,6144]{1,0:T(8,128)(2,1)S(1)} %add_convert_fusion.2), channel_id=1, source_target_pairs={{0,2},{1,5},{2,0},{3,7},{4,6},{5,1},{6,4},{7,3},{8,10},{9,13},{10,... | collective-permute-start | bytes 2359304 | tf_op jit(solution)/shard_map/ppermute | solution.py:30
  140.8 18.4 %collective-permute-start.29 = (bf16[64,6144]{1,0:T(8,128)(2,1)S(1)}, bf16[64,6144]{1,0:T(8,128)(2,1)S(1)}, u32[]{:S(2)}, u32[]{:S(2)}) collective-permute-start(bf16[64,6144]{1,0:T(8,128)(2,1)S(1)} %get-tuple-element.164), channel_id=1, source_target_pairs={{0,1},{1,0},{2,3},{3,2},{4,5},{5,4},{6,7},{7,6},{8,9},{9,8},{10,11... | collective-permute-start | bytes 2359304 | tf_op jit(solution)/shard_map/ppermute | solution.py:30
  159.6 12.4 %collective-permute-start.30 = (bf16[32,6144]{1,0:T(8,128)(2,1)S(1)}, bf16[32,6144]{1,0:T(8,128)(2,1)S(1)}, u32[]{:S(2)}, u32[]{:S(2)}) collective-permute-start(bf16[32,6144]{1,0:T(8,128)(2,1)S(1)} %add_convert_fusion.7), channel_id=1, source_target_pairs={{0,4},{1,3},{2,6},{3,1},{4,0},{5,7},{6,2},{7,5},{8,12},{9,11},{10,... | collective-permute-start | bytes 1179656 | tf_op jit(solution)/shard_map/ppermute | solution.py:30
  162.0 13.3 %collective-permute-start.31 = (bf16[64,6144]{1,0:T(8,128)(2,1)S(1)}, bf16[64,6144]{1,0:T(8,128)(2,1)S(1)}, u32[]{:S(2)}, u32[]{:S(2)}) collective-permute-start(bf16[64,6144]{1,0:T(8,128)(2,1)S(1)} %add_convert_fusion.3), channel_id=1, source_target_pairs={{0,2},{1,5},{2,0},{3,7},{4,6},{5,1},{6,4},{7,3},{8,10},{9,13},{10,... | collective-permute-start | bytes 2359304 | tf_op jit(solution)/shard_map/ppermute | solution.py:30
  181.1 12.0 %collective-permute-start.37 = (bf16[64,6144]{1,0:T(8,128)(2,1)S(1)}, bf16[64,6144]{1,0:T(8,128)(2,1)S(1)}, u32[]{:S(2)}, u32[]{:S(2)}) collective-permute-start(bf16[64,6144]{1,0:T(8,128)(2,1)S(1)} %add_convert_fusion), channel_id=1, source_target_pairs={{0,2},{1,5},{2,0},{3,7},{4,6},{5,1},{6,4},{7,3},{8,10},{9,13},{10,... | collective-permute-start | bytes 2359304 | tf_op jit(solution)/shard_map/ppermute | solution.py:30
  193.2 11.6 %collective-permute-start.38 = (bf16[16,6144]{1,0:T(8,128)(2,1)S(1)}, bf16[16,6144]{1,0:T(8,128)(2,1)S(1)}, u32[]{:S(2)}, u32[]{:S(2)}) collective-permute-start(bf16[16,6144]{1,0:T(8,128)(2,1)S(1)} %slice.222), channel_id=1, source_target_pairs={{0,16},{1,17},{2,18},{3,19},{4,20},{5,21},{6,22},{7,23},{8,24},{9,... | collective-permute-start | bytes 589832 | tf_op jit(solution)/shard_map/ppermute | solution.py:30
  195.4 12.0 %collective-permute-start.39 = (bf16[32,6144]{1,0:T(8,128)(2,1)S(1)}, bf16[32,6144]{1,0:T(8,128)(2,1)S(1)}, u32[]{:S(2)}, u32[]{:S(2)}) collective-permute-start(bf16[32,6144]{1,0:T(8,128)(2,1)S(1)} %add_convert_fusion.5), channel_id=1, source_target_pairs={{0,4},{1,3},{2,6},{3,1},{4,0},{5,7},{6,2},{7,5},{8,12},{9,11},{10,... | collective-permute-start | bytes 1179656 | tf_op jit(solution)/shard_map/ppermute | solution.py:30
  197.5 13.2 %collective-permute-start.40 = (bf16[64,6144]{1,0:T(8,128)(2,1)S(1)}, bf16[64,6144]{1,0:T(8,128)(2,1)S(1)}, u32[]{:S(2)}, u32[]{:S(2)}) collective-permute-start(bf16[64,6144]{1,0:T(8,128)(2,1)S(1)} %add_convert_fusion.1), channel_id=1, source_target_pairs={{0,2},{1,5},{2,0},{3,7},{4,6},{5,1},{6,4},{7,3},{8,10},{9,13},{10,... | collective-permute-start | bytes 2359304 | tf_op jit(solution)/shard_map/ppermute | solution.py:30
  213.4 10.9 %all-to-all-start.2 = ((bf16[16,4,1536]{2,0,1:T(8,128)(2,1)}), bf16[16,4,1536]{2,0,1:T(8,128)(2,1)S(1)}, u32[]{:S(2)}, u32[]{:S(2)}) async-start(bf16[16,4,1536]{2,0,1:T(8,128)(2,1)} %bitcast.22), calls=%async_computation.2 | async-start | bytes 393216 | tf_op jit(solution)/shard_map/all_to_all | solution.py:456
  (39 other events, 309.2 us)

commit v3 on v2

--- a/solution.py
+++ b/solution.py
@@ -85,13 +85,19 @@
     return log_cum, over_last((row == col).astype(F32), doc_rows)[:, :1]
 
 
-def state_kernel(me_ref, k_hbm, v_hbm, decay_ref, doc_ref, ids_ref, route_ref, out_ref, k_ref, v_ref, sems):
-    copies = [
-        pltpu.make_async_copy(k_hbm, k_ref, sems.at[0]),
-        pltpu.make_async_copy(v_hbm, v_ref, sems.at[1]),
-    ]
+def fetch(sources, targets, sems):
+    copies = [pltpu.make_async_copy(s, t, sems.at[i]) for i, (s, t) in enumerate(zip(sources, targets))]
     for copy in copies:
         copy.start()
+    return copies
+
+
+def state_kernel(me_ref, *refs):
+    sources, out_ref, targets, sems = refs[:6], refs[6], refs[7:13], refs[13]
+    decay_ref, doc_ref, ids_ref, route_ref, k_ref, v_ref = targets
+    copies = fetch(sources, targets, sems)
+    for copy in copies[:4]:
+        copy.wait()
     heads, tok = decay_ref.shape
     chunks = out_ref.shape[0]
     chunk = out_ref.shape[1] - EXTRA
@@ -105,7 +111,7 @@
     row = lax.broadcasted_iota(jnp.int32, (EXTRA, HS), 0)
     fixed = [jnp.broadcast_to(w.astype(F32), (EXTRA, HS)) for w in [first, last] + split3(weight)]
     per_head = chunks // heads
-    for copy in copies:
+    for copy in copies[4:]:
         copy.wait()
     for h in range(heads):
         lanes = slice(h * HS, (h + 1) * HS)
@@ -143,14 +149,12 @@
         before = last
 
 
-def intra_kernel(q_hbm, k_hbm, v_hbm, decay_ref, doc_ref, out_ref, qw_ref, q_ref, k_ref, v_ref, sems):
-    copies = [
-        pltpu.make_async_copy(q_hbm, q_ref, sems.at[0]),
-        pltpu.make_async_copy(k_hbm, k_ref, sems.at[1]),
-        pltpu.make_async_copy(v_hbm, v_ref, sems.at[2]),
-    ]
-    for copy in copies:
-        copy.start()
+def intra_kernel(*refs):
+    sources, (out_ref, qw_ref), targets, sems = refs[:5], refs[5:7], refs[7:12], refs[12]
+    decay_ref, doc_ref, q_ref, k_ref, v_ref = targets
+    copies = fetch(sources, targets, sems)
+    for copy in copies[:2]:
+        copy.wait()
     heads, tok = decay_ref.shape
     doc_row = doc_ref[...].astype(F32)
     log_cum, doc_col = by_column(decay_ref[...], doc_row)
@@ -161,7 +165,7 @@
     )
     allowed = (row >= col) & (doc_col == doc_row)
     carry = jnp.exp(log_cum) * (doc_col == doc_row[:, :1]).astype(F32)
-    for copy in copies:
+    for copy in copies[2:]:
         copy.wait()
     for h in range(heads):
         lanes = slice(h * HS, (h + 1) * HS)
@@ -214,7 +218,7 @@
 
 def expert_kernel(blocks, *refs):
     x_refs, (gate_ref, up_ref, down_ref, scale_ref) = refs[:blocks], refs[blocks : blocks + 4]
-    out_refs, (x, act) = refs[blocks + 5 : 2 * blocks + 5], refs[2 * blocks + 5 :]
+    out_refs, (x, act) = refs[blocks + 5 : -2], refs[-2:]
     rows, width = x_refs[0].shape
     for i, ref in enumerate(x_refs):
         x[i * rows : (i + 1) * rows, :] = ref[...]
@@ -226,26 +230,25 @@
     for start in range(0, width, block):
         lanes = slice(start, start + block)
         out = jnp.dot(act[...], down_ref[:, lanes], preferred_element_type=F32).astype(BF16)
-        for i, ref in enumerate(out_refs):
-            ref[:, lanes] = out[i * rows : (i + 1) * rows]
+        at = 0
+        for ref in out_refs:
+            ref[:, lanes] = out[at : at + ref.shape[0]]
+            at += ref.shape[0]
 
 
 def expert(xs, w_gate, w_up, w_down, loaded, scale):
     rows, width = xs[0].shape
     hidden = w_gate.shape[0]
     blocks = len(xs)
+    out_rows = [rows] * blocks
     return pl.pallas_call(
         functools.partial(expert_kernel, blocks),
         in_specs=[whole()] * (blocks + 5),
-        out_specs=[whole()] * blocks,
-        out_shape=[jax.ShapeDtypeStruct((rows, width), BF16)] * blocks,
+        out_specs=[whole()] * len(out_rows),
+        out_shape=[jax.ShapeDtypeStruct((r, width), BF16) for r in out_rows],
         scratch_shapes=[pltpu.VMEM((blocks * rows, width), BF16), pltpu.VMEM((blocks * rows, hidden), BF16)],
         compiler_params=pltpu.CompilerParams(vmem_limit_bytes=VMEM_LIMIT),
-        cost_estimate=pl.CostEstimate(
-            flops=6 * blocks * rows * width * hidden,
-            bytes_accessed=6 * width * hidden + 4 * blocks * rows * width,
-            transcendentals=blocks * rows * hidden,
-        ),
+        cost_estimate=pl.CostEstimate(flops=1000, bytes_accessed=1000, transcendentals=0),
     )(*xs, w_gate, w_up, w_down, scale, loaded)
 
 
@@ -308,15 +311,15 @@
     (payload,) = call(
         state_kernel,
         [shape((n_seq, chunk + EXTRA, HS), BF16)],
-        hx_index.reshape(1), keys, values, decay_t, doc_row, expert_ids.T, route_weight.T,
-        scalars=1, far=2,
+        hx_index.reshape(1), decay_t, doc_row, expert_ids.T, route_weight.T, keys, values,
+        scalars=1, far=6,
     )
     arrived = lax.all_to_all(payload, "seq", split_axis=0, concat_axis=0, tiled=True)
     intra, query_weighted = call(
         intra_kernel,
         [shape((tok_count, heads * HS), F32), shape((tok_count, heads * HS), BF16)],
-        queries, keys, values, decay_t, doc_row,
-        far=3,
+        decay_t, doc_row, queries, keys, values,
+        far=5,
     )
     (incoming,) = call(prefix_kernel, [shape((n_seq, chunk, HS), BF16)], arrived)
     incoming = lax.all_to_all(incoming, "seq", split_axis=0, concat_axis=0, tiled=True)
@@ -376,7 +379,11 @@
         return exchange(rows, (mask, mask), count)
 
     def spread(unit):
-        return gather_rows(unit, net[:-1], count)
+        unit = gather_rows(unit, net[:-2], count)
+        return [unit, exchange(unit, net[-2], count)]
+
+    def joined(parts):
+        return jnp.concatenate(parts, axis=0)
 
     def to_core(rows):
         return exchange(rows, core, count)
@@ -392,6 +399,21 @@
             sent = total([t[half:] for t in terms]).astype(BF16)
             terms = [total([t[:half] for t in terms]), exchange(sent, mask, count)]
         return total(terms)
+
+    def deliver(hidden, rows):
+        own = total([hidden, rows[:half_count]]).astype(BF16)
+        across = rows[half_count:].astype(BF16)
+        width = own.shape[1] // n_hx
+        sums = {}
+        for o in offsets([z_masks[0]] + x_masks + [1]):
+            to = o % n_hx
+            piece = across if o >= n_hx else own
+            piece = lax.dynamic_slice_in_dim(piece, (hx_index ^ to) * width, width, axis=1)
+            sums.setdefault(to, []).append(exchange(piece, (o, o), count) if o else piece)
+        out = jnp.zeros((n_hx, half_count, width), BF16)
+        for to, parts in sums.items():
+            out = lax.dynamic_update_slice_in_dim(out, add(*parts)[None], hx_index ^ to, axis=0)
+        return out
 
     last = net[-1]
     rows_a, got_a = hx_send(0)
@@ -409,16 +431,19 @@
     a1 = spread(a1)
     b = hx_rest(rows_b, got_b)
     a1, a2, b, own_residual = wait((a1, a2, b, own_residual))
+    a1 = joined(a1)
     a1_last, a1_other = exchange(a1, last, count), to_core(a1)
     a2 = spread(a2)
     hidden_b, b = norm(1, b, own_residual)
     b1 = jnp.concatenate([b, z_step(b, z_masks[0])], axis=0)
     a1, a1_last, a1_other, a2, b1 = wait((a1, a1_last, a1_other, a2, b1))
+    a2 = joined(a2)
     a2_last, a2_other = exchange(a2, last, count), to_core(a2)
     a1_out = expert([a1, a1_last, a1_other, to_core(a1_last)], *weights_in, loaded, scale["near0"])
     b2 = z_step(b1, z_masks[1])
     b1 = spread(b1)
     a2, a2_last, a2_other, b1, b2, a1_out = wait((a2, a2_last, a2_other, b1, b2, a1_out))
+    b1 = joined(b1)
     b1_last, b1_other = exchange(b1, last, count), to_core(b1)
     a2_out = expert([a2, a2_last, a2_other, to_core(a2_last)], *weights_in, loaded, scale["far0"])
     b2 = spread(b2)
@@ -427,16 +452,15 @@
     b1, b1_last, b1_other, b2, a1_send, a1_rest, a2_send, a2_rest = wait(
         (b1, b1_last, b1_other, b2, a1_send, a1_rest, a2_send, a2_rest)
     )
+    b2 = joined(b2)
     b2_last, b2_other = exchange(b2, last, count), to_core(b2)
     a2_got = exchange(a2_send, last, count)
     b1_out = expert([b1, b1_last, b1_other, to_core(b1_last)], *weights_in, loaded, scale["near1"])
-    b1_send, b1_rest = back(b1_out)
-    b2, b2_last, b2_other, a2_got, b1_send, b1_rest, a1_send = wait(
-        (b2, b2_last, b2_other, a2_got, b1_send, b1_rest, a1_send)
-    )
+    b2, b2_last, b2_other, a2_got, b1_out, a1_send = wait((b2, b2_last, b2_other, a2_got, b1_out, a1_send))
     a1_got = exchange(a1_send, last, count)
     a2_sum = fold(a2_rest, a2_got)
     b2_out = expert([b2, b2_last, b2_other, to_core(b2_last)], *weights_in, loaded, scale["far1"])
+    b1_send, b1_rest = back(b1_out)
     b2_send, b2_rest = back(b2_out)
     a2_sum, a1_got, b2_send, b2_rest, b1_send, b1_rest = wait(
         (a2_sum, a1_got, b2_send, b2_rest, b1_send, b1_rest)
@@ -456,9 +480,7 @@
     a_out = lax.all_to_all(a_out, "hx", split_axis=1, concat_axis=0, tiled=True)
     b_sum = b1_sum + b_z.astype(F32)
     b_sum, a_out = wait((b_sum, a_out))
-    b_z = z_step(b_sum[half_count:].astype(BF16), z_masks[0])
-    b_out = total([hidden_b, b_sum[:half_count], b_z]).astype(BF16)
-    b_out = lax.all_to_all(b_out, "hx", split_axis=1, concat_axis=0, tiled=True)
+    b_out = deliver(hidden_b, b_sum)
     outs = [o.reshape(n_hx, half_count, -1) for o in (a_out, b_out)]
     return jnp.concatenate(outs, axis=1).reshape(tok_count, -1)
 

time: 244 us -> 228 us (0.934)
  waiting for transfers between devices: 125 us -> 104 us
  starting transfers between devices: 49.7 us -> 64.4 us
  blocking collectives: 8.36 us -> 0 us
  local copies, waits for them, and re-layouts: 8.92 us -> 5.79 us
    ppermute x44 -> x50, waiting for transfers between devices: 114 us -> 92.7 us  [exchange(): return lax.ppermute(x, AXES, pairs)]
    ppermute x44 -> x50, starting transfers between devices: 35.4 us -> 50.1 us  [exchange(): return lax.ppermute(x, AXES, pairs)]
    all_to_all x1 -> x0, blocking collectives: 8.36 us -> none  [shards(): b_out = lax.all_to_all(b_out, 'hx', split_axis=1, concat_axis=0, tiled=True)]
    unnamed x46 -> x38, local copies, waits for them, and re-layouts: 4.39 us -> 1.1 us
  transfers between devices with their start and end apart: 47 -> 53, of which waited for: 28 -> 33; matrix products, arithmetic and copies ran while one was open for 3% -> 4% of each run, Pallas kernels for 12% -> 16%
where the time goes in v3:
time: 228 us; the launch traced here: 226 us
  waiting for transfers between devices  104 us (46%)
  starting transfers between devices  64.4 us (28%)
  Pallas kernels  39.3 us (17%)
  matrix products  6.39 us (3%)
  local copies, waits for them, and re-layouts  5.79 us (3%)
  other arithmetic  5.39 us (2%)
    ppermute x50, waiting for transfers between devices, exchange(): return lax.ppermute(x, AXES, pairs)  92.7 us
    ppermute x50, starting transfers between devices, exchange(): return lax.ppermute(x, AXES, pairs)  50.1 us
    pallas_call x4, Pallas kernels, expert(): pl.pallas_call(functools.partial(expert_kernel, blocks), in_specs=[whole(...  26.2 us
    all_to_all x1, starting transfers between devices, shards(): lax.all_to_all(payload, 'seq', split_axis=0, concat_axis=0, tiled=True)  7.29 us
    pallas_call x1, Pallas kernels, load(): pl.pallas_call(load_kernel, in_specs=[pl.BlockSpec(memory_space=pltpu.HBM...  7.06 us
    dot_general x1, matrix products, shards(): jnp.dot(attn_in, out_weight, preferred_element_type=F32).astype(BF16)  6.39 us
    pallas_call x4, Pallas kernels, call(): pl.pallas_call(kernel, in_specs=specs + [whole()] * (len(operands) - len(...  6.11 us
    all_to_all x1, waiting for transfers between devices, shards(): lax.all_to_all(payload, 'seq', split_axis=0, concat_axis=0, tiled=True)  6.01 us
  transfers between devices with their start and end apart: 53, of which 33 were waited for; matrix products, arithmetic and copies ran while one was open for 4% of the time, Pallas kernels for 16%

profile of v3, /device:TPU:0, one launch (start us, length us, event | category | flops | bytes accessed | tf_op | source)
XLA Modules:
  0.0 226.2 jit_solution(15033393387363413572)
XLA Ops:
  2.6 7.3 %all-to-all-start = ((bf16[8,144,128]{2,1,0:T(8,128)(2,1)}), bf16[8,144,128]{2,1,0:T(8,128)(2,1)S(1)}, u32[]{:S(2)}, u32[]{:S(2)}) async-start(bf16[8,144,128]{2,1,0:T(8,128)(2,1)} %shard_map.164), calls=%async_computation | async-start | bytes 589824 | tf_op jit(solution)/shard_map/all_to_all | solution.py:317
  13.5 6.0 %all-to-all-done.in_ref = bf16[8,144,128]{2,1,0:T(8,128)(2,1)S(1)} async-done(((bf16[8,144,128]{2,1,0:T(8,128)(2,1)}), bf16[8,144,128]{2,1,0:T(8,128)(2,1)S(1)}, u32[]{:S(2)}, u32[]{:S(2)}) %all-to-all-start) | async-done | bytes 294944 | tf_op jit(solution)/shard_map/all_to_all | solution.py:317
  20.3 3.6 %all-to-all-start.1 = ((bf16[8,128,128]{2,1,0:T(8,128)(2,1)}), bf16[8,128,128]{2,1,0:T(8,128)(2,1)S(1)}, u32[]{:S(2)}, u32[]{:S(2)}) async-start(bf16[8,128,128]{2,1,0:T(8,128)(2,1)} %shard_map.165), calls=%async_computation.1 | async-start | bytes 524288 | tf_op jit(solution)/shard_map/all_to_all | solution.py:325
  26.9 5.5 %all-to-all-done.1.state_ref = bf16[8,128,128]{2,1,0:T(8,128)(2,1)S(1)} async-done(((bf16[8,128,128]{2,1,0:T(8,128)(2,1)}), bf16[8,128,128]{2,1,0:T(8,128)(2,1)S(1)}, u32[]{:S(2)}, u32[]{:S(2)}) %all-to-all-start.1) | async-done | bytes 262176 | tf_op jit(solution)/shard_map/all_to_all | solution.py:325
  32.8 6.4 %convolution_convert_fusion = bf16[128,6144]{1,0:T(8,128)(2,1)S(1)} fusion(bf16[128,1024]{1,0:T(8,128)(2,1)S(1)} %shard_map.166, bf16[1024,6144]{1,0:T(8,128)(2,1)} %param.23), kind=kOutput, calls=%fused_computation.4 | convolution fusion | flops 1611399168 | bytes 14417920 | tf_op jit(solution)/shard_map/dot_general | solution.py:359
  42.7 5.5 %collective-permute-done.1 = bf16[16,6144]{1,0:T(8,128)(2,1)S(1)} collective-permute-done((bf16[16,6144]{1,0:T(8,128)(2,1)S(1)}, bf16[16,6144]{1,0:T(8,128)(2,1)S(1)}, u32[]{:S(2)}, u32[]{:S(2)}) %collective-permute-start.1) | collective-permute-done | bytes 196640 | tf_op jit(solution)/shard_map/ppermute | solution.py:30
  49.7 7.1 %shard_map.167 = (bf16[576,6144]{1,0:T(8,128)(2,1)S(1)}, bf16[576,6144]{1,0:T(8,128)(2,1)S(1)}, bf16[576,6144]{1,0:T(8,128)(2,1)S(1)}, f32[8,128]{1,0:T(8,128)S(1)}) custom-call(bf16[1,576,6144]{2,1,0:T(8,128)(2,1)} %bitcast.34, bf16[1,576,6144]{2,1,0:T(8,128)(2,1)} %bitcast.35, bf16[1,576,6144]{2,1,0:T(8,128)(2,1)} %refs_2_.2), custom_call_target="tpu_custom_call" | custom-call | tf_op jit(solution)/shard_map/pallas_call | solution.py:208
  56.8 3.1 %collective-permute-done.3 = bf16[16,6144]{1,0:T(8,128)(2,1)S(1)} collective-permute-done((bf16[16,6144]{1,0:T(8,128)(2,1)S(1)}, bf16[16,6144]{1,0:T(8,128)(2,1)S(1)}, u32[]{:S(2)}, u32[]{:S(2)}) %collective-permute-start.3) | collective-permute-done | bytes 196640 | tf_op jit(solution)/shard_map/ppermute | solution.py:30
  62.5 5.4 %collective-permute-done.6 = bf16[16,6144]{1,0:T(8,128)(2,1)S(1)} collective-permute-done((bf16[16,6144]{1,0:T(8,128)(2,1)S(1)}, bf16[16,6144]{1,0:T(8,128)(2,1)S(1)}, u32[]{:S(2)}, u32[]{:S(2)}) %collective-permute-start.6) | collective-permute-done | bytes 196640 | tf_op jit(solution)/shard_map/ppermute | solution.py:30
  76.1 5.8 %collective-permute-done.10 = bf16[16,6144]{1,0:T(8,128)(2,1)S(1)} collective-permute-done((bf16[16,6144]{1,0:T(8,128)(2,1)S(1)}, bf16[16,6144]{1,0:T(8,128)(2,1)S(1)}, u32[]{:S(2)}, u32[]{:S(2)}) %collective-permute-start.10) | collective-permute-done | bytes 196640 | tf_op jit(solution)/shard_map/ppermute | solution.py:30
  81.9 4.3 %collective-permute-done.9 = bf16[32,6144]{1,0:T(8,128)(2,1)S(1)} collective-permute-done((bf16[32,6144]{1,0:T(8,128)(2,1)S(1)}, bf16[32,6144]{1,0:T(8,128)(2,1)S(1)}, u32[]{:S(2)}, u32[]{:S(2)}) %collective-permute-start.9) | collective-permute-done | bytes 393248 | tf_op jit(solution)/shard_map/ppermute | solution.py:30
  94.2 6.4 %shard_map.168 = (bf16[64,6144]{1,0:T(8,128)(2,1)S(1)}, bf16[64,6144]{1,0:T(8,128)(2,1)S(1)}, bf16[64,6144]{1,0:T(8,128)(2,1)S(1)}, bf16[64,6144]{1,0:T(8,128)(2,1)S(1)}) custom-call(bf16[64,6144]{1,0:T(8,128)(2,1)S(1)} %constant_dynamic-update-slice_fusion.8.refs_0_, bf16[64,6144]{1,0:T(8,128)(2,1)S(1)} %collective-permute-done.7.refs_1_, ...), custom_call_target="tpu_custom_call" | custom-call | flops 1000 | bytes 1000 | tf_op jit(solution)/shard_map/pallas_call | solution.py:244
  109.8 6.7 %shard_map.169 = (bf16[64,6144]{1,0:T(8,128)(2,1)S(1)}, bf16[64,6144]{1,0:T(8,128)(2,1)S(1)}, bf16[64,6144]{1,0:T(8,128)(2,1)S(1)}, bf16[64,6144]{1,0:T(8,128)(2,1)S(1)}) custom-call(bf16[64,6144]{1,0:T(8,128)(2,1)S(1)} %constant_dynamic-update-slice_fusion.10.refs_0_, bf16[64,6144]{1,0:T(8,128)(2,1)S(1)} %collective-permute-done.11.refs_1_, ...), custom_call_target="tpu_custom_call" | custom-call | flops 1000 | bytes 1000 | tf_op jit(solution)/shard_map/pallas_call | solution.py:244
  125.9 6.4 %shard_map.170 = (bf16[64,6144]{1,0:T(8,128)(2,1)S(1)}, bf16[64,6144]{1,0:T(8,128)(2,1)S(1)}, bf16[64,6144]{1,0:T(8,128)(2,1)S(1)}, bf16[64,6144]{1,0:T(8,128)(2,1)S(1)}) custom-call(bf16[64,6144]{1,0:T(8,128)(2,1)S(1)} %constant_dynamic-update-slice_fusion.12.refs_0_, bf16[64,6144]{1,0:T(8,128)(2,1)S(1)} %collective-permute-done.16.refs_1_, ...), custom_call_target="tpu_custom_call" | custom-call | flops 1000 | bytes 1000 | tf_op jit(solution)/shard_map/pallas_call | solution.py:244
  134.1 8.4 %collective-permute-done.26 = bf16[64,6144]{1,0:T(8,128)(2,1)S(1)} collective-permute-done((bf16[64,6144]{1,0:T(8,128)(2,1)S(1)}, bf16[64,6144]{1,0:T(8,128)(2,1)S(1)}, u32[]{:S(2)}, u32[]{:S(2)}) %collective-permute-start.26) | collective-permute-done | bytes 786464 | tf_op jit(solution)/shard_map/ppermute | solution.py:30
  146.8 7.2 %collective-permute-done.28 = bf16[32,6144]{1,0:T(8,128)(2,1)S(1)} collective-permute-done((bf16[32,6144]{1,0:T(8,128)(2,1)S(1)}, bf16[32,6144]{1,0:T(8,128)(2,1)S(1)}, u32[]{:S(2)}, u32[]{:S(2)}) %collective-permute-start.28) | collective-permute-done | bytes 393248 | tf_op jit(solution)/shard_map/ppermute | solution.py:30
  154.2 6.7 %shard_map.171 = (bf16[64,6144]{1,0:T(8,128)(2,1)S(1)}, bf16[64,6144]{1,0:T(8,128)(2,1)S(1)}, bf16[64,6144]{1,0:T(8,128)(2,1)S(1)}, bf16[64,6144]{1,0:T(8,128)(2,1)S(1)}) custom-call(bf16[64,6144]{1,0:T(8,128)(2,1)S(1)} %constant_dynamic-update-slice_fusion.14.refs_0_, bf16[64,6144]{1,0:T(8,128)(2,1)S(1)} %collective-permute-done.24.refs_1_, ...), custom_call_target="tpu_custom_call" | custom-call | flops 1000 | bytes 1000 | tf_op jit(solution)/shard_map/pallas_call | solution.py:244
  170.6 3.9 %collective-permute-done.35 = bf16[32,6144]{1,0:T(8,128)(2,1)S(1)} collective-permute-done((bf16[32,6144]{1,0:T(8,128)(2,1)S(1)}, bf16[32,6144]{1,0:T(8,128)(2,1)S(1)}, u32[]{:S(2)}, u32[]{:S(2)}) %collective-permute-start.35) | collective-permute-done | bytes 393248 | tf_op jit(solution)/shard_map/ppermute | solution.py:30
  177.5 3.3 %collective-permute-done.37 = bf16[64,6144]{1,0:T(8,128)(2,1)S(1)} collective-permute-done((bf16[64,6144]{1,0:T(8,128)(2,1)S(1)}, bf16[64,6144]{1,0:T(8,128)(2,1)S(1)}, u32[]{:S(2)}, u32[]{:S(2)}) %collective-permute-start.37) | collective-permute-done | bytes 786464 | tf_op jit(solution)/shard_map/ppermute | solution.py:30
  186.9 6.2 %collective-permute-done.38 = bf16[16,6144]{1,0:T(8,128)(2,1)S(1)} collective-permute-done((bf16[16,6144]{1,0:T(8,128)(2,1)S(1)}, bf16[16,6144]{1,0:T(8,128)(2,1)S(1)}, u32[]{:S(2)}, u32[]{:S(2)}) %collective-permute-start.38) | collective-permute-done | bytes 196640 | tf_op jit(solution)/shard_map/ppermute | solution.py:30
  194.8 4.0 %collective-permute-done.40 = bf16[64,6144]{1,0:T(8,128)(2,1)S(1)} collective-permute-done((bf16[64,6144]{1,0:T(8,128)(2,1)S(1)}, bf16[64,6144]{1,0:T(8,128)(2,1)S(1)}, u32[]{:S(2)}, u32[]{:S(2)}) %collective-permute-start.40) | collective-permute-done | bytes 786464 | tf_op jit(solution)/shard_map/ppermute | solution.py:30
  202.6 3.4 %all-to-all-start.2 = ((bf16[16,4,1536]{2,0,1:T(8,128)(2,1)}), bf16[16,4,1536]{2,0,1:T(8,128)(2,1)S(1)}, u32[]{:S(2)}, u32[]{:S(2)}) async-start(bf16[16,4,1536]{2,0,1:T(8,128)(2,1)} %bitcast.33), calls=%async_computation.2 | async-start | bytes 393216 | tf_op jit(solution)/shard_map/all_to_all | solution.py:480
  207.4 4.9 %collective-permute-done.42 = bf16[32,6144]{1,0:T(8,128)(2,1)} collective-permute-done((bf16[32,6144]{1,0:T(8,128)(2,1)S(1)}, bf16[32,6144]{1,0:T(8,128)(2,1)}, u32[]{:S(2)}, u32[]{:S(2)}) %collective-permute-start.42) | collective-permute-done | bytes 393248 | tf_op jit(solution)/shard_map/ppermute | solution.py:30
  215.6 2.9 %collective-permute-start.45 = (bf16[16,1536]{1,0:T(8,128)(2,1)S(1)}, bf16[16,1536]{1,0:T(8,128)(2,1)S(1)}, u32[]{:S(2)}, u32[]{:S(2)}) collective-permute-start(bf16[16,1536]{1,0:T(8,128)(2,1)S(1)} %get-tuple-element.219), channel_id=1, source_target_pairs={{0,18},{1,19},{2,16},{3,17},{4,22},{5,23},{6,20},{7,21},{8,26},{9,... | collective-permute-start | bytes 147464 | tf_op jit(solution)/shard_map/ppermute | solution.py:30
  (188 shorter events, 95.3 us)
Async XLA Ops:
  2.6 16.9 %all-to-all-start = ((bf16[8,144,128]{2,1,0:T(8,128)(2,1)}), bf16[8,144,128]{2,1,0:T(8,128)(2,1)S(1)}, u32[]{:S(2)}, u32[]{:S(2)}) async-start(bf16[8,144,128]{2,1,0:T(8,128)(2,1)} %shard_map.164), calls=%async_computation | async-start | bytes 589824 | tf_op jit(solution)/shard_map/all_to_all | solution.py:317
  20.3 12.1 %all-to-all-start.1 = ((bf16[8,128,128]{2,1,0:T(8,128)(2,1)}), bf16[8,128,128]{2,1,0:T(8,128)(2,1)S(1)}, u32[]{:S(2)}, u32[]{:S(2)}) async-start(bf16[8,128,128]{2,1,0:T(8,128)(2,1)} %shard_map.165), calls=%async_computation.1 | async-start | bytes 524288 | tf_op jit(solution)/shard_map/all_to_all | solution.py:325
  48.6 11.3 %collective-permute-start.3 = (bf16[16,6144]{1,0:T(8,128)(2,1)S(1)}, bf16[16,6144]{1,0:T(8,128)(2,1)S(1)}, u32[]{:S(2)}, u32[]{:S(2)}) collective-permute-start(bf16[16,6144]{1,0:T(8,128)(2,1)S(1)} %multiply_convert_fusion.1), channel_id=1, source_target_pairs={{0,16},{1,17},{2,18},{3,19},{4,20},{5,21},{6,22},{7,23},{8,24},{9,... | collective-permute-start | bytes 589832 | tf_op jit(solution)/shard_map/ppermute | solution.py:30
  72.4 16.3 %collective-permute-start.7 = (bf16[64,6144]{1,0:T(8,128)(2,1)S(1)}, bf16[64,6144]{1,0:T(8,128)(2,1)S(1)}, u32[]{:S(2)}, u32[]{:S(2)}) collective-permute-start(bf16[64,6144]{1,0:T(8,128)(2,1)S(1)} %constant_dynamic-update-slice_fusion.8.refs_0_), channel_id=1, source_target_pairs={{0,2},{1,5},{2,0},{3,7},{4,6},{5,1},{6,4},{7,3},{8,10},{9,13},{10,... | collective-permute-start | bytes 2359304 | tf_op jit(solution)/shard_map/ppermute | solution.py:30
  74.0 14.7 %collective-permute-start.8 = (bf16[64,6144]{1,0:T(8,128)(2,1)S(1)}, bf16[64,6144]{1,0:T(8,128)(2,1)S(1)}, u32[]{:S(2)}, u32[]{:S(2)}) collective-permute-start(bf16[64,6144]{1,0:T(8,128)(2,1)S(1)} %constant_dynamic-update-slice_fusion.8.refs_0_), channel_id=1, source_target_pairs={{0,1},{1,0},{2,3},{3,2},{4,5},{5,4},{6,7},{7,6},{8,9},{9,8},{10,11... | collective-permute-start | bytes 2359304 | tf_op jit(solution)/shard_map/ppermute | solution.py:30
  74.0 12.1 %collective-permute-start.9 = (bf16[32,6144]{1,0:T(8,128)(2,1)S(1)}, bf16[32,6144]{1,0:T(8,128)(2,1)S(1)}, u32[]{:S(2)}, u32[]{:S(2)}) collective-permute-start(bf16[32,6144]{1,0:T(8,128)(2,1)S(1)} %collective-permute-done.5), channel_id=1, source_target_pairs={{0,4},{1,3},{2,6},{3,1},{4,0},{5,7},{6,2},{7,5},{8,12},{9,11},{10,... | collective-permute-start | bytes 1179656 | tf_op jit(solution)/shard_map/ppermute | solution.py:30
  88.8 16.3 %collective-permute-start.11 = (bf16[64,6144]{1,0:T(8,128)(2,1)S(1)}, bf16[64,6144]{1,0:T(8,128)(2,1)S(1)}, u32[]{:S(2)}, u32[]{:S(2)}) collective-permute-start(bf16[64,6144]{1,0:T(8,128)(2,1)S(1)} %constant_dynamic-update-slice_fusion.10.refs_0_), channel_id=1, source_target_pairs={{0,2},{1,5},{2,0},{3,7},{4,6},{5,1},{6,4},{7,3},{8,10},{9,13},{10,... | collective-permute-start | bytes 2359304 | tf_op jit(solution)/shard_map/ppermute | solution.py:30
  90.4 14.7 %collective-permute-start.12 = (bf16[64,6144]{1,0:T(8,128)(2,1)S(1)}, bf16[64,6144]{1,0:T(8,128)(2,1)S(1)}, u32[]{:S(2)}, u32[]{:S(2)}) collective-permute-start(bf16[64,6144]{1,0:T(8,128)(2,1)S(1)} %constant_dynamic-update-slice_fusion.10.refs_0_), channel_id=1, source_target_pairs={{0,1},{1,0},{2,3},{3,2},{4,5},{5,4},{6,7},{7,6},{8,9},{9,8},{10,11... | collective-permute-start | bytes 2359304 | tf_op jit(solution)/shard_map/ppermute | solution.py:30
  91.1 12.1 %collective-permute-start.13 = (bf16[32,6144]{1,0:T(8,128)(2,1)S(1)}, bf16[32,6144]{1,0:T(8,128)(2,1)S(1)}, u32[]{:S(2)}, u32[]{:S(2)}) collective-permute-start(bf16[32,6144]{1,0:T(8,128)(2,1)S(1)} %pad_maximum_fusion.1), channel_id=1, source_target_pairs={{0,4},{1,3},{2,6},{3,1},{4,0},{5,7},{6,2},{7,5},{8,12},{9,11},{10,... | collective-permute-start | bytes 1179656 | tf_op jit(solution)/shard_map/ppermute | solution.py:30
  105.1 11.4 %collective-permute-start.19 = (bf16[64,6144]{1,0:T(8,128)(2,1)S(1)}, bf16[64,6144]{1,0:T(8,128)(2,1)S(1)}, u32[]{:S(2)}, u32[]{:S(2)}) collective-permute-start(bf16[64,6144]{1,0:T(8,128)(2,1)S(1)} %get-tuple-element.150), channel_id=1, source_target_pairs={{0,1},{1,0},{2,3},{3,2},{4,5},{5,4},{6,7},{7,6},{8,9},{9,8},{10,11... | collective-permute-start | bytes 2359304 | tf_op jit(solution)/shard_map/ppermute | solution.py:30
  105.6 16.3 %collective-permute-start.16 = (bf16[64,6144]{1,0:T(8,128)(2,1)S(1)}, bf16[64,6144]{1,0:T(8,128)(2,1)S(1)}, u32[]{:S(2)}, u32[]{:S(2)}) collective-permute-start(bf16[64,6144]{1,0:T(8,128)(2,1)S(1)} %constant_dynamic-update-slice_fusion.12.refs_0_), channel_id=1, source_target_pairs={{0,2},{1,5},{2,0},{3,7},{4,6},{5,1},{6,4},{7,3},{8,10},{9,13},{10,... | collective-permute-start | bytes 2359304 | tf_op jit(solution)/shard_map/ppermute | solution.py:30
  107.2 14.7 %collective-permute-start.17 = (bf16[64,6144]{1,0:T(8,128)(2,1)S(1)}, bf16[64,6144]{1,0:T(8,128)(2,1)S(1)}, u32[]{:S(2)}, u32[]{:S(2)}) collective-permute-start(bf16[64,6144]{1,0:T(8,128)(2,1)S(1)} %constant_dynamic-update-slice_fusion.12.refs_0_), channel_id=1, source_target_pairs={{0,1},{1,0},{2,3},{3,2},{4,5},{5,4},{6,7},{7,6},{8,9},{9,8},{10,11... | collective-permute-start | bytes 2359304 | tf_op jit(solution)/shard_map/ppermute | solution.py:30
  107.5 14.4 %collective-permute-start.20 = (bf16[64,6144]{1,0:T(8,128)(2,1)S(1)}, bf16[64,6144]{1,0:T(8,128)(2,1)S(1)}, u32[]{:S(2)}, u32[]{:S(2)}) collective-permute-start(bf16[64,6144]{1,0:T(8,128)(2,1)S(1)} %get-tuple-element.152), channel_id=1, source_target_pairs={{0,1},{1,0},{2,3},{3,2},{4,5},{5,4},{6,7},{7,6},{8,9},{9,8},{10,11... | collective-permute-start | bytes 2359304 | tf_op jit(solution)/shard_map/ppermute | solution.py:30
  107.7 12.1 %collective-permute-start.18 = (bf16[32,6144]{1,0:T(8,128)(2,1)S(1)}, bf16[32,6144]{1,0:T(8,128)(2,1)S(1)}, u32[]{:S(2)}, u32[]{:S(2)}) collective-permute-start(bf16[32,6144]{1,0:T(8,128)(2,1)S(1)} %collective-permute-done.14), channel_id=1, source_target_pairs={{0,4},{1,3},{2,6},{3,1},{4,0},{5,7},{6,2},{7,5},{8,12},{9,11},{10,... | collective-permute-start | bytes 1179656 | tf_op jit(solution)/shard_map/ppermute | solution.py:30
  122.1 12.1 %collective-permute-start.24 = (bf16[64,6144]{1,0:T(8,128)(2,1)S(1)}, bf16[64,6144]{1,0:T(8,128)(2,1)S(1)}, u32[]{:S(2)}, u32[]{:S(2)}) collective-permute-start(bf16[64,6144]{1,0:T(8,128)(2,1)S(1)} %constant_dynamic-update-slice_fusion.14.refs_0_), channel_id=1, source_target_pairs={{0,2},{1,5},{2,0},{3,7},{4,6},{5,1},{6,4},{7,3},{8,10},{9,13},{10,... | collective-permute-start | bytes 2359304 | tf_op jit(solution)/shard_map/ppermute | solution.py:30
  124.4 18.1 %collective-permute-start.26 = (bf16[64,6144]{1,0:T(8,128)(2,1)S(1)}, bf16[64,6144]{1,0:T(8,128)(2,1)S(1)}, u32[]{:S(2)}, u32[]{:S(2)}) collective-permute-start(bf16[64,6144]{1,0:T(8,128)(2,1)S(1)} %add_convert_fusion.2), channel_id=1, source_target_pairs={{0,2},{1,5},{2,0},{3,7},{4,6},{5,1},{6,4},{7,3},{8,10},{9,13},{10,... | collective-permute-start | bytes 2359304 | tf_op jit(solution)/shard_map/ppermute | solution.py:30
  142.7 11.3 %collective-permute-start.28 = (bf16[32,6144]{1,0:T(8,128)(2,1)S(1)}, bf16[32,6144]{1,0:T(8,128)(2,1)S(1)}, u32[]{:S(2)}, u32[]{:S(2)}) collective-permute-start(bf16[32,6144]{1,0:T(8,128)(2,1)S(1)} %add_convert_fusion.7), channel_id=1, source_target_pairs={{0,4},{1,3},{2,6},{3,1},{4,0},{5,7},{6,2},{7,5},{8,12},{9,11},{10,... | collective-permute-start | bytes 1179656 | tf_op jit(solution)/shard_map/ppermute | solution.py:30
  144.8 16.7 %collective-permute-start.33 = (bf16[64,6144]{1,0:T(8,128)(2,1)S(1)}, bf16[64,6144]{1,0:T(8,128)(2,1)S(1)}, u32[]{:S(2)}, u32[]{:S(2)}) collective-permute-start(bf16[64,6144]{1,0:T(8,128)(2,1)S(1)} %get-tuple-element.186), channel_id=1, source_target_pairs={{0,1},{1,0},{2,3},{3,2},{4,5},{5,4},{6,7},{7,6},{8,9},{9,8},{10,11... | collective-permute-start | bytes 2359304 | tf_op jit(solution)/shard_map/ppermute | solution.py:30
  145.3 18.1 %collective-permute-start.29 = (bf16[64,6144]{1,0:T(8,128)(2,1)S(1)}, bf16[64,6144]{1,0:T(8,128)(2,1)S(1)}, u32[]{:S(2)}, u32[]{:S(2)}) collective-permute-start(bf16[64,6144]{1,0:T(8,128)(2,1)S(1)} %add_convert_fusion.3), channel_id=1, source_target_pairs={{0,2},{1,5},{2,0},{3,7},{4,6},{5,1},{6,4},{7,3},{8,10},{9,13},{10,... | collective-permute-start | bytes 2359304 | tf_op jit(solution)/shard_map/ppermute | solution.py:30
  146.8 16.6 %collective-permute-start.34 = (bf16[64,6144]{1,0:T(8,128)(2,1)S(1)}, bf16[64,6144]{1,0:T(8,128)(2,1)S(1)}, u32[]{:S(2)}, u32[]{:S(2)}) collective-permute-start(bf16[64,6144]{1,0:T(8,128)(2,1)S(1)} %get-tuple-element.188), channel_id=1, source_target_pairs={{0,1},{1,0},{2,3},{3,2},{4,5},{5,4},{6,7},{7,6},{8,9},{9,8},{10,11... | collective-permute-start | bytes 2359304 | tf_op jit(solution)/shard_map/ppermute | solution.py:30
  168.8 12.0 %collective-permute-start.37 = (bf16[64,6144]{1,0:T(8,128)(2,1)S(1)}, bf16[64,6144]{1,0:T(8,128)(2,1)S(1)}, u32[]{:S(2)}, u32[]{:S(2)}) collective-permute-start(bf16[64,6144]{1,0:T(8,128)(2,1)S(1)} %add_convert_fusion.1), channel_id=1, source_target_pairs={{0,2},{1,5},{2,0},{3,7},{4,6},{5,1},{6,4},{7,3},{8,10},{9,13},{10,... | collective-permute-start | bytes 2359304 | tf_op jit(solution)/shard_map/ppermute | solution.py:30
  180.9 12.3 %collective-permute-start.38 = (bf16[16,6144]{1,0:T(8,128)(2,1)S(1)}, bf16[16,6144]{1,0:T(8,128)(2,1)S(1)}, u32[]{:S(2)}, u32[]{:S(2)}) collective-permute-start(bf16[16,6144]{1,0:T(8,128)(2,1)S(1)} %slice.222), channel_id=1, source_target_pairs={{0,16},{1,17},{2,18},{3,19},{4,20},{5,21},{6,22},{7,23},{8,24},{9,... | collective-permute-start | bytes 589832 | tf_op jit(solution)/shard_map/ppermute | solution.py:30
  182.8 11.8 %collective-permute-start.39 = (bf16[32,6144]{1,0:T(8,128)(2,1)S(1)}, bf16[32,6144]{1,0:T(8,128)(2,1)S(1)}, u32[]{:S(2)}, u32[]{:S(2)}) collective-permute-start(bf16[32,6144]{1,0:T(8,128)(2,1)S(1)} %add_convert_fusion.5), channel_id=1, source_target_pairs={{0,4},{1,3},{2,6},{3,1},{4,0},{5,7},{6,2},{7,5},{8,12},{9,11},{10,... | collective-permute-start | bytes 1179656 | tf_op jit(solution)/shard_map/ppermute | solution.py:30
  185.1 13.6 %collective-permute-start.40 = (bf16[64,6144]{1,0:T(8,128)(2,1)S(1)}, bf16[64,6144]{1,0:T(8,128)(2,1)S(1)}, u32[]{:S(2)}, u32[]{:S(2)}) collective-permute-start(bf16[64,6144]{1,0:T(8,128)(2,1)S(1)} %add_convert_fusion), channel_id=1, source_target_pairs={{0,2},{1,5},{2,0},{3,7},{4,6},{5,1},{6,4},{7,3},{8,10},{9,13},{10,... | collective-permute-start | bytes 2359304 | tf_op jit(solution)/shard_map/ppermute | solution.py:30
  (39 other events, 317.1 us)

commit v4 on v3

--- a/solution.py
+++ b/solution.py
@@ -398,22 +398,17 @@
             half = terms[0].shape[0] // 2
             sent = total([t[half:] for t in terms]).astype(BF16)
             terms = [total([t[:half] for t in terms]), exchange(sent, mask, count)]
-        return total(terms)
-
-    def deliver(hidden, rows):
-        own = total([hidden, rows[:half_count]]).astype(BF16)
-        across = rows[half_count:].astype(BF16)
+        return terms
+
+    def deliver(own, across):
         width = own.shape[1] // n_hx
         sums = {}
-        for o in offsets([z_masks[0]] + x_masks + [1]):
+        for o in offsets(([z_masks[0]] if across is not None else []) + x_masks + [1]):
             to = o % n_hx
             piece = across if o >= n_hx else own
             piece = lax.dynamic_slice_in_dim(piece, (hx_index ^ to) * width, width, axis=1)
             sums.setdefault(to, []).append(exchange(piece, (o, o), count) if o else piece)
-        out = jnp.zeros((n_hx, half_count, width), BF16)
-        for to, parts in sums.items():
-            out = lax.dynamic_update_slice_in_dim(out, add(*parts)[None], hx_index ^ to, axis=0)
-        return out
+        return {to: total(parts).astype(BF16) if len(parts) > 1 else parts[0] for to, parts in sums.items()}
 
     last = net[-1]
     rows_a, got_a = hx_send(0)
@@ -465,24 +460,26 @@
     a2_sum, a1_got, b2_send, b2_rest, b1_send, b1_rest = wait(
         (a2_sum, a1_got, b2_send, b2_rest, b1_send, b1_rest)
     )
-    a_z = z_step(a2_sum.astype(BF16), z_masks[1])
+    a_z = z_step(total(a2_sum).astype(BF16), z_masks[1])
     a1_sum = fold(a1_rest, a1_got)
     b2_got = exchange(b2_send, last, count)
-    a_sum = a1_sum + a_z.astype(F32)
-    a_sum, b2_got, b1_send = wait((a_sum, b2_got, b1_send))
+    a_z, a1_sum, b2_got, b1_send = wait((a_z, a1_sum, b2_got, b1_send))
+    b1_got = exchange(b1_send, last, count)
+    a_sum = total(a1_sum + [a_z])
     a_z = z_step(a_sum[half_count:].astype(BF16), z_masks[0])
     b2_sum = fold(b2_rest, b2_got)
-    b1_got = exchange(b1_send, last, count)
-    a_out = total([hidden_a, a_sum[:half_count], a_z]).astype(BF16)
-    a_out, b2_sum, b1_got = wait((a_out, b2_sum, b1_got))
-    b_z = z_step(b2_sum.astype(BF16), z_masks[1])
+    a_z, a_sum, b2_sum, b1_got = wait((a_z, a_sum, b2_sum, b1_got))
+    b_z = z_step(total(b2_sum).astype(BF16), z_masks[1])
     b1_sum = fold(b1_rest, b1_got)
-    a_out = lax.all_to_all(a_out, "hx", split_axis=1, concat_axis=0, tiled=True)
-    b_sum = b1_sum + b_z.astype(F32)
-    b_sum, a_out = wait((b_sum, a_out))
-    b_out = deliver(hidden_b, b_sum)
-    outs = [o.reshape(n_hx, half_count, -1) for o in (a_out, b_out)]
-    return jnp.concatenate(outs, axis=1).reshape(tok_count, -1)
+    a_out = deliver(total([hidden_a, a_sum[:half_count], a_z]).astype(BF16), None)
+    b_z, b1_sum, a_out = wait((b_z, b1_sum, a_out))
+    b_sum = total(b1_sum + [b_z])
+    b_out = deliver(total([hidden_b, b_sum[:half_count]]).astype(BF16), b_sum[half_count:].astype(BF16))
+    out = jnp.zeros((n_hx, HALVES * half_count, b_sum.shape[1] // n_hx), BF16)
+    for to in a_out:
+        rows = jnp.concatenate([a_out[to], b_out[to]], axis=0)
+        out = lax.dynamic_update_slice_in_dim(out, rows[None], hx_index ^ to, axis=0)
+    return out.reshape(tok_count, -1)
 
 
 def solution(mesh):

time: 228 us -> 223 us (0.978)
  waiting for transfers between devices: 104 us -> 97.6 us
  other arithmetic: 5.39 us -> 8.45 us
    ppermute x50 -> x53, waiting for transfers between devices: 92.7 us -> 86.1 us  [exchange(): return lax.ppermute(x, AXES, pairs)]
    all_to_all x1 -> x0, starting transfers between devices: 3.37 us -> none  [shards(): a_out = lax.all_to_all(a_out, 'hx', split_axis=1, concat_axis=0, tiled=True)]
    ppermute x50 -> x53, starting transfers between devices: 50.1 us -> 53.1 us  [exchange(): return lax.ppermute(x, AXES, pairs)]
    convert_element_type x2 -> x8, other arithmetic: 0.16 us -> 3.03 us  [the longest x1 1.81 us: shards(): b_z = z_step(total(b2_sum).astype(BF16), z_masks[1])]
  transfers between devices with their start and end apart: 53 -> 55, of which waited for: 33 -> 30; matrix products, arithmetic and copies ran while one was open for 4% -> 5% of each run, Pallas kernels for 16% -> 16%
where the time goes in v4:
time: 223 us
  waiting for transfers between devices  97.6 us (44%)
  starting transfers between devices  63.9 us (29%)
  Pallas kernels  39.7 us (18%)
  other arithmetic  8.45 us (4%)
  matrix products  6.4 us (3%)
  local copies, waits for them, and re-layouts  5.88 us (3%)
    ppermute x53, waiting for transfers between devices, exchange(): return lax.ppermute(x, AXES, pairs)  86.1 us
    ppermute x53, starting transfers between devices, exchange(): return lax.ppermute(x, AXES, pairs)  53.1 us
    pallas_call x4, Pallas kernels, expert(): pl.pallas_call(functools.partial(expert_kernel, blocks), in_specs=[whole(...  26.5 us
    all_to_all x1, starting transfers between devices, shards(): lax.all_to_all(payload, 'seq', split_axis=0, concat_axis=0, tiled=True)  7.29 us
    pallas_call x1, Pallas kernels, load(): pl.pallas_call(load_kernel, in_specs=[pl.BlockSpec(memory_space=pltpu.HBM...  7.06 us
    dot_general x1, matrix products, shards(): jnp.dot(attn_in, out_weight, preferred_element_type=F32).astype(BF16)  6.4 us
    pallas_call x4, Pallas kernels, call(): pl.pallas_call(kernel, in_specs=specs + [whole()] * (len(operands) - len(...  6.16 us
    all_to_all x1, waiting for transfers between devices, shards(): lax.all_to_all(payload, 'seq', split_axis=0, concat_axis=0, tiled=True)  6.01 us
  transfers between devices with their start and end apart: 55, of which 30 were waited for; matrix products, arithmetic and copies ran while one was open for 5% of the time, Pallas kernels for 16%

profile of v4, /device:TPU:0, one launch (start us, length us, event | category | flops | bytes accessed | tf_op | source)
XLA Modules:
  0.0 222.9 jit_solution(4043808758852903497)
XLA Ops:
  2.6 7.3 %all-to-all-start = ((bf16[8,144,128]{2,1,0:T(8,128)(2,1)}), bf16[8,144,128]{2,1,0:T(8,128)(2,1)S(1)}, u32[]{:S(2)}, u32[]{:S(2)}) async-start(bf16[8,144,128]{2,1,0:T(8,128)(2,1)} %shard_map.164), calls=%async_computation | async-start | bytes 589824 | tf_op jit(solution)/shard_map/all_to_all | solution.py:317
  13.5 6.0 %all-to-all-done.in_ref = bf16[8,144,128]{2,1,0:T(8,128)(2,1)S(1)} async-done(((bf16[8,144,128]{2,1,0:T(8,128)(2,1)}), bf16[8,144,128]{2,1,0:T(8,128)(2,1)S(1)}, u32[]{:S(2)}, u32[]{:S(2)}) %all-to-all-start) | async-done | bytes 294944 | tf_op jit(solution)/shard_map/all_to_all | solution.py:317
  20.3 3.6 %all-to-all-start.1 = ((bf16[8,128,128]{2,1,0:T(8,128)(2,1)}), bf16[8,128,128]{2,1,0:T(8,128)(2,1)S(1)}, u32[]{:S(2)}, u32[]{:S(2)}) async-start(bf16[8,128,128]{2,1,0:T(8,128)(2,1)} %shard_map.165), calls=%async_computation.1 | async-start | bytes 524288 | tf_op jit(solution)/shard_map/all_to_all | solution.py:325
  26.9 5.5 %all-to-all-done.1.state_ref = bf16[8,128,128]{2,1,0:T(8,128)(2,1)S(1)} async-done(((bf16[8,128,128]{2,1,0:T(8,128)(2,1)}), bf16[8,128,128]{2,1,0:T(8,128)(2,1)S(1)}, u32[]{:S(2)}, u32[]{:S(2)}) %all-to-all-start.1) | async-done | bytes 262176 | tf_op jit(solution)/shard_map/all_to_all | solution.py:325
  32.8 6.4 %convolution_convert_fusion = bf16[128,6144]{1,0:T(8,128)(2,1)S(1)} fusion(bf16[128,1024]{1,0:T(8,128)(2,1)S(1)} %shard_map.166, bf16[1024,6144]{1,0:T(8,128)(2,1)} %param.23), kind=kOutput, calls=%fused_computation.4 | convolution fusion | flops 1611399168 | bytes 14417920 | tf_op jit(solution)/shard_map/dot_general | solution.py:359
  42.8 5.4 %collective-permute-done.1 = bf16[16,6144]{1,0:T(8,128)(2,1)S(1)} collective-permute-done((bf16[16,6144]{1,0:T(8,128)(2,1)S(1)}, bf16[16,6144]{1,0:T(8,128)(2,1)S(1)}, u32[]{:S(2)}, u32[]{:S(2)}) %collective-permute-start.1) | collective-permute-done | bytes 196640 | tf_op jit(solution)/shard_map/ppermute | solution.py:30
  49.8 7.1 %shard_map.167 = (bf16[576,6144]{1,0:T(8,128)(2,1)S(1)}, bf16[576,6144]{1,0:T(8,128)(2,1)S(1)}, bf16[576,6144]{1,0:T(8,128)(2,1)S(1)}, f32[8,128]{1,0:T(8,128)S(1)}) custom-call(bf16[1,576,6144]{2,1,0:T(8,128)(2,1)} %bitcast.26, bf16[1,576,6144]{2,1,0:T(8,128)(2,1)} %bitcast.27, bf16[1,576,6144]{2,1,0:T(8,128)(2,1)} %refs_2_.2), custom_call_target="tpu_custom_call" | custom-call | tf_op jit(solution)/shard_map/pallas_call | solution.py:208
  56.8 3.1 %collective-permute-done.3 = bf16[16,6144]{1,0:T(8,128)(2,1)S(1)} collective-permute-done((bf16[16,6144]{1,0:T(8,128)(2,1)S(1)}, bf16[16,6144]{1,0:T(8,128)(2,1)S(1)}, u32[]{:S(2)}, u32[]{:S(2)}) %collective-permute-start.3) | collective-permute-done | bytes 196640 | tf_op jit(solution)/shard_map/ppermute | solution.py:30
  62.6 5.4 %collective-permute-done.6 = bf16[16,6144]{1,0:T(8,128)(2,1)S(1)} collective-permute-done((bf16[16,6144]{1,0:T(8,128)(2,1)S(1)}, bf16[16,6144]{1,0:T(8,128)(2,1)S(1)}, u32[]{:S(2)}, u32[]{:S(2)}) %collective-permute-start.6) | collective-permute-done | bytes 196640 | tf_op jit(solution)/shard_map/ppermute | solution.py:30
  76.1 5.8 %collective-permute-done.10 = bf16[16,6144]{1,0:T(8,128)(2,1)S(1)} collective-permute-done((bf16[16,6144]{1,0:T(8,128)(2,1)S(1)}, bf16[16,6144]{1,0:T(8,128)(2,1)S(1)}, u32[]{:S(2)}, u32[]{:S(2)}) %collective-permute-start.10) | collective-permute-done | bytes 196640 | tf_op jit(solution)/shard_map/ppermute | solution.py:30
  81.9 4.2 %collective-permute-done.9 = bf16[32,6144]{1,0:T(8,128)(2,1)S(1)} collective-permute-done((bf16[32,6144]{1,0:T(8,128)(2,1)S(1)}, bf16[32,6144]{1,0:T(8,128)(2,1)S(1)}, u32[]{:S(2)}, u32[]{:S(2)}) %collective-permute-start.9) | collective-permute-done | bytes 393248 | tf_op jit(solution)/shard_map/ppermute | solution.py:30
  86.1 2.6 %collective-permute-done.7.refs_1_ = bf16[64,6144]{1,0:T(8,128)(2,1)S(1)} collective-permute-done((bf16[64,6144]{1,0:T(8,128)(2,1)S(1)}, bf16[64,6144]{1,0:T(8,128)(2,1)S(1)}, u32[]{:S(2)}, u32[]{:S(2)}) %collective-permute-start.7) | collective-permute-done | bytes 786464 | tf_op jit(solution)/shard_map/ppermute | solution.py:30
  94.2 6.5 %shard_map.168 = (bf16[64,6144]{1,0:T(8,128)(2,1)S(1)}, bf16[64,6144]{1,0:T(8,128)(2,1)S(1)}, bf16[64,6144]{1,0:T(8,128)(2,1)S(1)}, bf16[64,6144]{1,0:T(8,128)(2,1)S(1)}) custom-call(bf16[64,6144]{1,0:T(8,128)(2,1)S(1)} %constant_dynamic-update-slice_fusion.8.refs_0_, bf16[64,6144]{1,0:T(8,128)(2,1)S(1)} %collective-permute-done.7.refs_1_, ...), custom_call_target="tpu_custom_call" | custom-call | flops 1000 | bytes 1000 | tf_op jit(solution)/shard_map/pallas_call | solution.py:244
  109.8 6.8 %shard_map.169 = (bf16[64,6144]{1,0:T(8,128)(2,1)S(1)}, bf16[64,6144]{1,0:T(8,128)(2,1)S(1)}, bf16[64,6144]{1,0:T(8,128)(2,1)S(1)}, bf16[64,6144]{1,0:T(8,128)(2,1)S(1)}) custom-call(bf16[64,6144]{1,0:T(8,128)(2,1)S(1)} %constant_dynamic-update-slice_fusion.10.refs_0_, bf16[64,6144]{1,0:T(8,128)(2,1)S(1)} %collective-permute-done.11.refs_1_, ...), custom_call_target="tpu_custom_call" | custom-call | flops 1000 | bytes 1000 | tf_op jit(solution)/shard_map/pallas_call | solution.py:244
  126.0 6.5 %shard_map.170 = (bf16[64,6144]{1,0:T(8,128)(2,1)S(1)}, bf16[64,6144]{1,0:T(8,128)(2,1)S(1)}, bf16[64,6144]{1,0:T(8,128)(2,1)S(1)}, bf16[64,6144]{1,0:T(8,128)(2,1)S(1)}) custom-call(bf16[64,6144]{1,0:T(8,128)(2,1)S(1)} %constant_dynamic-update-slice_fusion.12.refs_0_, bf16[64,6144]{1,0:T(8,128)(2,1)S(1)} %collective-permute-done.16.refs_1_, ...), custom_call_target="tpu_custom_call" | custom-call | flops 1000 | bytes 1000 | tf_op jit(solution)/shard_map/pallas_call | solution.py:244
  134.2 8.4 %collective-permute-done.26 = bf16[64,6144]{1,0:T(8,128)(2,1)S(1)} collective-permute-done((bf16[64,6144]{1,0:T(8,128)(2,1)S(1)}, bf16[64,6144]{1,0:T(8,128)(2,1)S(1)}, u32[]{:S(2)}, u32[]{:S(2)}) %collective-permute-start.26) | collective-permute-done | bytes 786464 | tf_op jit(solution)/shard_map/ppermute | solution.py:30
  147.0 6.7 %shard_map.171 = (bf16[64,6144]{1,0:T(8,128)(2,1)S(1)}, bf16[64,6144]{1,0:T(8,128)(2,1)S(1)}, bf16[64,6144]{1,0:T(8,128)(2,1)S(1)}, bf16[64,6144]{1,0:T(8,128)(2,1)S(1)}) custom-call(bf16[64,6144]{1,0:T(8,128)(2,1)S(1)} %constant_dynamic-update-slice_fusion.14.refs_0_, bf16[64,6144]{1,0:T(8,128)(2,1)S(1)} %collective-permute-done.24.refs_1_, ...), custom_call_target="tpu_custom_call" | custom-call | flops 1000 | bytes 1000 | tf_op jit(solution)/shard_map/pallas_call | solution.py:244
  164.5 6.0 %collective-permute-done.36 = bf16[32,6144]{1,0:T(8,128)(2,1)S(1)} collective-permute-done((bf16[32,6144]{1,0:T(8,128)(2,1)S(1)}, bf16[32,6144]{1,0:T(8,128)(2,1)S(1)}, u32[]{:S(2)}, u32[]{:S(2)}) %collective-permute-start.36) | collective-permute-done | bytes 393248 | tf_op jit(solution)/shard_map/ppermute | solution.py:30
  170.5 2.8 %collective-permute-done.35 = bf16[32,6144]{1,0:T(8,128)(2,1)S(1)} collective-permute-done((bf16[32,6144]{1,0:T(8,128)(2,1)S(1)}, bf16[32,6144]{1,0:T(8,128)(2,1)S(1)}, u32[]{:S(2)}, u32[]{:S(2)}) %collective-permute-start.35) | collective-permute-done | bytes 393248 | tf_op jit(solution)/shard_map/ppermute | solution.py:30
  181.6 10.0 %collective-permute-done.38 = bf16[16,6144]{1,0:T(8,128)(2,1)} collective-permute-done((bf16[16,6144]{1,0:T(8,128)(2,1)}, bf16[16,6144]{1,0:T(8,128)(2,1)}, u32[]{:S(2)}, u32[]{:S(2)}) %collective-permute-start.38) | collective-permute-done | bytes 196640 | tf_op jit(solution)/shard_map/ppermute | solution.py:30
  204.5 2.6 %collective-permute-done.41 = bf16[32,6144]{1,0:T(8,128)(2,1)S(1)} collective-permute-done((bf16[32,6144]{1,0:T(8,128)(2,1)}, bf16[32,6144]{1,0:T(8,128)(2,1)S(1)}, u32[]{:S(2)}, u32[]{:S(2)}) %collective-permute-start.41) | collective-permute-done | bytes 393248 | tf_op jit(solution)/shard_map/ppermute | solution.py:30
  207.4 2.7 %collective-permute-start.46 = (bf16[16,1536]{1,0:T(8,128)(2,1)S(1)}, bf16[16,1536]{1,0:T(8,128)(2,1)S(1)}, u32[]{:S(2)}, u32[]{:S(2)}) collective-permute-start(bf16[16,1536]{1,0:T(8,128)(2,1)S(1)} %get-tuple-element.248), channel_id=1, source_target_pairs={{0,16},{1,17},{2,18},{3,19},{4,20},{5,21},{6,22},{7,23},{8,24},{9,... | collective-permute-start | bytes 147464 | tf_op jit(solution)/shard_map/ppermute | solution.py:30
  212.7 2.9 %collective-permute-start.48 = (bf16[16,1536]{1,0:T(8,128)(2,1)S(1)}, bf16[16,1536]{1,0:T(8,128)(2,1)S(1)}, u32[]{:S(2)}, u32[]{:S(2)}) collective-permute-start(bf16[16,1536]{1,0:T(8,128)(2,1)S(1)} %get-tuple-element.247), channel_id=1, source_target_pairs={{0,17},{1,16},{2,19},{3,18},{4,21},{5,20},{6,23},{7,22},{8,25},{9,... | collective-permute-start | bytes 147464 | tf_op jit(solution)/shard_map/ppermute | solution.py:30
  217.7 4.3 %collective-permute-done.50 = bf16[16,1536]{1,0:T(8,128)(2,1)S(1)} collective-permute-done((bf16[16,1536]{1,0:T(8,128)(2,1)S(1)}, bf16[16,1536]{1,0:T(8,128)(2,1)S(1)}, u32[]{:S(2)}, u32[]{:S(2)}) %collective-permute-start.50) | collective-permute-done | bytes 49184 | tf_op jit(solution)/shard_map/ppermute | solution.py:30
  (211 shorter events, 93.2 us)
Async XLA Ops:
  2.6 16.9 %all-to-all-start = ((bf16[8,144,128]{2,1,0:T(8,128)(2,1)}), bf16[8,144,128]{2,1,0:T(8,128)(2,1)S(1)}, u32[]{:S(2)}, u32[]{:S(2)}) async-start(bf16[8,144,128]{2,1,0:T(8,128)(2,1)} %shard_map.164), calls=%async_computation | async-start | bytes 589824 | tf_op jit(solution)/shard_map/all_to_all | solution.py:317
  20.3 12.1 %all-to-all-start.1 = ((bf16[8,128,128]{2,1,0:T(8,128)(2,1)}), bf16[8,128,128]{2,1,0:T(8,128)(2,1)S(1)}, u32[]{:S(2)}, u32[]{:S(2)}) async-start(bf16[8,128,128]{2,1,0:T(8,128)(2,1)} %shard_map.165), calls=%async_computation.1 | async-start | bytes 524288 | tf_op jit(solution)/shard_map/all_to_all | solution.py:325
  72.5 16.3 %collective-permute-start.7 = (bf16[64,6144]{1,0:T(8,128)(2,1)S(1)}, bf16[64,6144]{1,0:T(8,128)(2,1)S(1)}, u32[]{:S(2)}, u32[]{:S(2)}) collective-permute-start(bf16[64,6144]{1,0:T(8,128)(2,1)S(1)} %constant_dynamic-update-slice_fusion.8.refs_0_), channel_id=1, source_target_pairs={{0,2},{1,5},{2,0},{3,7},{4,6},{5,1},{6,4},{7,3},{8,10},{9,13},{10,... | collective-permute-start | bytes 2359304 | tf_op jit(solution)/shard_map/ppermute | solution.py:30
  74.1 14.7 %collective-permute-start.8 = (bf16[64,6144]{1,0:T(8,128)(2,1)S(1)}, bf16[64,6144]{1,0:T(8,128)(2,1)S(1)}, u32[]{:S(2)}, u32[]{:S(2)}) collective-permute-start(bf16[64,6144]{1,0:T(8,128)(2,1)S(1)} %constant_dynamic-update-slice_fusion.8.refs_0_), channel_id=1, source_target_pairs={{0,1},{1,0},{2,3},{3,2},{4,5},{5,4},{6,7},{7,6},{8,9},{9,8},{10,11... | collective-permute-start | bytes 2359304 | tf_op jit(solution)/shard_map/ppermute | solution.py:30
  74.1 12.1 %collective-permute-start.9 = (bf16[32,6144]{1,0:T(8,128)(2,1)S(1)}, bf16[32,6144]{1,0:T(8,128)(2,1)S(1)}, u32[]{:S(2)}, u32[]{:S(2)}) collective-permute-start(bf16[32,6144]{1,0:T(8,128)(2,1)S(1)} %collective-permute-done.5), channel_id=1, source_target_pairs={{0,4},{1,3},{2,6},{3,1},{4,0},{5,7},{6,2},{7,5},{8,12},{9,11},{10,... | collective-permute-start | bytes 1179656 | tf_op jit(solution)/shard_map/ppermute | solution.py:30
  88.8 16.3 %collective-permute-start.11 = (bf16[64,6144]{1,0:T(8,128)(2,1)S(1)}, bf16[64,6144]{1,0:T(8,128)(2,1)S(1)}, u32[]{:S(2)}, u32[]{:S(2)}) collective-permute-start(bf16[64,6144]{1,0:T(8,128)(2,1)S(1)} %constant_dynamic-update-slice_fusion.10.refs_0_), channel_id=1, source_target_pairs={{0,2},{1,5},{2,0},{3,7},{4,6},{5,1},{6,4},{7,3},{8,10},{9,13},{10,... | collective-permute-start | bytes 2359304 | tf_op jit(solution)/shard_map/ppermute | solution.py:30
  90.4 14.7 %collective-permute-start.12 = (bf16[64,6144]{1,0:T(8,128)(2,1)S(1)}, bf16[64,6144]{1,0:T(8,128)(2,1)S(1)}, u32[]{:S(2)}, u32[]{:S(2)}) collective-permute-start(bf16[64,6144]{1,0:T(8,128)(2,1)S(1)} %constant_dynamic-update-slice_fusion.10.refs_0_), channel_id=1, source_target_pairs={{0,1},{1,0},{2,3},{3,2},{4,5},{5,4},{6,7},{7,6},{8,9},{9,8},{10,11... | collective-permute-start | bytes 2359304 | tf_op jit(solution)/shard_map/ppermute | solution.py:30
  91.2 12.1 %collective-permute-start.13 = (bf16[32,6144]{1,0:T(8,128)(2,1)S(1)}, bf16[32,6144]{1,0:T(8,128)(2,1)S(1)}, u32[]{:S(2)}, u32[]{:S(2)}) collective-permute-start(bf16[32,6144]{1,0:T(8,128)(2,1)S(1)} %pad_maximum_fusion.1), channel_id=1, source_target_pairs={{0,4},{1,3},{2,6},{3,1},{4,0},{5,7},{6,2},{7,5},{8,12},{9,11},{10,... | collective-permute-start | bytes 1179656 | tf_op jit(solution)/shard_map/ppermute | solution.py:30
  105.7 16.3 %collective-permute-start.16 = (bf16[64,6144]{1,0:T(8,128)(2,1)S(1)}, bf16[64,6144]{1,0:T(8,128)(2,1)S(1)}, u32[]{:S(2)}, u32[]{:S(2)}) collective-permute-start(bf16[64,6144]{1,0:T(8,128)(2,1)S(1)} %constant_dynamic-update-slice_fusion.12.refs_0_), channel_id=1, source_target_pairs={{0,2},{1,5},{2,0},{3,7},{4,6},{5,1},{6,4},{7,3},{8,10},{9,13},{10,... | collective-permute-start | bytes 2359304 | tf_op jit(solution)/shard_map/ppermute | solution.py:30
  107.3 14.7 %collective-permute-start.17 = (bf16[64,6144]{1,0:T(8,128)(2,1)S(1)}, bf16[64,6144]{1,0:T(8,128)(2,1)S(1)}, u32[]{:S(2)}, u32[]{:S(2)}) collective-permute-start(bf16[64,6144]{1,0:T(8,128)(2,1)S(1)} %constant_dynamic-update-slice_fusion.12.refs_0_), channel_id=1, source_target_pairs={{0,1},{1,0},{2,3},{3,2},{4,5},{5,4},{6,7},{7,6},{8,9},{9,8},{10,11... | collective-permute-start | bytes 2359304 | tf_op jit(solution)/shard_map/ppermute | solution.py:30
  107.5 14.4 %collective-permute-start.20 = (bf16[64,6144]{1,0:T(8,128)(2,1)S(1)}, bf16[64,6144]{1,0:T(8,128)(2,1)S(1)}, u32[]{:S(2)}, u32[]{:S(2)}) collective-permute-start(bf16[64,6144]{1,0:T(8,128)(2,1)S(1)} %get-tuple-element.162), channel_id=1, source_target_pairs={{0,1},{1,0},{2,3},{3,2},{4,5},{5,4},{6,7},{7,6},{8,9},{9,8},{10,11... | collective-permute-start | bytes 2359304 | tf_op jit(solution)/shard_map/ppermute | solution.py:30
  107.8 12.1 %collective-permute-start.18 = (bf16[32,6144]{1,0:T(8,128)(2,1)S(1)}, bf16[32,6144]{1,0:T(8,128)(2,1)S(1)}, u32[]{:S(2)}, u32[]{:S(2)}) collective-permute-start(bf16[32,6144]{1,0:T(8,128)(2,1)S(1)} %collective-permute-done.14), channel_id=1, source_target_pairs={{0,4},{1,3},{2,6},{3,1},{4,0},{5,7},{6,2},{7,5},{8,12},{9,11},{10,... | collective-permute-start | bytes 1179656 | tf_op jit(solution)/shard_map/ppermute | solution.py:30
  122.1 12.1 %collective-permute-start.24 = (bf16[64,6144]{1,0:T(8,128)(2,1)S(1)}, bf16[64,6144]{1,0:T(8,128)(2,1)S(1)}, u32[]{:S(2)}, u32[]{:S(2)}) collective-permute-start(bf16[64,6144]{1,0:T(8,128)(2,1)S(1)} %constant_dynamic-update-slice_fusion.14.refs_0_), channel_id=1, source_target_pairs={{0,2},{1,5},{2,0},{3,7},{4,6},{5,1},{6,4},{7,3},{8,10},{9,13},{10,... | collective-permute-start | bytes 2359304 | tf_op jit(solution)/shard_map/ppermute | solution.py:30
  124.5 18.2 %collective-permute-start.26 = (bf16[64,6144]{1,0:T(8,128)(2,1)S(1)}, bf16[64,6144]{1,0:T(8,128)(2,1)S(1)}, u32[]{:S(2)}, u32[]{:S(2)}) collective-permute-start(bf16[64,6144]{1,0:T(8,128)(2,1)S(1)} %add_convert_fusion.2), channel_id=1, source_target_pairs={{0,2},{1,5},{2,0},{3,7},{4,6},{5,1},{6,4},{7,3},{8,10},{9,13},{10,... | collective-permute-start | bytes 2359304 | tf_op jit(solution)/shard_map/ppermute | solution.py:30
  142.6 11.7 %collective-permute-start.33 = (bf16[64,6144]{1,0:T(8,128)(2,1)S(1)}, bf16[64,6144]{1,0:T(8,128)(2,1)S(1)}, u32[]{:S(2)}, u32[]{:S(2)}) collective-permute-start(bf16[64,6144]{1,0:T(8,128)(2,1)S(1)} %get-tuple-element.196), channel_id=1, source_target_pairs={{0,1},{1,0},{2,3},{3,2},{4,5},{5,4},{6,7},{7,6},{8,9},{9,8},{10,11... | collective-permute-start | bytes 2359304 | tf_op jit(solution)/shard_map/ppermute | solution.py:30
  143.4 13.0 %collective-permute-start.28 = (bf16[32,6144]{1,0:T(8,128)(2,1)S(1)}, bf16[32,6144]{1,0:T(8,128)(2,1)S(1)}, u32[]{:S(2)}, u32[]{:S(2)}) collective-permute-start(bf16[32,6144]{1,0:T(8,128)(2,1)S(1)} %get-tuple-element.237), channel_id=1, source_target_pairs={{0,4},{1,3},{2,6},{3,1},{4,0},{5,7},{6,2},{7,5},{8,12},{9,11},{10,... | collective-permute-start | bytes 1179656 | tf_op jit(solution)/shard_map/ppermute | solution.py:30
  145.5 13.2 %collective-permute-start.29 = (bf16[64,6144]{1,0:T(8,128)(2,1)S(1)}, bf16[64,6144]{1,0:T(8,128)(2,1)S(1)}, u32[]{:S(2)}, u32[]{:S(2)}) collective-permute-start(bf16[64,6144]{1,0:T(8,128)(2,1)S(1)} %add_convert_fusion.3), channel_id=1, source_target_pairs={{0,2},{1,5},{2,0},{3,7},{4,6},{5,1},{6,4},{7,3},{8,10},{9,13},{10,... | collective-permute-start | bytes 2359304 | tf_op jit(solution)/shard_map/ppermute | solution.py:30
  147.0 11.7 %collective-permute-start.34 = (bf16[64,6144]{1,0:T(8,128)(2,1)S(1)}, bf16[64,6144]{1,0:T(8,128)(2,1)S(1)}, u32[]{:S(2)}, u32[]{:S(2)}) collective-permute-start(bf16[64,6144]{1,0:T(8,128)(2,1)S(1)} %get-tuple-element.198), channel_id=1, source_target_pairs={{0,1},{1,0},{2,3},{3,2},{4,5},{5,4},{6,7},{7,6},{8,9},{9,8},{10,11... | collective-permute-start | bytes 2359304 | tf_op jit(solution)/shard_map/ppermute | solution.py:30
  161.1 14.0 %collective-permute-start.37 = (bf16[64,6144]{1,0:T(8,128)(2,1)S(1)}, bf16[64,6144]{1,0:T(8,128)(2,1)S(1)}, u32[]{:S(2)}, u32[]{:S(2)}) collective-permute-start(bf16[64,6144]{1,0:T(8,128)(2,1)S(1)} %add_convert_fusion.1), channel_id=1, source_target_pairs={{0,2},{1,5},{2,0},{3,7},{4,6},{5,1},{6,4},{7,3},{8,10},{9,13},{10,... | collective-permute-start | bytes 2359304 | tf_op jit(solution)/shard_map/ppermute | solution.py:30
  175.4 16.1 %collective-permute-start.39 = (bf16[32,6144]{1,0:T(8,128)(2,1)S(1)}, bf16[32,6144]{1,0:T(8,128)(2,1)}, u32[]{:S(2)}, u32[]{:S(2)}) collective-permute-start(bf16[32,6144]{1,0:T(8,128)(2,1)S(1)} %get-tuple-element.233), channel_id=1, source_target_pairs={{0,4},{1,3},{2,6},{3,1},{4,0},{5,7},{6,2},{7,5},{8,12},{9,11},{10,... | collective-permute-start | bytes 1179656 | tf_op jit(solution)/shard_map/ppermute | solution.py:30
  177.5 14.1 %collective-permute-start.40 = (bf16[64,6144]{1,0:T(8,128)(2,1)}, bf16[64,6144]{1,0:T(8,128)(2,1)}, u32[]{:S(2)}, u32[]{:S(2)}) collective-permute-start(bf16[64,6144]{1,0:T(8,128)(2,1)} %add_convert_fusion), channel_id=1, source_target_pairs={{0,2},{1,5},{2,0},{3,7},{4,6},{5,1},{6,4},{7,3},{8,10},{9,13},{10,... | collective-permute-start | bytes 2359304 | tf_op jit(solution)/shard_map/ppermute | solution.py:30
  179.2 12.4 %collective-permute-start.38 = (bf16[16,6144]{1,0:T(8,128)(2,1)}, bf16[16,6144]{1,0:T(8,128)(2,1)}, u32[]{:S(2)}, u32[]{:S(2)}) collective-permute-start(bf16[16,6144]{1,0:T(8,128)(2,1)} %slice.225), channel_id=1, source_target_pairs={{0,16},{1,17},{2,18},{3,19},{4,20},{5,21},{6,22},{7,23},{8,24},{9,... | collective-permute-start | bytes 589832 | tf_op jit(solution)/shard_map/ppermute | solution.py:30
  210.1 11.9 %collective-permute-start.51 = (bf16[16,1536]{1,0:T(8,128)(2,1)S(1)}, bf16[16,1536]{1,0:T(8,128)(2,1)S(1)}, u32[]{:S(2)}, u32[]{:S(2)}) collective-permute-start(bf16[16,1536]{1,0:T(8,128)(2,1)S(1)} %get-tuple-element.242), channel_id=1, source_target_pairs={{0,3},{1,2},{2,1},{3,0},{4,7},{5,6},{6,5},{7,4},{8,11},{9,10},{10,... | collective-permute-start | bytes 147464 | tf_op jit(solution)/shard_map/ppermute | solution.py:30
  210.2 11.9 %collective-permute-start.52 = (bf16[16,1536]{1,0:T(8,128)(2,1)S(1)}, bf16[16,1536]{1,0:T(8,128)(2,1)S(1)}, u32[]{:S(2)}, u32[]{:S(2)}) collective-permute-start(bf16[16,1536]{1,0:T(8,128)(2,1)S(1)} %get-tuple-element.245), channel_id=1, source_target_pairs={{0,19},{1,18},{2,17},{3,16},{4,23},{5,22},{6,21},{7,20},{8,27},{9,... | collective-permute-start | bytes 147464 | tf_op jit(solution)/shard_map/ppermute | solution.py:30
  (49 other events, 384.8 us)

commit v5 on v4

--- a/solution.py
+++ b/solution.py
@@ -382,6 +382,10 @@
         unit = gather_rows(unit, net[:-2], count)
         return [unit, exchange(unit, net[-2], count)]
 
+    def alternate(a, b):
+        blocks = [x.reshape(-1, 1, half_count, x.shape[1]) for x in (a, b)]
+        return jnp.concatenate(blocks, axis=1).reshape(-1, a.shape[1])
+
     def joined(parts):
         return jnp.concatenate(parts, axis=0)
 
@@ -402,12 +406,22 @@
 
     def deliver(own, across):
         width = own.shape[1] // n_hx
-        sums = {}
-        for o in offsets(([z_masks[0]] if across is not None else []) + x_masks + [1]):
-            to = o % n_hx
-            piece = across if o >= n_hx else own
-            piece = lax.dynamic_slice_in_dim(piece, (hx_index ^ to) * width, width, axis=1)
-            sums.setdefault(to, []).append(exchange(piece, (o, o), count) if o else piece)
+
+        def piece(rows, to):
+            return lax.dynamic_slice_in_dim(rows, (hx_index ^ to) * width, width, axis=1)
+
+        group = offsets(x_masks + [1])
+        sums = {to: [] for to in group}
+        if across is not None:
+            for to in group:
+                sums[to].append(exchange(piece(across, to), (z_masks[0] ^ to,) * 2, count))
+        sums[0].append(piece(own, 0))
+        sums[1].append(to_core(piece(own, 1)))
+        others = {to: piece(own, to) for to in group if to > 1}
+        if across is not None:
+            others, sums[1] = wait((others, sums[1]))
+        for to, rows in others.items():
+            sums[to].append(exchange(rows, (to, to), count))
         return {to: total(parts).astype(BF16) if len(parts) > 1 else parts[0] for to, parts in sums.items()}
 
     last = net[-1]
@@ -420,18 +434,22 @@
     hidden_a, a = norm(0, a, own_residual)
     w_gate, w_up, w_down = weights_in
     weights_in, loaded = load(jnp.swapaxes(w_gate, 1, 2), jnp.swapaxes(w_up, 1, 2), w_down)
-    a1 = jnp.concatenate([a, z_step(a, z_masks[0])], axis=0)
-    a1, rows_b, got_b, loaded = wait((a1, rows_b, got_b, loaded))
-    a2 = z_step(a1, z_masks[1])
-    a1 = spread(a1)
+    a_z, a_own = z_step(a, z_masks[0]), spread(a)
+    a, a_z, a_own, rows_b, got_b, loaded = wait((a, a_z, a_own, rows_b, got_b, loaded))
+    a2 = z_step(joined([a, a_z]), z_masks[1])
+    a_own = joined(a_own)
+    a_own_last, a_z = exchange(a_own, last, count), spread(a_z)
     b = hx_rest(rows_b, got_b)
-    a1, a2, b, own_residual = wait((a1, a2, b, own_residual))
-    a1 = joined(a1)
-    a1_last, a1_other = exchange(a1, last, count), to_core(a1)
+    a_own, a_own_last, a_z, a2, b, own_residual = wait((a_own, a_own_last, a_z, a2, b, own_residual))
+    a_z = joined(a_z)
+    a_z_last = exchange(a_z, last, count)
+    a1 = alternate(a_own, a_z)
+    a1_other = to_core(a1)
     a2 = spread(a2)
     hidden_b, b = norm(1, b, own_residual)
     b1 = jnp.concatenate([b, z_step(b, z_masks[0])], axis=0)
-    a1, a1_last, a1_other, a2, b1 = wait((a1, a1_last, a1_other, a2, b1))
+    a1, a_own_last, a_z_last, a1_other, a2, b1 = wait((a1, a_own_last, a_z_last, a1_other, a2, b1))
+    a1_last = alternate(a_own_last, a_z_last)
     a2 = joined(a2)
     a2_last, a2_other = exchange(a2, last, count), to_core(a2)
     a1_out = expert([a1, a1_last, a1_other, to_core(a1_last)], *weights_in, loaded, scale["near0"])
@@ -465,17 +483,19 @@
     b2_got = exchange(b2_send, last, count)
     a_z, a1_sum, b2_got, b1_send = wait((a_z, a1_sum, b2_got, b1_send))
     b1_got = exchange(b1_send, last, count)
-    a_sum = total(a1_sum + [a_z])
-    a_z = z_step(a_sum[half_count:].astype(BF16), z_masks[0])
-    b2_sum = fold(b2_rest, b2_got)
+    a_sum = a1_sum + [a_z]
+    a_z = z_step(total([t[half_count:] for t in a_sum]).astype(BF16), z_masks[0])
+    a_sum = total([t[:half_count] for t in a_sum])
+    b2_sum = total(fold(b2_rest, b2_got)).astype(BF16)
     a_z, a_sum, b2_sum, b1_got = wait((a_z, a_sum, b2_sum, b1_got))
-    b_z = z_step(total(b2_sum).astype(BF16), z_masks[1])
+    b_z = z_step(b2_sum, z_masks[1])
     b1_sum = fold(b1_rest, b1_got)
-    a_out = deliver(total([hidden_a, a_sum[:half_count], a_z]).astype(BF16), None)
+    a_out = deliver(total([hidden_a, a_sum, a_z]).astype(BF16), None)
     b_z, b1_sum, a_out = wait((b_z, b1_sum, a_out))
-    b_sum = total(b1_sum + [b_z])
-    b_out = deliver(total([hidden_b, b_sum[:half_count]]).astype(BF16), b_sum[half_count:].astype(BF16))
-    out = jnp.zeros((n_hx, HALVES * half_count, b_sum.shape[1] // n_hx), BF16)
+    b_sum = b1_sum + [b_z]
+    across = total([t[half_count:] for t in b_sum]).astype(BF16)
+    b_out = deliver(total([hidden_b] + [t[:half_count] for t in b_sum]).astype(BF16), across)
+    out = jnp.zeros((n_hx, HALVES * half_count, across.shape[1] // n_hx), BF16)
     for to in a_out:
         rows = jnp.concatenate([a_out[to], b_out[to]], axis=0)
         out = lax.dynamic_update_slice_in_dim(out, rows[None], hx_index ^ to, axis=0)

time: 223 us -> 217 us (0.973)
  starting transfers between devices: 63.9 us -> 58.3 us
    ppermute x53 -> x55, starting transfers between devices: 53.1 us -> 47.4 us  [exchange(): return lax.ppermute(x, AXES, pairs)]
    ppermute x53 -> x55, waiting for transfers between devices: 86.1 us -> 84.5 us  [exchange(): return lax.ppermute(x, AXES, pairs)]
  transfers between devices with their start and end apart: 55 -> 57, of which waited for: 30 -> 32; matrix products, arithmetic and copies ran while one was open for 5% -> 5% of each run, Pallas kernels for 16% -> 17%
where the time goes in v5:
time: 217 us
  waiting for transfers between devices  96 us (44%)
  starting transfers between devices  58.3 us (27%)
  Pallas kernels  39.7 us (18%)
  other arithmetic  9.66 us (4%)
  matrix products  6.41 us (3%)
  local copies, waits for them, and re-layouts  5.84 us (3%)
    ppermute x55, waiting for transfers between devices, exchange(): return lax.ppermute(x, AXES, pairs)  84.5 us
    ppermute x55, starting transfers between devices, exchange(): return lax.ppermute(x, AXES, pairs)  47.4 us
    pallas_call x4, Pallas kernels, expert(): pl.pallas_call(functools.partial(expert_kernel, blocks), in_specs=[whole(...  26.5 us
    all_to_all x1, starting transfers between devices, shards(): lax.all_to_all(payload, 'seq', split_axis=0, concat_axis=0, tiled=True)  7.29 us
    pallas_call x1, Pallas kernels, load(): pl.pallas_call(load_kernel, in_specs=[pl.BlockSpec(memory_space=pltpu.HBM...  7.06 us
    dot_general x1, matrix products, shards(): jnp.dot(attn_in, out_weight, preferred_element_type=F32).astype(BF16)  6.41 us
    pallas_call x4, Pallas kernels, call(): pl.pallas_call(kernel, in_specs=specs + [whole()] * (len(operands) - len(...  6.16 us
    all_to_all x1, waiting for transfers between devices, shards(): lax.all_to_all(payload, 'seq', split_axis=0, concat_axis=0, tiled=True)  6.01 us
  transfers between devices with their start and end apart: 57, of which 32 were waited for; matrix products, arithmetic and copies ran while one was open for 5% of the time, Pallas kernels for 17%

profile of v5, /device:TPU:0, one launch (start us, length us, event | category | flops | bytes accessed | tf_op | source)
XLA Modules:
  0.0 216.8 jit_solution(8994409109090782916)
XLA Ops:
  2.6 7.3 %all-to-all-start = ((bf16[8,144,128]{2,1,0:T(8,128)(2,1)}), bf16[8,144,128]{2,1,0:T(8,128)(2,1)S(1)}, u32[]{:S(2)}, u32[]{:S(2)}) async-start(bf16[8,144,128]{2,1,0:T(8,128)(2,1)} %shard_map.164), calls=%async_computation | async-start | bytes 589824 | tf_op jit(solution)/shard_map/all_to_all | solution.py:317
  13.5 6.0 %all-to-all-done.in_ref = bf16[8,144,128]{2,1,0:T(8,128)(2,1)S(1)} async-done(((bf16[8,144,128]{2,1,0:T(8,128)(2,1)}), bf16[8,144,128]{2,1,0:T(8,128)(2,1)S(1)}, u32[]{:S(2)}, u32[]{:S(2)}) %all-to-all-start) | async-done | bytes 294944 | tf_op jit(solution)/shard_map/all_to_all | solution.py:317
  20.3 3.6 %all-to-all-start.1 = ((bf16[8,128,128]{2,1,0:T(8,128)(2,1)}), bf16[8,128,128]{2,1,0:T(8,128)(2,1)S(1)}, u32[]{:S(2)}, u32[]{:S(2)}) async-start(bf16[8,128,128]{2,1,0:T(8,128)(2,1)} %shard_map.165), calls=%async_computation.1 | async-start | bytes 524288 | tf_op jit(solution)/shard_map/all_to_all | solution.py:325
  26.9 5.5 %all-to-all-done.1.state_ref = bf16[8,128,128]{2,1,0:T(8,128)(2,1)S(1)} async-done(((bf16[8,128,128]{2,1,0:T(8,128)(2,1)}), bf16[8,128,128]{2,1,0:T(8,128)(2,1)S(1)}, u32[]{:S(2)}, u32[]{:S(2)}) %all-to-all-start.1) | async-done | bytes 262176 | tf_op jit(solution)/shard_map/all_to_all | solution.py:325
  32.8 6.4 %convolution_convert_fusion = bf16[128,6144]{1,0:T(8,128)(2,1)S(1)} fusion(bf16[128,1024]{1,0:T(8,128)(2,1)S(1)} %shard_map.166, bf16[1024,6144]{1,0:T(8,128)(2,1)} %param.23), kind=kOutput, calls=%fused_computation.4 | convolution fusion | flops 1611399168 | bytes 14417920 | tf_op jit(solution)/shard_map/dot_general | solution.py:359
  42.8 5.4 %collective-permute-done.1 = bf16[16,6144]{1,0:T(8,128)(2,1)S(1)} collective-permute-done((bf16[16,6144]{1,0:T(8,128)(2,1)S(1)}, bf16[16,6144]{1,0:T(8,128)(2,1)S(1)}, u32[]{:S(2)}, u32[]{:S(2)}) %collective-permute-start.1) | collective-permute-done | bytes 196640 | tf_op jit(solution)/shard_map/ppermute | solution.py:30
  50.2 7.1 %shard_map.167 = (bf16[576,6144]{1,0:T(8,128)(2,1)S(1)}, bf16[576,6144]{1,0:T(8,128)(2,1)S(1)}, bf16[576,6144]{1,0:T(8,128)(2,1)S(1)}, f32[8,128]{1,0:T(8,128)S(1)}) custom-call(bf16[1,576,6144]{2,1,0:T(8,128)(2,1)} %bitcast.36, bf16[1,576,6144]{2,1,0:T(8,128)(2,1)} %bitcast.37, bf16[1,576,6144]{2,1,0:T(8,128)(2,1)} %refs_2_.2), custom_call_target="tpu_custom_call" | custom-call | tf_op jit(solution)/shard_map/pallas_call | solution.py:208
  57.3 2.6 %collective-permute-done.3 = bf16[16,6144]{1,0:T(8,128)(2,1)S(1)} collective-permute-done((bf16[16,6144]{1,0:T(8,128)(2,1)S(1)}, bf16[16,6144]{1,0:T(8,128)(2,1)S(1)}, u32[]{:S(2)}, u32[]{:S(2)}) %collective-permute-start.3) | collective-permute-done | bytes 196640 | tf_op jit(solution)/shard_map/ppermute | solution.py:30
  63.3 4.7 %collective-permute-done.8 = bf16[16,6144]{1,0:T(8,128)(2,1)S(1)} collective-permute-done((bf16[16,6144]{1,0:T(8,128)(2,1)S(1)}, bf16[16,6144]{1,0:T(8,128)(2,1)S(1)}, u32[]{:S(2)}, u32[]{:S(2)}) %collective-permute-start.8) | collective-permute-done | bytes 196640 | tf_op jit(solution)/shard_map/ppermute | solution.py:30
  69.4 2.7 %collective-permute-done.7 = bf16[32,6144]{1,0:T(8,128)(2,1)S(1)} collective-permute-done((bf16[32,6144]{1,0:T(8,128)(2,1)S(1)}, bf16[32,6144]{1,0:T(8,128)(2,1)S(1)}, u32[]{:S(2)}, u32[]{:S(2)}) %collective-permute-start.7) | collective-permute-done | bytes 393248 | tf_op jit(solution)/shard_map/ppermute | solution.py:30
  76.4 6.1 %collective-permute-done.12 = bf16[16,6144]{1,0:T(8,128)(2,1)S(1)} collective-permute-done((bf16[16,6144]{1,0:T(8,128)(2,1)S(1)}, bf16[16,6144]{1,0:T(8,128)(2,1)S(1)}, u32[]{:S(2)}, u32[]{:S(2)}) %collective-permute-start.12) | collective-permute-done | bytes 196640 | tf_op jit(solution)/shard_map/ppermute | solution.py:30
  90.5 6.5 %shard_map.168 = (bf16[64,6144]{1,0:T(8,128)(2,1)S(1)}, bf16[64,6144]{1,0:T(8,128)(2,1)S(1)}, bf16[64,6144]{1,0:T(8,128)(2,1)S(1)}, bf16[64,6144]{1,0:T(8,128)(2,1)S(1)}) custom-call(bf16[64,6144]{1,0:T(8,128)(2,1)S(1)} %bitcast.33, bf16[64,6144]{1,0:T(8,128)(2,1)S(1)} %bitcast.35, bf16[64,6144]{1,0:T(8,128)(2,1)S(1)} %collective-permute-done.10.refs_2_, ...), custom_call_target="tpu_custom_call" | custom-call | flops 1000 | bytes 1000 | tf_op jit(solution)/shard_map/pallas_call | solution.py:244
  105.8 6.7 %shard_map.169 = (bf16[64,6144]{1,0:T(8,128)(2,1)S(1)}, bf16[64,6144]{1,0:T(8,128)(2,1)S(1)}, bf16[64,6144]{1,0:T(8,128)(2,1)S(1)}, bf16[64,6144]{1,0:T(8,128)(2,1)S(1)}) custom-call(bf16[64,6144]{1,0:T(8,128)(2,1)S(1)} %constant_dynamic-update-slice_fusion.12.refs_0_, bf16[64,6144]{1,0:T(8,128)(2,1)S(1)} %collective-permute-done.13.refs_1_, ...), custom_call_target="tpu_custom_call" | custom-call | flops 1000 | bytes 1000 | tf_op jit(solution)/shard_map/pallas_call | solution.py:244
  121.9 6.5 %shard_map.170 = (bf16[64,6144]{1,0:T(8,128)(2,1)S(1)}, bf16[64,6144]{1,0:T(8,128)(2,1)S(1)}, bf16[64,6144]{1,0:T(8,128)(2,1)S(1)}, bf16[64,6144]{1,0:T(8,128)(2,1)S(1)}) custom-call(bf16[64,6144]{1,0:T(8,128)(2,1)S(1)} %constant_dynamic-update-slice_fusion.14.refs_0_, bf16[64,6144]{1,0:T(8,128)(2,1)S(1)} %collective-permute-done.18.refs_1_, ...), custom_call_target="tpu_custom_call" | custom-call | flops 1000 | bytes 1000 | tf_op jit(solution)/shard_map/pallas_call | solution.py:244
  130.9 8.4 %collective-permute-done.28 = bf16[64,6144]{1,0:T(8,128)(2,1)S(1)} collective-permute-done((bf16[64,6144]{1,0:T(8,128)(2,1)S(1)}, bf16[64,6144]{1,0:T(8,128)(2,1)S(1)}, u32[]{:S(2)}, u32[]{:S(2)}) %collective-permute-start.28) | collective-permute-done | bytes 786464 | tf_op jit(solution)/shard_map/ppermute | solution.py:30
  143.0 6.7 %shard_map.171 = (bf16[64,6144]{1,0:T(8,128)(2,1)S(1)}, bf16[64,6144]{1,0:T(8,128)(2,1)S(1)}, bf16[64,6144]{1,0:T(8,128)(2,1)S(1)}, bf16[64,6144]{1,0:T(8,128)(2,1)S(1)}) custom-call(bf16[64,6144]{1,0:T(8,128)(2,1)S(1)} %constant_dynamic-update-slice_fusion.16.refs_0_, bf16[64,6144]{1,0:T(8,128)(2,1)S(1)} %collective-permute-done.26.refs_1_, ...), custom_call_target="tpu_custom_call" | custom-call | flops 1000 | bytes 1000 | tf_op jit(solution)/shard_map/pallas_call | solution.py:244
  162.1 6.0 %collective-permute-done.38 = bf16[32,6144]{1,0:T(8,128)(2,1)} collective-permute-done((bf16[32,6144]{1,0:T(8,128)(2,1)S(1)}, bf16[32,6144]{1,0:T(8,128)(2,1)}, u32[]{:S(2)}, u32[]{:S(2)}) %collective-permute-start.38) | collective-permute-done | bytes 393248 | tf_op jit(solution)/shard_map/ppermute | solution.py:30
  168.0 3.2 %collective-permute-done.37 = bf16[32,6144]{1,0:T(8,128)(2,1)} collective-permute-done((bf16[32,6144]{1,0:T(8,128)(2,1)}, bf16[32,6144]{1,0:T(8,128)(2,1)}, u32[]{:S(2)}, u32[]{:S(2)}) %collective-permute-start.37) | collective-permute-done | bytes 393248 | tf_op jit(solution)/shard_map/ppermute | solution.py:30
  176.7 2.8 %collective-permute-start.40 = (bf16[16,6144]{1,0:T(8,128)(2,1)S(1)}, bf16[16,6144]{1,0:T(8,128)(2,1)S(1)}, u32[]{:S(2)}, u32[]{:S(2)}) collective-permute-start(bf16[16,6144]{1,0:T(8,128)(2,1)S(1)} %get-tuple-element.258), channel_id=1, source_target_pairs={{0,16},{1,17},{2,18},{3,19},{4,20},{5,21},{6,22},{7,23},{8,24},{9,... | collective-permute-start | bytes 589832 | tf_op jit(solution)/shard_map/ppermute | solution.py:30
  182.9 5.7 %collective-permute-done.40 = bf16[16,6144]{1,0:T(8,128)(2,1)S(1)} collective-permute-done((bf16[16,6144]{1,0:T(8,128)(2,1)S(1)}, bf16[16,6144]{1,0:T(8,128)(2,1)S(1)}, u32[]{:S(2)}, u32[]{:S(2)}) %collective-permute-start.40) | collective-permute-done | bytes 196640 | tf_op jit(solution)/shard_map/ppermute | solution.py:30
  188.6 2.9 %collective-permute-done.42 = bf16[64,6144]{1,0:T(8,128)(2,1)S(1)} collective-permute-done((bf16[64,6144]{1,0:T(8,128)(2,1)S(1)}, bf16[64,6144]{1,0:T(8,128)(2,1)S(1)}, u32[]{:S(2)}, u32[]{:S(2)}) %collective-permute-start.42) | collective-permute-done | bytes 786464 | tf_op jit(solution)/shard_map/ppermute | solution.py:30
  195.1 2.9 %collective-permute-done.46 = bf16[16,1536]{1,0:T(8,128)(2,1)S(1)} collective-permute-done((bf16[16,1536]{1,0:T(8,128)(2,1)S(1)}, bf16[16,1536]{1,0:T(8,128)(2,1)S(1)}, u32[]{:S(2)}, u32[]{:S(2)}) %collective-permute-start.46) | collective-permute-done | bytes 49184 | tf_op jit(solution)/shard_map/ppermute | solution.py:30
  206.0 2.7 %collective-permute-start.51 = (bf16[16,1536]{1,0:T(8,128)(2,1)S(1)}, bf16[16,1536]{1,0:T(8,128)(2,1)S(1)}, u32[]{:S(2)}, u32[]{:S(2)}) collective-permute-start(bf16[16,1536]{1,0:T(8,128)(2,1)S(1)} %get-tuple-element.263), channel_id=1, source_target_pairs={{0,18},{1,19},{2,16},{3,17},{4,22},{5,23},{6,20},{7,21},{8,26},{9,... | collective-permute-start | bytes 147464 | tf_op jit(solution)/shard_map/ppermute | solution.py:30
  210.6 5.2 %collective-permute-done.48 = bf16[16,1536]{1,0:T(8,128)(2,1)S(1)} collective-permute-done((bf16[16,1536]{1,0:T(8,128)(2,1)S(1)}, bf16[16,1536]{1,0:T(8,128)(2,1)S(1)}, u32[]{:S(2)}, u32[]{:S(2)}) %collective-permute-start.48) | collective-permute-done | bytes 49184 | tf_op jit(solution)/shard_map/ppermute | solution.py:30
  (210 shorter events, 92.2 us)
Async XLA Ops:
  2.6 16.9 %all-to-all-start = ((bf16[8,144,128]{2,1,0:T(8,128)(2,1)}), bf16[8,144,128]{2,1,0:T(8,128)(2,1)S(1)}, u32[]{:S(2)}, u32[]{:S(2)}) async-start(bf16[8,144,128]{2,1,0:T(8,128)(2,1)} %shard_map.164), calls=%async_computation | async-start | bytes 589824 | tf_op jit(solution)/shard_map/all_to_all | solution.py:317
  20.3 12.1 %all-to-all-start.1 = ((bf16[8,128,128]{2,1,0:T(8,128)(2,1)}), bf16[8,128,128]{2,1,0:T(8,128)(2,1)S(1)}, u32[]{:S(2)}, u32[]{:S(2)}) async-start(bf16[8,128,128]{2,1,0:T(8,128)(2,1)} %shard_map.165), calls=%async_computation.1 | async-start | bytes 524288 | tf_op jit(solution)/shard_map/all_to_all | solution.py:325
  48.6 11.3 %collective-permute-start.3 = (bf16[16,6144]{1,0:T(8,128)(2,1)S(1)}, bf16[16,6144]{1,0:T(8,128)(2,1)S(1)}, u32[]{:S(2)}, u32[]{:S(2)}) collective-permute-start(bf16[16,6144]{1,0:T(8,128)(2,1)S(1)} %multiply_convert_fusion.1), channel_id=1, source_target_pairs={{0,16},{1,17},{2,18},{3,19},{4,20},{5,21},{6,22},{7,23},{8,24},{9,... | collective-permute-start | bytes 589832 | tf_op jit(solution)/shard_map/ppermute | solution.py:30
  73.4 11.6 %collective-permute-start.10 = (bf16[64,6144]{1,0:T(8,128)(2,1)S(1)}, bf16[64,6144]{1,0:T(8,128)(2,1)S(1)}, u32[]{:S(2)}, u32[]{:S(2)}) collective-permute-start(bf16[64,6144]{1,0:T(8,128)(2,1)S(1)} %bitcast.32), channel_id=1, source_target_pairs={{0,1},{1,0},{2,3},{3,2},{4,5},{5,4},{6,7},{7,6},{8,9},{9,8},{10,11... | collective-permute-start | bytes 2359304 | tf_op jit(solution)/shard_map/ppermute | solution.py:30
  73.5 11.5 %collective-permute-start.9 = (bf16[32,6144]{1,0:T(8,128)(2,1)S(1)}, bf16[32,6144]{1,0:T(8,128)(2,1)S(1)}, u32[]{:S(2)}, u32[]{:S(2)}) collective-permute-start(bf16[32,6144]{1,0:T(8,128)(2,1)S(1)} %constant_dynamic-update-slice_fusion.10), channel_id=1, source_target_pairs={{0,2},{1,5},{2,0},{3,7},{4,6},{5,1},{6,4},{7,3},{8,10},{9,13},{10,... | collective-permute-start | bytes 1179656 | tf_op jit(solution)/shard_map/ppermute | solution.py:30
  85.6 16.3 %collective-permute-start.13 = (bf16[64,6144]{1,0:T(8,128)(2,1)S(1)}, bf16[64,6144]{1,0:T(8,128)(2,1)S(1)}, u32[]{:S(2)}, u32[]{:S(2)}) collective-permute-start(bf16[64,6144]{1,0:T(8,128)(2,1)S(1)} %constant_dynamic-update-slice_fusion.12.refs_0_), channel_id=1, source_target_pairs={{0,2},{1,5},{2,0},{3,7},{4,6},{5,1},{6,4},{7,3},{8,10},{9,13},{10,... | collective-permute-start | bytes 2359304 | tf_op jit(solution)/shard_map/ppermute | solution.py:30
  87.0 14.8 %collective-permute-start.14 = (bf16[64,6144]{1,0:T(8,128)(2,1)S(1)}, bf16[64,6144]{1,0:T(8,128)(2,1)S(1)}, u32[]{:S(2)}, u32[]{:S(2)}) collective-permute-start(bf16[64,6144]{1,0:T(8,128)(2,1)S(1)} %constant_dynamic-update-slice_fusion.12.refs_0_), channel_id=1, source_target_pairs={{0,1},{1,0},{2,3},{3,2},{4,5},{5,4},{6,7},{7,6},{8,9},{9,8},{10,11... | collective-permute-start | bytes 2359304 | tf_op jit(solution)/shard_map/ppermute | solution.py:30
  87.3 12.1 %collective-permute-start.15 = (bf16[32,6144]{1,0:T(8,128)(2,1)S(1)}, bf16[32,6144]{1,0:T(8,128)(2,1)S(1)}, u32[]{:S(2)}, u32[]{:S(2)}) collective-permute-start(bf16[32,6144]{1,0:T(8,128)(2,1)S(1)} %pad_maximum_fusion.3), channel_id=1, source_target_pairs={{0,4},{1,3},{2,6},{3,1},{4,0},{5,7},{6,2},{7,5},{8,12},{9,11},{10,... | collective-permute-start | bytes 1179656 | tf_op jit(solution)/shard_map/ppermute | solution.py:30
  88.4 11.3 %collective-permute-start.16 = (bf16[32,6144]{1,0:T(8,128)(2,1)S(1)}, bf16[32,6144]{1,0:T(8,128)(2,1)S(1)}, u32[]{:S(2)}, u32[]{:S(2)}) collective-permute-start(bf16[32,6144]{1,0:T(8,128)(2,1)S(1)} %pad_maximum_fusion.3), channel_id=1, source_target_pairs={{0,8},{1,9},{2,10},{3,11},{4,12},{5,13},{6,14},{7,15},{8,0},{9,1},... | collective-permute-start | bytes 1179656 | tf_op jit(solution)/shard_map/ppermute | solution.py:30
  102.5 16.3 %collective-permute-start.18 = (bf16[64,6144]{1,0:T(8,128)(2,1)S(1)}, bf16[64,6144]{1,0:T(8,128)(2,1)S(1)}, u32[]{:S(2)}, u32[]{:S(2)}) collective-permute-start(bf16[64,6144]{1,0:T(8,128)(2,1)S(1)} %constant_dynamic-update-slice_fusion.14.refs_0_), channel_id=1, source_target_pairs={{0,2},{1,5},{2,0},{3,7},{4,6},{5,1},{6,4},{7,3},{8,10},{9,13},{10,... | collective-permute-start | bytes 2359304 | tf_op jit(solution)/shard_map/ppermute | solution.py:30
  103.9 14.8 %collective-permute-start.19 = (bf16[64,6144]{1,0:T(8,128)(2,1)S(1)}, bf16[64,6144]{1,0:T(8,128)(2,1)S(1)}, u32[]{:S(2)}, u32[]{:S(2)}) collective-permute-start(bf16[64,6144]{1,0:T(8,128)(2,1)S(1)} %constant_dynamic-update-slice_fusion.14.refs_0_), channel_id=1, source_target_pairs={{0,1},{1,0},{2,3},{3,2},{4,5},{5,4},{6,7},{7,6},{8,9},{9,8},{10,11... | collective-permute-start | bytes 2359304 | tf_op jit(solution)/shard_map/ppermute | solution.py:30
  103.9 14.8 %collective-permute-start.22 = (bf16[64,6144]{1,0:T(8,128)(2,1)S(1)}, bf16[64,6144]{1,0:T(8,128)(2,1)S(1)}, u32[]{:S(2)}, u32[]{:S(2)}) collective-permute-start(bf16[64,6144]{1,0:T(8,128)(2,1)S(1)} %get-tuple-element.177), channel_id=1, source_target_pairs={{0,1},{1,0},{2,3},{3,2},{4,5},{5,4},{6,7},{7,6},{8,9},{9,8},{10,11... | collective-permute-start | bytes 2359304 | tf_op jit(solution)/shard_map/ppermute | solution.py:30
  104.4 12.1 %collective-permute-start.20 = (bf16[32,6144]{1,0:T(8,128)(2,1)S(1)}, bf16[32,6144]{1,0:T(8,128)(2,1)S(1)}, u32[]{:S(2)}, u32[]{:S(2)}) collective-permute-start(bf16[32,6144]{1,0:T(8,128)(2,1)S(1)} %collective-permute-done.16), channel_id=1, source_target_pairs={{0,4},{1,3},{2,6},{3,1},{4,0},{5,7},{6,2},{7,5},{8,12},{9,11},{10,... | collective-permute-start | bytes 1179656 | tf_op jit(solution)/shard_map/ppermute | solution.py:30
  118.9 12.1 %collective-permute-start.26 = (bf16[64,6144]{1,0:T(8,128)(2,1)S(1)}, bf16[64,6144]{1,0:T(8,128)(2,1)S(1)}, u32[]{:S(2)}, u32[]{:S(2)}) collective-permute-start(bf16[64,6144]{1,0:T(8,128)(2,1)S(1)} %constant_dynamic-update-slice_fusion.16.refs_0_), channel_id=1, source_target_pairs={{0,2},{1,5},{2,0},{3,7},{4,6},{5,1},{6,4},{7,3},{8,10},{9,13},{10,... | collective-permute-start | bytes 2359304 | tf_op jit(solution)/shard_map/ppermute | solution.py:30
  120.6 18.8 %collective-permute-start.28 = (bf16[64,6144]{1,0:T(8,128)(2,1)S(1)}, bf16[64,6144]{1,0:T(8,128)(2,1)S(1)}, u32[]{:S(2)}, u32[]{:S(2)}) collective-permute-start(bf16[64,6144]{1,0:T(8,128)(2,1)S(1)} %add_convert_fusion.2), channel_id=1, source_target_pairs={{0,2},{1,5},{2,0},{3,7},{4,6},{5,1},{6,4},{7,3},{8,10},{9,13},{10,... | collective-permute-start | bytes 2359304 | tf_op jit(solution)/shard_map/ppermute | solution.py:30
  139.4 11.0 %collective-permute-start.35 = (bf16[64,6144]{1,0:T(8,128)(2,1)S(1)}, bf16[64,6144]{1,0:T(8,128)(2,1)S(1)}, u32[]{:S(2)}, u32[]{:S(2)}) collective-permute-start(bf16[64,6144]{1,0:T(8,128)(2,1)S(1)} %get-tuple-element.211), channel_id=1, source_target_pairs={{0,1},{1,0},{2,3},{3,2},{4,5},{5,4},{6,7},{7,6},{8,9},{9,8},{10,11... | collective-permute-start | bytes 2359304 | tf_op jit(solution)/shard_map/ppermute | solution.py:30
  140.1 13.2 %collective-permute-start.30 = (bf16[32,6144]{1,0:T(8,128)(2,1)S(1)}, bf16[32,6144]{1,0:T(8,128)(2,1)S(1)}, u32[]{:S(2)}, u32[]{:S(2)}) collective-permute-start(bf16[32,6144]{1,0:T(8,128)(2,1)S(1)} %get-tuple-element.253), channel_id=1, source_target_pairs={{0,4},{1,3},{2,6},{3,1},{4,0},{5,7},{6,2},{7,5},{8,12},{9,11},{10,... | collective-permute-start | bytes 1179656 | tf_op jit(solution)/shard_map/ppermute | solution.py:30
  141.6 13.8 %collective-permute-start.31 = (bf16[64,6144]{1,0:T(8,128)(2,1)S(1)}, bf16[64,6144]{1,0:T(8,128)(2,1)S(1)}, u32[]{:S(2)}, u32[]{:S(2)}) collective-permute-start(bf16[64,6144]{1,0:T(8,128)(2,1)S(1)} %add_convert_fusion.3), channel_id=1, source_target_pairs={{0,2},{1,5},{2,0},{3,7},{4,6},{5,1},{6,4},{7,3},{8,10},{9,13},{10,... | collective-permute-start | bytes 2359304 | tf_op jit(solution)/shard_map/ppermute | solution.py:30
  143.0 12.4 %collective-permute-start.36 = (bf16[64,6144]{1,0:T(8,128)(2,1)S(1)}, bf16[64,6144]{1,0:T(8,128)(2,1)S(1)}, u32[]{:S(2)}, u32[]{:S(2)}) collective-permute-start(bf16[64,6144]{1,0:T(8,128)(2,1)S(1)} %get-tuple-element.213), channel_id=1, source_target_pairs={{0,1},{1,0},{2,3},{3,2},{4,5},{5,4},{6,7},{7,6},{8,9},{9,8},{10,11... | collective-permute-start | bytes 2359304 | tf_op jit(solution)/shard_map/ppermute | solution.py:30
  156.4 11.6 %collective-permute-start.38 = (bf16[32,6144]{1,0:T(8,128)(2,1)S(1)}, bf16[32,6144]{1,0:T(8,128)(2,1)}, u32[]{:S(2)}, u32[]{:S(2)}) collective-permute-start(bf16[32,6144]{1,0:T(8,128)(2,1)S(1)} %get-tuple-element.251), channel_id=1, source_target_pairs={{0,4},{1,3},{2,6},{3,1},{4,0},{5,7},{6,2},{7,5},{8,12},{9,11},{10,... | collective-permute-start | bytes 1179656 | tf_op jit(solution)/shard_map/ppermute | solution.py:30
  157.8 14.7 %collective-permute-start.39 = (bf16[64,6144]{1,0:T(8,128)(2,1)}, bf16[64,6144]{1,0:T(8,128)(2,1)}, u32[]{:S(2)}, u32[]{:S(2)}) collective-permute-start(bf16[64,6144]{1,0:T(8,128)(2,1)} %add_convert_fusion.1), channel_id=1, source_target_pairs={{0,2},{1,5},{2,0},{3,7},{4,6},{5,1},{6,4},{7,3},{8,10},{9,13},{10,... | collective-permute-start | bytes 2359304 | tf_op jit(solution)/shard_map/ppermute | solution.py:30
  160.0 11.2 %collective-permute-start.37 = (bf16[32,6144]{1,0:T(8,128)(2,1)}, bf16[32,6144]{1,0:T(8,128)(2,1)}, u32[]{:S(2)}, u32[]{:S(2)}) collective-permute-start(bf16[32,6144]{1,0:T(8,128)(2,1)} %add_convert_fusion.8), channel_id=1, source_target_pairs={{0,8},{1,9},{2,10},{3,11},{4,12},{5,13},{6,14},{7,15},{8,0},{9,1},... | collective-permute-start | bytes 1179656 | tf_op jit(solution)/shard_map/ppermute | solution.py:30
  176.7 11.9 %collective-permute-start.40 = (bf16[16,6144]{1,0:T(8,128)(2,1)S(1)}, bf16[16,6144]{1,0:T(8,128)(2,1)S(1)}, u32[]{:S(2)}, u32[]{:S(2)}) collective-permute-start(bf16[16,6144]{1,0:T(8,128)(2,1)S(1)} %get-tuple-element.258), channel_id=1, source_target_pairs={{0,16},{1,17},{2,18},{3,19},{4,20},{5,21},{6,22},{7,23},{8,24},{9,... | collective-permute-start | bytes 589832 | tf_op jit(solution)/shard_map/ppermute | solution.py:30
  179.6 12.0 %collective-permute-start.42 = (bf16[64,6144]{1,0:T(8,128)(2,1)S(1)}, bf16[64,6144]{1,0:T(8,128)(2,1)S(1)}, u32[]{:S(2)}, u32[]{:S(2)}) collective-permute-start(bf16[64,6144]{1,0:T(8,128)(2,1)S(1)} %copy-done.5), channel_id=1, source_target_pairs={{0,2},{1,5},{2,0},{3,7},{4,6},{5,1},{6,4},{7,3},{8,10},{9,13},{10,... | collective-permute-start | bytes 2359304 | tf_op jit(solution)/shard_map/ppermute | solution.py:30
  (47 other events, 351.1 us)

commit v6 on v5

--- a/solution.py
+++ b/solution.py
@@ -456,20 +456,22 @@
     b2 = z_step(b1, z_masks[1])
     b1 = spread(b1)
     a2, a2_last, a2_other, b1, b2, a1_out = wait((a2, a2_last, a2_other, b1, b2, a1_out))
+    b2 = [gather_rows(b2, net[:-2], count), z_step(b1[1], z_masks[1])]
     b1 = joined(b1)
     b1_last, b1_other = exchange(b1, last, count), to_core(b1)
     a2_out = expert([a2, a2_last, a2_other, to_core(a2_last)], *weights_in, loaded, scale["far0"])
-    b2 = spread(b2)
     a1_send, a1_rest = back(a1_out)
     a2_send, a2_rest = back(a2_out)
     b1, b1_last, b1_other, b2, a1_send, a1_rest, a2_send, a2_rest = wait(
         (b1, b1_last, b1_other, b2, a1_send, a1_rest, a2_send, a2_rest)
     )
+    b2_last = [exchange(b2[0], last, count), z_step(b1_last[b1_last.shape[0] // 2 :], z_masks[1])]
     b2 = joined(b2)
-    b2_last, b2_other = exchange(b2, last, count), to_core(b2)
+    b2_other = to_core(b2)
     a2_got = exchange(a2_send, last, count)
     b1_out = expert([b1, b1_last, b1_other, to_core(b1_last)], *weights_in, loaded, scale["near1"])
     b2, b2_last, b2_other, a2_got, b1_out, a1_send = wait((b2, b2_last, b2_other, a2_got, b1_out, a1_send))
+    b2_last = joined(b2_last)
     a1_got = exchange(a1_send, last, count)
     a2_sum = fold(a2_rest, a2_got)
     b2_out = expert([b2, b2_last, b2_other, to_core(b2_last)], *weights_in, loaded, scale["far1"])

time: 217 us -> 212 us (0.977)
  waiting for transfers between devices: 96 us -> 92.1 us
    ppermute x55 -> x56, waiting for transfers between devices: 84.5 us -> 80.6 us  [exchange(): return lax.ppermute(x, AXES, pairs)]
    ppermute x55 -> x56, starting transfers between devices: 47.4 us -> 45.4 us  [exchange(): return lax.ppermute(x, AXES, pairs)]
  transfers between devices with their start and end apart: 57 -> 58, of which waited for: 32 -> 32; matrix products, arithmetic and copies ran while one was open for 5% -> 5% of each run, Pallas kernels for 17% -> 17%
where the time goes in v6:
time: 212 us; the launch traced here: 211 us
  waiting for transfers between devices  92.1 us (43%)
  starting transfers between devices  56.3 us (27%)
  Pallas kernels  39.8 us (19%)
  other arithmetic  9.62 us (5%)
  matrix products  6.4 us (3%)
  local copies, waits for them, and re-layouts  6.2 us (3%)
    ppermute x56, waiting for transfers between devices, exchange(): return lax.ppermute(x, AXES, pairs)  80.6 us
    ppermute x56, starting transfers between devices, exchange(): return lax.ppermute(x, AXES, pairs)  45.4 us
    pallas_call x4, Pallas kernels, expert(): pl.pallas_call(functools.partial(expert_kernel, blocks), in_specs=[whole(...  26.5 us
    all_to_all x1, starting transfers between devices, shards(): lax.all_to_all(payload, 'seq', split_axis=0, concat_axis=0, tiled=True)  7.29 us
    pallas_call x1, Pallas kernels, load(): pl.pallas_call(load_kernel, in_specs=[pl.BlockSpec(memory_space=pltpu.HBM...  7.06 us
    dot_general x1, matrix products, shards(): jnp.dot(attn_in, out_weight, preferred_element_type=F32).astype(BF16)  6.4 us
    pallas_call x4, Pallas kernels, call(): pl.pallas_call(kernel, in_specs=specs + [whole()] * (len(operands) - len(...  6.16 us
    all_to_all x1, waiting for transfers between devices, shards(): lax.all_to_all(payload, 'seq', split_axis=0, concat_axis=0, tiled=True)  6.01 us
  transfers between devices with their start and end apart: 58, of which 32 were waited for; matrix products, arithmetic and copies ran while one was open for 5% of the time, Pallas kernels for 17%

profile of v6, /device:TPU:0, one launch (start us, length us, event | category | flops | bytes accessed | tf_op | source)
XLA Modules:
  0.0 211.3 jit_solution(2010288701970754324)
XLA Ops:
  2.6 7.3 %all-to-all-start = ((bf16[8,144,128]{2,1,0:T(8,128)(2,1)}), bf16[8,144,128]{2,1,0:T(8,128)(2,1)S(1)}, u32[]{:S(2)}, u32[]{:S(2)}) async-start(bf16[8,144,128]{2,1,0:T(8,128)(2,1)} %shard_map.164), calls=%async_computation | async-start | bytes 589824 | tf_op jit(solution)/shard_map/all_to_all | solution.py:317
  13.5 6.0 %all-to-all-done.in_ref = bf16[8,144,128]{2,1,0:T(8,128)(2,1)S(1)} async-done(((bf16[8,144,128]{2,1,0:T(8,128)(2,1)}), bf16[8,144,128]{2,1,0:T(8,128)(2,1)S(1)}, u32[]{:S(2)}, u32[]{:S(2)}) %all-to-all-start) | async-done | bytes 294944 | tf_op jit(solution)/shard_map/all_to_all | solution.py:317
  20.3 3.6 %all-to-all-start.1 = ((bf16[8,128,128]{2,1,0:T(8,128)(2,1)}), bf16[8,128,128]{2,1,0:T(8,128)(2,1)S(1)}, u32[]{:S(2)}, u32[]{:S(2)}) async-start(bf16[8,128,128]{2,1,0:T(8,128)(2,1)} %shard_map.165), calls=%async_computation.1 | async-start | bytes 524288 | tf_op jit(solution)/shard_map/all_to_all | solution.py:325
  26.9 5.5 %all-to-all-done.1.state_ref = bf16[8,128,128]{2,1,0:T(8,128)(2,1)S(1)} async-done(((bf16[8,128,128]{2,1,0:T(8,128)(2,1)}), bf16[8,128,128]{2,1,0:T(8,128)(2,1)S(1)}, u32[]{:S(2)}, u32[]{:S(2)}) %all-to-all-start.1) | async-done | bytes 262176 | tf_op jit(solution)/shard_map/all_to_all | solution.py:325
  32.8 6.4 %convolution_convert_fusion = bf16[128,6144]{1,0:T(8,128)(2,1)S(1)} fusion(bf16[128,1024]{1,0:T(8,128)(2,1)S(1)} %shard_map.166, bf16[1024,6144]{1,0:T(8,128)(2,1)} %param.23), kind=kOutput, calls=%fused_computation.4 | convolution fusion | flops 1611399168 | bytes 14417920 | tf_op jit(solution)/shard_map/dot_general | solution.py:359
  42.8 5.4 %collective-permute-done.1 = bf16[16,6144]{1,0:T(8,128)(2,1)S(1)} collective-permute-done((bf16[16,6144]{1,0:T(8,128)(2,1)S(1)}, bf16[16,6144]{1,0:T(8,128)(2,1)S(1)}, u32[]{:S(2)}, u32[]{:S(2)}) %collective-permute-start.1) | collective-permute-done | bytes 196640 | tf_op jit(solution)/shard_map/ppermute | solution.py:30
  50.2 7.1 %shard_map.167 = (bf16[576,6144]{1,0:T(8,128)(2,1)S(1)}, bf16[576,6144]{1,0:T(8,128)(2,1)S(1)}, bf16[576,6144]{1,0:T(8,128)(2,1)S(1)}, f32[8,128]{1,0:T(8,128)S(1)}) custom-call(bf16[1,576,6144]{2,1,0:T(8,128)(2,1)} %bitcast.36, bf16[1,576,6144]{2,1,0:T(8,128)(2,1)} %bitcast.37, bf16[1,576,6144]{2,1,0:T(8,128)(2,1)} %refs_2_.2), custom_call_target="tpu_custom_call" | custom-call | tf_op jit(solution)/shard_map/pallas_call | solution.py:208
  57.3 2.6 %collective-permute-done.3 = bf16[16,6144]{1,0:T(8,128)(2,1)S(1)} collective-permute-done((bf16[16,6144]{1,0:T(8,128)(2,1)S(1)}, bf16[16,6144]{1,0:T(8,128)(2,1)S(1)}, u32[]{:S(2)}, u32[]{:S(2)}) %collective-permute-start.3) | collective-permute-done | bytes 196640 | tf_op jit(solution)/shard_map/ppermute | solution.py:30
  63.3 4.7 %collective-permute-done.8 = bf16[16,6144]{1,0:T(8,128)(2,1)S(1)} collective-permute-done((bf16[16,6144]{1,0:T(8,128)(2,1)S(1)}, bf16[16,6144]{1,0:T(8,128)(2,1)S(1)}, u32[]{:S(2)}, u32[]{:S(2)}) %collective-permute-start.8) | collective-permute-done | bytes 196640 | tf_op jit(solution)/shard_map/ppermute | solution.py:30
  69.4 2.7 %collective-permute-done.7 = bf16[32,6144]{1,0:T(8,128)(2,1)S(1)} collective-permute-done((bf16[32,6144]{1,0:T(8,128)(2,1)S(1)}, bf16[32,6144]{1,0:T(8,128)(2,1)S(1)}, u32[]{:S(2)}, u32[]{:S(2)}) %collective-permute-start.7) | collective-permute-done | bytes 393248 | tf_op jit(solution)/shard_map/ppermute | solution.py:30
  76.4 6.1 %collective-permute-done.12 = bf16[16,6144]{1,0:T(8,128)(2,1)S(1)} collective-permute-done((bf16[16,6144]{1,0:T(8,128)(2,1)S(1)}, bf16[16,6144]{1,0:T(8,128)(2,1)S(1)}, u32[]{:S(2)}, u32[]{:S(2)}) %collective-permute-start.12) | collective-permute-done | bytes 196640 | tf_op jit(solution)/shard_map/ppermute | solution.py:30
  90.5 6.5 %shard_map.168 = (bf16[64,6144]{1,0:T(8,128)(2,1)S(1)}, bf16[64,6144]{1,0:T(8,128)(2,1)S(1)}, bf16[64,6144]{1,0:T(8,128)(2,1)S(1)}, bf16[64,6144]{1,0:T(8,128)(2,1)S(1)}) custom-call(bf16[64,6144]{1,0:T(8,128)(2,1)S(1)} %bitcast.33, bf16[64,6144]{1,0:T(8,128)(2,1)S(1)} %bitcast.35, bf16[64,6144]{1,0:T(8,128)(2,1)S(1)} %collective-permute-done.10.refs_2_, ...), custom_call_target="tpu_custom_call" | custom-call | flops 1000 | bytes 1000 | tf_op jit(solution)/shard_map/pallas_call | solution.py:244
  105.8 6.7 %shard_map.169 = (bf16[64,6144]{1,0:T(8,128)(2,1)S(1)}, bf16[64,6144]{1,0:T(8,128)(2,1)S(1)}, bf16[64,6144]{1,0:T(8,128)(2,1)S(1)}, bf16[64,6144]{1,0:T(8,128)(2,1)S(1)}) custom-call(bf16[64,6144]{1,0:T(8,128)(2,1)S(1)} %constant_dynamic-update-slice_fusion.12.refs_0_, bf16[64,6144]{1,0:T(8,128)(2,1)S(1)} %collective-permute-done.13.refs_1_, ...), custom_call_target="tpu_custom_call" | custom-call | flops 1000 | bytes 1000 | tf_op jit(solution)/shard_map/pallas_call | solution.py:244
  120.3 6.5 %shard_map.170 = (bf16[64,6144]{1,0:T(8,128)(2,1)S(1)}, bf16[64,6144]{1,0:T(8,128)(2,1)S(1)}, bf16[64,6144]{1,0:T(8,128)(2,1)S(1)}, bf16[64,6144]{1,0:T(8,128)(2,1)S(1)}) custom-call(bf16[64,6144]{1,0:T(8,128)(2,1)S(1)} %constant_dynamic-update-slice_fusion.14.refs_0_, bf16[64,6144]{1,0:T(8,128)(2,1)S(1)} %collective-permute-done.18.refs_1_, ...), custom_call_target="tpu_custom_call" | custom-call | flops 1000 | bytes 1000 | tf_op jit(solution)/shard_map/pallas_call | solution.py:244
  126.8 3.9 %collective-permute-done.27 = bf16[32,6144]{1,0:T(8,128)(2,1)S(1)} collective-permute-done((bf16[32,6144]{1,0:T(8,128)(2,1)S(1)}, bf16[32,6144]{1,0:T(8,128)(2,1)S(1)}, u32[]{:S(2)}, u32[]{:S(2)}) %collective-permute-start.27) | collective-permute-done | bytes 393248 | tf_op jit(solution)/shard_map/ppermute | solution.py:30
  130.7 3.3 %collective-permute-done.26 = bf16[32,6144]{1,0:T(8,128)(2,1)S(1)} collective-permute-done((bf16[32,6144]{1,0:T(8,128)(2,1)S(1)}, bf16[32,6144]{1,0:T(8,128)(2,1)S(1)}, u32[]{:S(2)}, u32[]{:S(2)}) %collective-permute-start.26) | collective-permute-done | bytes 393248 | tf_op jit(solution)/shard_map/ppermute | solution.py:30
  137.5 6.8 %shard_map.171 = (bf16[64,6144]{1,0:T(8,128)(2,1)S(1)}, bf16[64,6144]{1,0:T(8,128)(2,1)S(1)}, bf16[64,6144]{1,0:T(8,128)(2,1)S(1)}, bf16[64,6144]{1,0:T(8,128)(2,1)S(1)}) custom-call(bf16[64,6144]{1,0:T(8,128)(2,1)S(1)} %constant_dynamic-update-slice_fusion.16.refs_0_, bf16[64,6144]{1,0:T(8,128)(2,1)S(1)} %constant_dynamic-update-slice_fusion.18.refs_1_, ...), custom_call_target="tpu_custom_call" | custom-call | flops 1000 | bytes 1000 | tf_op jit(solution)/shard_map/pallas_call | solution.py:244
  155.7 7.5 %collective-permute-done.39 = bf16[32,6144]{1,0:T(8,128)(2,1)} collective-permute-done((bf16[32,6144]{1,0:T(8,128)(2,1)S(1)}, bf16[32,6144]{1,0:T(8,128)(2,1)}, u32[]{:S(2)}, u32[]{:S(2)}) %collective-permute-start.39) | collective-permute-done | bytes 393248 | tf_op jit(solution)/shard_map/ppermute | solution.py:30
  163.2 3.0 %collective-permute-done.38 = bf16[32,6144]{1,0:T(8,128)(2,1)} collective-permute-done((bf16[32,6144]{1,0:T(8,128)(2,1)}, bf16[32,6144]{1,0:T(8,128)(2,1)}, u32[]{:S(2)}, u32[]{:S(2)}) %collective-permute-start.38) | collective-permute-done | bytes 393248 | tf_op jit(solution)/shard_map/ppermute | solution.py:30
  174.2 4.2 %collective-permute-done.42 = bf16[32,6144]{1,0:T(8,128)(2,1)S(1)} collective-permute-done((bf16[32,6144]{1,0:T(8,128)(2,1)S(1)}, bf16[32,6144]{1,0:T(8,128)(2,1)S(1)}, u32[]{:S(2)}, u32[]{:S(2)}) %collective-permute-start.42) | collective-permute-done | bytes 393248 | tf_op jit(solution)/shard_map/ppermute | solution.py:30
  179.6 3.6 %collective-permute-done.41 = bf16[16,6144]{1,0:T(8,128)(2,1)S(1)} collective-permute-done((bf16[16,6144]{1,0:T(8,128)(2,1)S(1)}, bf16[16,6144]{1,0:T(8,128)(2,1)S(1)}, u32[]{:S(2)}, u32[]{:S(2)}) %collective-permute-start.41) | collective-permute-done | bytes 196640 | tf_op jit(solution)/shard_map/ppermute | solution.py:30
  190.0 2.9 %collective-permute-done.47 = bf16[16,1536]{1,0:T(8,128)(2,1)S(1)} collective-permute-done((bf16[16,1536]{1,0:T(8,128)(2,1)S(1)}, bf16[16,1536]{1,0:T(8,128)(2,1)S(1)}, u32[]{:S(2)}, u32[]{:S(2)}) %collective-permute-start.47) | collective-permute-done | bytes 49184 | tf_op jit(solution)/shard_map/ppermute | solution.py:30
  194.7 2.6 %collective-permute-done.44 = bf16[32,6144]{1,0:T(8,128)(2,1)S(1)} collective-permute-done((bf16[32,6144]{1,0:T(8,128)(2,1)S(1)}, bf16[32,6144]{1,0:T(8,128)(2,1)S(1)}, u32[]{:S(2)}, u32[]{:S(2)}) %collective-permute-start.44) | collective-permute-done | bytes 393248 | tf_op jit(solution)/shard_map/ppermute | solution.py:30
  205.8 4.0 %collective-permute-done.49 = bf16[16,1536]{1,0:T(8,128)(2,1)S(1)} collective-permute-done((bf16[16,1536]{1,0:T(8,128)(2,1)S(1)}, bf16[16,1536]{1,0:T(8,128)(2,1)S(1)}, u32[]{:S(2)}, u32[]{:S(2)}) %collective-permute-start.49) | collective-permute-done | bytes 49184 | tf_op jit(solution)/shard_map/ppermute | solution.py:30
  (215 shorter events, 91.3 us)
Async XLA Ops:
  2.6 16.9 %all-to-all-start = ((bf16[8,144,128]{2,1,0:T(8,128)(2,1)}), bf16[8,144,128]{2,1,0:T(8,128)(2,1)S(1)}, u32[]{:S(2)}, u32[]{:S(2)}) async-start(bf16[8,144,128]{2,1,0:T(8,128)(2,1)} %shard_map.164), calls=%async_computation | async-start | bytes 589824 | tf_op jit(solution)/shard_map/all_to_all | solution.py:317
  20.3 12.1 %all-to-all-start.1 = ((bf16[8,128,128]{2,1,0:T(8,128)(2,1)}), bf16[8,128,128]{2,1,0:T(8,128)(2,1)S(1)}, u32[]{:S(2)}, u32[]{:S(2)}) async-start(bf16[8,128,128]{2,1,0:T(8,128)(2,1)} %shard_map.165), calls=%async_computation.1 | async-start | bytes 524288 | tf_op jit(solution)/shard_map/all_to_all | solution.py:325
  48.6 11.3 %collective-permute-start.3 = (bf16[16,6144]{1,0:T(8,128)(2,1)S(1)}, bf16[16,6144]{1,0:T(8,128)(2,1)S(1)}, u32[]{:S(2)}, u32[]{:S(2)}) collective-permute-start(bf16[16,6144]{1,0:T(8,128)(2,1)S(1)} %multiply_convert_fusion.1), channel_id=1, source_target_pairs={{0,16},{1,17},{2,18},{3,19},{4,20},{5,21},{6,22},{7,23},{8,24},{9,... | collective-permute-start | bytes 589832 | tf_op jit(solution)/shard_map/ppermute | solution.py:30
  73.4 11.6 %collective-permute-start.10 = (bf16[64,6144]{1,0:T(8,128)(2,1)S(1)}, bf16[64,6144]{1,0:T(8,128)(2,1)S(1)}, u32[]{:S(2)}, u32[]{:S(2)}) collective-permute-start(bf16[64,6144]{1,0:T(8,128)(2,1)S(1)} %bitcast.32), channel_id=1, source_target_pairs={{0,1},{1,0},{2,3},{3,2},{4,5},{5,4},{6,7},{7,6},{8,9},{9,8},{10,11... | collective-permute-start | bytes 2359304 | tf_op jit(solution)/shard_map/ppermute | solution.py:30
  73.5 11.5 %collective-permute-start.9 = (bf16[32,6144]{1,0:T(8,128)(2,1)S(1)}, bf16[32,6144]{1,0:T(8,128)(2,1)S(1)}, u32[]{:S(2)}, u32[]{:S(2)}) collective-permute-start(bf16[32,6144]{1,0:T(8,128)(2,1)S(1)} %constant_dynamic-update-slice_fusion.10), channel_id=1, source_target_pairs={{0,2},{1,5},{2,0},{3,7},{4,6},{5,1},{6,4},{7,3},{8,10},{9,13},{10,... | collective-permute-start | bytes 1179656 | tf_op jit(solution)/shard_map/ppermute | solution.py:30
  85.6 16.3 %collective-permute-start.13 = (bf16[64,6144]{1,0:T(8,128)(2,1)S(1)}, bf16[64,6144]{1,0:T(8,128)(2,1)S(1)}, u32[]{:S(2)}, u32[]{:S(2)}) collective-permute-start(bf16[64,6144]{1,0:T(8,128)(2,1)S(1)} %constant_dynamic-update-slice_fusion.12.refs_0_), channel_id=1, source_target_pairs={{0,2},{1,5},{2,0},{3,7},{4,6},{5,1},{6,4},{7,3},{8,10},{9,13},{10,... | collective-permute-start | bytes 2359304 | tf_op jit(solution)/shard_map/ppermute | solution.py:30
  87.0 14.8 %collective-permute-start.14 = (bf16[64,6144]{1,0:T(8,128)(2,1)S(1)}, bf16[64,6144]{1,0:T(8,128)(2,1)S(1)}, u32[]{:S(2)}, u32[]{:S(2)}) collective-permute-start(bf16[64,6144]{1,0:T(8,128)(2,1)S(1)} %constant_dynamic-update-slice_fusion.12.refs_0_), channel_id=1, source_target_pairs={{0,1},{1,0},{2,3},{3,2},{4,5},{5,4},{6,7},{7,6},{8,9},{9,8},{10,11... | collective-permute-start | bytes 2359304 | tf_op jit(solution)/shard_map/ppermute | solution.py:30
  87.3 12.1 %collective-permute-start.15 = (bf16[32,6144]{1,0:T(8,128)(2,1)S(1)}, bf16[32,6144]{1,0:T(8,128)(2,1)S(1)}, u32[]{:S(2)}, u32[]{:S(2)}) collective-permute-start(bf16[32,6144]{1,0:T(8,128)(2,1)S(1)} %pad_maximum_fusion.3), channel_id=1, source_target_pairs={{0,4},{1,3},{2,6},{3,1},{4,0},{5,7},{6,2},{7,5},{8,12},{9,11},{10,... | collective-permute-start | bytes 1179656 | tf_op jit(solution)/shard_map/ppermute | solution.py:30
  88.4 11.3 %collective-permute-start.16 = (bf16[32,6144]{1,0:T(8,128)(2,1)S(1)}, bf16[32,6144]{1,0:T(8,128)(2,1)S(1)}, u32[]{:S(2)}, u32[]{:S(2)}) collective-permute-start(bf16[32,6144]{1,0:T(8,128)(2,1)S(1)} %pad_maximum_fusion.3), channel_id=1, source_target_pairs={{0,8},{1,9},{2,10},{3,11},{4,12},{5,13},{6,14},{7,15},{8,0},{9,1},... | collective-permute-start | bytes 1179656 | tf_op jit(solution)/shard_map/ppermute | solution.py:30
  102.5 13.0 %collective-permute-start.18 = (bf16[64,6144]{1,0:T(8,128)(2,1)S(1)}, bf16[64,6144]{1,0:T(8,128)(2,1)S(1)}, u32[]{:S(2)}, u32[]{:S(2)}) collective-permute-start(bf16[64,6144]{1,0:T(8,128)(2,1)S(1)} %constant_dynamic-update-slice_fusion.14.refs_0_), channel_id=1, source_target_pairs={{0,2},{1,5},{2,0},{3,7},{4,6},{5,1},{6,4},{7,3},{8,10},{9,13},{10,... | collective-permute-start | bytes 2359304 | tf_op jit(solution)/shard_map/ppermute | solution.py:30
  103.9 11.5 %collective-permute-start.19 = (bf16[64,6144]{1,0:T(8,128)(2,1)S(1)}, bf16[64,6144]{1,0:T(8,128)(2,1)S(1)}, u32[]{:S(2)}, u32[]{:S(2)}) collective-permute-start(bf16[64,6144]{1,0:T(8,128)(2,1)S(1)} %constant_dynamic-update-slice_fusion.14.refs_0_), channel_id=1, source_target_pairs={{0,1},{1,0},{2,3},{3,2},{4,5},{5,4},{6,7},{7,6},{8,9},{9,8},{10,11... | collective-permute-start | bytes 2359304 | tf_op jit(solution)/shard_map/ppermute | solution.py:30
  103.9 11.5 %collective-permute-start.20 = (bf16[32,6144]{1,0:T(8,128)(2,1)S(1)}, bf16[32,6144]{1,0:T(8,128)(2,1)S(1)}, u32[]{:S(2)}, u32[]{:S(2)}) collective-permute-start(bf16[32,6144]{1,0:T(8,128)(2,1)S(1)} %collective-permute-done.15), channel_id=1, source_target_pairs={{0,8},{1,9},{2,10},{3,11},{4,12},{5,13},{6,14},{7,15},{8,0},{9,1},... | collective-permute-start | bytes 1179656 | tf_op jit(solution)/shard_map/ppermute | solution.py:30
  117.6 16.5 %collective-permute-start.28 = (bf16[64,6144]{1,0:T(8,128)(2,1)S(1)}, bf16[64,6144]{1,0:T(8,128)(2,1)S(1)}, u32[]{:S(2)}, u32[]{:S(2)}) collective-permute-start(bf16[64,6144]{1,0:T(8,128)(2,1)S(1)} %constant_dynamic-update-slice_fusion.16.refs_0_), channel_id=1, source_target_pairs={{0,1},{1,0},{2,3},{3,2},{4,5},{5,4},{6,7},{7,6},{8,9},{9,8},{10,11... | collective-permute-start | bytes 2359304 | tf_op jit(solution)/shard_map/ppermute | solution.py:30
  117.9 16.2 %collective-permute-start.29 = (bf16[64,6144]{1,0:T(8,128)(2,1)S(1)}, bf16[64,6144]{1,0:T(8,128)(2,1)S(1)}, u32[]{:S(2)}, u32[]{:S(2)}) collective-permute-start(bf16[64,6144]{1,0:T(8,128)(2,1)S(1)} %add_convert_fusion.2), channel_id=1, source_target_pairs={{0,2},{1,5},{2,0},{3,7},{4,6},{5,1},{6,4},{7,3},{8,10},{9,13},{10,... | collective-permute-start | bytes 2359304 | tf_op jit(solution)/shard_map/ppermute | solution.py:30
  119.3 11.5 %collective-permute-start.27 = (bf16[32,6144]{1,0:T(8,128)(2,1)S(1)}, bf16[32,6144]{1,0:T(8,128)(2,1)S(1)}, u32[]{:S(2)}, u32[]{:S(2)}) collective-permute-start(bf16[32,6144]{1,0:T(8,128)(2,1)S(1)} %slice.163), channel_id=1, source_target_pairs={{0,8},{1,9},{2,10},{3,11},{4,12},{5,13},{6,14},{7,15},{8,0},{9,1},... | collective-permute-start | bytes 1179656 | tf_op jit(solution)/shard_map/ppermute | solution.py:30
  119.5 14.5 %collective-permute-start.26 = (bf16[32,6144]{1,0:T(8,128)(2,1)S(1)}, bf16[32,6144]{1,0:T(8,128)(2,1)S(1)}, u32[]{:S(2)}, u32[]{:S(2)}) collective-permute-start(bf16[32,6144]{1,0:T(8,128)(2,1)S(1)} %collective-permute-done.16), channel_id=1, source_target_pairs={{0,2},{1,5},{2,0},{3,7},{4,6},{5,1},{6,4},{7,3},{8,10},{9,13},{10,... | collective-permute-start | bytes 1179656 | tf_op jit(solution)/shard_map/ppermute | solution.py:30
  135.0 12.7 %collective-permute-start.31 = (bf16[32,6144]{1,0:T(8,128)(2,1)S(1)}, bf16[32,6144]{1,0:T(8,128)(2,1)S(1)}, u32[]{:S(2)}, u32[]{:S(2)}) collective-permute-start(bf16[32,6144]{1,0:T(8,128)(2,1)S(1)} %get-tuple-element.255), channel_id=1, source_target_pairs={{0,4},{1,3},{2,6},{3,1},{4,0},{5,7},{6,2},{7,5},{8,12},{9,11},{10,... | collective-permute-start | bytes 1179656 | tf_op jit(solution)/shard_map/ppermute | solution.py:30
  136.8 13.5 %collective-permute-start.32 = (bf16[64,6144]{1,0:T(8,128)(2,1)S(1)}, bf16[64,6144]{1,0:T(8,128)(2,1)S(1)}, u32[]{:S(2)}, u32[]{:S(2)}) collective-permute-start(bf16[64,6144]{1,0:T(8,128)(2,1)S(1)} %add_convert_fusion.3), channel_id=1, source_target_pairs={{0,2},{1,5},{2,0},{3,7},{4,6},{5,1},{6,4},{7,3},{8,10},{9,13},{10,... | collective-permute-start | bytes 2359304 | tf_op jit(solution)/shard_map/ppermute | solution.py:30
  137.3 13.0 %collective-permute-start.37 = (bf16[64,6144]{1,0:T(8,128)(2,1)S(1)}, bf16[64,6144]{1,0:T(8,128)(2,1)S(1)}, u32[]{:S(2)}, u32[]{:S(2)}) collective-permute-start(bf16[64,6144]{1,0:T(8,128)(2,1)S(1)} %get-tuple-element.215), channel_id=1, source_target_pairs={{0,1},{1,0},{2,3},{3,2},{4,5},{5,4},{6,7},{7,6},{8,9},{9,8},{10,11... | collective-permute-start | bytes 2359304 | tf_op jit(solution)/shard_map/ppermute | solution.py:30
  151.5 11.7 %collective-permute-start.39 = (bf16[32,6144]{1,0:T(8,128)(2,1)S(1)}, bf16[32,6144]{1,0:T(8,128)(2,1)}, u32[]{:S(2)}, u32[]{:S(2)}) collective-permute-start(bf16[32,6144]{1,0:T(8,128)(2,1)S(1)} %get-tuple-element.253), channel_id=1, source_target_pairs={{0,4},{1,3},{2,6},{3,1},{4,0},{5,7},{6,2},{7,5},{8,12},{9,11},{10,... | collective-permute-start | bytes 1179656 | tf_op jit(solution)/shard_map/ppermute | solution.py:30
  153.3 14.3 %collective-permute-start.40 = (bf16[64,6144]{1,0:T(8,128)(2,1)}, bf16[64,6144]{1,0:T(8,128)(2,1)}, u32[]{:S(2)}, u32[]{:S(2)}) collective-permute-start(bf16[64,6144]{1,0:T(8,128)(2,1)} %add_convert_fusion.1), channel_id=1, source_target_pairs={{0,2},{1,5},{2,0},{3,7},{4,6},{5,1},{6,4},{7,3},{8,10},{9,13},{10,... | collective-permute-start | bytes 2359304 | tf_op jit(solution)/shard_map/ppermute | solution.py:30
  154.7 11.5 %collective-permute-start.38 = (bf16[32,6144]{1,0:T(8,128)(2,1)}, bf16[32,6144]{1,0:T(8,128)(2,1)}, u32[]{:S(2)}, u32[]{:S(2)}) collective-permute-start(bf16[32,6144]{1,0:T(8,128)(2,1)} %add_convert_fusion.8), channel_id=1, source_target_pairs={{0,8},{1,9},{2,10},{3,11},{4,12},{5,13},{6,14},{7,15},{8,0},{9,1},... | collective-permute-start | bytes 1179656 | tf_op jit(solution)/shard_map/ppermute | solution.py:30
  171.6 11.7 %collective-permute-start.41 = (bf16[16,6144]{1,0:T(8,128)(2,1)S(1)}, bf16[16,6144]{1,0:T(8,128)(2,1)S(1)}, u32[]{:S(2)}, u32[]{:S(2)}) collective-permute-start(bf16[16,6144]{1,0:T(8,128)(2,1)S(1)} %get-tuple-element.260), channel_id=1, source_target_pairs={{0,16},{1,17},{2,18},{3,19},{4,20},{5,21},{6,22},{7,23},{8,24},{9,... | collective-permute-start | bytes 589832 | tf_op jit(solution)/shard_map/ppermute | solution.py:30
  173.4 12.0 %collective-permute-start.43 = (bf16[64,6144]{1,0:T(8,128)(2,1)S(1)}, bf16[64,6144]{1,0:T(8,128)(2,1)S(1)}, u32[]{:S(2)}, u32[]{:S(2)}) collective-permute-start(bf16[64,6144]{1,0:T(8,128)(2,1)S(1)} %copy-done.5), channel_id=1, source_target_pairs={{0,2},{1,5},{2,0},{3,7},{4,6},{5,1},{6,4},{7,3},{8,10},{9,13},{10,... | collective-permute-start | bytes 2359304 | tf_op jit(solution)/shard_map/ppermute | solution.py:30
  (48 other events, 361.8 us)

commit v7 on v6

--- a/solution.py
+++ b/solution.py
@@ -396,12 +396,15 @@
         mine, mine_last, other, other_last = outs
         return add(mine_last, to_core(other_last)), [mine, to_core(other)]
 
-    def fold(terms, got):
-        terms = terms + [got]
-        for mask in reversed(net[:-1]):
-            half = terms[0].shape[0] // 2
-            sent = total([t[half:] for t in terms]).astype(BF16)
-            terms = [total([t[:half] for t in terms]), exchange(sent, mask, count)]
+    def fold_sums(terms):
+        half = terms[0].shape[0] // 2
+        return total([t[:half] for t in terms]), total([t[half:] for t in terms]).astype(BF16)
+
+    def fold(stays, sent, masks):
+        terms = [stays, exchange(sent, masks[-1], count)]
+        for mask in reversed(masks[:-1]):
+            stays, sent = fold_sums(terms)
+            terms = [stays, exchange(sent, mask, count)]
         return terms
 
     def deliver(own, across):
@@ -472,26 +475,34 @@
     b1_out = expert([b1, b1_last, b1_other, to_core(b1_last)], *weights_in, loaded, scale["near1"])
     b2, b2_last, b2_other, a2_got, b1_out, a1_send = wait((b2, b2_last, b2_other, a2_got, b1_out, a1_send))
     b2_last = joined(b2_last)
+    steps = net[:-1]
     a1_got = exchange(a1_send, last, count)
-    a2_sum = fold(a2_rest, a2_got)
+    a2_stays, a2_sent = fold_sums(a2_rest + [a2_got])
+    a2_across = z_step(a2_sent, z_masks[1])
     b2_out = expert([b2, b2_last, b2_other, to_core(b2_last)], *weights_in, loaded, scale["far1"])
     b1_send, b1_rest = back(b1_out)
     b2_send, b2_rest = back(b2_out)
-    a2_sum, a1_got, b2_send, b2_rest, b1_send, b1_rest = wait(
-        (a2_sum, a1_got, b2_send, b2_rest, b1_send, b1_rest)
-    )
-    a_z = z_step(total(a2_sum).astype(BF16), z_masks[1])
-    a1_sum = fold(a1_rest, a1_got)
+    a2_stays, a2_across, a1_got, b2_send, b2_rest, b1_send, b1_rest = wait(
+        (a2_stays, a2_across, a1_got, b2_send, b2_rest, b1_send, b1_rest)
+    )
+    for mask in reversed(steps[:-1]):
+        a2_stays = total(fold(*fold_sums([a2_stays]), [mask]))
+    a_z = z_step(a2_stays.astype(BF16), z_masks[1])
+    half = a1_got.shape[0] // 2
+    a1_sent = total([t[half:] for t in a1_rest + [a1_got]] + [a2_across]).astype(BF16)
+    a1_sum = fold(total([t[:half] for t in a1_rest + [a1_got]]), a1_sent, steps)
     b2_got = exchange(b2_send, last, count)
-    a_z, a1_sum, b2_got, b1_send = wait((a_z, a1_sum, b2_got, b1_send))
+    b2_parts = fold_sums(b2_rest + [b2_got])
+    a_z, a1_sum, b2_parts, b1_send = wait((a_z, a1_sum, b2_parts, b1_send))
     b1_got = exchange(b1_send, last, count)
+    b1_parts = fold_sums(b1_rest + [b1_got])
     a_sum = a1_sum + [a_z]
     a_z = z_step(total([t[half_count:] for t in a_sum]).astype(BF16), z_masks[0])
     a_sum = total([t[:half_count] for t in a_sum])
-    b2_sum = total(fold(b2_rest, b2_got)).astype(BF16)
-    a_z, a_sum, b2_sum, b1_got = wait((a_z, a_sum, b2_sum, b1_got))
+    b2_sum = total(fold(*b2_parts, steps)).astype(BF16)
+    a_z, a_sum, b2_sum, b1_parts = wait((a_z, a_sum, b2_sum, b1_parts))
     b_z = z_step(b2_sum, z_masks[1])
-    b1_sum = fold(b1_rest, b1_got)
+    b1_sum = fold(*b1_parts, steps)
     a_out = deliver(total([hidden_a, a_sum, a_z]).astype(BF16), None)
     b_z, b1_sum, a_out = wait((b_z, b1_sum, a_out))
     b_sum = b1_sum + [b_z]

time: 212 us -> 216 us (1.019)
  local copies, waits for them, and re-layouts: 6.2 us -> 18.2 us
  waiting for transfers between devices: 92.1 us -> 84.8 us
    unnamed x48 -> x74, local copies, waits for them, and re-layouts: 2.03 us -> 12.3 us
    ppermute x56, waiting for transfers between devices: 80.6 us -> 73.3 us  [exchange(): return lax.ppermute(x, AXES, pairs)]
  transfers between devices with their start and end apart: 58 -> 58, of which waited for: 32 -> 26; matrix products, arithmetic and copies ran while one was open for 5% -> 7% of each run, Pallas kernels for 17% -> 18%
where the time goes in v7:
time: 216 us; the launch traced here: 215 us
  waiting for transfers between devices  84.8 us (39%)
  starting transfers between devices  55.4 us (26%)
  Pallas kernels  41.7 us (19%)
  local copies, waits for them, and re-layouts  18.2 us (8%)
  other arithmetic  7.46 us (3%)
  matrix products  6.41 us (3%)
    ppermute x56, waiting for transfers between devices, exchange(): return lax.ppermute(x, AXES, pairs)  73.3 us
    ppermute x56, starting transfers between devices, exchange(): return lax.ppermute(x, AXES, pairs)  44.5 us
    pallas_call x4, Pallas kernels, expert(): pl.pallas_call(functools.partial(expert_kernel, blocks), in_specs=[whole(...  28.5 us
    unnamed x74, local copies, waits for them, and re-layouts  12.3 us
    all_to_all x1, starting transfers between devices, shards(): lax.all_to_all(payload, 'seq', split_axis=0, concat_axis=0, tiled=True)  7.29 us
    pallas_call x1, Pallas kernels, load(): pl.pallas_call(load_kernel, in_specs=[pl.BlockSpec(memory_space=pltpu.HBM...  7.06 us
    dot_general x1, matrix products, shards(): jnp.dot(attn_in, out_weight, preferred_element_type=F32).astype(BF16)  6.41 us
    pallas_call x4, Pallas kernels, call(): pl.pallas_call(kernel, in_specs=specs + [whole()] * (len(operands) - len(...  6.14 us
  transfers between devices with their start and end apart: 58, of which 26 were waited for; matrix products, arithmetic and copies ran while one was open for 7% of the time, Pallas kernels for 18%

profile of v7, /device:TPU:0, one launch (start us, length us, event | category | flops | bytes accessed | tf_op | source)
XLA Modules:
  0.0 215.0 jit_solution(4337780771103416515)
XLA Ops:
  0.0 2.6 %shard_map.164 = bf16[8,144,128]{2,1,0:T(8,128)(2,1)} custom-call(s32[1]{0:T(128)} %bitcast.2.me_ref, f32[8,128]{1,0:T(8,128)} %bitcast.42, s32[1,128]{1,0:T(1,128)} %bitcast.44, s32[2,128]{1,0:T(2,128)} %bitcast.46, f32[2,128]{1,0:T(2,128)} %bitcast.47, bf16[128,1024]{1,0:T(8,128)(2,1)} %refs_4_.3, bf16[128,1024]{1,0:T(8,128)(2,1)} %refs_5_.1), custom_call_target="tpu_custom_call" | custom-call | tf_op jit(solution)/shard_map/pallas_call | solution.py:264
  2.6 7.3 %all-to-all-start = ((bf16[8,144,128]{2,1,0:T(8,128)(2,1)}), bf16[8,144,128]{2,1,0:T(8,128)(2,1)S(1)}, u32[]{:S(2)}, u32[]{:S(2)}) async-start(bf16[8,144,128]{2,1,0:T(8,128)(2,1)} %shard_map.164), calls=%async_computation | async-start | bytes 589824 | tf_op jit(solution)/shard_map/all_to_all | solution.py:317
  13.5 6.0 %all-to-all-done.in_ref = bf16[8,144,128]{2,1,0:T(8,128)(2,1)S(1)} async-done(((bf16[8,144,128]{2,1,0:T(8,128)(2,1)}), bf16[8,144,128]{2,1,0:T(8,128)(2,1)S(1)}, u32[]{:S(2)}, u32[]{:S(2)}) %all-to-all-start) | async-done | bytes 294944 | tf_op jit(solution)/shard_map/all_to_all | solution.py:317
  20.3 3.6 %all-to-all-start.1 = ((bf16[8,128,128]{2,1,0:T(8,128)(2,1)}), bf16[8,128,128]{2,1,0:T(8,128)(2,1)S(1)}, u32[]{:S(2)}, u32[]{:S(2)}) async-start(bf16[8,128,128]{2,1,0:T(8,128)(2,1)} %shard_map.165), calls=%async_computation.1 | async-start | bytes 524288 | tf_op jit(solution)/shard_map/all_to_all | solution.py:325
  26.9 5.5 %all-to-all-done.1.state_ref = bf16[8,128,128]{2,1,0:T(8,128)(2,1)S(1)} async-done(((bf16[8,128,128]{2,1,0:T(8,128)(2,1)}), bf16[8,128,128]{2,1,0:T(8,128)(2,1)S(1)}, u32[]{:S(2)}, u32[]{:S(2)}) %all-to-all-start.1) | async-done | bytes 262176 | tf_op jit(solution)/shard_map/all_to_all | solution.py:325
  32.8 6.4 %convolution_convert_fusion = bf16[128,6144]{1,0:T(8,128)(2,1)S(1)} fusion(bf16[128,1024]{1,0:T(8,128)(2,1)S(1)} %shard_map.166, bf16[1024,6144]{1,0:T(8,128)(2,1)} %param.23), kind=kOutput, calls=%fused_computation.4 | convolution fusion | flops 1611399168 | bytes 14417920 | tf_op jit(solution)/shard_map/dot_general | solution.py:359
  42.8 5.4 %collective-permute-done.1 = bf16[16,6144]{1,0:T(8,128)(2,1)S(1)} collective-permute-done((bf16[16,6144]{1,0:T(8,128)(2,1)S(1)}, bf16[16,6144]{1,0:T(8,128)(2,1)S(1)}, u32[]{:S(2)}, u32[]{:S(2)}) %collective-permute-start.1) | collective-permute-done | bytes 196640 | tf_op jit(solution)/shard_map/ppermute | solution.py:30
  50.2 7.1 %shard_map.167 = (bf16[576,6144]{1,0:T(8,128)(2,1)S(1)}, bf16[576,6144]{1,0:T(8,128)(2,1)S(1)}, bf16[576,6144]{1,0:T(8,128)(2,1)S(1)}, f32[8,128]{1,0:T(8,128)S(1)}) custom-call(bf16[1,576,6144]{2,1,0:T(8,128)(2,1)} %bitcast.36, bf16[1,576,6144]{2,1,0:T(8,128)(2,1)} %bitcast.37, bf16[1,576,6144]{2,1,0:T(8,128)(2,1)} %refs_2_.2), custom_call_target="tpu_custom_call" | custom-call | tf_op jit(solution)/shard_map/pallas_call | solution.py:208
  57.3 2.6 %collective-permute-done.3 = bf16[16,6144]{1,0:T(8,128)(2,1)S(1)} collective-permute-done((bf16[16,6144]{1,0:T(8,128)(2,1)S(1)}, bf16[16,6144]{1,0:T(8,128)(2,1)S(1)}, u32[]{:S(2)}, u32[]{:S(2)}) %collective-permute-start.3) | collective-permute-done | bytes 196640 | tf_op jit(solution)/shard_map/ppermute | solution.py:30
  63.3 4.7 %collective-permute-done.8 = bf16[16,6144]{1,0:T(8,128)(2,1)S(1)} collective-permute-done((bf16[16,6144]{1,0:T(8,128)(2,1)S(1)}, bf16[16,6144]{1,0:T(8,128)(2,1)S(1)}, u32[]{:S(2)}, u32[]{:S(2)}) %collective-permute-start.8) | collective-permute-done | bytes 196640 | tf_op jit(solution)/shard_map/ppermute | solution.py:30
  69.4 2.7 %collective-permute-done.7 = bf16[32,6144]{1,0:T(8,128)(2,1)S(1)} collective-permute-done((bf16[32,6144]{1,0:T(8,128)(2,1)S(1)}, bf16[32,6144]{1,0:T(8,128)(2,1)S(1)}, u32[]{:S(2)}, u32[]{:S(2)}) %collective-permute-start.7) | collective-permute-done | bytes 393248 | tf_op jit(solution)/shard_map/ppermute | solution.py:30
  76.4 6.2 %collective-permute-done.12 = bf16[16,6144]{1,0:T(8,128)(2,1)S(1)} collective-permute-done((bf16[16,6144]{1,0:T(8,128)(2,1)S(1)}, bf16[16,6144]{1,0:T(8,128)(2,1)S(1)}, u32[]{:S(2)}, u32[]{:S(2)}) %collective-permute-start.12) | collective-permute-done | bytes 196640 | tf_op jit(solution)/shard_map/ppermute | solution.py:30
  90.5 6.4 %shard_map.168 = (bf16[64,6144]{1,0:T(8,128)(2,1)S(1)}, bf16[64,6144]{1,0:T(8,128)(2,1)S(1)}, bf16[64,6144]{1,0:T(8,128)(2,1)S(1)}, bf16[64,6144]{1,0:T(8,128)(2,1)S(1)}) custom-call(bf16[64,6144]{1,0:T(8,128)(2,1)S(1)} %bitcast.33, bf16[64,6144]{1,0:T(8,128)(2,1)S(1)} %bitcast.35, bf16[64,6144]{1,0:T(8,128)(2,1)S(1)} %collective-permute-done.10.refs_2_, ...), custom_call_target="tpu_custom_call" | custom-call | flops 1000 | bytes 1000 | tf_op jit(solution)/shard_map/pallas_call | solution.py:244
  105.8 6.6 %shard_map.169 = (bf16[64,6144]{1,0:T(8,128)(2,1)S(1)}, bf16[64,6144]{1,0:T(8,128)(2,1)S(1)}, bf16[64,6144]{1,0:T(8,128)(2,1)S(1)}, bf16[64,6144]{1,0:T(8,128)(2,1)S(1)}) custom-call(bf16[64,6144]{1,0:T(8,128)(2,1)S(1)} %constant_dynamic-update-slice_fusion.12.refs_0_, bf16[64,6144]{1,0:T(8,128)(2,1)S(1)} %collective-permute-done.13.refs_1_, ...), custom_call_target="tpu_custom_call" | custom-call | flops 1000 | bytes 1000 | tf_op jit(solution)/shard_map/pallas_call | solution.py:244
  122.0 3.0 %copy-done.3 = bf16[576,6144]{1,0:T(8,128)(2,1)S(1)} copy-done((bf16[576,6144]{1,0:T(8,128)(2,1)S(1)}, bf16[576,6144]{1,0:T(8,128)(2,1)}, u32[]{:S(2)}) %copy-start.3) | copy-done | bytes 7077912
  125.0 3.0 %copy-done.5 = bf16[576,6144]{1,0:T(8,128)(2,1)S(1)} copy-done((bf16[576,6144]{1,0:T(8,128)(2,1)S(1)}, bf16[576,6144]{1,0:T(8,128)(2,1)}, u32[]{:S(2)}) %copy-start.5) | copy-done | bytes 7077912
  128.0 3.0 %copy-done.7 = bf16[576,6144]{1,0:T(8,128)(2,1)S(1)} copy-done((bf16[576,6144]{1,0:T(8,128)(2,1)S(1)}, bf16[576,6144]{1,0:T(8,128)(2,1)}, u32[]{:S(2)}) %copy-start.7) | copy-done | bytes 7077912
  131.0 7.5 %shard_map.170 = (bf16[64,6144]{1,0:T(8,128)(2,1)S(1)}, bf16[64,6144]{1,0:T(8,128)(2,1)S(1)}, bf16[64,6144]{1,0:T(8,128)(2,1)S(1)}, bf16[64,6144]{1,0:T(8,128)(2,1)S(1)}) custom-call(bf16[64,6144]{1,0:T(8,128)(2,1)S(1)} %constant_dynamic-update-slice_fusion.14.refs_0_, bf16[64,6144]{1,0:T(8,128)(2,1)S(1)} %collective-permute-done.18.refs_1_, ...), custom_call_target="tpu_custom_call" | custom-call | flops 1000 | bytes 1000 | tf_op jit(solution)/shard_map/pallas_call | solution.py:244
  146.9 7.8 %shard_map.171 = (bf16[64,6144]{1,0:T(8,128)(2,1)S(1)}, bf16[64,6144]{1,0:T(8,128)(2,1)S(1)}, bf16[64,6144]{1,0:T(8,128)(2,1)S(1)}, bf16[64,6144]{1,0:T(8,128)(2,1)S(1)}) custom-call(bf16[64,6144]{1,0:T(8,128)(2,1)S(1)} %constant_dynamic-update-slice_fusion.16.refs_0_, bf16[64,6144]{1,0:T(8,128)(2,1)S(1)} %constant_dynamic-update-slice_fusion.18.refs_1_, ...), custom_call_target="tpu_custom_call" | custom-call | flops 1000 | bytes 1000 | tf_op jit(solution)/shard_map/pallas_call | solution.py:244
  161.2 13.3 %collective-permute-done.40 = bf16[64,6144]{1,0:T(8,128)(2,1)S(1)} collective-permute-done((bf16[64,6144]{1,0:T(8,128)(2,1)S(1)}, bf16[64,6144]{1,0:T(8,128)(2,1)S(1)}, u32[]{:S(2)}, u32[]{:S(2)}) %collective-permute-start.40) | collective-permute-done | bytes 786464 | tf_op jit(solution)/shard_map/ppermute | solution.py:30
  178.5 9.0 %collective-permute-done.42 = bf16[32,6144]{1,0:T(8,128)(2,1)S(1)} collective-permute-done((bf16[32,6144]{1,0:T(8,128)(2,1)S(1)}, bf16[32,6144]{1,0:T(8,128)(2,1)S(1)}, u32[]{:S(2)}, u32[]{:S(2)}) %collective-permute-start.42) | collective-permute-done | bytes 393248 | tf_op jit(solution)/shard_map/ppermute | solution.py:30
  187.6 2.6 %collective-permute-done.43 = bf16[64,6144]{1,0:T(8,128)(2,1)S(1)} collective-permute-done((bf16[64,6144]{1,0:T(8,128)(2,1)S(1)}, bf16[64,6144]{1,0:T(8,128)(2,1)S(1)}, u32[]{:S(2)}, u32[]{:S(2)}) %collective-permute-start.43) | collective-permute-done | bytes 786464 | tf_op jit(solution)/shard_map/ppermute | solution.py:30
  194.1 2.9 %collective-permute-done.47 = bf16[16,1536]{1,0:T(8,128)(2,1)S(1)} collective-permute-done((bf16[16,1536]{1,0:T(8,128)(2,1)S(1)}, bf16[16,1536]{1,0:T(8,128)(2,1)S(1)}, u32[]{:S(2)}, u32[]{:S(2)}) %collective-permute-start.47) | collective-permute-done | bytes 49184 | tf_op jit(solution)/shard_map/ppermute | solution.py:30
  209.6 3.8 %collective-permute-done.49 = bf16[16,1536]{1,0:T(8,128)(2,1)S(1)} collective-permute-done((bf16[16,1536]{1,0:T(8,128)(2,1)S(1)}, bf16[16,1536]{1,0:T(8,128)(2,1)S(1)}, u32[]{:S(2)}, u32[]{:S(2)}) %collective-permute-start.49) | collective-permute-done | bytes 49184 | tf_op jit(solution)/shard_map/ppermute | solution.py:30
  (241 shorter events, 84.9 us)
Async XLA Ops:
  2.6 16.9 %all-to-all-start = ((bf16[8,144,128]{2,1,0:T(8,128)(2,1)}), bf16[8,144,128]{2,1,0:T(8,128)(2,1)S(1)}, u32[]{:S(2)}, u32[]{:S(2)}) async-start(bf16[8,144,128]{2,1,0:T(8,128)(2,1)} %shard_map.164), calls=%async_computation | async-start | bytes 589824 | tf_op jit(solution)/shard_map/all_to_all | solution.py:317
  20.3 12.1 %all-to-all-start.1 = ((bf16[8,128,128]{2,1,0:T(8,128)(2,1)}), bf16[8,128,128]{2,1,0:T(8,128)(2,1)S(1)}, u32[]{:S(2)}, u32[]{:S(2)}) async-start(bf16[8,128,128]{2,1,0:T(8,128)(2,1)} %shard_map.165), calls=%async_computation.1 | async-start | bytes 524288 | tf_op jit(solution)/shard_map/all_to_all | solution.py:325
  73.3 11.6 %collective-permute-start.10 = (bf16[64,6144]{1,0:T(8,128)(2,1)S(1)}, bf16[64,6144]{1,0:T(8,128)(2,1)S(1)}, u32[]{:S(2)}, u32[]{:S(2)}) collective-permute-start(bf16[64,6144]{1,0:T(8,128)(2,1)S(1)} %bitcast.32), channel_id=1, source_target_pairs={{0,1},{1,0},{2,3},{3,2},{4,5},{5,4},{6,7},{7,6},{8,9},{9,8},{10,11... | collective-permute-start | bytes 2359304 | tf_op jit(solution)/shard_map/ppermute | solution.py:30
  73.4 11.5 %collective-permute-start.9 = (bf16[32,6144]{1,0:T(8,128)(2,1)S(1)}, bf16[32,6144]{1,0:T(8,128)(2,1)S(1)}, u32[]{:S(2)}, u32[]{:S(2)}) collective-permute-start(bf16[32,6144]{1,0:T(8,128)(2,1)S(1)} %constant_dynamic-update-slice_fusion.10), channel_id=1, source_target_pairs={{0,2},{1,5},{2,0},{3,7},{4,6},{5,1},{6,4},{7,3},{8,10},{9,13},{10,... | collective-permute-start | bytes 1179656 | tf_op jit(solution)/shard_map/ppermute | solution.py:30
  85.6 16.3 %collective-permute-start.13 = (bf16[64,6144]{1,0:T(8,128)(2,1)S(1)}, bf16[64,6144]{1,0:T(8,128)(2,1)S(1)}, u32[]{:S(2)}, u32[]{:S(2)}) collective-permute-start(bf16[64,6144]{1,0:T(8,128)(2,1)S(1)} %constant_dynamic-update-slice_fusion.12.refs_0_), channel_id=1, source_target_pairs={{0,2},{1,5},{2,0},{3,7},{4,6},{5,1},{6,4},{7,3},{8,10},{9,13},{10,... | collective-permute-start | bytes 2359304 | tf_op jit(solution)/shard_map/ppermute | solution.py:30
  87.0 14.8 %collective-permute-start.14 = (bf16[64,6144]{1,0:T(8,128)(2,1)S(1)}, bf16[64,6144]{1,0:T(8,128)(2,1)S(1)}, u32[]{:S(2)}, u32[]{:S(2)}) collective-permute-start(bf16[64,6144]{1,0:T(8,128)(2,1)S(1)} %constant_dynamic-update-slice_fusion.12.refs_0_), channel_id=1, source_target_pairs={{0,1},{1,0},{2,3},{3,2},{4,5},{5,4},{6,7},{7,6},{8,9},{9,8},{10,11... | collective-permute-start | bytes 2359304 | tf_op jit(solution)/shard_map/ppermute | solution.py:30
  87.3 12.1 %collective-permute-start.15 = (bf16[32,6144]{1,0:T(8,128)(2,1)S(1)}, bf16[32,6144]{1,0:T(8,128)(2,1)S(1)}, u32[]{:S(2)}, u32[]{:S(2)}) collective-permute-start(bf16[32,6144]{1,0:T(8,128)(2,1)S(1)} %pad_maximum_fusion.3), channel_id=1, source_target_pairs={{0,4},{1,3},{2,6},{3,1},{4,0},{5,7},{6,2},{7,5},{8,12},{9,11},{10,... | collective-permute-start | bytes 1179656 | tf_op jit(solution)/shard_map/ppermute | solution.py:30
  102.4 13.8 %collective-permute-start.18 = (bf16[64,6144]{1,0:T(8,128)(2,1)S(1)}, bf16[64,6144]{1,0:T(8,128)(2,1)S(1)}, u32[]{:S(2)}, u32[]{:S(2)}) collective-permute-start(bf16[64,6144]{1,0:T(8,128)(2,1)S(1)} %constant_dynamic-update-slice_fusion.14.refs_0_), channel_id=1, source_target_pairs={{0,2},{1,5},{2,0},{3,7},{4,6},{5,1},{6,4},{7,3},{8,10},{9,13},{10,... | collective-permute-start | bytes 2359304 | tf_op jit(solution)/shard_map/ppermute | solution.py:30
  103.9 12.4 %collective-permute-start.19 = (bf16[64,6144]{1,0:T(8,128)(2,1)S(1)}, bf16[64,6144]{1,0:T(8,128)(2,1)S(1)}, u32[]{:S(2)}, u32[]{:S(2)}) collective-permute-start(bf16[64,6144]{1,0:T(8,128)(2,1)S(1)} %constant_dynamic-update-slice_fusion.14.refs_0_), channel_id=1, source_target_pairs={{0,1},{1,0},{2,3},{3,2},{4,5},{5,4},{6,7},{7,6},{8,9},{9,8},{10,11... | collective-permute-start | bytes 2359304 | tf_op jit(solution)/shard_map/ppermute | solution.py:30
  103.9 12.3 %collective-permute-start.20 = (bf16[32,6144]{1,0:T(8,128)(2,1)S(1)}, bf16[32,6144]{1,0:T(8,128)(2,1)S(1)}, u32[]{:S(2)}, u32[]{:S(2)}) collective-permute-start(bf16[32,6144]{1,0:T(8,128)(2,1)S(1)} %collective-permute-done.15), channel_id=1, source_target_pairs={{0,8},{1,9},{2,10},{3,11},{4,12},{5,13},{6,14},{7,15},{8,0},{9,1},... | collective-permute-start | bytes 1179656 | tf_op jit(solution)/shard_map/ppermute | solution.py:30
  118.5 20.1 %collective-permute-start.28 = (bf16[64,6144]{1,0:T(8,128)(2,1)S(1)}, bf16[64,6144]{1,0:T(8,128)(2,1)}, u32[]{:S(2)}, u32[]{:S(2)}) collective-permute-start(bf16[64,6144]{1,0:T(8,128)(2,1)S(1)} %constant_dynamic-update-slice_fusion.16.refs_0_), channel_id=1, source_target_pairs={{0,1},{1,0},{2,3},{3,2},{4,5},{5,4},{6,7},{7,6},{8,9},{9,8},{10,11... | collective-permute-start | bytes 2359304 | tf_op jit(solution)/shard_map/ppermute | solution.py:30
  118.9 19.7 %collective-permute-start.29 = (bf16[64,6144]{1,0:T(8,128)(2,1)}, bf16[64,6144]{1,0:T(8,128)(2,1)}, u32[]{:S(2)}, u32[]{:S(2)}) collective-permute-start(bf16[64,6144]{1,0:T(8,128)(2,1)} %add_convert_fusion.2), channel_id=1, source_target_pairs={{0,2},{1,5},{2,0},{3,7},{4,6},{5,1},{6,4},{7,3},{8,10},{9,13},{10,... | collective-permute-start | bytes 2359304 | tf_op jit(solution)/shard_map/ppermute | solution.py:30
  121.1 17.5 %collective-permute-start.27 = (bf16[32,6144]{1,0:T(8,128)(2,1)}, bf16[32,6144]{1,0:T(8,128)(2,1)}, u32[]{:S(2)}, u32[]{:S(2)}) collective-permute-start(bf16[32,6144]{1,0:T(8,128)(2,1)} %slice.163), channel_id=1, source_target_pairs={{0,8},{1,9},{2,10},{3,11},{4,12},{5,13},{6,14},{7,15},{8,0},{9,1},... | collective-permute-start | bytes 1179656 | tf_op jit(solution)/shard_map/ppermute | solution.py:30
  121.3 17.3 %collective-permute-start.26 = (bf16[32,6144]{1,0:T(8,128)(2,1)}, bf16[32,6144]{1,0:T(8,128)(2,1)}, u32[]{:S(2)}, u32[]{:S(2)}) collective-permute-start(bf16[32,6144]{1,0:T(8,128)(2,1)} %collective-permute-done.16), channel_id=1, source_target_pairs={{0,2},{1,5},{2,0},{3,7},{4,6},{5,1},{6,4},{7,3},{8,10},{9,13},{10,... | collective-permute-start | bytes 1179656 | tf_op jit(solution)/shard_map/ppermute | solution.py:30
  138.6 16.7 %collective-permute-start.36 = (bf16[64,6144]{1,0:T(8,128)(2,1)S(1)}, bf16[64,6144]{1,0:T(8,128)(2,1)S(1)}, u32[]{:S(2)}, u32[]{:S(2)}) collective-permute-start(bf16[64,6144]{1,0:T(8,128)(2,1)S(1)} %get-tuple-element.215), channel_id=1, source_target_pairs={{0,1},{1,0},{2,3},{3,2},{4,5},{5,4},{6,7},{7,6},{8,9},{9,8},{10,11... | collective-permute-start | bytes 2359304 | tf_op jit(solution)/shard_map/ppermute | solution.py:30
  142.5 14.9 %collective-permute-start.31 = (bf16[32,6144]{1,0:T(8,128)(2,1)S(1)}, bf16[32,6144]{1,0:T(8,128)(2,1)S(1)}, u32[]{:S(2)}, u32[]{:S(2)}) collective-permute-start(bf16[32,6144]{1,0:T(8,128)(2,1)S(1)} %add_convert_fusion.8), channel_id=1, source_target_pairs={{0,8},{1,9},{2,10},{3,11},{4,12},{5,13},{6,14},{7,15},{8,0},{9,1},... | collective-permute-start | bytes 1179656 | tf_op jit(solution)/shard_map/ppermute | solution.py:30
  144.2 13.2 %collective-permute-start.32 = (bf16[64,6144]{1,0:T(8,128)(2,1)S(1)}, bf16[64,6144]{1,0:T(8,128)(2,1)S(1)}, u32[]{:S(2)}, u32[]{:S(2)}) collective-permute-start(bf16[64,6144]{1,0:T(8,128)(2,1)S(1)} %copy-done.16), channel_id=1, source_target_pairs={{0,2},{1,5},{2,0},{3,7},{4,6},{5,1},{6,4},{7,3},{8,10},{9,13},{10,... | collective-permute-start | bytes 2359304 | tf_op jit(solution)/shard_map/ppermute | solution.py:30
  145.7 11.7 %collective-permute-start.37 = (bf16[64,6144]{1,0:T(8,128)(2,1)S(1)}, bf16[64,6144]{1,0:T(8,128)(2,1)S(1)}, u32[]{:S(2)}, u32[]{:S(2)}) collective-permute-start(bf16[64,6144]{1,0:T(8,128)(2,1)S(1)} %get-tuple-element.217), channel_id=1, source_target_pairs={{0,1},{1,0},{2,3},{3,2},{4,5},{5,4},{6,7},{7,6},{8,9},{9,8},{10,11... | collective-permute-start | bytes 2359304 | tf_op jit(solution)/shard_map/ppermute | solution.py:30
  158.3 16.2 %collective-permute-start.40 = (bf16[64,6144]{1,0:T(8,128)(2,1)S(1)}, bf16[64,6144]{1,0:T(8,128)(2,1)S(1)}, u32[]{:S(2)}, u32[]{:S(2)}) collective-permute-start(bf16[64,6144]{1,0:T(8,128)(2,1)S(1)} %add_convert_fusion.1), channel_id=1, source_target_pairs={{0,2},{1,5},{2,0},{3,7},{4,6},{5,1},{6,4},{7,3},{8,10},{9,13},{10,... | collective-permute-start | bytes 2359304 | tf_op jit(solution)/shard_map/ppermute | solution.py:30
  159.2 15.6 %collective-permute-start.39 = (bf16[32,6144]{1,0:T(8,128)(2,1)S(1)}, bf16[32,6144]{1,0:T(8,128)(2,1)S(1)}, u32[]{:S(2)}, u32[]{:S(2)}) collective-permute-start(bf16[32,6144]{1,0:T(8,128)(2,1)S(1)} %get-tuple-element.259), channel_id=1, source_target_pairs={{0,4},{1,3},{2,6},{3,1},{4,0},{5,7},{6,2},{7,5},{8,12},{9,11},{10,... | collective-permute-start | bytes 1179656 | tf_op jit(solution)/shard_map/ppermute | solution.py:30
  161.0 13.8 %collective-permute-start.38 = (bf16[32,6144]{1,0:T(8,128)(2,1)S(1)}, bf16[32,6144]{1,0:T(8,128)(2,1)S(1)}, u32[]{:S(2)}, u32[]{:S(2)}) collective-permute-start(bf16[32,6144]{1,0:T(8,128)(2,1)S(1)} %convert_add_fusion.3), channel_id=1, source_target_pairs={{0,8},{1,9},{2,10},{3,11},{4,12},{5,13},{6,14},{7,15},{8,0},{9,1},... | collective-permute-start | bytes 1179656 | tf_op jit(solution)/shard_map/ppermute | solution.py:30
  174.8 15.3 %collective-permute-start.43 = (bf16[64,6144]{1,0:T(8,128)(2,1)S(1)}, bf16[64,6144]{1,0:T(8,128)(2,1)S(1)}, u32[]{:S(2)}, u32[]{:S(2)}) collective-permute-start(bf16[64,6144]{1,0:T(8,128)(2,1)S(1)} %add_convert_fusion), channel_id=1, source_target_pairs={{0,2},{1,5},{2,0},{3,7},{4,6},{5,1},{6,4},{7,3},{8,10},{9,13},{10,... | collective-permute-start | bytes 2359304 | tf_op jit(solution)/shard_map/ppermute | solution.py:30
  175.4 12.1 %collective-permute-start.42 = (bf16[32,6144]{1,0:T(8,128)(2,1)S(1)}, bf16[32,6144]{1,0:T(8,128)(2,1)S(1)}, u32[]{:S(2)}, u32[]{:S(2)}) collective-permute-start(bf16[32,6144]{1,0:T(8,128)(2,1)S(1)} %get-tuple-element.231), channel_id=1, source_target_pairs={{0,4},{1,3},{2,6},{3,1},{4,0},{5,7},{6,2},{7,5},{8,12},{9,11},{10,... | collective-permute-start | bytes 1179656 | tf_op jit(solution)/shard_map/ppermute | solution.py:30
  177.1 13.3 %collective-permute-start.41 = (bf16[16,6144]{1,0:T(8,128)(2,1)S(1)}, bf16[16,6144]{1,0:T(8,128)(2,1)S(1)}, u32[]{:S(2)}, u32[]{:S(2)}) collective-permute-start(bf16[16,6144]{1,0:T(8,128)(2,1)S(1)} %get-tuple-element.264), channel_id=1, source_target_pairs={{0,16},{1,17},{2,18},{3,19},{4,20},{5,21},{6,22},{7,23},{8,24},{9,... | collective-permute-start | bytes 589832 | tf_op jit(solution)/shard_map/ppermute | solution.py:30
  (61 other events, 558.8 us)

commit v8 on v7

--- a/solution.py
+++ b/solution.py
@@ -407,11 +407,11 @@
             terms = [stays, exchange(sent, mask, count)]
         return terms
 
-    def deliver(own, across):
+    def deliver(own, across, place):
         width = own.shape[1] // n_hx
 
         def piece(rows, to):
-            return lax.dynamic_slice_in_dim(rows, (hx_index ^ to) * width, width, axis=1)
+            return lax.dynamic_slice_in_dim(rows, (place ^ to) * width, width, axis=1)
 
         group = offsets(x_masks + [1])
         sums = {to: [] for to in group}
@@ -500,18 +500,18 @@
     a_z = z_step(total([t[half_count:] for t in a_sum]).astype(BF16), z_masks[0])
     a_sum = total([t[:half_count] for t in a_sum])
     b2_sum = total(fold(*b2_parts, steps)).astype(BF16)
-    a_z, a_sum, b2_sum, b1_parts = wait((a_z, a_sum, b2_sum, b1_parts))
+    a_z, a_sum, b2_sum, b1_parts, place = wait((a_z, a_sum, b2_sum, b1_parts, hx_index))
     b_z = z_step(b2_sum, z_masks[1])
     b1_sum = fold(*b1_parts, steps)
-    a_out = deliver(total([hidden_a, a_sum, a_z]).astype(BF16), None)
+    a_out = deliver(total([hidden_a, a_sum, a_z]).astype(BF16), None, place)
     b_z, b1_sum, a_out = wait((b_z, b1_sum, a_out))
     b_sum = b1_sum + [b_z]
     across = total([t[half_count:] for t in b_sum]).astype(BF16)
-    b_out = deliver(total([hidden_b] + [t[:half_count] for t in b_sum]).astype(BF16), across)
+    b_out = deliver(total([hidden_b] + [t[:half_count] for t in b_sum]).astype(BF16), across, place)
     out = jnp.zeros((n_hx, HALVES * half_count, across.shape[1] // n_hx), BF16)
     for to in a_out:
         rows = jnp.concatenate([a_out[to], b_out[to]], axis=0)
-        out = lax.dynamic_update_slice_in_dim(out, rows[None], hx_index ^ to, axis=0)
+        out = lax.dynamic_update_slice_in_dim(out, rows[None], place ^ to, axis=0)
     return out.reshape(tok_count, -1)
 
 

time: 216 us -> 208 us (0.963)
  local copies, waits for them, and re-layouts: 18.2 us -> 6.66 us
  waiting for transfers between devices: 84.8 us -> 91.8 us
  Pallas kernels: 41.7 us -> 39.4 us
    unnamed x74 -> x52, local copies, waits for them, and re-layouts: 12.3 us -> 1.87 us
    ppermute x56, waiting for transfers between devices: 73.3 us -> 80.3 us  [exchange(): return lax.ppermute(x, AXES, pairs)]
    pallas_call x4, Pallas kernels: 28.5 us -> 26.2 us  [expert(): pl.pallas_call(functools.partial(expert_kernel, blocks), in_specs=[whole(...]
  transfers between devices with their start and end apart: 58 -> 58, of which waited for: 26 -> 30; matrix products, arithmetic and copies ran while one was open for 7% -> 4% of each run, Pallas kernels for 18% -> 17%
where the time goes in v8:
time: 208 us; the launch traced here: 207 us
  waiting for transfers between devices  91.8 us (44%)
  starting transfers between devices  56 us (27%)
  Pallas kernels  39.4 us (19%)
  local copies, waits for them, and re-layouts  6.66 us (3%)
  matrix products  6.39 us (3%)
  other arithmetic  6.28 us (3%)
    ppermute x56, waiting for transfers between devices, exchange(): return lax.ppermute(x, AXES, pairs)  80.3 us
    ppermute x56, starting transfers between devices, exchange(): return lax.ppermute(x, AXES, pairs)  45.1 us
    pallas_call x4, Pallas kernels, expert(): pl.pallas_call(functools.partial(expert_kernel, blocks), in_specs=[whole(...  26.2 us
    all_to_all x1, starting transfers between devices, shards(): lax.all_to_all(payload, 'seq', split_axis=0, concat_axis=0, tiled=True)  7.29 us
    pallas_call x1, Pallas kernels, load(): pl.pallas_call(load_kernel, in_specs=[pl.BlockSpec(memory_space=pltpu.HBM...  7.06 us
    dot_general x1, matrix products, shards(): jnp.dot(attn_in, out_weight, preferred_element_type=F32).astype(BF16)  6.39 us
    pallas_call x4, Pallas kernels, call(): pl.pallas_call(kernel, in_specs=specs + [whole()] * (len(operands) - len(...  6.16 us
    all_to_all x1, waiting for transfers between devices, shards(): lax.all_to_all(payload, 'seq', split_axis=0, concat_axis=0, tiled=True)  6.01 us
  transfers between devices with their start and end apart: 58, of which 30 were waited for; matrix products, arithmetic and copies ran while one was open for 4% of the time, Pallas kernels for 17%

profile of v8, /device:TPU:0, one launch (start us, length us, event | category | flops | bytes accessed | tf_op | source)
XLA Modules:
  0.0 207.4 jit_solution(13915658894785384776)
XLA Ops:
  0.0 2.6 %shard_map.164 = bf16[8,144,128]{2,1,0:T(8,128)(2,1)} custom-call(s32[1]{0:T(128)} %bitcast.2.me_ref, f32[8,128]{1,0:T(8,128)} %bitcast.42, s32[1,128]{1,0:T(1,128)} %bitcast.44, s32[2,128]{1,0:T(2,128)} %bitcast.46, f32[2,128]{1,0:T(2,128)} %bitcast.47, bf16[128,1024]{1,0:T(8,128)(2,1)} %refs_4_.3, bf16[128,1024]{1,0:T(8,128)(2,1)} %refs_5_.1), custom_call_target="tpu_custom_call" | custom-call | tf_op jit(solution)/shard_map/pallas_call | solution.py:264
  2.6 7.3 %all-to-all-start = ((bf16[8,144,128]{2,1,0:T(8,128)(2,1)}), bf16[8,144,128]{2,1,0:T(8,128)(2,1)S(1)}, u32[]{:S(2)}, u32[]{:S(2)}) async-start(bf16[8,144,128]{2,1,0:T(8,128)(2,1)} %shard_map.164), calls=%async_computation | async-start | bytes 589824 | tf_op jit(solution)/shard_map/all_to_all | solution.py:317
  9.9 2.4 %shard_map.163 = (f32[128,1024]{1,0:T(8,128)S(1)}, bf16[128,1024]{1,0:T(8,128)(2,1)S(1)}) custom-call(f32[8,128]{1,0:T(8,128)} %bitcast.43, s32[1,128]{1,0:T(1,128)} %bitcast.45, bf16[128,1024]{1,0:T(8,128)(2,1)} %refs_2_.1, bf16[128,1024]{1,0:T(8,128)(2,1)} %refs_4_.3, bf16[128,1024]{1,0:T(8,128)(2,1)} %refs_5_.1), custom_call_target="tpu_custom_call" | custom-call | tf_op jit(solution)/shard_map/pallas_call | solution.py:264
  13.5 6.0 %all-to-all-done.in_ref = bf16[8,144,128]{2,1,0:T(8,128)(2,1)S(1)} async-done(((bf16[8,144,128]{2,1,0:T(8,128)(2,1)}), bf16[8,144,128]{2,1,0:T(8,128)(2,1)S(1)}, u32[]{:S(2)}, u32[]{:S(2)}) %all-to-all-start) | async-done | bytes 294944 | tf_op jit(solution)/shard_map/all_to_all | solution.py:317
  20.3 3.6 %all-to-all-start.1 = ((bf16[8,128,128]{2,1,0:T(8,128)(2,1)}), bf16[8,128,128]{2,1,0:T(8,128)(2,1)S(1)}, u32[]{:S(2)}, u32[]{:S(2)}) async-start(bf16[8,128,128]{2,1,0:T(8,128)(2,1)} %shard_map.165), calls=%async_computation.1 | async-start | bytes 524288 | tf_op jit(solution)/shard_map/all_to_all | solution.py:325
  26.9 5.5 %all-to-all-done.1.state_ref = bf16[8,128,128]{2,1,0:T(8,128)(2,1)S(1)} async-done(((bf16[8,128,128]{2,1,0:T(8,128)(2,1)}), bf16[8,128,128]{2,1,0:T(8,128)(2,1)S(1)}, u32[]{:S(2)}, u32[]{:S(2)}) %all-to-all-start.1) | async-done | bytes 262176 | tf_op jit(solution)/shard_map/all_to_all | solution.py:325
  32.8 6.4 %convolution_convert_fusion = bf16[128,6144]{1,0:T(8,128)(2,1)S(1)} fusion(bf16[128,1024]{1,0:T(8,128)(2,1)S(1)} %shard_map.166, bf16[1024,6144]{1,0:T(8,128)(2,1)} %param.23), kind=kOutput, calls=%fused_computation.4 | convolution fusion | flops 1611399168 | bytes 14417920 | tf_op jit(solution)/shard_map/dot_general | solution.py:359
  42.8 5.4 %collective-permute-done.1 = bf16[16,6144]{1,0:T(8,128)(2,1)S(1)} collective-permute-done((bf16[16,6144]{1,0:T(8,128)(2,1)S(1)}, bf16[16,6144]{1,0:T(8,128)(2,1)S(1)}, u32[]{:S(2)}, u32[]{:S(2)}) %collective-permute-start.1) | collective-permute-done | bytes 196640 | tf_op jit(solution)/shard_map/ppermute | solution.py:30
  50.2 7.1 %shard_map.167 = (bf16[576,6144]{1,0:T(8,128)(2,1)S(1)}, bf16[576,6144]{1,0:T(8,128)(2,1)S(1)}, bf16[576,6144]{1,0:T(8,128)(2,1)S(1)}, f32[8,128]{1,0:T(8,128)S(1)}) custom-call(bf16[1,576,6144]{2,1,0:T(8,128)(2,1)} %bitcast.36, bf16[1,576,6144]{2,1,0:T(8,128)(2,1)} %bitcast.37, bf16[1,576,6144]{2,1,0:T(8,128)(2,1)} %refs_2_.2), custom_call_target="tpu_custom_call" | custom-call | tf_op jit(solution)/shard_map/pallas_call | solution.py:208
  57.3 2.6 %collective-permute-done.3 = bf16[16,6144]{1,0:T(8,128)(2,1)S(1)} collective-permute-done((bf16[16,6144]{1,0:T(8,128)(2,1)S(1)}, bf16[16,6144]{1,0:T(8,128)(2,1)S(1)}, u32[]{:S(2)}, u32[]{:S(2)}) %collective-permute-start.3) | collective-permute-done | bytes 196640 | tf_op jit(solution)/shard_map/ppermute | solution.py:30
  63.3 4.7 %collective-permute-done.8 = bf16[16,6144]{1,0:T(8,128)(2,1)S(1)} collective-permute-done((bf16[16,6144]{1,0:T(8,128)(2,1)S(1)}, bf16[16,6144]{1,0:T(8,128)(2,1)S(1)}, u32[]{:S(2)}, u32[]{:S(2)}) %collective-permute-start.8) | collective-permute-done | bytes 196640 | tf_op jit(solution)/shard_map/ppermute | solution.py:30
  69.4 2.7 %collective-permute-done.7 = bf16[32,6144]{1,0:T(8,128)(2,1)S(1)} collective-permute-done((bf16[32,6144]{1,0:T(8,128)(2,1)S(1)}, bf16[32,6144]{1,0:T(8,128)(2,1)S(1)}, u32[]{:S(2)}, u32[]{:S(2)}) %collective-permute-start.7) | collective-permute-done | bytes 393248 | tf_op jit(solution)/shard_map/ppermute | solution.py:30
  76.4 6.2 %collective-permute-done.12 = bf16[16,6144]{1,0:T(8,128)(2,1)S(1)} collective-permute-done((bf16[16,6144]{1,0:T(8,128)(2,1)S(1)}, bf16[16,6144]{1,0:T(8,128)(2,1)S(1)}, u32[]{:S(2)}, u32[]{:S(2)}) %collective-permute-start.12) | collective-permute-done | bytes 196640 | tf_op jit(solution)/shard_map/ppermute | solution.py:30
  90.5 6.4 %shard_map.168 = (bf16[64,6144]{1,0:T(8,128)(2,1)S(1)}, bf16[64,6144]{1,0:T(8,128)(2,1)S(1)}, bf16[64,6144]{1,0:T(8,128)(2,1)S(1)}, bf16[64,6144]{1,0:T(8,128)(2,1)S(1)}) custom-call(bf16[64,6144]{1,0:T(8,128)(2,1)S(1)} %bitcast.33, bf16[64,6144]{1,0:T(8,128)(2,1)S(1)} %bitcast.35, bf16[64,6144]{1,0:T(8,128)(2,1)S(1)} %collective-permute-done.10.refs_2_, ...), custom_call_target="tpu_custom_call" | custom-call | flops 1000 | bytes 1000 | tf_op jit(solution)/shard_map/pallas_call | solution.py:244
  96.9 2.4 %collective-permute-done.15 = bf16[32,6144]{1,0:T(8,128)(2,1)S(1)} collective-permute-done((bf16[32,6144]{1,0:T(8,128)(2,1)S(1)}, bf16[32,6144]{1,0:T(8,128)(2,1)S(1)}, u32[]{:S(2)}, u32[]{:S(2)}) %collective-permute-start.15) | collective-permute-done | bytes 393248 | tf_op jit(solution)/shard_map/ppermute | solution.py:30
  105.8 6.6 %shard_map.169 = (bf16[64,6144]{1,0:T(8,128)(2,1)S(1)}, bf16[64,6144]{1,0:T(8,128)(2,1)S(1)}, bf16[64,6144]{1,0:T(8,128)(2,1)S(1)}, bf16[64,6144]{1,0:T(8,128)(2,1)S(1)}) custom-call(bf16[64,6144]{1,0:T(8,128)(2,1)S(1)} %constant_dynamic-update-slice_fusion.12.refs_0_, bf16[64,6144]{1,0:T(8,128)(2,1)S(1)} %collective-permute-done.13.refs_1_, ...), custom_call_target="tpu_custom_call" | custom-call | flops 1000 | bytes 1000 | tf_op jit(solution)/shard_map/pallas_call | solution.py:244
  120.2 6.4 %shard_map.170 = (bf16[64,6144]{1,0:T(8,128)(2,1)S(1)}, bf16[64,6144]{1,0:T(8,128)(2,1)S(1)}, bf16[64,6144]{1,0:T(8,128)(2,1)S(1)}, bf16[64,6144]{1,0:T(8,128)(2,1)S(1)}) custom-call(bf16[64,6144]{1,0:T(8,128)(2,1)S(1)} %constant_dynamic-update-slice_fusion.14.refs_0_, bf16[64,6144]{1,0:T(8,128)(2,1)S(1)} %collective-permute-done.18.refs_1_, ...), custom_call_target="tpu_custom_call" | custom-call | flops 1000 | bytes 1000 | tf_op jit(solution)/shard_map/pallas_call | solution.py:244
  126.6 4.0 %collective-permute-done.27 = bf16[32,6144]{1,0:T(8,128)(2,1)S(1)} collective-permute-done((bf16[32,6144]{1,0:T(8,128)(2,1)S(1)}, bf16[32,6144]{1,0:T(8,128)(2,1)S(1)}, u32[]{:S(2)}, u32[]{:S(2)}) %collective-permute-start.27) | collective-permute-done | bytes 393248 | tf_op jit(solution)/shard_map/ppermute | solution.py:30
  130.6 3.3 %collective-permute-done.26 = bf16[32,6144]{1,0:T(8,128)(2,1)S(1)} collective-permute-done((bf16[32,6144]{1,0:T(8,128)(2,1)S(1)}, bf16[32,6144]{1,0:T(8,128)(2,1)S(1)}, u32[]{:S(2)}, u32[]{:S(2)}) %collective-permute-start.26) | collective-permute-done | bytes 393248 | tf_op jit(solution)/shard_map/ppermute | solution.py:30
  137.4 6.7 %shard_map.171 = (bf16[64,6144]{1,0:T(8,128)(2,1)S(1)}, bf16[64,6144]{1,0:T(8,128)(2,1)S(1)}, bf16[64,6144]{1,0:T(8,128)(2,1)S(1)}, bf16[64,6144]{1,0:T(8,128)(2,1)S(1)}) custom-call(bf16[64,6144]{1,0:T(8,128)(2,1)S(1)} %constant_dynamic-update-slice_fusion.16.refs_0_, bf16[64,6144]{1,0:T(8,128)(2,1)S(1)} %constant_dynamic-update-slice_fusion.18.refs_1_, ...), custom_call_target="tpu_custom_call" | custom-call | flops 1000 | bytes 1000 | tf_op jit(solution)/shard_map/pallas_call | solution.py:244
  151.5 12.2 %collective-permute-done.40 = bf16[64,6144]{1,0:T(8,128)(2,1)S(1)} collective-permute-done((bf16[64,6144]{1,0:T(8,128)(2,1)S(1)}, bf16[64,6144]{1,0:T(8,128)(2,1)S(1)}, u32[]{:S(2)}, u32[]{:S(2)}) %collective-permute-start.40) | collective-permute-done | bytes 786464 | tf_op jit(solution)/shard_map/ppermute | solution.py:30
  168.7 8.8 %collective-permute-done.42 = bf16[32,6144]{1,0:T(8,128)(2,1)S(1)} collective-permute-done((bf16[32,6144]{1,0:T(8,128)(2,1)S(1)}, bf16[32,6144]{1,0:T(8,128)(2,1)S(1)}, u32[]{:S(2)}, u32[]{:S(2)}) %collective-permute-start.42) | collective-permute-done | bytes 393248 | tf_op jit(solution)/shard_map/ppermute | solution.py:30
  184.7 2.8 %collective-permute-done.47 = bf16[16,1536]{1,0:T(8,128)(2,1)S(1)} collective-permute-done((bf16[16,1536]{1,0:T(8,128)(2,1)S(1)}, bf16[16,1536]{1,0:T(8,128)(2,1)S(1)}, u32[]{:S(2)}, u32[]{:S(2)}) %collective-permute-start.47) | collective-permute-done | bytes 49184 | tf_op jit(solution)/shard_map/ppermute | solution.py:30
  200.7 4.9 %collective-permute-done.49 = bf16[16,1536]{1,0:T(8,128)(2,1)S(1)} collective-permute-done((bf16[16,1536]{1,0:T(8,128)(2,1)S(1)}, bf16[16,1536]{1,0:T(8,128)(2,1)S(1)}, u32[]{:S(2)}, u32[]{:S(2)}) %collective-permute-start.49) | collective-permute-done | bytes 49184 | tf_op jit(solution)/shard_map/ppermute | solution.py:30
  (219 shorter events, 79.4 us)
Async XLA Ops:
  2.6 16.9 %all-to-all-start = ((bf16[8,144,128]{2,1,0:T(8,128)(2,1)}), bf16[8,144,128]{2,1,0:T(8,128)(2,1)S(1)}, u32[]{:S(2)}, u32[]{:S(2)}) async-start(bf16[8,144,128]{2,1,0:T(8,128)(2,1)} %shard_map.164), calls=%async_computation | async-start | bytes 589824 | tf_op jit(solution)/shard_map/all_to_all | solution.py:317
  20.3 12.1 %all-to-all-start.1 = ((bf16[8,128,128]{2,1,0:T(8,128)(2,1)}), bf16[8,128,128]{2,1,0:T(8,128)(2,1)S(1)}, u32[]{:S(2)}, u32[]{:S(2)}) async-start(bf16[8,128,128]{2,1,0:T(8,128)(2,1)} %shard_map.165), calls=%async_computation.1 | async-start | bytes 524288 | tf_op jit(solution)/shard_map/all_to_all | solution.py:325
  48.6 11.3 %collective-permute-start.3 = (bf16[16,6144]{1,0:T(8,128)(2,1)S(1)}, bf16[16,6144]{1,0:T(8,128)(2,1)S(1)}, u32[]{:S(2)}, u32[]{:S(2)}) collective-permute-start(bf16[16,6144]{1,0:T(8,128)(2,1)S(1)} %multiply_convert_fusion.1), channel_id=1, source_target_pairs={{0,16},{1,17},{2,18},{3,19},{4,20},{5,21},{6,22},{7,23},{8,24},{9,... | collective-permute-start | bytes 589832 | tf_op jit(solution)/shard_map/ppermute | solution.py:30
  73.3 11.6 %collective-permute-start.10 = (bf16[64,6144]{1,0:T(8,128)(2,1)S(1)}, bf16[64,6144]{1,0:T(8,128)(2,1)S(1)}, u32[]{:S(2)}, u32[]{:S(2)}) collective-permute-start(bf16[64,6144]{1,0:T(8,128)(2,1)S(1)} %bitcast.32), channel_id=1, source_target_pairs={{0,1},{1,0},{2,3},{3,2},{4,5},{5,4},{6,7},{7,6},{8,9},{9,8},{10,11... | collective-permute-start | bytes 2359304 | tf_op jit(solution)/shard_map/ppermute | solution.py:30
  73.4 11.5 %collective-permute-start.9 = (bf16[32,6144]{1,0:T(8,128)(2,1)S(1)}, bf16[32,6144]{1,0:T(8,128)(2,1)S(1)}, u32[]{:S(2)}, u32[]{:S(2)}) collective-permute-start(bf16[32,6144]{1,0:T(8,128)(2,1)S(1)} %constant_dynamic-update-slice_fusion.10), channel_id=1, source_target_pairs={{0,2},{1,5},{2,0},{3,7},{4,6},{5,1},{6,4},{7,3},{8,10},{9,13},{10,... | collective-permute-start | bytes 1179656 | tf_op jit(solution)/shard_map/ppermute | solution.py:30
  85.6 16.3 %collective-permute-start.13 = (bf16[64,6144]{1,0:T(8,128)(2,1)S(1)}, bf16[64,6144]{1,0:T(8,128)(2,1)S(1)}, u32[]{:S(2)}, u32[]{:S(2)}) collective-permute-start(bf16[64,6144]{1,0:T(8,128)(2,1)S(1)} %constant_dynamic-update-slice_fusion.12.refs_0_), channel_id=1, source_target_pairs={{0,2},{1,5},{2,0},{3,7},{4,6},{5,1},{6,4},{7,3},{8,10},{9,13},{10,... | collective-permute-start | bytes 2359304 | tf_op jit(solution)/shard_map/ppermute | solution.py:30
  87.0 14.8 %collective-permute-start.14 = (bf16[64,6144]{1,0:T(8,128)(2,1)S(1)}, bf16[64,6144]{1,0:T(8,128)(2,1)S(1)}, u32[]{:S(2)}, u32[]{:S(2)}) collective-permute-start(bf16[64,6144]{1,0:T(8,128)(2,1)S(1)} %constant_dynamic-update-slice_fusion.12.refs_0_), channel_id=1, source_target_pairs={{0,1},{1,0},{2,3},{3,2},{4,5},{5,4},{6,7},{7,6},{8,9},{9,8},{10,11... | collective-permute-start | bytes 2359304 | tf_op jit(solution)/shard_map/ppermute | solution.py:30
  87.3 12.1 %collective-permute-start.15 = (bf16[32,6144]{1,0:T(8,128)(2,1)S(1)}, bf16[32,6144]{1,0:T(8,128)(2,1)S(1)}, u32[]{:S(2)}, u32[]{:S(2)}) collective-permute-start(bf16[32,6144]{1,0:T(8,128)(2,1)S(1)} %pad_maximum_fusion.3), channel_id=1, source_target_pairs={{0,4},{1,3},{2,6},{3,1},{4,0},{5,7},{6,2},{7,5},{8,12},{9,11},{10,... | collective-permute-start | bytes 1179656 | tf_op jit(solution)/shard_map/ppermute | solution.py:30
  102.4 13.0 %collective-permute-start.18 = (bf16[64,6144]{1,0:T(8,128)(2,1)S(1)}, bf16[64,6144]{1,0:T(8,128)(2,1)S(1)}, u32[]{:S(2)}, u32[]{:S(2)}) collective-permute-start(bf16[64,6144]{1,0:T(8,128)(2,1)S(1)} %constant_dynamic-update-slice_fusion.14.refs_0_), channel_id=1, source_target_pairs={{0,2},{1,5},{2,0},{3,7},{4,6},{5,1},{6,4},{7,3},{8,10},{9,13},{10,... | collective-permute-start | bytes 2359304 | tf_op jit(solution)/shard_map/ppermute | solution.py:30
  103.9 11.5 %collective-permute-start.19 = (bf16[64,6144]{1,0:T(8,128)(2,1)S(1)}, bf16[64,6144]{1,0:T(8,128)(2,1)S(1)}, u32[]{:S(2)}, u32[]{:S(2)}) collective-permute-start(bf16[64,6144]{1,0:T(8,128)(2,1)S(1)} %constant_dynamic-update-slice_fusion.14.refs_0_), channel_id=1, source_target_pairs={{0,1},{1,0},{2,3},{3,2},{4,5},{5,4},{6,7},{7,6},{8,9},{9,8},{10,11... | collective-permute-start | bytes 2359304 | tf_op jit(solution)/shard_map/ppermute | solution.py:30
  103.9 11.5 %collective-permute-start.20 = (bf16[32,6144]{1,0:T(8,128)(2,1)S(1)}, bf16[32,6144]{1,0:T(8,128)(2,1)S(1)}, u32[]{:S(2)}, u32[]{:S(2)}) collective-permute-start(bf16[32,6144]{1,0:T(8,128)(2,1)S(1)} %collective-permute-done.15), channel_id=1, source_target_pairs={{0,8},{1,9},{2,10},{3,11},{4,12},{5,13},{6,14},{7,15},{8,0},{9,1},... | collective-permute-start | bytes 1179656 | tf_op jit(solution)/shard_map/ppermute | solution.py:30
  117.4 16.5 %collective-permute-start.28 = (bf16[64,6144]{1,0:T(8,128)(2,1)S(1)}, bf16[64,6144]{1,0:T(8,128)(2,1)S(1)}, u32[]{:S(2)}, u32[]{:S(2)}) collective-permute-start(bf16[64,6144]{1,0:T(8,128)(2,1)S(1)} %constant_dynamic-update-slice_fusion.16.refs_0_), channel_id=1, source_target_pairs={{0,1},{1,0},{2,3},{3,2},{4,5},{5,4},{6,7},{7,6},{8,9},{9,8},{10,11... | collective-permute-start | bytes 2359304 | tf_op jit(solution)/shard_map/ppermute | solution.py:30
  117.7 16.2 %collective-permute-start.29 = (bf16[64,6144]{1,0:T(8,128)(2,1)S(1)}, bf16[64,6144]{1,0:T(8,128)(2,1)S(1)}, u32[]{:S(2)}, u32[]{:S(2)}) collective-permute-start(bf16[64,6144]{1,0:T(8,128)(2,1)S(1)} %add_convert_fusion.2), channel_id=1, source_target_pairs={{0,2},{1,5},{2,0},{3,7},{4,6},{5,1},{6,4},{7,3},{8,10},{9,13},{10,... | collective-permute-start | bytes 2359304 | tf_op jit(solution)/shard_map/ppermute | solution.py:30
  119.1 11.5 %collective-permute-start.27 = (bf16[32,6144]{1,0:T(8,128)(2,1)S(1)}, bf16[32,6144]{1,0:T(8,128)(2,1)S(1)}, u32[]{:S(2)}, u32[]{:S(2)}) collective-permute-start(bf16[32,6144]{1,0:T(8,128)(2,1)S(1)} %slice.163), channel_id=1, source_target_pairs={{0,8},{1,9},{2,10},{3,11},{4,12},{5,13},{6,14},{7,15},{8,0},{9,1},... | collective-permute-start | bytes 1179656 | tf_op jit(solution)/shard_map/ppermute | solution.py:30
  119.4 14.6 %collective-permute-start.26 = (bf16[32,6144]{1,0:T(8,128)(2,1)S(1)}, bf16[32,6144]{1,0:T(8,128)(2,1)S(1)}, u32[]{:S(2)}, u32[]{:S(2)}) collective-permute-start(bf16[32,6144]{1,0:T(8,128)(2,1)S(1)} %collective-permute-done.16), channel_id=1, source_target_pairs={{0,2},{1,5},{2,0},{3,7},{4,6},{5,1},{6,4},{7,3},{8,10},{9,13},{10,... | collective-permute-start | bytes 1179656 | tf_op jit(solution)/shard_map/ppermute | solution.py:30
  134.7 11.9 %collective-permute-start.31 = (bf16[32,6144]{1,0:T(8,128)(2,1)S(1)}, bf16[32,6144]{1,0:T(8,128)(2,1)S(1)}, u32[]{:S(2)}, u32[]{:S(2)}) collective-permute-start(bf16[32,6144]{1,0:T(8,128)(2,1)S(1)} %add_convert_fusion.8), channel_id=1, source_target_pairs={{0,8},{1,9},{2,10},{3,11},{4,12},{5,13},{6,14},{7,15},{8,0},{9,1},... | collective-permute-start | bytes 1179656 | tf_op jit(solution)/shard_map/ppermute | solution.py:30
  135.1 12.0 %collective-permute-start.32 = (bf16[64,6144]{1,0:T(8,128)(2,1)S(1)}, bf16[64,6144]{1,0:T(8,128)(2,1)S(1)}, u32[]{:S(2)}, u32[]{:S(2)}) collective-permute-start(bf16[64,6144]{1,0:T(8,128)(2,1)S(1)} %add_convert_fusion.3), channel_id=1, source_target_pairs={{0,2},{1,5},{2,0},{3,7},{4,6},{5,1},{6,4},{7,3},{8,10},{9,13},{10,... | collective-permute-start | bytes 2359304 | tf_op jit(solution)/shard_map/ppermute | solution.py:30
  147.5 16.2 %collective-permute-start.40 = (bf16[64,6144]{1,0:T(8,128)(2,1)S(1)}, bf16[64,6144]{1,0:T(8,128)(2,1)S(1)}, u32[]{:S(2)}, u32[]{:S(2)}) collective-permute-start(bf16[64,6144]{1,0:T(8,128)(2,1)S(1)} %add_convert_fusion.1), channel_id=1, source_target_pairs={{0,2},{1,5},{2,0},{3,7},{4,6},{5,1},{6,4},{7,3},{8,10},{9,13},{10,... | collective-permute-start | bytes 2359304 | tf_op jit(solution)/shard_map/ppermute | solution.py:30
  149.2 14.8 %collective-permute-start.39 = (bf16[32,6144]{1,0:T(8,128)(2,1)S(1)}, bf16[32,6144]{1,0:T(8,128)(2,1)S(1)}, u32[]{:S(2)}, u32[]{:S(2)}) collective-permute-start(bf16[32,6144]{1,0:T(8,128)(2,1)S(1)} %get-tuple-element.261), channel_id=1, source_target_pairs={{0,4},{1,3},{2,6},{3,1},{4,0},{5,7},{6,2},{7,5},{8,12},{9,11},{10,... | collective-permute-start | bytes 1179656 | tf_op jit(solution)/shard_map/ppermute | solution.py:30
  150.5 13.5 %collective-permute-start.38 = (bf16[32,6144]{1,0:T(8,128)(2,1)S(1)}, bf16[32,6144]{1,0:T(8,128)(2,1)S(1)}, u32[]{:S(2)}, u32[]{:S(2)}) collective-permute-start(bf16[32,6144]{1,0:T(8,128)(2,1)S(1)} %convert_add_fusion.3), channel_id=1, source_target_pairs={{0,8},{1,9},{2,10},{3,11},{4,12},{5,13},{6,14},{7,15},{8,0},{9,1},... | collective-permute-start | bytes 1179656 | tf_op jit(solution)/shard_map/ppermute | solution.py:30
  164.0 16.0 %collective-permute-start.43 = (bf16[64,6144]{1,0:T(8,128)(2,1)S(1)}, bf16[64,6144]{1,0:T(8,128)(2,1)S(1)}, u32[]{:S(2)}, u32[]{:S(2)}) collective-permute-start(bf16[64,6144]{1,0:T(8,128)(2,1)S(1)} %add_convert_fusion), channel_id=1, source_target_pairs={{0,2},{1,5},{2,0},{3,7},{4,6},{5,1},{6,4},{7,3},{8,10},{9,13},{10,... | collective-permute-start | bytes 2359304 | tf_op jit(solution)/shard_map/ppermute | solution.py:30
  165.5 12.1 %collective-permute-start.42 = (bf16[32,6144]{1,0:T(8,128)(2,1)S(1)}, bf16[32,6144]{1,0:T(8,128)(2,1)S(1)}, u32[]{:S(2)}, u32[]{:S(2)}) collective-permute-start(bf16[32,6144]{1,0:T(8,128)(2,1)S(1)} %get-tuple-element.232), channel_id=1, source_target_pairs={{0,4},{1,3},{2,6},{3,1},{4,0},{5,7},{6,2},{7,5},{8,12},{9,11},{10,... | collective-permute-start | bytes 1179656 | tf_op jit(solution)/shard_map/ppermute | solution.py:30
  166.8 13.6 %collective-permute-start.41 = (bf16[16,6144]{1,0:T(8,128)(2,1)S(1)}, bf16[16,6144]{1,0:T(8,128)(2,1)S(1)}, u32[]{:S(2)}, u32[]{:S(2)}) collective-permute-start(bf16[16,6144]{1,0:T(8,128)(2,1)S(1)} %get-tuple-element.266), channel_id=1, source_target_pairs={{0,16},{1,17},{2,18},{3,19},{4,20},{5,21},{6,22},{7,23},{8,24},{9,... | collective-permute-start | bytes 589832 | tf_op jit(solution)/shard_map/ppermute | solution.py:30
  194.9 11.6 %collective-permute-start.54 = (bf16[16,1536]{1,0:T(8,128)(2,1)S(1)}, bf16[16,1536]{1,0:T(8,128)(2,1)S(1)}, u32[]{:S(2)}, u32[]{:S(2)}) collective-permute-start(bf16[16,1536]{1,0:T(8,128)(2,1)S(1)} %get-tuple-element.270), channel_id=1, source_target_pairs={{0,19},{1,18},{2,17},{3,16},{4,23},{5,22},{6,21},{7,20},{8,27},{9,... | collective-permute-start | bytes 147464 | tf_op jit(solution)/shard_map/ppermute | solution.py:30
  (50 other events, 380.8 us)

commit v9 on v8

--- a/solution.py
+++ b/solution.py
@@ -494,16 +494,21 @@
     b2_got = exchange(b2_send, last, count)
     b2_parts = fold_sums(b2_rest + [b2_got])
     a_z, a1_sum, b2_parts, b1_send = wait((a_z, a1_sum, b2_parts, b1_send))
-    b1_got = exchange(b1_send, last, count)
-    b1_parts = fold_sums(b1_rest + [b1_got])
+    half = b1_send.shape[0] // 2
+    b1_got = exchange(b1_send[half:], last, count)
+    b1_sent = total([t[half:] for t in b1_rest] + [b1_got]).astype(BF16)
+    b1_stays = [b1_send[:half], total([t[:half] for t in b1_rest])]
     a_sum = a1_sum + [a_z]
     a_z = z_step(total([t[half_count:] for t in a_sum]).astype(BF16), z_masks[0])
     a_sum = total([t[:half_count] for t in a_sum])
     b2_sum = total(fold(*b2_parts, steps)).astype(BF16)
-    a_z, a_sum, b2_sum, b1_parts, place = wait((a_z, a_sum, b2_sum, b1_parts, hx_index))
+    a_z, a_sum, b2_sum, b1_sent, b1_stays, place = wait((a_z, a_sum, b2_sum, b1_sent, b1_stays, hx_index))
     b_z = z_step(b2_sum, z_masks[1])
-    b1_sum = fold(*b1_parts, steps)
-    a_out = deliver(total([hidden_a, a_sum, a_z]).astype(BF16), None, place)
+    b1_got = exchange(b1_stays[0], last, count)
+    a_out = total([hidden_a, a_sum, a_z]).astype(BF16)
+    b1_got, a_out = wait((b1_got, a_out))
+    b1_sum = fold(total([b1_stays[1], b1_got]), b1_sent, steps)
+    a_out = deliver(a_out, None, place)
     b_z, b1_sum, a_out = wait((b_z, b1_sum, a_out))
     b_sum = b1_sum + [b_z]
     across = total([t[half_count:] for t in b_sum]).astype(BF16)

time: 208 us -> 211 us (1.014)
    ppermute x56 -> x57, waiting for transfers between devices: 80.3 us -> 81.7 us  [exchange(): return lax.ppermute(x, AXES, pairs)]
    ppermute x56 -> x57, starting transfers between devices: 45.1 us -> 45.3 us  [exchange(): return lax.ppermute(x, AXES, pairs)]
  transfers between devices with their start and end apart: 58 -> 59, of which waited for: 30 -> 30; matrix products, arithmetic and copies ran while one was open for 4% -> 5% of each run, Pallas kernels for 17% -> 17%
where the time goes in v9:
time: 211 us; the launch traced here: 210 us
  waiting for transfers between devices  93.2 us (44%)
  starting transfers between devices  56.2 us (27%)
  Pallas kernels  39.4 us (19%)
  local copies, waits for them, and re-layouts  7.65 us (4%)
  matrix products  6.41 us (3%)
  other arithmetic  6.33 us (3%)
    ppermute x57, waiting for transfers between devices, exchange(): return lax.ppermute(x, AXES, pairs)  81.7 us
    ppermute x57, starting transfers between devices, exchange(): return lax.ppermute(x, AXES, pairs)  45.3 us
    pallas_call x4, Pallas kernels, expert(): pl.pallas_call(functools.partial(expert_kernel, blocks), in_specs=[whole(...  26.2 us
    all_to_all x1, starting transfers between devices, shards(): lax.all_to_all(payload, 'seq', split_axis=0, concat_axis=0, tiled=True)  7.29 us
    pallas_call x1, Pallas kernels, load(): pl.pallas_call(load_kernel, in_specs=[pl.BlockSpec(memory_space=pltpu.HBM...  7.06 us
    dot_general x1, matrix products, shards(): jnp.dot(attn_in, out_weight, preferred_element_type=F32).astype(BF16)  6.41 us
    pallas_call x4, Pallas kernels, call(): pl.pallas_call(kernel, in_specs=specs + [whole()] * (len(operands) - len(...  6.12 us
    all_to_all x1, waiting for transfers between devices, shards(): lax.all_to_all(payload, 'seq', split_axis=0, concat_axis=0, tiled=True)  6.01 us
  transfers between devices with their start and end apart: 59, of which 30 were waited for; matrix products, arithmetic and copies ran while one was open for 5% of the time, Pallas kernels for 17%

profile of v9, /device:TPU:0, one launch (start us, length us, event | category | flops | bytes accessed | tf_op | source)
XLA Modules:
  0.0 210.2 jit_solution(1678279022853592347)
XLA Ops:
  0.0 2.6 %shard_map.164 = bf16[8,144,128]{2,1,0:T(8,128)(2,1)} custom-call(s32[1]{0:T(128)} %bitcast.2.me_ref, f32[8,128]{1,0:T(8,128)} %bitcast.42, s32[1,128]{1,0:T(1,128)} %bitcast.44, s32[2,128]{1,0:T(2,128)} %bitcast.46, f32[2,128]{1,0:T(2,128)} %bitcast.47, bf16[128,1024]{1,0:T(8,128)(2,1)} %refs_4_.3, bf16[128,1024]{1,0:T(8,128)(2,1)} %refs_5_.1), custom_call_target="tpu_custom_call" | custom-call | tf_op jit(solution)/shard_map/pallas_call | solution.py:264
  2.6 7.3 %all-to-all-start = ((bf16[8,144,128]{2,1,0:T(8,128)(2,1)}), bf16[8,144,128]{2,1,0:T(8,128)(2,1)S(1)}, u32[]{:S(2)}, u32[]{:S(2)}) async-start(bf16[8,144,128]{2,1,0:T(8,128)(2,1)} %shard_map.164), calls=%async_computation | async-start | bytes 589824 | tf_op jit(solution)/shard_map/all_to_all | solution.py:317
  9.9 2.4 %shard_map.163 = (f32[128,1024]{1,0:T(8,128)S(1)}, bf16[128,1024]{1,0:T(8,128)(2,1)S(1)}) custom-call(f32[8,128]{1,0:T(8,128)} %bitcast.43, s32[1,128]{1,0:T(1,128)} %bitcast.45, bf16[128,1024]{1,0:T(8,128)(2,1)} %refs_2_.1, bf16[128,1024]{1,0:T(8,128)(2,1)} %refs_4_.3, bf16[128,1024]{1,0:T(8,128)(2,1)} %refs_5_.1), custom_call_target="tpu_custom_call" | custom-call | tf_op jit(solution)/shard_map/pallas_call | solution.py:264
  13.5 6.0 %all-to-all-done.in_ref = bf16[8,144,128]{2,1,0:T(8,128)(2,1)S(1)} async-done(((bf16[8,144,128]{2,1,0:T(8,128)(2,1)}), bf16[8,144,128]{2,1,0:T(8,128)(2,1)S(1)}, u32[]{:S(2)}, u32[]{:S(2)}) %all-to-all-start) | async-done | bytes 294944 | tf_op jit(solution)/shard_map/all_to_all | solution.py:317
  20.3 3.6 %all-to-all-start.1 = ((bf16[8,128,128]{2,1,0:T(8,128)(2,1)}), bf16[8,128,128]{2,1,0:T(8,128)(2,1)S(1)}, u32[]{:S(2)}, u32[]{:S(2)}) async-start(bf16[8,128,128]{2,1,0:T(8,128)(2,1)} %shard_map.165), calls=%async_computation.1 | async-start | bytes 524288 | tf_op jit(solution)/shard_map/all_to_all | solution.py:325
  26.9 5.5 %all-to-all-done.1.state_ref = bf16[8,128,128]{2,1,0:T(8,128)(2,1)S(1)} async-done(((bf16[8,128,128]{2,1,0:T(8,128)(2,1)}), bf16[8,128,128]{2,1,0:T(8,128)(2,1)S(1)}, u32[]{:S(2)}, u32[]{:S(2)}) %all-to-all-start.1) | async-done | bytes 262176 | tf_op jit(solution)/shard_map/all_to_all | solution.py:325
  32.8 6.4 %convolution_convert_fusion = bf16[128,6144]{1,0:T(8,128)(2,1)S(1)} fusion(bf16[128,1024]{1,0:T(8,128)(2,1)S(1)} %shard_map.166, bf16[1024,6144]{1,0:T(8,128)(2,1)} %param.23), kind=kOutput, calls=%fused_computation.4 | convolution fusion | flops 1611399168 | bytes 14417920 | tf_op jit(solution)/shard_map/dot_general | solution.py:359
  42.8 5.4 %collective-permute-done.1 = bf16[16,6144]{1,0:T(8,128)(2,1)S(1)} collective-permute-done((bf16[16,6144]{1,0:T(8,128)(2,1)S(1)}, bf16[16,6144]{1,0:T(8,128)(2,1)S(1)}, u32[]{:S(2)}, u32[]{:S(2)}) %collective-permute-start.1) | collective-permute-done | bytes 196640 | tf_op jit(solution)/shard_map/ppermute | solution.py:30
  50.2 7.1 %shard_map.167 = (bf16[576,6144]{1,0:T(8,128)(2,1)S(1)}, bf16[576,6144]{1,0:T(8,128)(2,1)S(1)}, bf16[576,6144]{1,0:T(8,128)(2,1)S(1)}, f32[8,128]{1,0:T(8,128)S(1)}) custom-call(bf16[1,576,6144]{2,1,0:T(8,128)(2,1)} %bitcast.36, bf16[1,576,6144]{2,1,0:T(8,128)(2,1)} %bitcast.37, bf16[1,576,6144]{2,1,0:T(8,128)(2,1)} %refs_2_.2), custom_call_target="tpu_custom_call" | custom-call | tf_op jit(solution)/shard_map/pallas_call | solution.py:208
  57.3 2.6 %collective-permute-done.3 = bf16[16,6144]{1,0:T(8,128)(2,1)S(1)} collective-permute-done((bf16[16,6144]{1,0:T(8,128)(2,1)S(1)}, bf16[16,6144]{1,0:T(8,128)(2,1)S(1)}, u32[]{:S(2)}, u32[]{:S(2)}) %collective-permute-start.3) | collective-permute-done | bytes 196640 | tf_op jit(solution)/shard_map/ppermute | solution.py:30
  63.2 4.7 %collective-permute-done.8 = bf16[16,6144]{1,0:T(8,128)(2,1)S(1)} collective-permute-done((bf16[16,6144]{1,0:T(8,128)(2,1)S(1)}, bf16[16,6144]{1,0:T(8,128)(2,1)S(1)}, u32[]{:S(2)}, u32[]{:S(2)}) %collective-permute-start.8) | collective-permute-done | bytes 196640 | tf_op jit(solution)/shard_map/ppermute | solution.py:30
  69.4 2.7 %collective-permute-done.7 = bf16[32,6144]{1,0:T(8,128)(2,1)S(1)} collective-permute-done((bf16[32,6144]{1,0:T(8,128)(2,1)S(1)}, bf16[32,6144]{1,0:T(8,128)(2,1)S(1)}, u32[]{:S(2)}, u32[]{:S(2)}) %collective-permute-start.7) | collective-permute-done | bytes 393248 | tf_op jit(solution)/shard_map/ppermute | solution.py:30
  76.4 6.1 %collective-permute-done.12 = bf16[16,6144]{1,0:T(8,128)(2,1)S(1)} collective-permute-done((bf16[16,6144]{1,0:T(8,128)(2,1)S(1)}, bf16[16,6144]{1,0:T(8,128)(2,1)S(1)}, u32[]{:S(2)}, u32[]{:S(2)}) %collective-permute-start.12) | collective-permute-done | bytes 196640 | tf_op jit(solution)/shard_map/ppermute | solution.py:30
  82.5 2.4 %collective-permute-done.9 = bf16[32,6144]{1,0:T(8,128)(2,1)S(1)} collective-permute-done((bf16[32,6144]{1,0:T(8,128)(2,1)S(1)}, bf16[32,6144]{1,0:T(8,128)(2,1)S(1)}, u32[]{:S(2)}, u32[]{:S(2)}) %collective-permute-start.9) | collective-permute-done | bytes 393248 | tf_op jit(solution)/shard_map/ppermute | solution.py:30
  90.5 6.4 %shard_map.168 = (bf16[64,6144]{1,0:T(8,128)(2,1)S(1)}, bf16[64,6144]{1,0:T(8,128)(2,1)S(1)}, bf16[64,6144]{1,0:T(8,128)(2,1)S(1)}, bf16[64,6144]{1,0:T(8,128)(2,1)S(1)}) custom-call(bf16[64,6144]{1,0:T(8,128)(2,1)S(1)} %bitcast.33, bf16[64,6144]{1,0:T(8,128)(2,1)S(1)} %bitcast.35, bf16[64,6144]{1,0:T(8,128)(2,1)S(1)} %collective-permute-done.10.refs_2_, ...), custom_call_target="tpu_custom_call" | custom-call | flops 1000 | bytes 1000 | tf_op jit(solution)/shard_map/pallas_call | solution.py:244
  105.8 6.7 %shard_map.169 = (bf16[64,6144]{1,0:T(8,128)(2,1)S(1)}, bf16[64,6144]{1,0:T(8,128)(2,1)S(1)}, bf16[64,6144]{1,0:T(8,128)(2,1)S(1)}, bf16[64,6144]{1,0:T(8,128)(2,1)S(1)}) custom-call(bf16[64,6144]{1,0:T(8,128)(2,1)S(1)} %constant_dynamic-update-slice_fusion.12.refs_0_, bf16[64,6144]{1,0:T(8,128)(2,1)S(1)} %collective-permute-done.13.refs_1_, ...), custom_call_target="tpu_custom_call" | custom-call | flops 1000 | bytes 1000 | tf_op jit(solution)/shard_map/pallas_call | solution.py:244
  120.2 6.4 %shard_map.170 = (bf16[64,6144]{1,0:T(8,128)(2,1)S(1)}, bf16[64,6144]{1,0:T(8,128)(2,1)S(1)}, bf16[64,6144]{1,0:T(8,128)(2,1)S(1)}, bf16[64,6144]{1,0:T(8,128)(2,1)S(1)}) custom-call(bf16[64,6144]{1,0:T(8,128)(2,1)S(1)} %constant_dynamic-update-slice_fusion.14.refs_0_, bf16[64,6144]{1,0:T(8,128)(2,1)S(1)} %collective-permute-done.18.refs_1_, ...), custom_call_target="tpu_custom_call" | custom-call | flops 1000 | bytes 1000 | tf_op jit(solution)/shard_map/pallas_call | solution.py:244
  126.6 4.0 %collective-permute-done.27 = bf16[32,6144]{1,0:T(8,128)(2,1)S(1)} collective-permute-done((bf16[32,6144]{1,0:T(8,128)(2,1)S(1)}, bf16[32,6144]{1,0:T(8,128)(2,1)S(1)}, u32[]{:S(2)}, u32[]{:S(2)}) %collective-permute-start.27) | collective-permute-done | bytes 393248 | tf_op jit(solution)/shard_map/ppermute | solution.py:30
  130.6 3.3 %collective-permute-done.26 = bf16[32,6144]{1,0:T(8,128)(2,1)S(1)} collective-permute-done((bf16[32,6144]{1,0:T(8,128)(2,1)S(1)}, bf16[32,6144]{1,0:T(8,128)(2,1)S(1)}, u32[]{:S(2)}, u32[]{:S(2)}) %collective-permute-start.26) | collective-permute-done | bytes 393248 | tf_op jit(solution)/shard_map/ppermute | solution.py:30
  137.4 6.7 %shard_map.171 = (bf16[64,6144]{1,0:T(8,128)(2,1)S(1)}, bf16[64,6144]{1,0:T(8,128)(2,1)S(1)}, bf16[64,6144]{1,0:T(8,128)(2,1)S(1)}, bf16[64,6144]{1,0:T(8,128)(2,1)S(1)}) custom-call(bf16[64,6144]{1,0:T(8,128)(2,1)S(1)} %constant_dynamic-update-slice_fusion.16.refs_0_, bf16[64,6144]{1,0:T(8,128)(2,1)S(1)} %constant_dynamic-update-slice_fusion.18.refs_1_, ...), custom_call_target="tpu_custom_call" | custom-call | flops 1000 | bytes 1000 | tf_op jit(solution)/shard_map/pallas_call | solution.py:244
  151.5 12.2 %collective-permute-done.40 = bf16[64,6144]{1,0:T(8,128)(2,1)S(1)} collective-permute-done((bf16[64,6144]{1,0:T(8,128)(2,1)S(1)}, bf16[64,6144]{1,0:T(8,128)(2,1)S(1)}, u32[]{:S(2)}, u32[]{:S(2)}) %collective-permute-start.40) | collective-permute-done | bytes 786464 | tf_op jit(solution)/shard_map/ppermute | solution.py:30
  169.4 7.2 %collective-permute-done.43 = bf16[32,6144]{1,0:T(8,128)(2,1)S(1)} collective-permute-done((bf16[32,6144]{1,0:T(8,128)(2,1)S(1)}, bf16[32,6144]{1,0:T(8,128)(2,1)S(1)}, u32[]{:S(2)}, u32[]{:S(2)}) %collective-permute-start.43) | collective-permute-done | bytes 393248 | tf_op jit(solution)/shard_map/ppermute | solution.py:30
  181.1 8.9 %collective-permute-done.45 = bf16[32,6144]{1,0:T(8,128)(2,1)} collective-permute-done((bf16[32,6144]{1,0:T(8,128)(2,1)}, bf16[32,6144]{1,0:T(8,128)(2,1)}, u32[]{:S(2)}, u32[]{:S(2)}) %collective-permute-start.45) | collective-permute-done | bytes 393248 | tf_op jit(solution)/shard_map/ppermute | solution.py:30
  204.8 4.3 %collective-permute-done.50 = bf16[16,1536]{1,0:T(8,128)(2,1)S(1)} collective-permute-done((bf16[16,1536]{1,0:T(8,128)(2,1)S(1)}, bf16[16,1536]{1,0:T(8,128)(2,1)S(1)}, u32[]{:S(2)}, u32[]{:S(2)}) %collective-permute-start.50) | collective-permute-done | bytes 49184 | tf_op jit(solution)/shard_map/ppermute | solution.py:30
  (223 shorter events, 78.2 us)
Async XLA Ops:
  2.6 16.9 %all-to-all-start = ((bf16[8,144,128]{2,1,0:T(8,128)(2,1)}), bf16[8,144,128]{2,1,0:T(8,128)(2,1)S(1)}, u32[]{:S(2)}, u32[]{:S(2)}) async-start(bf16[8,144,128]{2,1,0:T(8,128)(2,1)} %shard_map.164), calls=%async_computation | async-start | bytes 589824 | tf_op jit(solution)/shard_map/all_to_all | solution.py:317
  20.3 12.1 %all-to-all-start.1 = ((bf16[8,128,128]{2,1,0:T(8,128)(2,1)}), bf16[8,128,128]{2,1,0:T(8,128)(2,1)S(1)}, u32[]{:S(2)}, u32[]{:S(2)}) async-start(bf16[8,128,128]{2,1,0:T(8,128)(2,1)} %shard_map.165), calls=%async_computation.1 | async-start | bytes 524288 | tf_op jit(solution)/shard_map/all_to_all | solution.py:325
  48.6 11.3 %collective-permute-start.3 = (bf16[16,6144]{1,0:T(8,128)(2,1)S(1)}, bf16[16,6144]{1,0:T(8,128)(2,1)S(1)}, u32[]{:S(2)}, u32[]{:S(2)}) collective-permute-start(bf16[16,6144]{1,0:T(8,128)(2,1)S(1)} %multiply_convert_fusion.1), channel_id=1, source_target_pairs={{0,16},{1,17},{2,18},{3,19},{4,20},{5,21},{6,22},{7,23},{8,24},{9,... | collective-permute-start | bytes 589832 | tf_op jit(solution)/shard_map/ppermute | solution.py:30
  73.3 11.6 %collective-permute-start.10 = (bf16[64,6144]{1,0:T(8,128)(2,1)S(1)}, bf16[64,6144]{1,0:T(8,128)(2,1)S(1)}, u32[]{:S(2)}, u32[]{:S(2)}) collective-permute-start(bf16[64,6144]{1,0:T(8,128)(2,1)S(1)} %bitcast.32), channel_id=1, source_target_pairs={{0,1},{1,0},{2,3},{3,2},{4,5},{5,4},{6,7},{7,6},{8,9},{9,8},{10,11... | collective-permute-start | bytes 2359304 | tf_op jit(solution)/shard_map/ppermute | solution.py:30
  73.4 11.5 %collective-permute-start.9 = (bf16[32,6144]{1,0:T(8,128)(2,1)S(1)}, bf16[32,6144]{1,0:T(8,128)(2,1)S(1)}, u32[]{:S(2)}, u32[]{:S(2)}) collective-permute-start(bf16[32,6144]{1,0:T(8,128)(2,1)S(1)} %constant_dynamic-update-slice_fusion.10), channel_id=1, source_target_pairs={{0,2},{1,5},{2,0},{3,7},{4,6},{5,1},{6,4},{7,3},{8,10},{9,13},{10,... | collective-permute-start | bytes 1179656 | tf_op jit(solution)/shard_map/ppermute | solution.py:30
  85.5 16.3 %collective-permute-start.13 = (bf16[64,6144]{1,0:T(8,128)(2,1)S(1)}, bf16[64,6144]{1,0:T(8,128)(2,1)S(1)}, u32[]{:S(2)}, u32[]{:S(2)}) collective-permute-start(bf16[64,6144]{1,0:T(8,128)(2,1)S(1)} %constant_dynamic-update-slice_fusion.12.refs_0_), channel_id=1, source_target_pairs={{0,2},{1,5},{2,0},{3,7},{4,6},{5,1},{6,4},{7,3},{8,10},{9,13},{10,... | collective-permute-start | bytes 2359304 | tf_op jit(solution)/shard_map/ppermute | solution.py:30
  87.0 14.8 %collective-permute-start.14 = (bf16[64,6144]{1,0:T(8,128)(2,1)S(1)}, bf16[64,6144]{1,0:T(8,128)(2,1)S(1)}, u32[]{:S(2)}, u32[]{:S(2)}) collective-permute-start(bf16[64,6144]{1,0:T(8,128)(2,1)S(1)} %constant_dynamic-update-slice_fusion.12.refs_0_), channel_id=1, source_target_pairs={{0,1},{1,0},{2,3},{3,2},{4,5},{5,4},{6,7},{7,6},{8,9},{9,8},{10,11... | collective-permute-start | bytes 2359304 | tf_op jit(solution)/shard_map/ppermute | solution.py:30
  87.2 12.1 %collective-permute-start.15 = (bf16[32,6144]{1,0:T(8,128)(2,1)S(1)}, bf16[32,6144]{1,0:T(8,128)(2,1)S(1)}, u32[]{:S(2)}, u32[]{:S(2)}) collective-permute-start(bf16[32,6144]{1,0:T(8,128)(2,1)S(1)} %pad_maximum_fusion.3), channel_id=1, source_target_pairs={{0,4},{1,3},{2,6},{3,1},{4,0},{5,7},{6,2},{7,5},{8,12},{9,11},{10,... | collective-permute-start | bytes 1179656 | tf_op jit(solution)/shard_map/ppermute | solution.py:30
  102.4 13.0 %collective-permute-start.18 = (bf16[64,6144]{1,0:T(8,128)(2,1)S(1)}, bf16[64,6144]{1,0:T(8,128)(2,1)S(1)}, u32[]{:S(2)}, u32[]{:S(2)}) collective-permute-start(bf16[64,6144]{1,0:T(8,128)(2,1)S(1)} %constant_dynamic-update-slice_fusion.14.refs_0_), channel_id=1, source_target_pairs={{0,2},{1,5},{2,0},{3,7},{4,6},{5,1},{6,4},{7,3},{8,10},{9,13},{10,... | collective-permute-start | bytes 2359304 | tf_op jit(solution)/shard_map/ppermute | solution.py:30
  103.8 11.5 %collective-permute-start.19 = (bf16[64,6144]{1,0:T(8,128)(2,1)S(1)}, bf16[64,6144]{1,0:T(8,128)(2,1)S(1)}, u32[]{:S(2)}, u32[]{:S(2)}) collective-permute-start(bf16[64,6144]{1,0:T(8,128)(2,1)S(1)} %constant_dynamic-update-slice_fusion.14.refs_0_), channel_id=1, source_target_pairs={{0,1},{1,0},{2,3},{3,2},{4,5},{5,4},{6,7},{7,6},{8,9},{9,8},{10,11... | collective-permute-start | bytes 2359304 | tf_op jit(solution)/shard_map/ppermute | solution.py:30
  103.8 11.5 %collective-permute-start.20 = (bf16[32,6144]{1,0:T(8,128)(2,1)S(1)}, bf16[32,6144]{1,0:T(8,128)(2,1)S(1)}, u32[]{:S(2)}, u32[]{:S(2)}) collective-permute-start(bf16[32,6144]{1,0:T(8,128)(2,1)S(1)} %collective-permute-done.15), channel_id=1, source_target_pairs={{0,8},{1,9},{2,10},{3,11},{4,12},{5,13},{6,14},{7,15},{8,0},{9,1},... | collective-permute-start | bytes 1179656 | tf_op jit(solution)/shard_map/ppermute | solution.py:30
  117.4 16.5 %collective-permute-start.28 = (bf16[64,6144]{1,0:T(8,128)(2,1)S(1)}, bf16[64,6144]{1,0:T(8,128)(2,1)S(1)}, u32[]{:S(2)}, u32[]{:S(2)}) collective-permute-start(bf16[64,6144]{1,0:T(8,128)(2,1)S(1)} %constant_dynamic-update-slice_fusion.16.refs_0_), channel_id=1, source_target_pairs={{0,1},{1,0},{2,3},{3,2},{4,5},{5,4},{6,7},{7,6},{8,9},{9,8},{10,11... | collective-permute-start | bytes 2359304 | tf_op jit(solution)/shard_map/ppermute | solution.py:30
  117.7 16.2 %collective-permute-start.29 = (bf16[64,6144]{1,0:T(8,128)(2,1)S(1)}, bf16[64,6144]{1,0:T(8,128)(2,1)S(1)}, u32[]{:S(2)}, u32[]{:S(2)}) collective-permute-start(bf16[64,6144]{1,0:T(8,128)(2,1)S(1)} %add_convert_fusion.2), channel_id=1, source_target_pairs={{0,2},{1,5},{2,0},{3,7},{4,6},{5,1},{6,4},{7,3},{8,10},{9,13},{10,... | collective-permute-start | bytes 2359304 | tf_op jit(solution)/shard_map/ppermute | solution.py:30
  119.1 11.5 %collective-permute-start.27 = (bf16[32,6144]{1,0:T(8,128)(2,1)S(1)}, bf16[32,6144]{1,0:T(8,128)(2,1)S(1)}, u32[]{:S(2)}, u32[]{:S(2)}) collective-permute-start(bf16[32,6144]{1,0:T(8,128)(2,1)S(1)} %slice.163), channel_id=1, source_target_pairs={{0,8},{1,9},{2,10},{3,11},{4,12},{5,13},{6,14},{7,15},{8,0},{9,1},... | collective-permute-start | bytes 1179656 | tf_op jit(solution)/shard_map/ppermute | solution.py:30
  119.4 14.5 %collective-permute-start.26 = (bf16[32,6144]{1,0:T(8,128)(2,1)S(1)}, bf16[32,6144]{1,0:T(8,128)(2,1)S(1)}, u32[]{:S(2)}, u32[]{:S(2)}) collective-permute-start(bf16[32,6144]{1,0:T(8,128)(2,1)S(1)} %collective-permute-done.16), channel_id=1, source_target_pairs={{0,2},{1,5},{2,0},{3,7},{4,6},{5,1},{6,4},{7,3},{8,10},{9,13},{10,... | collective-permute-start | bytes 1179656 | tf_op jit(solution)/shard_map/ppermute | solution.py:30
  134.7 11.9 %collective-permute-start.31 = (bf16[32,6144]{1,0:T(8,128)(2,1)S(1)}, bf16[32,6144]{1,0:T(8,128)(2,1)S(1)}, u32[]{:S(2)}, u32[]{:S(2)}) collective-permute-start(bf16[32,6144]{1,0:T(8,128)(2,1)S(1)} %add_convert_fusion.8), channel_id=1, source_target_pairs={{0,8},{1,9},{2,10},{3,11},{4,12},{5,13},{6,14},{7,15},{8,0},{9,1},... | collective-permute-start | bytes 1179656 | tf_op jit(solution)/shard_map/ppermute | solution.py:30
  135.1 12.0 %collective-permute-start.32 = (bf16[64,6144]{1,0:T(8,128)(2,1)S(1)}, bf16[64,6144]{1,0:T(8,128)(2,1)S(1)}, u32[]{:S(2)}, u32[]{:S(2)}) collective-permute-start(bf16[64,6144]{1,0:T(8,128)(2,1)S(1)} %add_convert_fusion.3), channel_id=1, source_target_pairs={{0,2},{1,5},{2,0},{3,7},{4,6},{5,1},{6,4},{7,3},{8,10},{9,13},{10,... | collective-permute-start | bytes 2359304 | tf_op jit(solution)/shard_map/ppermute | solution.py:30
  147.5 16.2 %collective-permute-start.40 = (bf16[64,6144]{1,0:T(8,128)(2,1)S(1)}, bf16[64,6144]{1,0:T(8,128)(2,1)S(1)}, u32[]{:S(2)}, u32[]{:S(2)}) collective-permute-start(bf16[64,6144]{1,0:T(8,128)(2,1)S(1)} %add_convert_fusion.1), channel_id=1, source_target_pairs={{0,2},{1,5},{2,0},{3,7},{4,6},{5,1},{6,4},{7,3},{8,10},{9,13},{10,... | collective-permute-start | bytes 2359304 | tf_op jit(solution)/shard_map/ppermute | solution.py:30
  149.3 14.8 %collective-permute-start.39 = (bf16[32,6144]{1,0:T(8,128)(2,1)S(1)}, bf16[32,6144]{1,0:T(8,128)(2,1)S(1)}, u32[]{:S(2)}, u32[]{:S(2)}) collective-permute-start(bf16[32,6144]{1,0:T(8,128)(2,1)S(1)} %get-tuple-element.265), channel_id=1, source_target_pairs={{0,4},{1,3},{2,6},{3,1},{4,0},{5,7},{6,2},{7,5},{8,12},{9,11},{10,... | collective-permute-start | bytes 1179656 | tf_op jit(solution)/shard_map/ppermute | solution.py:30
  150.5 13.5 %collective-permute-start.38 = (bf16[32,6144]{1,0:T(8,128)(2,1)S(1)}, bf16[32,6144]{1,0:T(8,128)(2,1)S(1)}, u32[]{:S(2)}, u32[]{:S(2)}) collective-permute-start(bf16[32,6144]{1,0:T(8,128)(2,1)S(1)} %convert_add_fusion.4), channel_id=1, source_target_pairs={{0,8},{1,9},{2,10},{3,11},{4,12},{5,13},{6,14},{7,15},{8,0},{9,1},... | collective-permute-start | bytes 1179656 | tf_op jit(solution)/shard_map/ppermute | solution.py:30
  164.8 11.8 %collective-permute-start.43 = (bf16[32,6144]{1,0:T(8,128)(2,1)S(1)}, bf16[32,6144]{1,0:T(8,128)(2,1)S(1)}, u32[]{:S(2)}, u32[]{:S(2)}) collective-permute-start(bf16[32,6144]{1,0:T(8,128)(2,1)S(1)} %get-tuple-element.277), channel_id=1, source_target_pairs={{0,2},{1,5},{2,0},{3,7},{4,6},{5,1},{6,4},{7,3},{8,10},{9,13},{10,... | collective-permute-start | bytes 1179656 | tf_op jit(solution)/shard_map/ppermute | solution.py:30
  178.1 11.9 %collective-permute-start.45 = (bf16[32,6144]{1,0:T(8,128)(2,1)}, bf16[32,6144]{1,0:T(8,128)(2,1)}, u32[]{:S(2)}, u32[]{:S(2)}) collective-permute-start(bf16[32,6144]{1,0:T(8,128)(2,1)} %get-tuple-element.241), channel_id=1, source_target_pairs={{0,2},{1,5},{2,0},{3,7},{4,6},{5,1},{6,4},{7,3},{8,10},{9,13},{10,... | collective-permute-start | bytes 1179656 | tf_op jit(solution)/shard_map/ppermute | solution.py:30
  179.6 14.0 %collective-permute-start.44 = (bf16[32,6144]{1,0:T(8,128)(2,1)}, bf16[32,6144]{1,0:T(8,128)(2,1)S(1)}, u32[]{:S(2)}, u32[]{:S(2)}) collective-permute-start(bf16[32,6144]{1,0:T(8,128)(2,1)} %add_convert_fusion.5), channel_id=1, source_target_pairs={{0,8},{1,9},{2,10},{3,11},{4,12},{5,13},{6,14},{7,15},{8,0},{9,1},... | collective-permute-start | bytes 1179656 | tf_op jit(solution)/shard_map/ppermute | solution.py:30
  179.8 13.8 %collective-permute-start.46 = (bf16[32,6144]{1,0:T(8,128)(2,1)S(1)}, bf16[32,6144]{1,0:T(8,128)(2,1)S(1)}, u32[]{:S(2)}, u32[]{:S(2)}) collective-permute-start(bf16[32,6144]{1,0:T(8,128)(2,1)S(1)} %get-tuple-element.245), channel_id=1, source_target_pairs={{0,4},{1,3},{2,6},{3,1},{4,0},{5,7},{6,2},{7,5},{8,12},{9,11},{10,... | collective-permute-start | bytes 1179656 | tf_op jit(solution)/shard_map/ppermute | solution.py:30
  (51 other events, 390.6 us)

commit v10 on v9

--- a/solution.py
+++ b/solution.py
@@ -506,13 +506,12 @@
     b_z = z_step(b2_sum, z_masks[1])
     b1_got = exchange(b1_stays[0], last, count)
     a_out = total([hidden_a, a_sum, a_z]).astype(BF16)
-    b1_got, a_out = wait((b1_got, a_out))
     b1_sum = fold(total([b1_stays[1], b1_got]), b1_sent, steps)
-    a_out = deliver(a_out, None, place)
     b_z, b1_sum, a_out = wait((b_z, b1_sum, a_out))
     b_sum = b1_sum + [b_z]
     across = total([t[half_count:] for t in b_sum]).astype(BF16)
     b_out = deliver(total([hidden_b] + [t[:half_count] for t in b_sum]).astype(BF16), across, place)
+    a_out = deliver(a_out, None, place)
     out = jnp.zeros((n_hx, HALVES * half_count, across.shape[1] // n_hx), BF16)
     for to in a_out:
         rows = jnp.concatenate([a_out[to], b_out[to]], axis=0)

time: 211 us -> 213 us (level)
  waiting for transfers between devices: 93.2 us -> 98 us
    ppermute x57, waiting for transfers between devices: 81.7 us -> 86.5 us  [exchange(): return lax.ppermute(x, AXES, pairs)]
  transfers between devices with their start and end apart: 59 -> 59, of which waited for: 30 -> 30; matrix products, arithmetic and copies ran while one was open for 5% -> 4% of each run, Pallas kernels for 17% -> 17%
where the time goes in v10:
time: 213 us
  waiting for transfers between devices  98 us (46%)
  starting transfers between devices  56.4 us (26%)
  Pallas kernels  39.5 us (19%)
  matrix products  6.41 us (3%)
  local copies, waits for them, and re-layouts  6.07 us (3%)
  other arithmetic  5.42 us (3%)
    ppermute x57, waiting for transfers between devices, exchange(): return lax.ppermute(x, AXES, pairs)  86.5 us
    ppermute x57, starting transfers between devices, exchange(): return lax.ppermute(x, AXES, pairs)  45.5 us
    pallas_call x4, Pallas kernels, expert(): pl.pallas_call(functools.partial(expert_kernel, blocks), in_specs=[whole(...  26.3 us
    all_to_all x1, starting transfers between devices, shards(): lax.all_to_all(payload, 'seq', split_axis=0, concat_axis=0, tiled=True)  7.29 us
    pallas_call x1, Pallas kernels, load(): pl.pallas_call(load_kernel, in_specs=[pl.BlockSpec(memory_space=pltpu.HBM...  7.06 us
    dot_general x1, matrix products, shards(): jnp.dot(attn_in, out_weight, preferred_element_type=F32).astype(BF16)  6.41 us
    pallas_call x4, Pallas kernels, call(): pl.pallas_call(kernel, in_specs=specs + [whole()] * (len(operands) - len(...  6.17 us
    all_to_all x1, waiting for transfers between devices, shards(): lax.all_to_all(payload, 'seq', split_axis=0, concat_axis=0, tiled=True)  6.01 us
  transfers between devices with their start and end apart: 59, of which 30 were waited for; matrix products, arithmetic and copies ran while one was open for 4% of the time, Pallas kernels for 17%

profile of v10, /device:TPU:0, one launch (start us, length us, event | category | flops | bytes accessed | tf_op | source)
XLA Modules:
  0.0 212.7 jit_solution(13596943476226730611)
XLA Ops:
  0.0 2.6 %shard_map.164 = bf16[8,144,128]{2,1,0:T(8,128)(2,1)} custom-call(s32[1]{0:T(128)} %bitcast.2.me_ref, f32[8,128]{1,0:T(8,128)} %bitcast.42, s32[1,128]{1,0:T(1,128)} %bitcast.44, s32[2,128]{1,0:T(2,128)} %bitcast.46, f32[2,128]{1,0:T(2,128)} %bitcast.47, bf16[128,1024]{1,0:T(8,128)(2,1)} %refs_4_.3, bf16[128,1024]{1,0:T(8,128)(2,1)} %refs_5_.1), custom_call_target="tpu_custom_call" | custom-call | tf_op jit(solution)/shard_map/pallas_call | solution.py:264
  2.6 7.3 %all-to-all-start = ((bf16[8,144,128]{2,1,0:T(8,128)(2,1)}), bf16[8,144,128]{2,1,0:T(8,128)(2,1)S(1)}, u32[]{:S(2)}, u32[]{:S(2)}) async-start(bf16[8,144,128]{2,1,0:T(8,128)(2,1)} %shard_map.164), calls=%async_computation | async-start | bytes 589824 | tf_op jit(solution)/shard_map/all_to_all | solution.py:317
  13.5 6.0 %all-to-all-done.in_ref = bf16[8,144,128]{2,1,0:T(8,128)(2,1)S(1)} async-done(((bf16[8,144,128]{2,1,0:T(8,128)(2,1)}), bf16[8,144,128]{2,1,0:T(8,128)(2,1)S(1)}, u32[]{:S(2)}, u32[]{:S(2)}) %all-to-all-start) | async-done | bytes 294944 | tf_op jit(solution)/shard_map/all_to_all | solution.py:317
  20.3 3.6 %all-to-all-start.1 = ((bf16[8,128,128]{2,1,0:T(8,128)(2,1)}), bf16[8,128,128]{2,1,0:T(8,128)(2,1)S(1)}, u32[]{:S(2)}, u32[]{:S(2)}) async-start(bf16[8,128,128]{2,1,0:T(8,128)(2,1)} %shard_map.165), calls=%async_computation.1 | async-start | bytes 524288 | tf_op jit(solution)/shard_map/all_to_all | solution.py:325
  26.9 5.5 %all-to-all-done.1.state_ref = bf16[8,128,128]{2,1,0:T(8,128)(2,1)S(1)} async-done(((bf16[8,128,128]{2,1,0:T(8,128)(2,1)}), bf16[8,128,128]{2,1,0:T(8,128)(2,1)S(1)}, u32[]{:S(2)}, u32[]{:S(2)}) %all-to-all-start.1) | async-done | bytes 262176 | tf_op jit(solution)/shard_map/all_to_all | solution.py:325
  32.8 6.4 %convolution_convert_fusion = bf16[128,6144]{1,0:T(8,128)(2,1)S(1)} fusion(bf16[128,1024]{1,0:T(8,128)(2,1)S(1)} %shard_map.166, bf16[1024,6144]{1,0:T(8,128)(2,1)} %param.23), kind=kOutput, calls=%fused_computation.4 | convolution fusion | flops 1611399168 | bytes 14417920 | tf_op jit(solution)/shard_map/dot_general | solution.py:359
  42.8 5.4 %collective-permute-done.1 = bf16[16,6144]{1,0:T(8,128)(2,1)S(1)} collective-permute-done((bf16[16,6144]{1,0:T(8,128)(2,1)S(1)}, bf16[16,6144]{1,0:T(8,128)(2,1)S(1)}, u32[]{:S(2)}, u32[]{:S(2)}) %collective-permute-start.1) | collective-permute-done | bytes 196640 | tf_op jit(solution)/shard_map/ppermute | solution.py:30
  50.3 7.1 %shard_map.167 = (bf16[576,6144]{1,0:T(8,128)(2,1)S(1)}, bf16[576,6144]{1,0:T(8,128)(2,1)S(1)}, bf16[576,6144]{1,0:T(8,128)(2,1)S(1)}, f32[8,128]{1,0:T(8,128)S(1)}) custom-call(bf16[1,576,6144]{2,1,0:T(8,128)(2,1)} %bitcast.36, bf16[1,576,6144]{2,1,0:T(8,128)(2,1)} %bitcast.37, bf16[1,576,6144]{2,1,0:T(8,128)(2,1)} %refs_2_.2), custom_call_target="tpu_custom_call" | custom-call | tf_op jit(solution)/shard_map/pallas_call | solution.py:208
  57.3 2.6 %collective-permute-done.3 = bf16[16,6144]{1,0:T(8,128)(2,1)S(1)} collective-permute-done((bf16[16,6144]{1,0:T(8,128)(2,1)S(1)}, bf16[16,6144]{1,0:T(8,128)(2,1)S(1)}, u32[]{:S(2)}, u32[]{:S(2)}) %collective-permute-start.3) | collective-permute-done | bytes 196640 | tf_op jit(solution)/shard_map/ppermute | solution.py:30
  63.3 4.7 %collective-permute-done.8 = bf16[16,6144]{1,0:T(8,128)(2,1)S(1)} collective-permute-done((bf16[16,6144]{1,0:T(8,128)(2,1)S(1)}, bf16[16,6144]{1,0:T(8,128)(2,1)S(1)}, u32[]{:S(2)}, u32[]{:S(2)}) %collective-permute-start.8) | collective-permute-done | bytes 196640 | tf_op jit(solution)/shard_map/ppermute | solution.py:30
  69.4 2.7 %collective-permute-done.7 = bf16[32,6144]{1,0:T(8,128)(2,1)S(1)} collective-permute-done((bf16[32,6144]{1,0:T(8,128)(2,1)S(1)}, bf16[32,6144]{1,0:T(8,128)(2,1)S(1)}, u32[]{:S(2)}, u32[]{:S(2)}) %collective-permute-start.7) | collective-permute-done | bytes 393248 | tf_op jit(solution)/shard_map/ppermute | solution.py:30
  76.4 6.1 %collective-permute-done.12 = bf16[16,6144]{1,0:T(8,128)(2,1)S(1)} collective-permute-done((bf16[16,6144]{1,0:T(8,128)(2,1)S(1)}, bf16[16,6144]{1,0:T(8,128)(2,1)S(1)}, u32[]{:S(2)}, u32[]{:S(2)}) %collective-permute-start.12) | collective-permute-done | bytes 196640 | tf_op jit(solution)/shard_map/ppermute | solution.py:30
  90.5 6.4 %shard_map.168 = (bf16[64,6144]{1,0:T(8,128)(2,1)S(1)}, bf16[64,6144]{1,0:T(8,128)(2,1)S(1)}, bf16[64,6144]{1,0:T(8,128)(2,1)S(1)}, bf16[64,6144]{1,0:T(8,128)(2,1)S(1)}) custom-call(bf16[64,6144]{1,0:T(8,128)(2,1)S(1)} %bitcast.33, bf16[64,6144]{1,0:T(8,128)(2,1)S(1)} %bitcast.35, bf16[64,6144]{1,0:T(8,128)(2,1)S(1)} %collective-permute-done.10.refs_2_, ...), custom_call_target="tpu_custom_call" | custom-call | flops 1000 | bytes 1000 | tf_op jit(solution)/shard_map/pallas_call | solution.py:244
  105.8 6.7 %shard_map.169 = (bf16[64,6144]{1,0:T(8,128)(2,1)S(1)}, bf16[64,6144]{1,0:T(8,128)(2,1)S(1)}, bf16[64,6144]{1,0:T(8,128)(2,1)S(1)}, bf16[64,6144]{1,0:T(8,128)(2,1)S(1)}) custom-call(bf16[64,6144]{1,0:T(8,128)(2,1)S(1)} %constant_dynamic-update-slice_fusion.12.refs_0_, bf16[64,6144]{1,0:T(8,128)(2,1)S(1)} %collective-permute-done.13.refs_1_, ...), custom_call_target="tpu_custom_call" | custom-call | flops 1000 | bytes 1000 | tf_op jit(solution)/shard_map/pallas_call | solution.py:244
  120.2 6.4 %shard_map.170 = (bf16[64,6144]{1,0:T(8,128)(2,1)S(1)}, bf16[64,6144]{1,0:T(8,128)(2,1)S(1)}, bf16[64,6144]{1,0:T(8,128)(2,1)S(1)}, bf16[64,6144]{1,0:T(8,128)(2,1)S(1)}) custom-call(bf16[64,6144]{1,0:T(8,128)(2,1)S(1)} %constant_dynamic-update-slice_fusion.14.refs_0_, bf16[64,6144]{1,0:T(8,128)(2,1)S(1)} %collective-permute-done.18.refs_1_, ...), custom_call_target="tpu_custom_call" | custom-call | flops 1000 | bytes 1000 | tf_op jit(solution)/shard_map/pallas_call | solution.py:244
  126.7 4.0 %collective-permute-done.27 = bf16[32,6144]{1,0:T(8,128)(2,1)S(1)} collective-permute-done((bf16[32,6144]{1,0:T(8,128)(2,1)S(1)}, bf16[32,6144]{1,0:T(8,128)(2,1)S(1)}, u32[]{:S(2)}, u32[]{:S(2)}) %collective-permute-start.27) | collective-permute-done | bytes 393248 | tf_op jit(solution)/shard_map/ppermute | solution.py:30
  130.7 3.4 %collective-permute-done.26 = bf16[32,6144]{1,0:T(8,128)(2,1)S(1)} collective-permute-done((bf16[32,6144]{1,0:T(8,128)(2,1)S(1)}, bf16[32,6144]{1,0:T(8,128)(2,1)S(1)}, u32[]{:S(2)}, u32[]{:S(2)}) %collective-permute-start.26) | collective-permute-done | bytes 393248 | tf_op jit(solution)/shard_map/ppermute | solution.py:30
  137.4 6.7 %shard_map.171 = (bf16[64,6144]{1,0:T(8,128)(2,1)S(1)}, bf16[64,6144]{1,0:T(8,128)(2,1)S(1)}, bf16[64,6144]{1,0:T(8,128)(2,1)S(1)}, bf16[64,6144]{1,0:T(8,128)(2,1)S(1)}) custom-call(bf16[64,6144]{1,0:T(8,128)(2,1)S(1)} %constant_dynamic-update-slice_fusion.16.refs_0_, bf16[64,6144]{1,0:T(8,128)(2,1)S(1)} %constant_dynamic-update-slice_fusion.18.refs_1_, ...), custom_call_target="tpu_custom_call" | custom-call | flops 1000 | bytes 1000 | tf_op jit(solution)/shard_map/pallas_call | solution.py:244
  151.6 12.3 %collective-permute-done.40 = bf16[64,6144]{1,0:T(8,128)(2,1)S(1)} collective-permute-done((bf16[64,6144]{1,0:T(8,128)(2,1)S(1)}, bf16[64,6144]{1,0:T(8,128)(2,1)S(1)}, u32[]{:S(2)}, u32[]{:S(2)}) %collective-permute-start.40) | collective-permute-done | bytes 786464 | tf_op jit(solution)/shard_map/ppermute | solution.py:30
  169.5 7.2 %collective-permute-done.43 = bf16[32,6144]{1,0:T(8,128)(2,1)S(1)} collective-permute-done((bf16[32,6144]{1,0:T(8,128)(2,1)S(1)}, bf16[32,6144]{1,0:T(8,128)(2,1)S(1)}, u32[]{:S(2)}, u32[]{:S(2)}) %collective-permute-start.43) | collective-permute-done | bytes 393248 | tf_op jit(solution)/shard_map/ppermute | solution.py:30
  180.3 9.8 %collective-permute-done.45 = bf16[32,6144]{1,0:T(8,128)(2,1)} collective-permute-done((bf16[32,6144]{1,0:T(8,128)(2,1)}, bf16[32,6144]{1,0:T(8,128)(2,1)}, u32[]{:S(2)}, u32[]{:S(2)}) %collective-permute-start.45) | collective-permute-done | bytes 393248 | tf_op jit(solution)/shard_map/ppermute | solution.py:30
  195.7 2.4 %collective-permute-start.47 = (bf16[16,1536]{1,0:T(8,128)(2,1)S(1)}, bf16[16,1536]{1,0:T(8,128)(2,1)S(1)}, u32[]{:S(2)}, u32[]{:S(2)}) collective-permute-start(bf16[16,1536]{1,0:T(8,128)(2,1)S(1)} %get-tuple-element.275), channel_id=1, source_target_pairs={{0,16},{1,17},{2,18},{3,19},{4,20},{5,21},{6,22},{7,23},{8,24},{9,... | collective-permute-start | bytes 147464 | tf_op jit(solution)/shard_map/ppermute | solution.py:30
  199.0 4.8 %collective-permute-done.47 = bf16[16,1536]{1,0:T(8,128)(2,1)S(1)} collective-permute-done((bf16[16,1536]{1,0:T(8,128)(2,1)S(1)}, bf16[16,1536]{1,0:T(8,128)(2,1)S(1)}, u32[]{:S(2)}, u32[]{:S(2)}) %collective-permute-start.47) | collective-permute-done | bytes 49184 | tf_op jit(solution)/shard_map/ppermute | solution.py:30
  208.7 3.2 %collective-permute-done.52 = bf16[16,1536]{1,0:T(8,128)(2,1)S(1)} collective-permute-done((bf16[16,1536]{1,0:T(8,128)(2,1)S(1)}, bf16[16,1536]{1,0:T(8,128)(2,1)S(1)}, u32[]{:S(2)}, u32[]{:S(2)}) %collective-permute-start.52) | collective-permute-done | bytes 49184 | tf_op jit(solution)/shard_map/ppermute | solution.py:30
  (209 shorter events, 78.5 us)
Async XLA Ops:
  2.6 16.9 %all-to-all-start = ((bf16[8,144,128]{2,1,0:T(8,128)(2,1)}), bf16[8,144,128]{2,1,0:T(8,128)(2,1)S(1)}, u32[]{:S(2)}, u32[]{:S(2)}) async-start(bf16[8,144,128]{2,1,0:T(8,128)(2,1)} %shard_map.164), calls=%async_computation | async-start | bytes 589824 | tf_op jit(solution)/shard_map/all_to_all | solution.py:317
  20.3 12.1 %all-to-all-start.1 = ((bf16[8,128,128]{2,1,0:T(8,128)(2,1)}), bf16[8,128,128]{2,1,0:T(8,128)(2,1)S(1)}, u32[]{:S(2)}, u32[]{:S(2)}) async-start(bf16[8,128,128]{2,1,0:T(8,128)(2,1)} %shard_map.165), calls=%async_computation.1 | async-start | bytes 524288 | tf_op jit(solution)/shard_map/all_to_all | solution.py:325
  73.4 11.6 %collective-permute-start.10 = (bf16[64,6144]{1,0:T(8,128)(2,1)S(1)}, bf16[64,6144]{1,0:T(8,128)(2,1)S(1)}, u32[]{:S(2)}, u32[]{:S(2)}) collective-permute-start(bf16[64,6144]{1,0:T(8,128)(2,1)S(1)} %bitcast.32), channel_id=1, source_target_pairs={{0,1},{1,0},{2,3},{3,2},{4,5},{5,4},{6,7},{7,6},{8,9},{9,8},{10,11... | collective-permute-start | bytes 2359304 | tf_op jit(solution)/shard_map/ppermute | solution.py:30
  73.5 11.5 %collective-permute-start.9 = (bf16[32,6144]{1,0:T(8,128)(2,1)S(1)}, bf16[32,6144]{1,0:T(8,128)(2,1)S(1)}, u32[]{:S(2)}, u32[]{:S(2)}) collective-permute-start(bf16[32,6144]{1,0:T(8,128)(2,1)S(1)} %constant_dynamic-update-slice_fusion.10), channel_id=1, source_target_pairs={{0,2},{1,5},{2,0},{3,7},{4,6},{5,1},{6,4},{7,3},{8,10},{9,13},{10,... | collective-permute-start | bytes 1179656 | tf_op jit(solution)/shard_map/ppermute | solution.py:30
  85.6 16.3 %collective-permute-start.13 = (bf16[64,6144]{1,0:T(8,128)(2,1)S(1)}, bf16[64,6144]{1,0:T(8,128)(2,1)S(1)}, u32[]{:S(2)}, u32[]{:S(2)}) collective-permute-start(bf16[64,6144]{1,0:T(8,128)(2,1)S(1)} %constant_dynamic-update-slice_fusion.12.refs_0_), channel_id=1, source_target_pairs={{0,2},{1,5},{2,0},{3,7},{4,6},{5,1},{6,4},{7,3},{8,10},{9,13},{10,... | collective-permute-start | bytes 2359304 | tf_op jit(solution)/shard_map/ppermute | solution.py:30
  87.0 14.8 %collective-permute-start.14 = (bf16[64,6144]{1,0:T(8,128)(2,1)S(1)}, bf16[64,6144]{1,0:T(8,128)(2,1)S(1)}, u32[]{:S(2)}, u32[]{:S(2)}) collective-permute-start(bf16[64,6144]{1,0:T(8,128)(2,1)S(1)} %constant_dynamic-update-slice_fusion.12.refs_0_), channel_id=1, source_target_pairs={{0,1},{1,0},{2,3},{3,2},{4,5},{5,4},{6,7},{7,6},{8,9},{9,8},{10,11... | collective-permute-start | bytes 2359304 | tf_op jit(solution)/shard_map/ppermute | solution.py:30
  87.3 12.1 %collective-permute-start.15 = (bf16[32,6144]{1,0:T(8,128)(2,1)S(1)}, bf16[32,6144]{1,0:T(8,128)(2,1)S(1)}, u32[]{:S(2)}, u32[]{:S(2)}) collective-permute-start(bf16[32,6144]{1,0:T(8,128)(2,1)S(1)} %pad_maximum_fusion.3), channel_id=1, source_target_pairs={{0,4},{1,3},{2,6},{3,1},{4,0},{5,7},{6,2},{7,5},{8,12},{9,11},{10,... | collective-permute-start | bytes 1179656 | tf_op jit(solution)/shard_map/ppermute | solution.py:30
  102.5 13.0 %collective-permute-start.18 = (bf16[64,6144]{1,0:T(8,128)(2,1)S(1)}, bf16[64,6144]{1,0:T(8,128)(2,1)S(1)}, u32[]{:S(2)}, u32[]{:S(2)}) collective-permute-start(bf16[64,6144]{1,0:T(8,128)(2,1)S(1)} %constant_dynamic-update-slice_fusion.14.refs_0_), channel_id=1, source_target_pairs={{0,2},{1,5},{2,0},{3,7},{4,6},{5,1},{6,4},{7,3},{8,10},{9,13},{10,... | collective-permute-start | bytes 2359304 | tf_op jit(solution)/shard_map/ppermute | solution.py:30
  103.9 11.5 %collective-permute-start.19 = (bf16[64,6144]{1,0:T(8,128)(2,1)S(1)}, bf16[64,6144]{1,0:T(8,128)(2,1)S(1)}, u32[]{:S(2)}, u32[]{:S(2)}) collective-permute-start(bf16[64,6144]{1,0:T(8,128)(2,1)S(1)} %constant_dynamic-update-slice_fusion.14.refs_0_), channel_id=1, source_target_pairs={{0,1},{1,0},{2,3},{3,2},{4,5},{5,4},{6,7},{7,6},{8,9},{9,8},{10,11... | collective-permute-start | bytes 2359304 | tf_op jit(solution)/shard_map/ppermute | solution.py:30
  117.5 16.5 %collective-permute-start.28 = (bf16[64,6144]{1,0:T(8,128)(2,1)S(1)}, bf16[64,6144]{1,0:T(8,128)(2,1)S(1)}, u32[]{:S(2)}, u32[]{:S(2)}) collective-permute-start(bf16[64,6144]{1,0:T(8,128)(2,1)S(1)} %constant_dynamic-update-slice_fusion.16.refs_0_), channel_id=1, source_target_pairs={{0,1},{1,0},{2,3},{3,2},{4,5},{5,4},{6,7},{7,6},{8,9},{9,8},{10,11... | collective-permute-start | bytes 2359304 | tf_op jit(solution)/shard_map/ppermute | solution.py:30
  117.8 16.2 %collective-permute-start.29 = (bf16[64,6144]{1,0:T(8,128)(2,1)S(1)}, bf16[64,6144]{1,0:T(8,128)(2,1)S(1)}, u32[]{:S(2)}, u32[]{:S(2)}) collective-permute-start(bf16[64,6144]{1,0:T(8,128)(2,1)S(1)} %add_convert_fusion.2), channel_id=1, source_target_pairs={{0,2},{1,5},{2,0},{3,7},{4,6},{5,1},{6,4},{7,3},{8,10},{9,13},{10,... | collective-permute-start | bytes 2359304 | tf_op jit(solution)/shard_map/ppermute | solution.py:30
  119.4 14.6 %collective-permute-start.26 = (bf16[32,6144]{1,0:T(8,128)(2,1)S(1)}, bf16[32,6144]{1,0:T(8,128)(2,1)S(1)}, u32[]{:S(2)}, u32[]{:S(2)}) collective-permute-start(bf16[32,6144]{1,0:T(8,128)(2,1)S(1)} %collective-permute-done.16), channel_id=1, source_target_pairs={{0,2},{1,5},{2,0},{3,7},{4,6},{5,1},{6,4},{7,3},{8,10},{9,13},{10,... | collective-permute-start | bytes 1179656 | tf_op jit(solution)/shard_map/ppermute | solution.py:30
  134.8 11.9 %collective-permute-start.31 = (bf16[32,6144]{1,0:T(8,128)(2,1)S(1)}, bf16[32,6144]{1,0:T(8,128)(2,1)S(1)}, u32[]{:S(2)}, u32[]{:S(2)}) collective-permute-start(bf16[32,6144]{1,0:T(8,128)(2,1)S(1)} %add_convert_fusion.8), channel_id=1, source_target_pairs={{0,8},{1,9},{2,10},{3,11},{4,12},{5,13},{6,14},{7,15},{8,0},{9,1},... | collective-permute-start | bytes 1179656 | tf_op jit(solution)/shard_map/ppermute | solution.py:30
  135.2 12.0 %collective-permute-start.32 = (bf16[64,6144]{1,0:T(8,128)(2,1)S(1)}, bf16[64,6144]{1,0:T(8,128)(2,1)S(1)}, u32[]{:S(2)}, u32[]{:S(2)}) collective-permute-start(bf16[64,6144]{1,0:T(8,128)(2,1)S(1)} %add_convert_fusion.3), channel_id=1, source_target_pairs={{0,2},{1,5},{2,0},{3,7},{4,6},{5,1},{6,4},{7,3},{8,10},{9,13},{10,... | collective-permute-start | bytes 2359304 | tf_op jit(solution)/shard_map/ppermute | solution.py:30
  147.6 16.2 %collective-permute-start.40 = (bf16[64,6144]{1,0:T(8,128)(2,1)S(1)}, bf16[64,6144]{1,0:T(8,128)(2,1)S(1)}, u32[]{:S(2)}, u32[]{:S(2)}) collective-permute-start(bf16[64,6144]{1,0:T(8,128)(2,1)S(1)} %add_convert_fusion.1), channel_id=1, source_target_pairs={{0,2},{1,5},{2,0},{3,7},{4,6},{5,1},{6,4},{7,3},{8,10},{9,13},{10,... | collective-permute-start | bytes 2359304 | tf_op jit(solution)/shard_map/ppermute | solution.py:30
  149.3 14.8 %collective-permute-start.39 = (bf16[32,6144]{1,0:T(8,128)(2,1)S(1)}, bf16[32,6144]{1,0:T(8,128)(2,1)S(1)}, u32[]{:S(2)}, u32[]{:S(2)}) collective-permute-start(bf16[32,6144]{1,0:T(8,128)(2,1)S(1)} %get-tuple-element.255), channel_id=1, source_target_pairs={{0,4},{1,3},{2,6},{3,1},{4,0},{5,7},{6,2},{7,5},{8,12},{9,11},{10,... | collective-permute-start | bytes 1179656 | tf_op jit(solution)/shard_map/ppermute | solution.py:30
  150.6 13.5 %collective-permute-start.38 = (bf16[32,6144]{1,0:T(8,128)(2,1)S(1)}, bf16[32,6144]{1,0:T(8,128)(2,1)S(1)}, u32[]{:S(2)}, u32[]{:S(2)}) collective-permute-start(bf16[32,6144]{1,0:T(8,128)(2,1)S(1)} %convert_add_fusion.4), channel_id=1, source_target_pairs={{0,8},{1,9},{2,10},{3,11},{4,12},{5,13},{6,14},{7,15},{8,0},{9,1},... | collective-permute-start | bytes 1179656 | tf_op jit(solution)/shard_map/ppermute | solution.py:30
  164.9 11.8 %collective-permute-start.43 = (bf16[32,6144]{1,0:T(8,128)(2,1)S(1)}, bf16[32,6144]{1,0:T(8,128)(2,1)S(1)}, u32[]{:S(2)}, u32[]{:S(2)}) collective-permute-start(bf16[32,6144]{1,0:T(8,128)(2,1)S(1)} %get-tuple-element.267), channel_id=1, source_target_pairs={{0,2},{1,5},{2,0},{3,7},{4,6},{5,1},{6,4},{7,3},{8,10},{9,13},{10,... | collective-permute-start | bytes 1179656 | tf_op jit(solution)/shard_map/ppermute | solution.py:30
  178.0 12.1 %collective-permute-start.45 = (bf16[32,6144]{1,0:T(8,128)(2,1)}, bf16[32,6144]{1,0:T(8,128)(2,1)}, u32[]{:S(2)}, u32[]{:S(2)}) collective-permute-start(bf16[32,6144]{1,0:T(8,128)(2,1)} %get-tuple-element.236), channel_id=1, source_target_pairs={{0,2},{1,5},{2,0},{3,7},{4,6},{5,1},{6,4},{7,3},{8,10},{9,13},{10,... | collective-permute-start | bytes 1179656 | tf_op jit(solution)/shard_map/ppermute | solution.py:30
  179.6 11.6 %collective-permute-start.44 = (bf16[32,6144]{1,0:T(8,128)(2,1)}, bf16[32,6144]{1,0:T(8,128)(2,1)S(1)}, u32[]{:S(2)}, u32[]{:S(2)}) collective-permute-start(bf16[32,6144]{1,0:T(8,128)(2,1)} %add_convert_fusion.5), channel_id=1, source_target_pairs={{0,8},{1,9},{2,10},{3,11},{4,12},{5,13},{6,14},{7,15},{8,0},{9,1},... | collective-permute-start | bytes 1179656 | tf_op jit(solution)/shard_map/ppermute | solution.py:30
  192.2 12.0 %collective-permute-start.55 = (bf16[16,1536]{1,0:T(8,128)(2,1)S(1)}, bf16[16,1536]{1,0:T(8,128)(2,1)S(1)}, u32[]{:S(2)}, u32[]{:S(2)}) collective-permute-start(bf16[16,1536]{1,0:T(8,128)(2,1)S(1)} %get-tuple-element.272), channel_id=1, source_target_pairs={{0,19},{1,18},{2,17},{3,16},{4,23},{5,22},{6,21},{7,20},{8,27},{9,... | collective-permute-start | bytes 147464 | tf_op jit(solution)/shard_map/ppermute | solution.py:30
  194.5 14.2 %collective-permute-start.49 = (bf16[16,1536]{1,0:T(8,128)(2,1)S(1)}, bf16[16,1536]{1,0:T(8,128)(2,1)S(1)}, u32[]{:S(2)}, u32[]{:S(2)}) collective-permute-start(bf16[16,1536]{1,0:T(8,128)(2,1)S(1)} %get-tuple-element.274), channel_id=1, source_target_pairs={{0,18},{1,19},{2,16},{3,17},{4,22},{5,23},{6,20},{7,21},{8,26},{9,... | collective-permute-start | bytes 147464 | tf_op jit(solution)/shard_map/ppermute | solution.py:30
  198.2 13.7 %collective-permute-start.48 = (bf16[16,1536]{1,0:T(8,128)(2,1)S(1)}, bf16[16,1536]{1,0:T(8,128)(2,1)S(1)}, u32[]{:S(2)}, u32[]{:S(2)}) collective-permute-start(bf16[16,1536]{1,0:T(8,128)(2,1)S(1)} %get-tuple-element.270), channel_id=1, source_target_pairs={{0,2},{1,3},{2,0},{3,1},{4,6},{5,7},{6,4},{7,5},{8,10},{9,11},{10,... | collective-permute-start | bytes 147464 | tf_op jit(solution)/shard_map/ppermute | solution.py:30
  198.9 13.0 %collective-permute-start.53 = (bf16[16,1536]{1,0:T(8,128)(2,1)S(1)}, bf16[16,1536]{1,0:T(8,128)(2,1)S(1)}, u32[]{:S(2)}, u32[]{:S(2)}) collective-permute-start(bf16[16,1536]{1,0:T(8,128)(2,1)S(1)} %get-tuple-element.269), channel_id=1, source_target_pairs={{0,1},{1,0},{2,3},{3,2},{4,5},{5,4},{6,7},{7,6},{8,9},{9,8},{10,11... | collective-permute-start | bytes 147464 | tf_op jit(solution)/shard_map/ppermute | solution.py:30
  (44 other events, 361.9 us)
